TPU v7x, 256 devices: a whole 4x4x8 slice. The times are simulated.
256 devices in a mesh: ka: 8 (over z_hi, core), wa: 32 (over x, z_lo, y).
Axes of the slice: x: 4, y: 4, z: 8 (z_hi: 4, z_lo: 2; z = z_hi * 2 + z_lo), core: 2. Of those that a mesh axis runs over, the one named last changes fastest.
Arguments:
- coeff_val: bfloat16 [16, 128, 65536], P('ka', None, 'wa'), may hold values from -6 to 6
- coeff_cond: bfloat16 [16, 1024, 65536], P('ka', None, 'wa'), may hold values from -6 to 6
- miller: int32 [3, 65536], P(None, 'wa'), may hold values from -8 to 7
- energy_val: float32 [16, 128], P('ka'), may hold values from -12 to -1
- energy_cond: float32 [16, 1024], P('ka'), may hold values from 1 to 16
- orbit_val: bfloat16 [16, 128, 16384], P('ka', None, 'wa'), may hold values from -6 to 6
- orbit_cond: bfloat16 [16, 1024, 16384], P('ka', None, 'wa'), may hold values from -6 to 6
- zeta: bfloat16 [4096, 16384], P('wa'), may hold values from -0.046875 to 0.046875
- freqs: float32 [4], replicated, may hold values from 0.2 to 10
- kweight: int32 [16], P('ka'), may hold values from 1 to 8
Outputs:
- wing: float32 [3, 4, 4096], P(None, None, 'wa')
- head: float32 [3, 4], replicated
All inputs are finite; a program needn't handle non-finite values.
Results may differ from a plain program's by a relative error of at most 0.008.
Values sent between devices are 32-bit elements; how exact they have to be, the bound alone decides.
No kernel may reach another device: no remote copies, remote signals or barrier semaphores. Data moves between devices by JAX's collectives and lax.ppermute only.
A program may use at most 128 MiB of HBM per device.

v0:
```python
import jax
import jax.numpy as jnp
from jax import lax
from jax.sharding import PartitionSpec as P


def transition_factors(energy_gap, freqs):
    return 4.0 / (energy_gap[None] ** 2 + freqs[:, None, None] ** 2)


def local(
    coeff_val,
    coeff_cond,
    miller,
    energy_val,
    energy_cond,
    orbit_val,
    orbit_cond,
    zeta,
    freqs,
    kweight,
):
    kcount, nval, npw_dev = coeff_val.shape
    ncond = coeff_cond.shape[1]
    nfreq = freqs.shape[0]
    slab_rows = zeta.shape[0]
    pw_factor = float(npw_dev * lax.axis_size("wa")) ** (-0.5)
    pair_factor = float(nval * ncond) ** (-0.5)
    weights = kweight.astype(jnp.float32)
    weight_sum = jnp.sum(weights)
    momenta = miller.astype(jnp.float32)
    wing_acc = jnp.zeros((3 * nfreq, slab_rows), jnp.float32)
    head_acc = jnp.zeros((3, nfreq), jnp.float32)
    for kpoint in range(kcount):
        weighted = (coeff_val[kpoint][None] * momenta[:, None, :]).astype(jnp.bfloat16)
        partial_mom = jnp.einsum(
            "avg,cg->avc", weighted, coeff_cond[kpoint], preferred_element_type=jnp.float32
        )
        energy_gap = energy_cond[kpoint][None, :] - energy_val[kpoint][:, None]
        factors = transition_factors(energy_gap, freqs)
        momentum = lax.psum(partial_mom, "wa") * pw_factor
        head_term = jnp.sum(
            momentum[:, None] ** 2 * (factors / energy_gap[None])[None], axis=(2, 3)
        ) / float(nval * ncond)
        amplitude = (
            (momentum[:, None] * factors[None]).astype(jnp.bfloat16).reshape(3 * nfreq, nval, ncond)
        )
        expanded = jnp.einsum(
            "xvc,cm->xvm", amplitude, orbit_cond[kpoint], preferred_element_type=jnp.float32
        )
        pair_sum = (
            jnp.sum(orbit_val[kpoint].astype(jnp.float32)[None] * expanded, axis=1) * pair_factor
        )
        zeta_cols = zeta.astype(jnp.float32)
        wing_term = lax.dot_general(
            lax.all_gather(pair_sum, "wa", axis=1, tiled=True),
            zeta_cols,
            (((1,), (1,)), ((), ())),
            precision=lax.Precision.HIGHEST,
            preferred_element_type=jnp.float32,
        )
        wing_acc = wing_acc + weights[kpoint] * wing_term
        head_acc = head_acc + weights[kpoint] * head_term
    wing_all, head_all, weight_all = lax.psum((wing_acc, head_acc, weight_sum), "ka")
    return ((wing_all / weight_all).reshape(3, nfreq, slab_rows), head_all / weight_all)


def solution(mesh):
    return jax.shard_map(
        local,
        mesh=mesh,
        in_specs=(
            P("ka", None, "wa"),
            P("ka", None, "wa"),
            P(None, "wa"),
            P("ka", None),
            P("ka", None),
            P("ka", None, "wa"),
            P("ka", None, "wa"),
            P("wa", None),
            P(),
            P("ka"),
        ),
        out_specs=(P(None, None, "wa"), P()),
        check_vma=False,
    )
```

profile of v0, /device:TPU:8, one launch (start us, length us, event | category | flops | bytes accessed | tf_op | source)
XLA Modules:
  0.0 566.8 jit_solution(4453445485869951958)
XLA Ops:
  7.2 0.0 all-reduce.4.cloned.1.call-start
  7.2 0.8 convert_element_type.47
  8.0 0.0 slice-start
  8.0 1.6 bitcast_convert_fusion
  9.6 0.0 slice-start.1
  9.6 5.3 fusion
  14.9 0.0 slice-done
  14.9 0.0 slice-done.1
  14.9 3.0 fusion.2
  17.9 0.0 copy-start.8
  17.9 0.0 copy-start.9
  17.9 0.0 copy-start.6
  17.9 0.0 copy-start.5
  17.9 0.0 copy-start.4
  17.9 0.0 all-reduce.4.cloned.1.call-update
  18.0 0.6 copy-done.8
  18.6 0.0 copy-done.9
  18.6 0.6 fusion.22
  20.5 0.6 convert_reduce_fusion
  21.1 0.0 copy-done.6
  21.1 0.0 copy-done.5
  21.1 0.0 copy-done.4
  21.1 0.1 bitcast_convert_fusion.2
  21.2 0.2 broadcast_subtract_fusion
  21.4 3.2 fusion.6
  24.6 318.2 %all-reduce.4.cloned.1.call-done = (f32[3,128,1024]{2,1,0:T(8,128)}, f32[3,128,1024]{2,1,0:T(8,128)}) async-done(((f32[3,128,1024]{2,1,0:T(8,128)}, f32[3,128,1024]{2,1,0:T(8,128)}), (f32[3,128,1024]{2,1,0:T(8,128)}, f32[3,128,1024]{2,1,0:T(8,128)})) %all-reduce.4.cloned.1.call-update) | async-done | bytes 3145744 | tf_op jit(solution)/shard_map/psum | solution.py:41
  342.8 2.8 fusion.19
  345.6 0.0 copy-done.3
  345.6 0.0 copy-start.7
  345.6 0.7 multiply_convert_fusion.1
  346.4 0.8 copy-done.7
  347.2 1.9 multiply_reduce_fusion.3
  349.1 82.2 %all_gather.6 = f32[12,16384]{1,0:T(8,128)S(1)} all-gather(f32[12,512]{1,0:T(8,128)S(1)} %broadcast_multiply_fusion.3), channel_id=1, replica_groups=mesh['ka'=8,'wa'=32] {'wa'}, dimensions={1}, use_global_device_ids=true | all-gather | bytes 811008 | tf_op jit(solution)/shard_map/all_gather | solution.py:56
  431.4 0.0 copy-done.2
  431.4 0.7 multiply_convert_fusion
  432.1 0.0 copy-start.1
  432.1 1.9 multiply_reduce_fusion.2
  434.0 86.1 %all_gather.7 = f32[12,16384]{1,0:T(8,128)S(1)} all-gather(f32[12,512]{1,0:T(8,128)S(1)} %broadcast_multiply_fusion.2), channel_id=1, replica_groups=mesh['ka'=8,'wa'=32] {'wa'}, dimensions={1}, use_global_device_ids=true | all-gather | bytes 811008 | tf_op jit(solution)/shard_map/all_gather | solution.py:56
  520.1 0.0 copy-done.1
  520.1 0.8 multiply_reduce_fusion
  521.0 1.0 multiply_reduce_fusion.1
  522.0 0.4 copy-done
  522.3 4.0 convolution_multiply_fusion.1
  526.3 4.0 fusion.12
  530.4 27.2 %all-reduce.1 = (f32[12,128]{1,0:T(8,128)S(1)}, f32[]{:T(128)}, f32[3,4]{1,0:T(4,128)S(1)}) all-reduce(f32[12,128]{1,0:T(8,128)S(1)} %fusion.12, f32[]{:T(128)} %convert_reduce_fusion, f32[3,4]{1,0:T(4,128)S(1)} %multiply_add_fusion), channel_id=1, replica_groups=mesh['ka'=8,'wa'=32] {'ka'}, use_global_device_ids=true, to_apply=%region_4.0 | all-reduce | flops 1549 | bytes 12392 | tf_op jit(solution)/shard_map/psum | solution.py:64
  557.5 0.6 broadcast_divide_fusion
  558.2 0.6 reshape.170
  558.8 1.2 broadcast_divide_fusion.1
  (11 shorter events, 0.0 us)
Async XLA Ops:
  7.2 335.6 %all-reduce.4.cloned.1.call-start = ((), (), s32[]{:S(2)}) async-start(), calls=%async_computation | async-start | bytes 6291456 | tf_op jit(solution)/shard_map/psum | solution.py:41
  8.0 6.9 %slice-start = ((s8[8388608]{0:T(1024)(128)(4,1)}), s8[4194304]{0:T(1024)(128)(4,1)S(1)}, s32[]{:S(2)}) async-start(s8[8388608]{0:T(1024)(128)(4,1)} %bitcast.48), calls=%async_computation.1 | async-start | bytes 8388608
  9.6 5.4 slice-start.1
  17.9 0.7 copy-start.8
  17.9 0.7 copy-start.9
  17.9 3.2 copy-start.6
  17.9 3.2 copy-start.5
  17.9 3.2 copy-start.4
  342.8 2.8 copy-start.3
  345.6 1.6 copy-start.7
  347.2 84.1 %copy-start.2 = (f32[4,128,1024]{2,1,0:T(8,128)S(1)}, f32[4,128,1024]{2,1,0:T(8,128)}, u32[]{:S(2)}) copy-start(f32[4,128,1024]{2,1,0:T(8,128)} %get-tuple-element.27) | copy-start | bytes 6291460
  432.1 88.0 %copy-start.1 = (f32[4,128,1024]{2,1,0:T(8,128)S(1)}, f32[4,128,1024]{2,1,0:T(8,128)}, u32[]{:S(2)}) copy-start(f32[4,128,1024]{2,1,0:T(8,128)} %get-tuple-element.28) | copy-start | bytes 6291460
  520.1 2.2 copy-start
Sparse Core Ops, SparseCore 0:
  18.1 324.6 all-reduce.3
where the time goes:
time: 567 us
  waiting for transfers between devices  318 us (56%)
  blocking collectives  196 us (35%)
  matrix products  20 us (4%)
  between operations  15.5 us (3%)
  other arithmetic  14.5 us (3%)
    psum x1, waiting for transfers between devices, local(): momentum = lax.psum(partial_mom, 'wa') * pw_factor  318 us
    all_gather x2, blocking collectives, local(): lax.all_gather(pair_sum, 'wa', axis=1, tiled=True)  168 us
    psum x1, blocking collectives, local(): lax.psum((wing_acc, head_acc, weight_sum), 'ka')  27.2 us
  transfers between devices with their start and end apart: 1, of which 1 were waited for; matrix products, arithmetic and copies ran while one was open for 1% of the time, Pallas kernels for 0%

commit v1 on v0

v1 whole, which is shorter than its diff:
```python
import jax
import jax.numpy as jnp
from jax import lax
from jax.sharding import PartitionSpec as P


def split3(value):
    high = value.astype(jnp.bfloat16)
    rest = value - high.astype(jnp.float32)
    mid = rest.astype(jnp.bfloat16)
    low = (rest - mid.astype(jnp.float32)).astype(jnp.bfloat16)
    return high, mid, low


def everyone(value, axis):
    parts = lax.axis_size(axis)
    return lax.all_to_all(jnp.broadcast_to(value[None], (parts,) + value.shape), axis, 0, 0)


def local(
    coeff_val,
    coeff_cond,
    miller,
    energy_val,
    energy_cond,
    orbit_val,
    orbit_cond,
    zeta,
    freqs,
    kweight,
):
    kcount, nval, npw_dev = coeff_val.shape
    ncond = coeff_cond.shape[1]
    nfreq = freqs.shape[0]
    slab_rows = zeta.shape[0]
    ways = lax.axis_size("wa")
    rows = ncond // ways
    me = lax.axis_index("wa")
    points = orbit_val.shape[2]
    pw_factor = float(npw_dev * ways) ** (-0.5)
    pair_factor = float(nval * ncond) ** (-0.5)
    weights = kweight.astype(jnp.float32)
    momenta = miller.astype(jnp.float32)

    partials = []
    for kpoint in range(kcount):
        weighted = (coeff_val[kpoint][None] * momenta[:, None, :]).astype(jnp.bfloat16)
        partials.append(
            jnp.einsum("cg,avg->cav", coeff_cond[kpoint], weighted, preferred_element_type=jnp.float32)
        )
    partial_mom = jnp.stack(partials, axis=0).reshape(kcount, ways, rows, 3, nval)
    partial_mom = partial_mom.transpose(1, 0, 2, 3, 4)
    received = lax.all_to_all(partial_mom, "wa", 0, 0)
    mine = jnp.sum(received, axis=0) * pw_factor

    gap = energy_cond[:, :, None] - energy_val[:, None, :]
    factors = 4.0 / (gap[:, None] ** 2 + freqs[None, :, None, None] ** 2)

    my_gap = lax.dynamic_slice_in_dim(gap, me * rows, rows, 1)
    my_factors = lax.dynamic_slice_in_dim(factors, me * rows, rows, 2)
    ratio = weights[:, None, None, None] * my_factors / my_gap[:, None]
    head_part = jnp.einsum(
        "kcav,kwcv->aw", mine * mine, ratio, precision=lax.Precision.HIGHEST
    ) / float(nval * ncond)

    momentum = everyone(mine, "wa")
    momentum = momentum.transpose(1, 0, 2, 3, 4).reshape(kcount, ncond, 3, nval)
    pair = jnp.zeros((3 * nfreq, points), jnp.float32)
    for kpoint in range(kcount):
        amplitude = (
            momentum[kpoint][:, :, None, :] * factors[kpoint].transpose(1, 0, 2)[:, None]
        ).astype(jnp.bfloat16)
        expanded = jnp.einsum(
            "cxv,cm->xvm",
            amplitude.reshape(ncond, 3 * nfreq, nval),
            orbit_cond[kpoint],
            preferred_element_type=jnp.float32,
        )
        pair_k = jnp.sum(orbit_val[kpoint].astype(jnp.float32)[None] * expanded, axis=1)
        pair = pair + (weights[kpoint] * pair_factor) * pair_k

    tail = jnp.concatenate([head_part.reshape(-1), jnp.sum(weights)[None]])
    message = jnp.concatenate([pair, jnp.pad(tail, (0, points - tail.shape[0]))[None]], axis=0)
    gathered = everyone(message, "wa")
    tail = jnp.sum(gathered[:, 3 * nfreq, :slab_rows], axis=0)
    whole = gathered[:, : 3 * nfreq].transpose(1, 0, 2).reshape(3 * nfreq, ways * points)
    terms = lax.dot_general(
        jnp.concatenate(split3(whole), axis=0),
        zeta,
        (((1,), (1,)), ((), ())),
        preferred_element_type=jnp.float32,
    )
    wing = jnp.sum(terms.reshape(3, 3 * nfreq, slab_rows), axis=0)
    total = jnp.sum(everyone(jnp.concatenate([wing, tail[None]], axis=0), "ka"), axis=0)
    scale = 1.0 / (total[3 * nfreq, 3 * nfreq] / ways)
    wing = total[: 3 * nfreq] * scale
    head = total[3 * nfreq, : 3 * nfreq] * scale
    return wing.reshape(3, nfreq, slab_rows), head.reshape(3, nfreq)


def solution(mesh):
    return jax.shard_map(
        local,
        mesh=mesh,
        in_specs=(
            P("ka", None, "wa"),
            P("ka", None, "wa"),
            P(None, "wa"),
            P("ka", None),
            P("ka", None),
            P("ka", None, "wa"),
            P("ka", None, "wa"),
            P("wa", None),
            P(),
            P("ka"),
        ),
        out_specs=(P(None, None, "wa"), P()),
        check_vma=False,
    )
```

time: 567 us -> 173 us (0.31)
  waiting for transfers between devices: 318 us -> 18.5 us
  blocking collectives: 196 us -> 84.1 us
  local copies, waits for them, and re-layouts: 3.05 us -> 30.8 us
  between operations: 15.5 us -> 2.91 us
    psum x1 -> x0, waiting for transfers between devices: 318 us -> none  [local(): momentum = lax.psum(partial_mom, 'wa') * pw_factor]
    all_gather x2 -> x0, blocking collectives: 168 us -> none  [local(): lax.all_gather(pair_sum, 'wa', axis=1, tiled=True)]
    all_to_all x0 -> x3, blocking collectives: none -> 84.1 us  [the longest x1 47.7 us: local(): received = lax.all_to_all(partial_mom, 'wa', 0, 0)]
    psum x1 -> x0, blocking collectives: 27.2 us -> none  [local(): lax.psum((wing_acc, head_acc, weight_sum), 'ka')]
    all_to_all x0 -> x1, waiting for transfers between devices: none -> 18.5 us  [everyone(): lax.all_to_all(jnp.broadcast_to(value[None], (parts,) + value.shape), axi...]
    transpose x0 -> x6, local copies, waits for them, and re-layouts: none -> 10 us  [the longest x3 9.04 us: local(): factors[kpoint].transpose(1, 0, 2)[:, None]]
    mul x0 -> x3, local copies, waits for them, and re-layouts: none -> 6.88 us  [the longest x2 6.22 us: local(): momentum[kpoint][:, :, None, :]]
  transfers between devices with their start and end apart: 1 -> 1, of which waited for: 1 -> 1; matrix products, arithmetic and copies ran while one was open for 1% -> 12% of each run, Pallas kernels for 0% -> 0%
where the time goes in v1:
time: 173 us; the launch traced here: 172 us
  blocking collectives  84.1 us (49%)
  local copies, waits for them, and re-layouts  30.8 us (18%)
  waiting for transfers between devices  18.5 us (11%)
  matrix products  16.4 us (9%)
  other arithmetic  13.7 us (8%)
  starting transfers between devices  5.2 us (3%)
  between operations  2.91 us (2%)
    all_to_all x1, blocking collectives, local(): received = lax.all_to_all(partial_mom, 'wa', 0, 0)  47.7 us
    all_to_all x2, blocking collectives, everyone(): lax.all_to_all(jnp.broadcast_to(value[None], (parts,) + value.shape), axi...  36.4 us
    all_to_all x1, waiting for transfers between devices, everyone(): lax.all_to_all(jnp.broadcast_to(value[None], (parts,) + value.shape), axi...  18.5 us
    dot_general x2, matrix products, local(): jnp.einsum('cg,avg->cav', coeff_cond[kpoint], weighted, preferred_element...  9.52 us
    transpose x3, local copies, waits for them, and re-layouts, local(): factors[kpoint].transpose(1, 0, 2)[:, None]  9.04 us
    mul x2, local copies, waits for them, and re-layouts, local(): momentum[kpoint][:, :, None, :]  6.22 us
    all_to_all x1, starting transfers between devices, everyone(): lax.all_to_all(jnp.broadcast_to(value[None], (parts,) + value.shape), axi...  5.2 us
    unnamed x31, local copies, waits for them, and re-layouts  4.45 us
  transfers between devices with their start and end apart: 1, of which 1 were waited for; matrix products, arithmetic and copies ran while one was open for 12% of the time, Pallas kernels for 0%

profile of v1, /device:TPU:8, one launch (start us, length us, event | category | flops | bytes accessed | tf_op | source)
XLA Modules:
  0.0 171.5 jit_solution(16517598311180952880)
XLA Ops:
  0.6 2.4 %bitcast_convert_fusion.1 = (f32[128,2048]{1,0:T(8,128)}, f32[128,2048]{1,0:T(8,128)S(1)}) fusion(bf16[2,128,2048]{2,1,0:T(8,128)(2,1)} %param.10), kind=kLoop, calls=%fused_computation.40 | loop fusion | flops 524288 | bytes 3145728 | tf_op jit(solution)/shard_map/mul | solution.py:47
  3.1 4.0 %fusion.13 = f32[1024,3,128]{0,2,1:T(8,128)S(1)} fusion(bf16[2,1024,2048]{2,1,0:T(8,128)(2,1)} %param.11, f32[128,2048]{1,0:T(8,128)S(1)} %get-tuple-element.9, f32[3,2048]{1,0:T(4,128)S(1)} %convert_element_type.62), kind=kOutput, calls=%fused_computation.22 | convolution fusion | flops 1612185600 | bytes 6840320 | tf_op jit(solution)/shard_map/cg,avg->cav/dot_general | solution.py:49
  7.1 0.5 copy.49
  7.6 5.5 %fusion.10 = f32[1024,3,128]{0,2,1:T(8,128)} fusion(bf16[2,1024,2048]{2,1,0:T(8,128)(2,1)} %param.11, f32[3,2048]{1,0:T(4,128)S(1)} %convert_element_type.62, f32[128,2048]{1,0:T(8,128)} %get-tuple-element.8), kind=kOutput, calls=%fused_computation.21 | convolution fusion | flops 1612185600 | bytes 6840320 | tf_op jit(solution)/shard_map/cg,avg->cav/dot_general | solution.py:49
  13.1 1.9 %copy.48 = f32[1024,3,128]{2,0,1:T(8,128)S(1)} copy(f32[1024,3,128]{0,2,1:T(8,128)} %fusion.10) | data formatting | bytes 3145728 | tf_op jit(solution)/shard_map/cg,avg->cav/dot_general | solution.py:49
  14.9 0.3 maximum_bitcast_fusion
  15.3 0.4 copy.50
  15.7 47.7 %all_to_all.20 = f32[32,2,32,3,128]{4,2,3,1,0:T(8,128)S(1)} all-to-all(f32[32,2,32,3,128]{4,2,3,1,0:T(8,128)S(1)} %copy.50), channel_id=1, replica_groups=mesh['ka'=8,'wa'=32] {'wa'}, dimensions={0} | all-to-all | bytes 6291456 | tf_op jit(solution)/shard_map/all_to_all | solution.py:53
  63.4 0.2 reduce_sum.63
  63.6 2.1 %broadcast_in_dim.12 = f32[32,2,32,3,128]{4,2,3,1,0:T(8,128)} broadcast(f32[2,32,3,128]{3,1,2,0:T(8,128)S(1)} %get-tuple-element.14), dimensions={1,2,3,4} | broadcast | bytes 3244032 | tf_op jit(solution)/shard_map/broadcast_in_dim | solution.py:17
  65.7 5.2 %all-to-all-start.1 = ((f32[32,2,32,3,128]{4,2,3,1,0:T(8,128)}), f32[32,2,32,3,128]{4,2,3,1,0:T(8,128)S(1)}, u32[]{:S(2)}, u32[]{:S(2)}) async-start(f32[32,2,32,3,128]{4,2,3,1,0:T(8,128)} %broadcast_in_dim.12), calls=%async_computation.1 | async-start | bytes 6291456 | tf_op jit(solution)/shard_map/all_to_all | solution.py:17
  70.9 1.0 copy.54
  72.0 4.0 %broadcast_subtract_fusion = (f32[2,1024,128]{2,0,1:T(2,128)}, f32[2,1024,128]{2,0,1:T(2,128)S(1)}) fusion(f32[2,128]{1,0:T(2,128)S(1)} %copy-done.9, f32[2,1024]{0,1:T(8,128)} %copy.54), kind=kLoop, calls=%fused_computation.41 | loop fusion | flops 524288 | bytes 2106368 | tf_op jit(solution)/shard_map/sub | solution.py:56
  75.9 1.2 add_divide_fusion
  77.2 3.1 %slice_bitcast_fusion.1 = (f32[1024,4,128]{2,1,0:T(4,128)}, f32[1024,4,128]{2,1,0:T(4,128)}) fusion(f32[2,4,1024,128]{3,1,0,2:T(4,128)S(1)} %add_divide_fusion), kind=kLoop, calls=%fused_computation.16 | loop fusion | bytes 8388608 | tf_op jit(solution)/shard_map/transpose | solution.py:71
  80.3 0.1 copy-done
  80.4 3.0 %copy.57 = f32[1024,4,128]{0,2,1:T(8,128)} copy(f32[1024,4,128]{2,1,0:T(4,128)} %get-tuple-element.3) | data formatting | bytes 4194304 | tf_op jit(solution)/shard_map/transpose | solution.py:71
  83.4 3.0 %copy.55 = f32[1024,4,128]{0,2,1:T(8,128)} copy(f32[1024,4,128]{2,1,0:T(4,128)} %get-tuple-element.2) | data formatting | bytes 4194304 | tf_op jit(solution)/shard_map/transpose | solution.py:71
  86.4 0.6 fusion.37
  88.2 0.6 convert_reduce_fusion
  88.8 0.8 constant_dynamic-slice_fusion
  89.6 0.9 bitcast_convert_fusion.3
  90.5 1.6 fusion.22
  92.2 0.7 select_maximum_fusion
  92.9 18.5 %all-to-all-done.1 = f32[32,2,32,3,128]{4,2,3,1,0:T(8,128)S(1)} async-done(((f32[32,2,32,3,128]{4,2,3,1,0:T(8,128)}), f32[32,2,32,3,128]{4,2,3,1,0:T(8,128)S(1)}, u32[]{:S(2)}, u32[]{:S(2)}) %all-to-all-start.1) | async-done | bytes 3145760 | tf_op jit(solution)/shard_map/all_to_all | solution.py:17
  111.4 0.3 copy.71
  111.7 2.0 %fusion.36 = (f32[1,32,32,3,128]{4,2,1,3,0:T(8,128)}, f32[1,32,32,3,128]{4,2,1,3,0:T(8,128)}) fusion(f32[2,32,32,3,128]{4,2,1,3,0:T(8,128)S(1)} %bitcast.75), kind=kLoop, calls=%fused_computation.64 | loop fusion | bytes 6291456 | tf_op jit(solution)/shard_map/slice | solution.py:71
  113.7 3.2 %copy.56 = f32[1024,3,128]{0,2,1:T(8,128)} copy(f32[1024,3,128]{2,0,1:T(8,128)} %bitcast.80) | data formatting | bytes 3145728 | tf_op jit(solution)/shard_map/mul | solution.py:71
  116.9 3.0 %copy.53 = f32[1024,3,128]{0,2,1:T(8,128)} copy(f32[1024,3,128]{2,0,1:T(8,128)} %bitcast.79) | data formatting | bytes 3145728 | tf_op jit(solution)/shard_map/mul | solution.py:71
  119.9 2.3 %multiply_convert_fusion = bf16[1024,3,4,128]{0,3,2,1:T(8,128)(2,1)S(1)} fusion(f32[1024,4,128]{0,2,1:T(8,128)S(1)} %copy-done.1, f32[1024,3,128]{0,2,1:T(8,128)} %copy.56), kind=kLoop, calls=%fused_computation | loop fusion | flops 3145728 | bytes 6815744 | tf_op jit(solution)/shard_map/convert_element_type | solution.py:72
  122.2 0.2 copy-done.3
  122.4 0.7 multiply_convert_fusion.1
  123.2 0.2 copy-done.6
  123.4 0.7 copy-done.11
  124.1 1.9 %multiply_reduce_fusion = f32[12,512]{1,0:T(8,128)S(1)} fusion(bf16[1024,12,128]{0,2,1:T(8,128)(2,1)S(1)} %bitcast.84, f32[128,512]{1,0:T(8,128)S(1)} %copy-done.6, bf16[2,1024,512]{2,1,0:T(8,128)(2,1)S(1)} %copy-done.11), kind=kOutput, calls=%fused_computation.11 | convolution fusion | flops 1612179456 | bytes 4481024 | tf_op jit(solution)/shard_map/cxv,cm->xvm/dot_general | solution.py:73
  126.0 1.9 %multiply_reduce_fusion.1 = f32[12,512]{1,0:T(8,128)S(1)} fusion(bf16[1024,12,128]{0,2,1:T(8,128)(2,1)S(1)} %bitcast.83, f32[128,512]{1,0:T(8,128)S(1)} %copy-done.5, bf16[2,1024,512]{2,1,0:T(8,128)(2,1)S(1)} %copy-done.11), kind=kOutput, calls=%fused_computation.12 | convolution fusion | flops 1612179456 | bytes 4481024 | tf_op jit(solution)/shard_map/cxv,cm->xvm/dot_general | solution.py:73
  127.9 0.1 broadcast_in_dim.15
  128.1 20.8 %all_to_all.21 = f32[32,13,512]{2,1,0:T(8,128)S(1)} all-to-all(f32[32,13,512]{2,1,0:T(8,128)S(1)} %broadcast_in_dim.15), channel_id=1, replica_groups=mesh['ka'=8,'wa'=32] {'wa'}, dimensions={0} | all-to-all | bytes 1703936 | tf_op jit(solution)/shard_map/all_to_all | solution.py:17
  149.0 0.5 copy.59
  149.4 0.1 pad.18
  149.6 0.6 copy.67
  150.2 0.1 fusion.27
  150.4 1.4 copy-done.10
  151.8 1.5 fusion.16
  153.4 15.6 %all_to_all.22 = f32[8,13,128]{2,1,0:T(8,128)S(1)} all-to-all(f32[8,13,128]{2,1,0:T(8,128)S(1)} %broadcast_in_dim.17), channel_id=1, replica_groups=mesh['ka'=8,'wa'=32] {'ka'}, dimensions={0} | all-to-all | bytes 106496 | tf_op jit(solution)/shard_map/all_to_all | solution.py:17
  168.9 0.6 slice.85
  170.2 0.6 reshape.86
  170.8 0.7 mul.214
  (40 shorter events, 0.4 us)
Async XLA Ops:
  0.6 2.4 %copy-start.7 = (s32[3,2048]{1,0:T(4,128)S(1)}, s32[3,2048]{1,0:T(4,128)}, u32[]{:S(2)}) copy-start(s32[3,2048]{1,0:T(4,128)} %param.12) | copy-start | bytes 73732
  65.7 5.2 %copy-start.12 = (f32[4]{0:T(128)S(1)}, f32[4]{0:T(128)}, u32[]{:S(2)}) copy-start(f32[4]{0:T(128)} %param.18) | copy-start | bytes 52
  65.7 5.2 %copy-start.8 = (f32[2,1024]{1,0:T(2,128)S(1)}, f32[2,1024]{1,0:T(2,128)}, u32[]{:S(2)}) copy-start(f32[2,1024]{1,0:T(2,128)} %param.14) | copy-start | bytes 24580
  65.7 6.3 %copy-start.13 = (s32[2]{0:T(128)S(1)}, s32[2]{0:T(128)}, u32[]{:S(2)}) copy-start(s32[2]{0:T(128)} %param.19) | copy-start | bytes 28
  65.7 6.3 %copy-start.9 = (f32[2,128]{1,0:T(2,128)S(1)}, f32[2,128]{1,0:T(2,128)}, u32[]{:S(2)}) copy-start(f32[2,128]{1,0:T(2,128)} %param.13) | copy-start | bytes 3076
  65.7 45.7 %all-to-all-start.1 = ((f32[32,2,32,3,128]{4,2,3,1,0:T(8,128)}), f32[32,2,32,3,128]{4,2,3,1,0:T(8,128)S(1)}, u32[]{:S(2)}, u32[]{:S(2)}) async-start(f32[32,2,32,3,128]{4,2,3,1,0:T(8,128)} %broadcast_in_dim.12), calls=%async_computation.1 | async-start | bytes 6291456 | tf_op jit(solution)/shard_map/all_to_all | solution.py:17
  77.2 3.2 %copy-start = (f32[2,4,1024,128]{3,1,0,2:T(4,128)}, f32[2,4,1024,128]{3,1,0,2:T(4,128)S(1)}, u32[]{:S(2)}) copy-start(f32[2,4,1024,128]{3,1,0,2:T(4,128)S(1)} %add_divide_fusion) | copy-start | bytes 12582916
  83.4 6.2 %copy-start.4 = (bf16[2,128,512]{2,1,0:T(8,128)(2,1)S(1)}, bf16[2,128,512]{2,1,0:T(8,128)(2,1)}, u32[]{:S(2)}) copy-start(bf16[2,128,512]{2,1,0:T(8,128)(2,1)} %param.15) | copy-start | bytes 786436
  113.7 6.2 %copy-start.1 = (f32[1024,4,128]{0,2,1:T(8,128)S(1)}, f32[1024,4,128]{0,2,1:T(8,128)}, u32[]{:S(2)}) copy-start(f32[1024,4,128]{0,2,1:T(8,128)} %copy.57) | copy-start | bytes 6291460
  119.9 2.3 %copy-start.2 = (f32[1024,4,128]{0,2,1:T(8,128)S(1)}, f32[1024,4,128]{0,2,1:T(8,128)}, u32[]{:S(2)}) copy-start(f32[1024,4,128]{0,2,1:T(8,128)} %copy.55) | copy-start | bytes 6291460
  119.9 2.5 %copy-start.3 = (f32[1024,3,128]{0,2,1:T(8,128)S(1)}, f32[1024,3,128]{0,2,1:T(8,128)}, u32[]{:S(2)}) copy-start(f32[1024,3,128]{0,2,1:T(8,128)} %copy.53) | copy-start | bytes 4718596
  122.4 0.9 copy-start.6
  122.4 1.7 copy-start.11
  124.1 1.9 %copy-start.5 = (f32[128,512]{1,0:T(8,128)S(1)}, f32[128,512]{1,0:T(8,128)}, u32[]{:S(2)}) copy-start(f32[128,512]{1,0:T(8,128)} %get-tuple-element.12) | copy-start | bytes 786436
  149.6 2.2 %copy-start.10 = (bf16[128,16384]{1,0:T(8,128)(2,1)S(1)}, bf16[128,16384]{1,0:T(8,128)(2,1)}, u32[]{:S(2)}) copy-start(bf16[128,16384]{1,0:T(8,128)(2,1)} %param.17) | copy-start | bytes 12582916

commit v2 on v0

v2 whole, which is shorter than its diff:
```python
import functools

import jax
import jax.numpy as jnp
from jax import lax
from jax.experimental import pallas as pl
from jax.experimental.pallas import tpu as pltpu
from jax.sharding import PartitionSpec as P

MASKS = ((8, 24, 1, 3, 4), (1, 3, 8, 24, 4))
CB, VB = 4, 8
F32, BF16 = jnp.float32, jnp.bfloat16
VMEM, SMEM = pl.BlockSpec(memory_space=pltpu.VMEM), pl.BlockSpec(memory_space=pltpu.SMEM)
QUARTERS = (((0, 0), (1, 0), (0, 1), (2, 1)), ((2, 0), (3, 0), (1, 1), (3, 1)))


def code_of(index, kpoint):
    x, z, y = index >> 3, (index >> 2) & 1, index & 3
    pairs_x = (((x ^ (x >> 1)) & 1) << 1) | (x >> 1)
    pairs_y = (((y ^ (y >> 1)) & 1) << 1) | (y >> 1)
    return (pairs_x, pairs_y << 1 | z) if kpoint == 0 else (pairs_y, pairs_x << 1 | z)


def swap(value, axis, mask):
    size = lax.axis_size(axis)
    return lax.ppermute(value, axis, [(i, i ^ mask) for i in range(size)])


def everyone(value, axis):
    parts = lax.axis_size(axis)
    return lax.all_to_all(jnp.broadcast_to(value[None], (parts,) + value.shape), axis, 0, 0)


def scattered(parts, masks):
    keep_a, send_a, keep_b, send_b = parts
    got_a, got_b = swap(send_a, "wa", masks[0]), swap(send_b, "wa", masks[1])
    send_a, send_b = keep_a[VB:] + got_a[VB:], keep_b[VB:] + got_b[VB:]
    keep_a, keep_b = keep_a[:VB] + got_a[:VB], keep_b[:VB] + got_b[:VB]
    got_a, got_b = swap(send_a, "wa", masks[1]), swap(send_b, "wa", masks[0])
    half = VB // 2
    keep = jnp.stack([keep_a[:half] + got_a[:half], keep_b[:half] + got_b[:half]])
    send = jnp.stack([keep_a[half:] + got_a[half:], keep_b[half:] + got_b[half:]])
    got = swap(send, "wa", masks[2])
    half = half // 2
    keep, send = keep[:, :half] + got[:, :half], keep[:, half:] + got[:, half:]
    return keep + swap(send, "wa", masks[3])


def gathered_chunks(held, masks):
    for mask in (masks[3], masks[2]):
        held = jnp.concatenate([held, swap(held, "wa", mask)], axis=1)
    held_a, held_b = held[0], held[1]
    got_a, got_b = swap(held_a, "wa", masks[1]), swap(held_b, "wa", masks[0])
    held_a, held_b = jnp.concatenate([held_a, got_a]), jnp.concatenate([held_b, got_b])
    got_a, got_b = swap(held_a, "wa", masks[0]), swap(held_b, "wa", masks[1])
    return (held_a, held_b), (got_a, got_b)


def momentum_kernel(kpoint, place_ref, val_ref, miller_ref, cond_ref, keep_a, send_a, keep_b, send_b, weighted):
    nval = val_ref.shape[0]
    rows = nval // VB
    cols = keep_a.shape[3]
    step = pl.program_id(0)
    _, me_v = code_of(place_ref[0], kpoint)

    @pl.when(step == 0)
    def _():
        for place in range(VB):
            source = pl.multiple_of((place ^ me_v) * rows, rows)
            block = val_ref[pl.ds(source, rows), :].astype(F32)
            for axis in range(3):
                factor = miller_ref[axis : axis + 1, :].astype(F32)
                weighted[axis * nval + place * rows : axis * nval + (place + 1) * rows, :] = (
                    block * factor
                ).astype(BF16)

    result = lax.dot_general(
        weighted[...], cond_ref[...], (((1,), (1,)), ((), ())), preferred_element_type=F32
    )

    def store(out, other, first):
        for eighth in range(VB):
            for axis in range(3):
                start = axis * nval + eighth * rows
                out[other * VB + eighth, axis] = result[start : start + rows, first : first + cols]

    high, low = step // 2, step % 2
    pl.when(high == 0)(lambda: store(keep_a, low, 0))
    pl.when(high == 1)(lambda: store(send_a, low, 0))
    pl.when(low == 0)(lambda: store(keep_b, high, cols))
    pl.when(low == 1)(lambda: store(send_b, high, cols))


def partial_momentum(kpoint, place, val, miller, cond):
    nval, depth = val.shape
    ncond = cond.shape[0]
    rows, cols = nval // VB, ncond // CB
    half = jax.ShapeDtypeStruct((CB * VB // 2, 3, rows, cols // 2), F32)
    return pl.pallas_call(
        functools.partial(momentum_kernel, kpoint),
        grid_spec=pltpu.PrefetchScalarGridSpec(
            num_scalar_prefetch=1,
            grid=(CB,),
            in_specs=[
                pl.BlockSpec((nval, depth), lambda i, me: (0, 0)),
                pl.BlockSpec((3, depth), lambda i, me: (0, 0)),
                pl.BlockSpec((cols, depth), lambda i, me: (i ^ code_of(me[0], kpoint)[0], 0)),
            ],
            out_specs=[pl.BlockSpec(half.shape, lambda i, me: (0, 0, 0, 0))] * 4,
            scratch_shapes=[pltpu.VMEM((3 * nval, depth), BF16)],
        ),
        out_shape=[half] * 4,
        cost_estimate=pl.CostEstimate(
            flops=2 * 3 * nval * ncond * depth,
            bytes_accessed=2 * (nval + ncond) * depth + 12 * nval * ncond,
            transcendentals=0,
        ),
        compiler_params=pltpu.CompilerParams(vmem_limit_bytes=20 << 20),
        name="partial_momentum",
    )(place, val, miller, cond)


def pair_kernel(half, place_ref, weight_ref, freq_ref, energy_val, energy_cond, orbit_val, orbit_cond, *refs):
    kcount, nval, points = orbit_val.shape
    ncond = orbit_cond.shape[1]
    nfreq = freq_ref.shape[0]
    chunks, refs = refs[: 2 * kcount], refs[2 * kcount :]
    before, refs = (refs[0], refs[1:]) if half else (None, refs)
    outs, (total, amplitude, level, orbits, weight) = refs[:-5], refs[-5:]
    rows, cols = chunks[0].shape[2:]
    scale = float(nval * ncond) ** (-0.5)
    tops = 3 * nfreq
    for k in range(kcount):
        me_c, me_v = code_of(place_ref[0], k)
        level[k] = jnp.transpose(jnp.broadcast_to(energy_val[k : k + 1, :], (nval, nval)))
        top = []
        for piece, (quarter, side) in enumerate(QUARTERS[half]):
            start = pl.multiple_of(((quarter ^ me_c) * 2 + side) * cols, cols)
            top.append(energy_cond[k : k + 1, pl.ds(start, cols)])
            orbits[k, piece * cols : (piece + 1) * cols, :] = orbit_cond[k, pl.ds(start, cols), :]

        def factors_of(gap):
            square = gap * gap
            return [4.0 / (square + freq_ref[w] * freq_ref[w]) for w in range(nfreq)]

        def eighth(place, carry, k=k, me_v=me_v, top=top):
            mine = pl.ds(pl.multiple_of(place * rows, rows), rows)
            theirs = pl.ds(pl.multiple_of((place ^ me_v) * rows, rows), rows)
            weight[k, mine, :] = orbit_val[k, theirs, :].astype(F32) * (weight_ref[k] * scale)
            bottom = level[k, theirs, :]
            for piece in range(4):
                factors = factors_of(top[piece] - bottom)
                for axis in range(3):
                    momentum = chunks[2 * k + piece // 2][(piece % 2) * VB + place, axis]
                    for w in range(nfreq):
                        start = pl.multiple_of((axis * nfreq + w) * nval + place * rows, rows)
                        amplitude[k, pl.ds(start, rows), piece * cols : (piece + 1) * cols] = (
                            momentum * factors[w]
                        ).astype(BF16)
            return carry

        lax.fori_loop(0, VB, eighth, 0, unroll=2)
        for axis in range(3):
            first = axis * nfreq * nval
            expanded = jnp.dot(
                amplitude[k, first : first + nfreq * nval, :], orbits[k], preferred_element_type=F32
            )
            for w in range(nfreq):
                row = slice(axis * nfreq + w, axis * nfreq + w + 1)
                value = jnp.sum(expanded[w * nval : (w + 1) * nval] * weight[k], axis=0, keepdims=True)
                if k > 0:
                    value = value + total[row, :]
                elif half:
                    value = value + before[row, :]
                total[row, :] = value

        if not half:
            bottom = level[k, pl.ds(pl.multiple_of(me_v * rows, rows), rows), :]
            for w in range(nfreq):
                lanes = slice(w * cols, (w + 1) * cols)
                for axis in range(3):
                    value = 0.0
                    for side in range(2):
                        gap = top[2 * side] - bottom
                        ratio = factors_of(gap)[w] / gap
                        momentum = chunks[2 * k + side][0, axis]
                        value = value + momentum * momentum * ratio
                    value = jnp.sum(value, axis=0, keepdims=True) * (weight_ref[k] / float(nval * ncond))
                    row = slice(tops + axis, tops + axis + 1)
                    total[row, lanes] = value + total[row, lanes] if k else value
            row = slice(tops + 3, tops + 4)
            value = jnp.full((1, points), weight_ref[k], F32)
            total[row, :] = value + total[row, :] if k else value
    if half:
        total[tops:, :] = before[tops:, :]
        keep, send = outs
        across = points // 2
        keep[...] = total[:, pl.ds(pl.multiple_of(place_ref[1] * across, across), across)]
        send[...] = total[:, pl.ds(pl.multiple_of((1 - place_ref[1]) * across, across), across)]
    else:
        outs[0][...] = total[...]


def pair_sums(half, place, weights, freqs, energy_val, energy_cond, orbit_val, orbit_cond, chunks, before):
    kcount, nval, points = orbit_val.shape
    ncond = orbit_cond.shape[1]
    nfreq = freqs.shape[0]
    height = 3 * nfreq + 4
    depth = ncond // 2
    operands = [energy_val, energy_cond, orbit_val, orbit_cond] + chunks + before
    if half:
        out_shape = [jax.ShapeDtypeStruct((height, points // 2), F32)] * 2
    else:
        out_shape = [jax.ShapeDtypeStruct((height, points), F32)]
    return pl.pallas_call(
        functools.partial(pair_kernel, half),
        out_shape=out_shape,
        in_specs=[SMEM] * 3 + [VMEM] * len(operands),
        out_specs=[VMEM] * len(out_shape),
        scratch_shapes=[
            pltpu.VMEM((height, points), F32),
            pltpu.VMEM((kcount, 3 * nfreq * nval, depth), BF16),
            pltpu.VMEM((kcount, nval, nval), F32),
            pltpu.VMEM((kcount, depth, points), BF16),
            pltpu.VMEM((kcount, nval, points), F32),
        ],
        cost_estimate=pl.CostEstimate(
            flops=kcount * 2 * 3 * nfreq * nval * depth * points,
            bytes_accessed=kcount * (12 * nval * depth + 4 * depth * points),
            transcendentals=0,
        ),
        compiler_params=pltpu.CompilerParams(vmem_limit_bytes=20 << 20),
        name="pair_sums",
    )(place, weights, freqs, *operands)


def wing_kernel(place_ref, gathered, zeta, out):
    ways, height, points = gathered.shape
    slab_rows = zeta.shape[0]
    tops = height - 4
    total = jnp.zeros((3 * height, slab_rows), F32)
    last = jnp.zeros((4, points), F32)
    for device in range(ways):
        value = gathered[device]
        last = last + value[tops:]
        pieces = []
        for _ in range(3):
            rounded = value.astype(BF16)
            pieces.append(rounded)
            value = value - rounded.astype(F32)
        start = pl.multiple_of((2 * device + place_ref[1]) * points, points)
        total = total + lax.dot_general(
            jnp.concatenate(pieces, axis=0),
            zeta[:, pl.ds(start, points)],
            (((1,), (1,)), ((), ())),
            preferred_element_type=F32,
        )
    total = total[:height] + total[height : 2 * height] + total[2 * height :]
    out[:tops] = total[:tops]
    lane = lax.broadcasted_iota(jnp.int32, (3, slab_rows), 1)
    across = points // 2
    head = jnp.zeros((3, slab_rows), F32)
    for tile in range(2):
        value = jnp.sum(last[:3, tile * across : (tile + 1) * across], axis=1, keepdims=True)
        head = jnp.where(lane == 2 * place_ref[1] + tile, value, head)
    out[tops : tops + 3] = head
    out[tops + 3 :] = last[3:, :slab_rows]


def wing_sums(place, gathered, zeta):
    ways, height, points = gathered.shape
    slab_rows = zeta.shape[0]
    return pl.pallas_call(
        wing_kernel,
        out_shape=jax.ShapeDtypeStruct((height, slab_rows), F32),
        in_specs=[SMEM, VMEM, VMEM],
        out_specs=VMEM,
        cost_estimate=pl.CostEstimate(
            flops=6 * height * slab_rows * ways * points,
            bytes_accessed=4 * slab_rows * ways * points + 4 * height * ways * points,
            transcendentals=0,
        ),
        compiler_params=pltpu.CompilerParams(vmem_limit_bytes=20 << 20),
        name="wing_sums",
    )(place, gathered, zeta)


def final_kernel(copies, one, two, wing, head):
    total = one[...] + two[...]
    tops = total.shape[0] - 4
    nfreq = wing.shape[1]
    scale = copies / total[tops + 3 :]
    for axis in range(3):
        wing[axis] = total[axis * nfreq : (axis + 1) * nfreq] * scale
    head[...] = total[tops : tops + 3, :nfreq] * scale[:, :nfreq]


def local(
    coeff_val,
    coeff_cond,
    miller,
    energy_val,
    energy_cond,
    orbit_val,
    orbit_cond,
    zeta,
    freqs,
    kweight,
):
    kcount, nval, npw_dev = coeff_val.shape
    nfreq = freqs.shape[0]
    slab_rows = zeta.shape[0]
    ways = lax.axis_size("wa")
    pw_factor = float(npw_dev * ways) ** (-0.5)
    weights = kweight.astype(F32)
    place = jnp.stack([lax.axis_index("wa"), lax.axis_index("ka") & 1]).astype(jnp.int32)

    mine = []
    for k in range(kcount):
        parts = partial_momentum(k, place, coeff_val[k], miller, coeff_cond[k])
        mine.append(scattered(parts, MASKS[k]))
    mine = jnp.stack(mine)
    mine = (mine + swap(mine, "wa", MASKS[0][4])[:, :, ::-1]) * pw_factor

    chunks = [gathered_chunks(mine[k], MASKS[k]) for k in range(kcount)]
    operands = (place, weights, freqs, energy_val, energy_cond, orbit_val, orbit_cond)
    (pair,) = pair_sums(0, *operands, [part for k in range(kcount) for part in chunks[k][0]], [])
    keep, send = pair_sums(1, *operands, [part for k in range(kcount) for part in chunks[k][1]], [pair])
    pair = keep + swap(send, "ka", 1)
    total = wing_sums(place, everyone(pair, "wa"), zeta)
    total = total + swap(total, "ka", 1)
    total = total + swap(total, "ka", 2)
    return pl.pallas_call(
        functools.partial(final_kernel, float(2 * ways)),
        out_shape=[
            jax.ShapeDtypeStruct((3, nfreq, slab_rows), F32),
            jax.ShapeDtypeStruct((3, nfreq), F32),
        ],
        in_specs=[VMEM] * 2,
        out_specs=[VMEM] * 2,
        name="final",
    )(total, swap(total, "ka", 6))


def solution(mesh):
    return jax.shard_map(
        local,
        mesh=mesh,
        in_specs=(
            P("ka", None, "wa"),
            P("ka", None, "wa"),
            P(None, "wa"),
            P("ka", None),
            P("ka", None),
            P("ka", None, "wa"),
            P("ka", None, "wa"),
            P("wa", None),
            P(),
            P("ka"),
        ),
        out_specs=(P(None, None, "wa"), P()),
        check_vma=False,
    )
```

time: 567 us -> 129 us (0.23)
  waiting for transfers between devices: 318 us -> 38.5 us
  blocking collectives: 196 us -> 17.7 us
  starting transfers between devices: 0.04 us -> 44.9 us
  matrix products: 20 us -> 0 us
  Pallas kernels: 0 us -> 16.8 us
  between operations: 15.5 us -> 1.03 us
  other arithmetic: 14.5 us -> 0.72 us
  local copies, waits for them, and re-layouts: 3.05 us -> 9.4 us
    psum x1 -> x0, waiting for transfers between devices: 318 us -> none  [local(): momentum = lax.psum(partial_mom, 'wa') * pw_factor]
    all_gather x2 -> x0, blocking collectives: 168 us -> none  [local(): lax.all_gather(pair_sum, 'wa', axis=1, tiled=True)]
    ppermute x0 -> x29, starting transfers between devices: none -> 44.9 us  [swap(): return lax.ppermute(value, axis, [(i, i ^ mask) for i in range(size)])]
    ppermute x0 -> x29, waiting for transfers between devices: none -> 38.5 us  [swap(): return lax.ppermute(value, axis, [(i, i ^ mask) for i in range(size)])]
    psum x1 -> x0, blocking collectives: 27.2 us -> none  [local(): lax.psum((wing_acc, head_acc, weight_sum), 'ka')]
    dot_general x6 -> x0, matrix products: 20 us -> none  [the longest x2 8.32 us: local(): jnp.einsum('avg,cg->avc', weighted, coeff_cond[kpoint], preferred_element...]
    all_to_all x0 -> x1, blocking collectives: none -> 17.7 us  [everyone(): lax.all_to_all(jnp.broadcast_to(value[None], (parts,) + value.shape), axi...]
    pallas_call x0 -> x6, Pallas kernels: none -> 16.8 us  [the longest x2 7.33 us: pair_sums(): pl.pallas_call(functools.partial(pair_kernel, half), out_shape=out_shape,...]
  transfers between devices with their start and end apart: 1 -> 29, of which waited for: 1 -> 18; matrix products, arithmetic and copies ran while one was open for 1% -> 0% of each run, Pallas kernels for 0% -> 6%
where the time goes in v2:
time: 129 us
  starting transfers between devices  44.9 us (35%)
  waiting for transfers between devices  38.5 us (30%)
  blocking collectives  17.7 us (14%)
  Pallas kernels  16.8 us (13%)
  local copies, waits for them, and re-layouts  9.4 us (7%)
    ppermute x29, starting transfers between devices, swap(): return lax.ppermute(value, axis, [(i, i ^ mask) for i in range(size)])  44.9 us
    ppermute x29, waiting for transfers between devices, swap(): return lax.ppermute(value, axis, [(i, i ^ mask) for i in range(size)])  38.5 us
    all_to_all x1, blocking collectives, everyone(): lax.all_to_all(jnp.broadcast_to(value[None], (parts,) + value.shape), axi...  17.7 us
    pallas_call x2, Pallas kernels, pair_sums(): pl.pallas_call(functools.partial(pair_kernel, half), out_shape=out_shape,...  7.33 us
    pallas_call x2, Pallas kernels, partial_momentum(): pl.pallas_call(functools.partial(momentum_kernel, kpoint), grid_spec=pltp...  6.86 us
    squeeze x2, local copies, waits for them, and re-layouts, local(): parts = partial_momentum(k, place, coeff_val[k], miller, coeff_cond[k])  6.29 us
    unnamed x26, local copies, waits for them, and re-layouts  2.99 us
  transfers between devices with their start and end apart: 29, of which 18 were waited for; matrix products, arithmetic and copies ran while one was open for 0% of the time, Pallas kernels for 6%

profile of v2, /device:TPU:8, one launch (start us, length us, event | category | flops | bytes accessed | tf_op | source)
XLA Modules:
  0.0 129.1 jit_solution(13628711552138526399)
XLA Ops:
  0.7 6.2 %slice_bitcast_fusion.1 = (bf16[1024,2048]{1,0:T(8,128)(2,1)}, bf16[1024,2048]{1,0:T(8,128)(2,1)}) fusion(bf16[2,1024,2048]{2,1,0:T(8,128)(2,1)} %param.11), kind=kLoop, calls=%fused_computation.1 | loop fusion | bytes 16777216 | tf_op jit(solution)/shard_map/squeeze | solution.py:320
  7.0 2.3 %copy-done.2 = bf16[1024,2048]{1,0:T(8,128)(2,1)S(1)} copy-done((bf16[1024,2048]{1,0:T(8,128)(2,1)S(1)}, bf16[1024,2048]{1,0:T(8,128)(2,1)}, u32[]{:S(2)}) %copy-start.2) | copy-done | bytes 4194328
  9.4 3.4 %partial_momentum.2 = (f32[16,3,16,128]{3,2,1,0:T(8,128)S(1)}, f32[16,3,16,128]{3,2,1,0:T(8,128)S(1)}, f32[16,3,16,128]{3,2,1,0:T(8,128)S(1)}, f32[16,3,16,128]{3,2,1,0:T(8,128)S(1)}) custom-call(s32[2]{0:T(128)S(1)} %pad_add_fusion.place_ref, bf16[128,2048]{1,0:T(8,128)(2,1)S(1)} %get-tuple-element.24.val_ref, s32[3,2048]{1,0:T(4,128)S(1)} %copy-done.5, ...), custom_call_target="tpu_custom_call" | custom-call | flops 1610612736 | bytes 6291456 | tf_op jit(solution)/shard_map/partial_momentum/pallas_call | solution.py:99
  12.8 1.6 %collective-permute-start = (f32[16,3,16,128]{3,2,1,0:T(8,128)S(1)}, f32[16,3,16,128]{3,2,1,0:T(8,128)S(1)}, u32[]{:S(2)}, u32[]{:S(2)}) collective-permute-start(f32[16,3,16,128]{3,2,1,0:T(8,128)S(1)} %get-tuple-element.13), channel_id=1, source_target_pairs={{0,8},{1,9},{2,10},{3,11},{4,12},{5,13},{6,14},{7,15},{8,0},{9,1},... | collective-permute-start | bytes 1179656 | tf_op jit(solution)/shard_map/ppermute | solution.py:26
  14.4 2.1 %collective-permute-start.2 = (f32[16,3,16,128]{3,2,1,0:T(8,128)S(1)}, f32[16,3,16,128]{3,2,1,0:T(8,128)S(1)}, u32[]{:S(2)}, u32[]{:S(2)}) collective-permute-start(f32[16,3,16,128]{3,2,1,0:T(8,128)S(1)} %get-tuple-element.15), channel_id=1, source_target_pairs={{0,24},{1,25},{2,26},{3,27},{4,28},{5,29},{6,30},{7,31},{8,16},{9,... | collective-permute-start | bytes 1179656 | tf_op jit(solution)/shard_map/ppermute | solution.py:26
  16.5 3.4 %partial_momentum.3 = (f32[16,3,16,128]{3,2,1,0:T(8,128)S(1)}, f32[16,3,16,128]{3,2,1,0:T(8,128)S(1)}, f32[16,3,16,128]{3,2,1,0:T(8,128)S(1)}, f32[16,3,16,128]{3,2,1,0:T(8,128)S(1)}) custom-call(s32[2]{0:T(128)S(1)} %pad_add_fusion.place_ref, bf16[128,2048]{1,0:T(8,128)(2,1)S(1)} %get-tuple-element.25.val_ref, s32[3,2048]{1,0:T(4,128)S(1)} %copy-done.5, ...), custom_call_target="tpu_custom_call" | custom-call | flops 1610612736 | bytes 6291456 | tf_op jit(solution)/shard_map/partial_momentum/pallas_call | solution.py:99
  20.5 2.4 %collective-permute-start.8 = (f32[16,3,16,128]{3,2,1,0:T(8,128)S(1)}, f32[16,3,16,128]{3,2,1,0:T(8,128)S(1)}, u32[]{:S(2)}, u32[]{:S(2)}) collective-permute-start(f32[16,3,16,128]{3,2,1,0:T(8,128)S(1)} %get-tuple-element.19), channel_id=1, source_target_pairs={{0,3},{1,2},{2,1},{3,0},{4,7},{5,6},{6,5},{7,4},{8,11},{9,10},{10,... | collective-permute-start | bytes 1179656 | tf_op jit(solution)/shard_map/ppermute | solution.py:26
  22.9 0.9 collective-permute-done
  23.8 2.8 %collective-permute-start.1 = (f32[8,3,16,128]{3,2,1,0:T(8,128)S(1)}, f32[8,3,16,128]{3,2,1,0:T(8,128)S(1)}, u32[]{:S(2)}, u32[]{:S(2)}) collective-permute-start(f32[8,3,16,128]{3,2,1,0:T(8,128)S(1)} %get-tuple-element.27), channel_id=1, source_target_pairs={{0,24},{1,25},{2,26},{3,27},{4,28},{5,29},{6,30},{7,31},{8,16},{9,... | collective-permute-start | bytes 589832 | tf_op jit(solution)/shard_map/ppermute | solution.py:26
  27.0 3.3 %collective-permute-done.6 = f32[16,3,16,128]{3,2,1,0:T(8,128)S(1)} collective-permute-done((f32[16,3,16,128]{3,2,1,0:T(8,128)S(1)}, f32[16,3,16,128]{3,2,1,0:T(8,128)S(1)}, u32[]{:S(2)}, u32[]{:S(2)}) %collective-permute-start.6) | collective-permute-done | bytes 393248 | tf_op jit(solution)/shard_map/ppermute | solution.py:26
  30.4 1.7 %collective-permute-start.7 = (f32[8,3,16,128]{3,2,1,0:T(8,128)S(1)}, f32[8,3,16,128]{3,2,1,0:T(8,128)S(1)}, u32[]{:S(2)}, u32[]{:S(2)}) collective-permute-start(f32[8,3,16,128]{3,2,1,0:T(8,128)S(1)} %get-tuple-element.31), channel_id=1, source_target_pairs={{0,3},{1,2},{2,1},{3,0},{4,7},{5,6},{6,5},{7,4},{8,11},{9,10},{10,... | collective-permute-start | bytes 589832 | tf_op jit(solution)/shard_map/ppermute | solution.py:26
  32.1 2.0 %collective-permute-start.9 = (f32[8,3,16,128]{3,2,1,0:T(8,128)S(1)}, f32[8,3,16,128]{3,2,1,0:T(8,128)S(1)}, u32[]{:S(2)}, u32[]{:S(2)}) collective-permute-start(f32[8,3,16,128]{3,2,1,0:T(8,128)S(1)} %get-tuple-element.33), channel_id=1, source_target_pairs={{0,1},{1,0},{2,3},{3,2},{4,5},{5,4},{6,7},{7,6},{8,9},{9,8},{10,11... | collective-permute-start | bytes 589832 | tf_op jit(solution)/shard_map/ppermute | solution.py:26
  34.4 1.7 %collective-permute-done.7 = f32[8,3,16,128]{3,2,1,0:T(8,128)S(1)} collective-permute-done((f32[8,3,16,128]{3,2,1,0:T(8,128)S(1)}, f32[8,3,16,128]{3,2,1,0:T(8,128)S(1)}, u32[]{:S(2)}, u32[]{:S(2)}) %collective-permute-start.7) | collective-permute-done | bytes 196640 | tf_op jit(solution)/shard_map/ppermute | solution.py:26
  36.2 3.2 %collective-permute-done.9 = f32[8,3,16,128]{3,2,1,0:T(8,128)S(1)} collective-permute-done((f32[8,3,16,128]{3,2,1,0:T(8,128)S(1)}, f32[8,3,16,128]{3,2,1,0:T(8,128)S(1)}, u32[]{:S(2)}, u32[]{:S(2)}) %collective-permute-start.9) | collective-permute-done | bytes 196640 | tf_op jit(solution)/shard_map/ppermute | solution.py:26
  39.4 0.7 collective-permute-start.10
  40.0 1.4 %collective-permute-done.4 = f32[2,4,3,16,128]{4,3,2,1,0:T(8,128)S(1)} collective-permute-done((f32[2,4,3,16,128]{4,3,2,1,0:T(8,128)S(1)}, f32[2,4,3,16,128]{4,3,2,1,0:T(8,128)S(1)}, u32[]{:S(2)}, u32[]{:S(2)}) %collective-permute-start.4) | collective-permute-done | bytes 196640 | tf_op jit(solution)/shard_map/ppermute | solution.py:26
  41.4 1.0 collective-permute-start.5
  42.4 2.7 %collective-permute-done.10 = f32[2,4,3,16,128]{4,3,2,1,0:T(8,128)S(1)} collective-permute-done((f32[2,4,3,16,128]{4,3,2,1,0:T(8,128)S(1)}, f32[2,4,3,16,128]{4,3,2,1,0:T(8,128)S(1)}, u32[]{:S(2)}, u32[]{:S(2)}) %collective-permute-start.10) | collective-permute-done | bytes 196640 | tf_op jit(solution)/shard_map/ppermute | solution.py:26
  45.1 1.2 collective-permute-start.11
  46.4 4.7 %collective-permute-done.11 = f32[2,2,3,16,128]{4,3,2,1,0:T(8,128)S(1)} collective-permute-done((f32[2,2,3,16,128]{4,3,2,1,0:T(8,128)S(1)}, f32[2,2,3,16,128]{4,3,2,1,0:T(8,128)S(1)}, u32[]{:S(2)}, u32[]{:S(2)}) %collective-permute-start.11) | collective-permute-done | bytes 98336 | tf_op jit(solution)/shard_map/ppermute | solution.py:26
  51.2 2.0 %collective-permute-start.12 = (f32[2,2,2,3,16,128]{5,4,3,2,1,0:T(8,128)S(1)}, f32[2,2,2,3,16,128]{5,4,3,2,1,0:T(8,128)S(1)}, u32[]{:S(2)}, u32[]{:S(2)}) collective-permute-start(f32[2,2,2,3,16,128]{5,4,3,2,1,0:T(8,128)S(1)} %pad_maximum_fusion.8), channel_id=1, source_target_pairs={{0,4},{1,5},{2,6},{3,7},{4,0},{5,1},{6,2},{7,3},{8,12},{9,13},{10,... | collective-permute-start | bytes 589832 | tf_op jit(solution)/shard_map/ppermute | solution.py:26
  53.2 3.7 %collective-permute-done.12 = f32[2,2,2,3,16,128]{5,4,3,2,1,0:T(8,128)S(1)} collective-permute-done((f32[2,2,2,3,16,128]{5,4,3,2,1,0:T(8,128)S(1)}, f32[2,2,2,3,16,128]{5,4,3,2,1,0:T(8,128)S(1)}, u32[]{:S(2)}, u32[]{:S(2)}) %collective-permute-start.12) | collective-permute-done | bytes 196640 | tf_op jit(solution)/shard_map/ppermute | solution.py:26
  57.0 1.2 collective-permute-start.19
  58.2 0.9 collective-permute-start.13
  59.1 3.8 %collective-permute-done.19 = f32[2,2,3,16,128]{4,3,2,1,0:T(8,128)S(1)} collective-permute-done((f32[2,2,3,16,128]{4,3,2,1,0:T(8,128)S(1)}, f32[2,2,3,16,128]{4,3,2,1,0:T(8,128)S(1)}, u32[]{:S(2)}, u32[]{:S(2)}) %collective-permute-start.19) | collective-permute-done | bytes 98336 | tf_op jit(solution)/shard_map/ppermute | solution.py:26
  63.0 3.5 %collective-permute-start.14 = (f32[2,4,3,16,128]{4,3,2,1,0:T(8,128)S(1)}, f32[2,4,3,16,128]{4,3,2,1,0:T(8,128)S(1)}, u32[]{:S(2)}, u32[]{:S(2)}) collective-permute-start(f32[2,4,3,16,128]{4,3,2,1,0:T(8,128)S(1)} %pad_maximum_fusion.9), channel_id=1, source_target_pairs={{0,1},{1,0},{2,3},{3,2},{4,5},{5,4},{6,7},{7,6},{8,9},{9,8},{10,11... | collective-permute-start | bytes 589832 | tf_op jit(solution)/shard_map/ppermute | solution.py:26
  66.5 2.2 %collective-permute-done.20 = f32[2,4,3,16,128]{4,3,2,1,0:T(8,128)S(1)} collective-permute-done((f32[2,4,3,16,128]{4,3,2,1,0:T(8,128)S(1)}, f32[2,4,3,16,128]{4,3,2,1,0:T(8,128)S(1)}, u32[]{:S(2)}, u32[]{:S(2)}) %collective-permute-start.20) | collective-permute-done | bytes 196640 | tf_op jit(solution)/shard_map/ppermute | solution.py:26
  68.7 1.8 %collective-permute-start.23 = (f32[8,3,16,128]{3,2,1,0:T(8,128)S(1)}, f32[8,3,16,128]{3,2,1,0:T(8,128)S(1)}, u32[]{:S(2)}, u32[]{:S(2)}) collective-permute-start(f32[8,3,16,128]{3,2,1,0:T(8,128)S(1)} %get-tuple-element.34), channel_id=1, source_target_pairs={{0,1},{1,0},{2,3},{3,2},{4,5},{5,4},{6,7},{7,6},{8,9},{9,8},{10,11... | collective-permute-start | bytes 589832 | tf_op jit(solution)/shard_map/ppermute | solution.py:26
  70.6 0.9 collective-permute-start.21
  71.7 1.3 %collective-permute-start.17 = (f32[8,3,16,128]{3,2,1,0:T(8,128)S(1)}, f32[8,3,16,128]{3,2,1,0:T(8,128)S(1)}, u32[]{:S(2)}, u32[]{:S(2)}) collective-permute-start(f32[8,3,16,128]{3,2,1,0:T(8,128)S(1)} %get-tuple-element.36), channel_id=1, source_target_pairs={{0,8},{1,9},{2,10},{3,11},{4,12},{5,13},{6,14},{7,15},{8,0},{9,1},... | collective-permute-start | bytes 589832 | tf_op jit(solution)/shard_map/ppermute | solution.py:26
  73.1 2.1 %collective-permute-start.15 = (f32[8,3,16,128]{3,2,1,0:T(8,128)S(1)}, f32[8,3,16,128]{3,2,1,0:T(8,128)S(1)}, u32[]{:S(2)}, u32[]{:S(2)}) collective-permute-start(f32[8,3,16,128]{3,2,1,0:T(8,128)S(1)} %get-tuple-element.37), channel_id=1, source_target_pairs={{0,24},{1,25},{2,26},{3,27},{4,28},{5,29},{6,30},{7,31},{8,16},{9,... | collective-permute-start | bytes 589832 | tf_op jit(solution)/shard_map/ppermute | solution.py:26
  75.2 1.3 collective-permute-done.23
  76.5 1.1 collective-permute-start.24
  77.6 2.5 %collective-permute-start.22 = (f32[16,3,16,128]{3,2,1,0:T(8,128)S(1)}, f32[16,3,16,128]{3,2,1,0:T(8,128)S(1)}, u32[]{:S(2)}, u32[]{:S(2)}) collective-permute-start(f32[16,3,16,128]{3,2,1,0:T(8,128)S(1)} %pad_maximum_fusion.4.refs_2_), channel_id=1, source_target_pairs={{0,1},{1,0},{2,3},{3,2},{4,5},{5,4},{6,7},{7,6},{8,9},{9,8},{10,11... | collective-permute-start | bytes 1179656 | tf_op jit(solution)/shard_map/ppermute | solution.py:26
  80.2 2.3 %collective-permute-start.18 = (f32[16,3,16,128]{3,2,1,0:T(8,128)S(1)}, f32[16,3,16,128]{3,2,1,0:T(8,128)S(1)}, u32[]{:S(2)}, u32[]{:S(2)}) collective-permute-start(f32[16,3,16,128]{3,2,1,0:T(8,128)S(1)} %pad_maximum_fusion.2.refs_1_), channel_id=1, source_target_pairs={{0,24},{1,25},{2,26},{3,27},{4,28},{5,29},{6,30},{7,31},{8,16},{9,... | collective-permute-start | bytes 1179656 | tf_op jit(solution)/shard_map/ppermute | solution.py:26
  82.7 3.7 %pair_sums.2.refs_4_ = f32[16,512]{1,0:T(8,128)S(1)} custom-call(s32[2]{0:T(128)S(1)} %pad_add_fusion.place_ref, f32[2]{0:T(128)S(1)} %convert_element_type.3.weight_ref, f32[4]{0:T(128)S(1)} %copy-done.8, f32[2,128]{1,0:T(2,128)S(1)} %copy-done.7, f32[2,1024]{1,0:T(2,128)S(1)} %copy-done.6, bf16[2,128,512]{2,1,0:T(8,128)(2,1)S(1)} %copy-done.4, ...), custom_call_target="tpu_custom_call" | custom-call | flops 1610612736 | bytes 3670016 | tf_op jit(solution)/shard_map/pair_sums/pallas_call | solution.py:215
  86.4 2.9 %collective-permute-done.18.refs_1_ = f32[16,3,16,128]{3,2,1,0:T(8,128)S(1)} collective-permute-done((f32[16,3,16,128]{3,2,1,0:T(8,128)S(1)}, f32[16,3,16,128]{3,2,1,0:T(8,128)S(1)}, u32[]{:S(2)}, u32[]{:S(2)}) %collective-permute-start.18) | collective-permute-done | bytes 393248 | tf_op jit(solution)/shard_map/ppermute | solution.py:26
  89.3 1.1 collective-permute-done.16.refs_0_
  90.3 3.6 %pair_sums.3 = (f32[16,256]{1,0:T(8,128)S(1)}, f32[16,256]{1,0:T(8,128)S(1)}) custom-call(s32[2]{0:T(128)S(1)} %pad_add_fusion.place_ref, f32[2]{0:T(128)S(1)} %convert_element_type.3.weight_ref, f32[4]{0:T(128)S(1)} %copy-done.8, f32[2,128]{1,0:T(2,128)S(1)} %copy-done.7, f32[2,1024]{1,0:T(2,128)S(1)} %copy-done.6, bf16[2,128,512]{2,1,0:T(8,128)(2,1)S(1)} %copy-done.4, ...), custom_call_target="tpu_custom_call" | custom-call | flops 1610612736 | bytes 3670016 | tf_op jit(solution)/shard_map/pair_sums/pallas_call | solution.py:215
  94.1 1.2 collective-permute-done.25
  95.3 17.7 %all_to_all.5.gathered = f32[32,16,256]{2,1,0:T(8,128)S(1)} all-to-all(f32[32,16,256]{2,1,0:T(8,128)S(1)} %broadcast_in_dim.2), channel_id=1, replica_groups=mesh['ka'=8,'wa'=32] {'wa'}, dimensions={0} | all-to-all | bytes 1048576 | tf_op jit(solution)/shard_map/all_to_all | solution.py:31
  113.1 1.3 %wing_sums.1 = f32[16,128]{1,0:T(8,128)S(1)} custom-call(s32[2]{0:T(128)S(1)} %pad_add_fusion.place_ref, f32[32,16,256]{2,1,0:T(8,128)S(1)} %all_to_all.5.gathered, bf16[128,16384]{1,0:T(8,128)(2,1)S(1)} %copy-done), custom_call_target="tpu_custom_call" | custom-call | flops 100663296 | bytes 4718592 | tf_op jit(solution)/shard_map/wing_sums/pallas_call | solution.py:273
  114.4 1.2 collective-permute-done.26
  115.6 3.3 %collective-permute-start.27 = (f32[16,128]{1,0:T(8,128)S(1)}, f32[16,128]{1,0:T(8,128)S(1)}, u32[]{:S(2)}, u32[]{:S(2)}) collective-permute-start(f32[16,128]{1,0:T(8,128)S(1)} %add.102), channel_id=1, source_target_pairs={{0,64},{32,96},{64,0},{96,32},{128,192},{160,224},{192,128},{224,1... | collective-permute-start | bytes 24584 | tf_op jit(solution)/shard_map/ppermute | solution.py:26
  118.9 1.6 %collective-permute-done.27 = f32[16,128]{1,0:T(8,128)S(1)} collective-permute-done((f32[16,128]{1,0:T(8,128)S(1)}, f32[16,128]{1,0:T(8,128)S(1)}, u32[]{:S(2)}, u32[]{:S(2)}) %collective-permute-start.27) | collective-permute-done | bytes 8224 | tf_op jit(solution)/shard_map/ppermute | solution.py:26
  120.5 5.0 %collective-permute-start.28 = (f32[16,128]{1,0:T(8,128)S(1)}, f32[16,128]{1,0:T(8,128)S(1)}, u32[]{:S(2)}, u32[]{:S(2)}) collective-permute-start(f32[16,128]{1,0:T(8,128)S(1)} %add.103.one), channel_id=1, source_target_pairs={{0,192},{32,224},{64,128},{96,160},{128,64},{160,96},{192,0},{224,... | collective-permute-start | bytes 24584 | tf_op jit(solution)/shard_map/ppermute | solution.py:26
  125.5 1.6 %collective-permute-done.28.two = f32[16,128]{1,0:T(8,128)S(1)} collective-permute-done((f32[16,128]{1,0:T(8,128)S(1)}, f32[16,128]{1,0:T(8,128)S(1)}, u32[]{:S(2)}, u32[]{:S(2)}) %collective-permute-start.28) | collective-permute-done | bytes 8224 | tf_op jit(solution)/shard_map/ppermute | solution.py:26
  127.8 1.3 %final.1 = (f32[3,4,128]{2,1,0:T(4,128)}, f32[3,4]{1,0:T(4,128)}) custom-call(f32[16,128]{1,0:T(8,128)} %copy-done.10, f32[16,128]{1,0:T(8,128)} %copy-done.11), custom_call_target="tpu_custom_call" | custom-call | tf_op jit(solution)/shard_map/final/pallas_call | solution.py:333
  (78 shorter events, 3.2 us)
Async XLA Ops:
  0.6 6.2 %copy-start.9 = (bf16[2,128,2048]{2,1,0:T(8,128)(2,1)S(1)}, bf16[2,128,2048]{2,1,0:T(8,128)(2,1)}, u32[]{:S(2)}) copy-start(bf16[2,128,2048]{2,1,0:T(8,128)(2,1)} %param.10) | copy-start | bytes 3145732
  0.6 6.4 %copy-start.5 = (s32[3,2048]{1,0:T(4,128)S(1)}, s32[3,2048]{1,0:T(4,128)}, u32[]{:S(2)}) copy-start(s32[3,2048]{1,0:T(4,128)} %miller_ref.3) | copy-start | bytes 73732
  7.0 9.5 %copy-start.1 = (bf16[1024,2048]{1,0:T(8,128)(2,1)S(1)}, bf16[1024,2048]{1,0:T(8,128)(2,1)}, u32[]{:S(2)}) copy-start(bf16[1024,2048]{1,0:T(8,128)(2,1)} %get-tuple-element.23.cond_ref) | copy-start | bytes 12582916
  7.0 2.3 %copy-start.2 = (bf16[1024,2048]{1,0:T(8,128)(2,1)S(1)}, bf16[1024,2048]{1,0:T(8,128)(2,1)}, u32[]{:S(2)}) copy-start(bf16[1024,2048]{1,0:T(8,128)(2,1)} %get-tuple-element.22.cond_ref) | copy-start | bytes 12582916
  12.8 10.9 %collective-permute-start = (f32[16,3,16,128]{3,2,1,0:T(8,128)S(1)}, f32[16,3,16,128]{3,2,1,0:T(8,128)S(1)}, u32[]{:S(2)}, u32[]{:S(2)}) collective-permute-start(f32[16,3,16,128]{3,2,1,0:T(8,128)S(1)} %get-tuple-element.13), channel_id=1, source_target_pairs={{0,8},{1,9},{2,10},{3,11},{4,12},{5,13},{6,14},{7,15},{8,0},{9,1},... | collective-permute-start | bytes 1179656 | tf_op jit(solution)/shard_map/ppermute | solution.py:26
  14.4 12.3 %collective-permute-start.2 = (f32[16,3,16,128]{3,2,1,0:T(8,128)S(1)}, f32[16,3,16,128]{3,2,1,0:T(8,128)S(1)}, u32[]{:S(2)}, u32[]{:S(2)}) collective-permute-start(f32[16,3,16,128]{3,2,1,0:T(8,128)S(1)} %get-tuple-element.15), channel_id=1, source_target_pairs={{0,24},{1,25},{2,26},{3,27},{4,28},{5,29},{6,30},{7,31},{8,16},{9,... | collective-permute-start | bytes 1179656 | tf_op jit(solution)/shard_map/ppermute | solution.py:26
  19.9 10.4 %collective-permute-start.6 = (f32[16,3,16,128]{3,2,1,0:T(8,128)S(1)}, f32[16,3,16,128]{3,2,1,0:T(8,128)S(1)}, u32[]{:S(2)}, u32[]{:S(2)}) collective-permute-start(f32[16,3,16,128]{3,2,1,0:T(8,128)S(1)} %get-tuple-element.17), channel_id=1, source_target_pairs={{0,1},{1,0},{2,3},{3,2},{4,5},{5,4},{6,7},{7,6},{8,9},{9,8},{10,11... | collective-permute-start | bytes 1179656 | tf_op jit(solution)/shard_map/ppermute | solution.py:26
  20.5 11.6 %collective-permute-start.8 = (f32[16,3,16,128]{3,2,1,0:T(8,128)S(1)}, f32[16,3,16,128]{3,2,1,0:T(8,128)S(1)}, u32[]{:S(2)}, u32[]{:S(2)}) collective-permute-start(f32[16,3,16,128]{3,2,1,0:T(8,128)S(1)} %get-tuple-element.19), channel_id=1, source_target_pairs={{0,3},{1,2},{2,1},{3,0},{4,7},{5,6},{6,5},{7,4},{8,11},{9,10},{10,... | collective-permute-start | bytes 1179656 | tf_op jit(solution)/shard_map/ppermute | solution.py:26
  23.8 10.3 %collective-permute-start.1 = (f32[8,3,16,128]{3,2,1,0:T(8,128)S(1)}, f32[8,3,16,128]{3,2,1,0:T(8,128)S(1)}, u32[]{:S(2)}, u32[]{:S(2)}) collective-permute-start(f32[8,3,16,128]{3,2,1,0:T(8,128)S(1)} %get-tuple-element.27), channel_id=1, source_target_pairs={{0,24},{1,25},{2,26},{3,27},{4,28},{5,29},{6,30},{7,31},{8,16},{9,... | collective-permute-start | bytes 589832 | tf_op jit(solution)/shard_map/ppermute | solution.py:26
  26.7 7.4 %collective-permute-start.3 = (f32[8,3,16,128]{3,2,1,0:T(8,128)S(1)}, f32[8,3,16,128]{3,2,1,0:T(8,128)S(1)}, u32[]{:S(2)}, u32[]{:S(2)}) collective-permute-start(f32[8,3,16,128]{3,2,1,0:T(8,128)S(1)} %get-tuple-element.29), channel_id=1, source_target_pairs={{0,8},{1,9},{2,10},{3,11},{4,12},{5,13},{6,14},{7,15},{8,0},{9,1},... | collective-permute-start | bytes 589832 | tf_op jit(solution)/shard_map/ppermute | solution.py:26
  30.4 5.8 %collective-permute-start.7 = (f32[8,3,16,128]{3,2,1,0:T(8,128)S(1)}, f32[8,3,16,128]{3,2,1,0:T(8,128)S(1)}, u32[]{:S(2)}, u32[]{:S(2)}) collective-permute-start(f32[8,3,16,128]{3,2,1,0:T(8,128)S(1)} %get-tuple-element.31), channel_id=1, source_target_pairs={{0,3},{1,2},{2,1},{3,0},{4,7},{5,6},{6,5},{7,4},{8,11},{9,10},{10,... | collective-permute-start | bytes 589832 | tf_op jit(solution)/shard_map/ppermute | solution.py:26
  32.1 7.2 %collective-permute-start.9 = (f32[8,3,16,128]{3,2,1,0:T(8,128)S(1)}, f32[8,3,16,128]{3,2,1,0:T(8,128)S(1)}, u32[]{:S(2)}, u32[]{:S(2)}) collective-permute-start(f32[8,3,16,128]{3,2,1,0:T(8,128)S(1)} %get-tuple-element.33), channel_id=1, source_target_pairs={{0,1},{1,0},{2,3},{3,2},{4,5},{5,4},{6,7},{7,6},{8,9},{9,8},{10,11... | collective-permute-start | bytes 589832 | tf_op jit(solution)/shard_map/ppermute | solution.py:26
  34.2 7.2 %collective-permute-start.4 = (f32[2,4,3,16,128]{4,3,2,1,0:T(8,128)S(1)}, f32[2,4,3,16,128]{4,3,2,1,0:T(8,128)S(1)}, u32[]{:S(2)}, u32[]{:S(2)}) collective-permute-start(f32[2,4,3,16,128]{4,3,2,1,0:T(8,128)S(1)} %pad_maximum_fusion.6), channel_id=1, source_target_pairs={{0,1},{1,0},{2,3},{3,2},{4,5},{5,4},{6,7},{7,6},{8,9},{9,8},{10,11... | collective-permute-start | bytes 589832 | tf_op jit(solution)/shard_map/ppermute | solution.py:26
  39.4 5.8 %collective-permute-start.10 = (f32[2,4,3,16,128]{4,3,2,1,0:T(8,128)S(1)}, f32[2,4,3,16,128]{4,3,2,1,0:T(8,128)S(1)}, u32[]{:S(2)}, u32[]{:S(2)}) collective-permute-start(f32[2,4,3,16,128]{4,3,2,1,0:T(8,128)S(1)} %pad_maximum_fusion.7), channel_id=1, source_target_pairs={{0,8},{1,9},{2,10},{3,11},{4,12},{5,13},{6,14},{7,15},{8,0},{9,1},... | collective-permute-start | bytes 589832 | tf_op jit(solution)/shard_map/ppermute | solution.py:26
  41.4 4.9 %collective-permute-start.5 = (f32[2,2,3,16,128]{4,3,2,1,0:T(8,128)S(1)}, f32[2,2,3,16,128]{4,3,2,1,0:T(8,128)S(1)}, u32[]{:S(2)}, u32[]{:S(2)}) collective-permute-start(f32[2,2,3,16,128]{4,3,2,1,0:T(8,128)S(1)} %slice_add_fusion.13), channel_id=1, source_target_pairs={{0,3},{1,2},{2,1},{3,0},{4,7},{5,6},{6,5},{7,4},{8,11},{9,10},{10,... | collective-permute-start | bytes 294920 | tf_op jit(solution)/shard_map/ppermute | solution.py:26
  45.1 5.9 %collective-permute-start.11 = (f32[2,2,3,16,128]{4,3,2,1,0:T(8,128)S(1)}, f32[2,2,3,16,128]{4,3,2,1,0:T(8,128)S(1)}, u32[]{:S(2)}, u32[]{:S(2)}) collective-permute-start(f32[2,2,3,16,128]{4,3,2,1,0:T(8,128)S(1)} %slice_add_fusion.8), channel_id=1, source_target_pairs={{0,24},{1,25},{2,26},{3,27},{4,28},{5,29},{6,30},{7,31},{8,16},{9,... | collective-permute-start | bytes 294920 | tf_op jit(solution)/shard_map/ppermute | solution.py:26
  51.1 31.5 %copy-start.12 = (s32[2]{0:T(128)S(1)}, s32[2]{0:T(128)}, u32[]{:S(2)}) copy-start(s32[2]{0:T(128)} %param.19) | copy-start | bytes 28
  51.1 31.5 %copy-start.3 = (bf16[2,1024,512]{2,1,0:T(8,128)(2,1)S(1)}, bf16[2,1024,512]{2,1,0:T(8,128)(2,1)}, u32[]{:S(2)}) copy-start(bf16[2,1024,512]{2,1,0:T(8,128)(2,1)} %orbit_cond.3) | copy-start | bytes 6291460
  51.1 31.5 %copy-start.4 = (bf16[2,128,512]{2,1,0:T(8,128)(2,1)S(1)}, bf16[2,128,512]{2,1,0:T(8,128)(2,1)}, u32[]{:S(2)}) copy-start(bf16[2,128,512]{2,1,0:T(8,128)(2,1)} %orbit_val.3) | copy-start | bytes 786436
  51.1 31.5 %copy-start.6 = (f32[2,1024]{1,0:T(2,128)S(1)}, f32[2,1024]{1,0:T(2,128)}, u32[]{:S(2)}) copy-start(f32[2,1024]{1,0:T(2,128)} %energy_cond.3) | copy-start | bytes 24580
  51.1 31.5 %copy-start.7 = (f32[2,128]{1,0:T(2,128)S(1)}, f32[2,128]{1,0:T(2,128)}, u32[]{:S(2)}) copy-start(f32[2,128]{1,0:T(2,128)} %energy_val.3) | copy-start | bytes 3076
  51.1 31.5 %copy-start.8 = (f32[4]{0:T(128)S(1)}, f32[4]{0:T(128)}, u32[]{:S(2)}) copy-start(f32[4]{0:T(128)} %freq_ref.3) | copy-start | bytes 52
  51.2 5.8 %collective-permute-start.12 = (f32[2,2,2,3,16,128]{5,4,3,2,1,0:T(8,128)S(1)}, f32[2,2,2,3,16,128]{5,4,3,2,1,0:T(8,128)S(1)}, u32[]{:S(2)}, u32[]{:S(2)}) collective-permute-start(f32[2,2,2,3,16,128]{5,4,3,2,1,0:T(8,128)S(1)} %pad_maximum_fusion.8), channel_id=1, source_target_pairs={{0,4},{1,5},{2,6},{3,7},{4,0},{5,1},{6,2},{7,3},{8,12},{9,13},{10,... | collective-permute-start | bytes 589832 | tf_op jit(solution)/shard_map/ppermute | solution.py:26
  57.0 5.9 %collective-permute-start.19 = (f32[2,2,3,16,128]{4,3,2,1,0:T(8,128)S(1)}, f32[2,2,3,16,128]{4,3,2,1,0:T(8,128)S(1)}, u32[]{:S(2)}, u32[]{:S(2)}) collective-permute-start(f32[2,2,3,16,128]{4,3,2,1,0:T(8,128)S(1)} %get-tuple-element.46), channel_id=1, source_target_pairs={{0,24},{1,25},{2,26},{3,27},{4,28},{5,29},{6,30},{7,31},{8,16},{9,... | collective-permute-start | bytes 294920 | tf_op jit(solution)/shard_map/ppermute | solution.py:26
  58.2 4.8 %collective-permute-start.13 = (f32[2,2,3,16,128]{4,3,2,1,0:T(8,128)S(1)}, f32[2,2,3,16,128]{4,3,2,1,0:T(8,128)S(1)}, u32[]{:S(2)}, u32[]{:S(2)}) collective-permute-start(f32[2,2,3,16,128]{4,3,2,1,0:T(8,128)S(1)} %get-tuple-element.47), channel_id=1, source_target_pairs={{0,3},{1,2},{2,1},{3,0},{4,7},{5,6},{6,5},{7,4},{8,11},{9,10},{10,... | collective-permute-start | bytes 294920 | tf_op jit(solution)/shard_map/ppermute | solution.py:26
  62.9 5.8 %collective-permute-start.20 = (f32[2,4,3,16,128]{4,3,2,1,0:T(8,128)S(1)}, f32[2,4,3,16,128]{4,3,2,1,0:T(8,128)S(1)}, u32[]{:S(2)}, u32[]{:S(2)}) collective-permute-start(f32[2,4,3,16,128]{4,3,2,1,0:T(8,128)S(1)} %pad_maximum_fusion.10), channel_id=1, source_target_pairs={{0,8},{1,9},{2,10},{3,11},{4,12},{5,13},{6,14},{7,15},{8,0},{9,1},... | collective-permute-start | bytes 589832 | tf_op jit(solution)/shard_map/ppermute | solution.py:26
  63.0 8.6 %collective-permute-start.14 = (f32[2,4,3,16,128]{4,3,2,1,0:T(8,128)S(1)}, f32[2,4,3,16,128]{4,3,2,1,0:T(8,128)S(1)}, u32[]{:S(2)}, u32[]{:S(2)}) collective-permute-start(f32[2,4,3,16,128]{4,3,2,1,0:T(8,128)S(1)} %pad_maximum_fusion.9), channel_id=1, source_target_pairs={{0,1},{1,0},{2,3},{3,2},{4,5},{5,4},{6,7},{7,6},{8,9},{9,8},{10,11... | collective-permute-start | bytes 589832 | tf_op jit(solution)/shard_map/ppermute | solution.py:26
  68.7 7.7 %collective-permute-start.23 = (f32[8,3,16,128]{3,2,1,0:T(8,128)S(1)}, f32[8,3,16,128]{3,2,1,0:T(8,128)S(1)}, u32[]{:S(2)}, u32[]{:S(2)}) collective-permute-start(f32[8,3,16,128]{3,2,1,0:T(8,128)S(1)} %get-tuple-element.34), channel_id=1, source_target_pairs={{0,1},{1,0},{2,3},{3,2},{4,5},{5,4},{6,7},{7,6},{8,9},{9,8},{10,11... | collective-permute-start | bytes 589832 | tf_op jit(solution)/shard_map/ppermute | solution.py:26
  70.6 7.1 %collective-permute-start.21 = (f32[8,3,16,128]{3,2,1,0:T(8,128)S(1)}, f32[8,3,16,128]{3,2,1,0:T(8,128)S(1)}, u32[]{:S(2)}, u32[]{:S(2)}) collective-permute-start(f32[8,3,16,128]{3,2,1,0:T(8,128)S(1)} %get-tuple-element.35), channel_id=1, source_target_pairs={{0,3},{1,2},{2,1},{3,0},{4,7},{5,6},{6,5},{7,4},{8,11},{9,10},{10,... | collective-permute-start | bytes 589832 | tf_op jit(solution)/shard_map/ppermute | solution.py:26
  71.7 8.4 %collective-permute-start.17 = (f32[8,3,16,128]{3,2,1,0:T(8,128)S(1)}, f32[8,3,16,128]{3,2,1,0:T(8,128)S(1)}, u32[]{:S(2)}, u32[]{:S(2)}) collective-permute-start(f32[8,3,16,128]{3,2,1,0:T(8,128)S(1)} %get-tuple-element.36), channel_id=1, source_target_pairs={{0,8},{1,9},{2,10},{3,11},{4,12},{5,13},{6,14},{7,15},{8,0},{9,1},... | collective-permute-start | bytes 589832 | tf_op jit(solution)/shard_map/ppermute | solution.py:26
  73.1 9.4 %collective-permute-start.15 = (f32[8,3,16,128]{3,2,1,0:T(8,128)S(1)}, f32[8,3,16,128]{3,2,1,0:T(8,128)S(1)}, u32[]{:S(2)}, u32[]{:S(2)}) collective-permute-start(f32[8,3,16,128]{3,2,1,0:T(8,128)S(1)} %get-tuple-element.37), channel_id=1, source_target_pairs={{0,24},{1,25},{2,26},{3,27},{4,28},{5,29},{6,30},{7,31},{8,16},{9,... | collective-permute-start | bytes 589832 | tf_op jit(solution)/shard_map/ppermute | solution.py:26
  76.5 9.9 %collective-permute-start.24 = (f32[16,3,16,128]{3,2,1,0:T(8,128)S(1)}, f32[16,3,16,128]{3,2,1,0:T(8,128)S(1)}, u32[]{:S(2)}, u32[]{:S(2)}) collective-permute-start(f32[16,3,16,128]{3,2,1,0:T(8,128)S(1)} %pad_maximum_fusion.5.refs_3_), channel_id=1, source_target_pairs={{0,3},{1,2},{2,1},{3,0},{4,7},{5,6},{6,5},{7,4},{8,11},{9,10},{10,... | collective-permute-start | bytes 1179656 | tf_op jit(solution)/shard_map/ppermute | solution.py:26
  77.6 8.7 %collective-permute-start.22 = (f32[16,3,16,128]{3,2,1,0:T(8,128)S(1)}, f32[16,3,16,128]{3,2,1,0:T(8,128)S(1)}, u32[]{:S(2)}, u32[]{:S(2)}) collective-permute-start(f32[16,3,16,128]{3,2,1,0:T(8,128)S(1)} %pad_maximum_fusion.4.refs_2_), channel_id=1, source_target_pairs={{0,1},{1,0},{2,3},{3,2},{4,5},{5,4},{6,7},{7,6},{8,9},{9,8},{10,11... | collective-permute-start | bytes 1179656 | tf_op jit(solution)/shard_map/ppermute | solution.py:26
  80.2 9.1 %collective-permute-start.18 = (f32[16,3,16,128]{3,2,1,0:T(8,128)S(1)}, f32[16,3,16,128]{3,2,1,0:T(8,128)S(1)}, u32[]{:S(2)}, u32[]{:S(2)}) collective-permute-start(f32[16,3,16,128]{3,2,1,0:T(8,128)S(1)} %pad_maximum_fusion.2.refs_1_), channel_id=1, source_target_pairs={{0,24},{1,25},{2,26},{3,27},{4,28},{5,29},{6,30},{7,31},{8,16},{9,... | collective-permute-start | bytes 1179656 | tf_op jit(solution)/shard_map/ppermute | solution.py:26
  82.5 7.9 %collective-permute-start.16 = (f32[16,3,16,128]{3,2,1,0:T(8,128)S(1)}, f32[16,3,16,128]{3,2,1,0:T(8,128)S(1)}, u32[]{:S(2)}, u32[]{:S(2)}) collective-permute-start(f32[16,3,16,128]{3,2,1,0:T(8,128)S(1)} %pad_maximum_fusion.1.refs_0_), channel_id=1, source_target_pairs={{0,8},{1,9},{2,10},{3,11},{4,12},{5,13},{6,14},{7,15},{8,0},{9,1},... | collective-permute-start | bytes 1179656 | tf_op jit(solution)/shard_map/ppermute | solution.py:26
  86.3 26.7 %copy-start = (bf16[128,16384]{1,0:T(8,128)(2,1)S(1)}, bf16[128,16384]{1,0:T(8,128)(2,1)}, u32[]{:S(2)}) copy-start(bf16[128,16384]{1,0:T(8,128)(2,1)} %zeta.1) | copy-start | bytes 12582916
  94.0 1.3 collective-permute-start.25
  114.4 1.2 collective-permute-start.26
  115.6 4.9 %collective-permute-start.27 = (f32[16,128]{1,0:T(8,128)S(1)}, f32[16,128]{1,0:T(8,128)S(1)}, u32[]{:S(2)}, u32[]{:S(2)}) collective-permute-start(f32[16,128]{1,0:T(8,128)S(1)} %add.102), channel_id=1, source_target_pairs={{0,64},{32,96},{64,0},{96,32},{128,192},{160,224},{192,128},{224,1... | collective-permute-start | bytes 24584 | tf_op jit(solution)/shard_map/ppermute | solution.py:26
  120.5 6.7 %copy-start.10 = (f32[16,128]{1,0:T(8,128)}, f32[16,128]{1,0:T(8,128)S(1)}, u32[]{:S(2)}) copy-start(f32[16,128]{1,0:T(8,128)S(1)} %add.103.one) | copy-start | bytes 24580
  120.5 6.7 %collective-permute-start.28 = (f32[16,128]{1,0:T(8,128)S(1)}, f32[16,128]{1,0:T(8,128)S(1)}, u32[]{:S(2)}, u32[]{:S(2)}) collective-permute-start(f32[16,128]{1,0:T(8,128)S(1)} %add.103.one), channel_id=1, source_target_pairs={{0,192},{32,224},{64,128},{96,160},{128,64},{160,96},{192,0},{224,... | collective-permute-start | bytes 24584 | tf_op jit(solution)/shard_map/ppermute | solution.py:26
  127.2 0.6 copy-start.11

commit v3 on v2

v3 whole, which is shorter than its diff:
```python
import functools

import jax
import jax.numpy as jnp
from jax import lax
from jax.experimental import pallas as pl
from jax.experimental.pallas import tpu as pltpu
from jax.sharding import PartitionSpec as P

MASKS = (((8, 24, 1, 3, 4), (1, 3, 8, 24, 4)), ((24, 8, 1, 3, 4), (3, 1, 8, 24, 4)))
CB, VB = 4, 8
F32, BF16 = jnp.float32, jnp.bfloat16
VMEM, SMEM = pl.BlockSpec(memory_space=pltpu.VMEM), pl.BlockSpec(memory_space=pltpu.SMEM)
HBM = pl.BlockSpec(memory_space=pltpu.HBM)


def code_of(place, kpoint):
    index, core = place[0], place[1]
    x, z, y = index >> 3, (index >> 2) & 1, index & 3

    first, second = x + (y - x) * core, y + (x - y) * core
    one, two = (first ^ (first >> 1)) & 1, first >> 1
    quarter = one << 1 | two if kpoint == 0 else two << 1 | one
    return quarter, ((second ^ (second >> 1)) & 1) << 2 | (second >> 1) << 1 | z


def swap(value, axis, mask):
    return lax.ppermute(value, axis, [(i, i ^ mask) for i in range(lax.axis_size(axis))])


def cross(value, kpoint, dim):
    groups, ways = lax.axis_size("ka"), lax.axis_size("wa")
    pairs = [
        (group * ways + i, group * ways + (i ^ MASKS[kpoint][group & 1][dim]))
        for group in range(groups)
        for i in range(ways)
    ]
    return lax.ppermute(value, ("ka", "wa"), pairs)


def everyone(value, axis):
    parts = lax.axis_size(axis)
    return lax.all_to_all(jnp.broadcast_to(value[None], (parts,) + value.shape), axis, 0, 0)


def scattered(parts):
    held = []
    for kpoint, (keep, send) in enumerate(parts):
        got = cross(send, kpoint, 0)
        half = keep.shape[0] // 2
        more = cross(keep[half:] + got[half:], kpoint, 1)
        held.append((keep[:half] + got[:half], more))
    half = held[0][0].shape[0] // 2
    keep = jnp.stack([own[:half] + got[:half] for own, got in held])
    send = jnp.stack([own[half:] + got[half:] for own, got in held])
    got = cross(send, 0, 2)
    half = half // 2
    keep, send = keep[:, :half] + got[:, :half], keep[:, half:] + got[:, half:]
    return keep + cross(send, 0, 3)


def gathered_chunks(held):
    for dim in (3, 2):
        held = jnp.concatenate([held, cross(held, 0, dim)], axis=1)
    halves = []
    for kpoint in range(held.shape[0]):
        own = jnp.concatenate([held[kpoint], cross(held[kpoint], kpoint, 1)])
        halves.append((own, cross(own, kpoint, 0)))
    return halves


def momentum_kernel(kpoint, half, place_ref, miller_ref, val_ref, cond_ref, out, weighted, values, blocks, value_sems, sems):
    nval = values.shape[0]
    rows = nval // VB
    cols = out.shape[3]
    me_c, me_v = code_of(place_ref, kpoint)
    piece = nval // value_sems.shape[0]
    value_copies, copies = [], []
    for number in range(value_sems.shape[0]):
        lines = pl.ds(number * piece, piece)
        value_copies.append(
            pltpu.make_async_copy(val_ref.at[kpoint, lines], values.at[lines], value_sems.at[number])
        )
    for part in range(2):
        start = ((2 * half + part) ^ me_c) * cols
        piece = cols // sems.shape[1]
        for number in range(sems.shape[1]):
            source = pl.ds(pl.multiple_of(start + number * piece, piece), piece)
            copies.append(
                pltpu.make_async_copy(
                    cond_ref.at[kpoint, source],
                    blocks.at[part, pl.ds(number * piece, piece)],
                    sems.at[part, number],
                )
            )
    for copy in value_copies + copies:
        copy.start()
    for copy in value_copies:
        copy.wait()
    for place in range(VB):
        source = pl.multiple_of((place ^ me_v) * rows, rows)
        block = values[pl.ds(source, rows), :].astype(F32)
        for axis in range(3):
            factor = miller_ref[axis : axis + 1, :].astype(F32)
            weighted[axis * nval + place * rows : axis * nval + (place + 1) * rows, :] = (
                block * factor
            ).astype(BF16)
    for part in range(2):
        for copy in copies[part * sems.shape[1] : (part + 1) * sems.shape[1]]:
            copy.wait()
        result = lax.dot_general(
            weighted[...], blocks[part], (((1,), (1,)), ((), ())), preferred_element_type=F32
        )
        for eighth in range(VB):
            for axis in range(3):
                start = axis * nval + eighth * rows
                out[part * VB + eighth, axis] = result[start : start + rows]


def partial_momentum(kpoint, half, place, coeff_val, miller, coeff_cond):
    _, nval, depth = coeff_val.shape
    ncond = coeff_cond.shape[1]
    rows, cols = nval // VB, ncond // CB
    return pl.pallas_call(
        functools.partial(momentum_kernel, kpoint, half),
        out_shape=jax.ShapeDtypeStruct((CB * VB // 2, 3, rows, cols), F32),
        in_specs=[SMEM, VMEM, HBM, HBM],
        out_specs=VMEM,
        scratch_shapes=[
            pltpu.VMEM((3 * nval, depth), BF16),
            pltpu.VMEM((nval, depth), BF16),
            pltpu.VMEM((2, cols, depth), BF16),
            pltpu.SemaphoreType.DMA((4,)),
            pltpu.SemaphoreType.DMA((2, 8)),
        ],
        cost_estimate=pl.CostEstimate(
            flops=3 * nval * ncond * depth,
            bytes_accessed=(2 * nval + ncond) * depth + 6 * nval * ncond,
            transcendentals=0,
        ),
        compiler_params=pltpu.CompilerParams(vmem_limit_bytes=56 << 20),
        name="momentum_to_send" if half else "momentum_to_keep",
    )(place, miller, coeff_val, coeff_cond)


def pair_kernel(half, kpoints, place_ref, weight_ref, freq_ref, energy_val, energy_cond, orbit_val, orbit_cond, *refs):
    _, nval, points = orbit_val.shape
    ncond = orbit_cond.shape[1]
    nfreq = freq_ref.shape[0]
    count = len(kpoints)
    chunks, refs = refs[:count], refs[count:]
    before, refs = (refs[0], refs[1:]) if half else (None, refs)
    outs, (total, amplitude, level, orbits, weight) = refs[:-5], refs[-5:]
    rows, cols = chunks[0].shape[2:]
    scale = float(nval * ncond) ** (-0.5)
    tops = 3 * nfreq
    for spot, k in enumerate(kpoints):
        chunk = chunks[spot]
        me_c, me_v = code_of(place_ref, k)
        level[spot] = jnp.transpose(jnp.broadcast_to(energy_val[k : k + 1, :], (nval, nval)))
        top = []
        for part in range(2):
            start = pl.multiple_of(((2 * half + part) ^ me_c) * cols, cols)
            top.append(energy_cond[k : k + 1, pl.ds(start, cols)])
            orbits[spot, part * cols : (part + 1) * cols, :] = orbit_cond[k, pl.ds(start, cols), :]

        def bottom_of(where, spot=spot):
            return jnp.concatenate([level[spot, where, :]] * (cols // nval), axis=1)

        def factors_of(gap):
            square = gap * gap
            return [4.0 / (square + freq_ref[w] * freq_ref[w]) for w in range(nfreq)]

        def eighth(place, carry, k=k, spot=spot, me_v=me_v, top=top, chunk=chunk, bottom_of=bottom_of):
            mine = pl.ds(pl.multiple_of(place * rows, rows), rows)
            theirs = pl.ds(pl.multiple_of((place ^ me_v) * rows, rows), rows)
            weight[spot, mine, :] = orbit_val[k, theirs, :].astype(F32) * (weight_ref[k] * scale)
            bottom = bottom_of(theirs)
            for part in range(2):
                factors = factors_of(top[part] - bottom)
                for axis in range(3):
                    momentum = chunk[part * VB + place, axis]
                    for w in range(nfreq):
                        start = pl.multiple_of((axis * nfreq + w) * nval + place * rows, rows)
                        amplitude[spot, pl.ds(start, rows), part * cols : (part + 1) * cols] = (
                            momentum * factors[w]
                        ).astype(BF16)
            return carry

        lax.fori_loop(0, VB, eighth, 0, unroll=2)
        for axis in range(3):
            first = axis * nfreq * nval
            expanded = jnp.dot(
                amplitude[spot, first : first + nfreq * nval, :], orbits[spot], preferred_element_type=F32
            )
            for w in range(nfreq):
                row = slice(axis * nfreq + w, axis * nfreq + w + 1)
                value = jnp.sum(expanded[w * nval : (w + 1) * nval] * weight[spot], axis=0, keepdims=True)
                if spot > 0:
                    value = value + total[row, :]
                elif half:
                    value = value + before[row, :]
                total[row, :] = value

        if not half:
            bottom = bottom_of(pl.ds(pl.multiple_of(me_v * rows, rows), rows))
            gap = top[0] - bottom
            ratios = [factor / gap for factor in factors_of(gap)]
            for axis in range(3):
                square = chunk[0, axis] * chunk[0, axis]
                row = slice(tops + axis, tops + axis + 1)
                for w in range(nfreq):
                    value = jnp.sum(square * ratios[w], axis=0, keepdims=True)
                    value = (value[:, :nval] + value[:, nval:]) * (weight_ref[k] / float(nval * ncond))
                    lanes = slice(w * nval, (w + 1) * nval)
                    total[row, lanes] = value + total[row, lanes] if spot else value
            row = slice(tops + 3, tops + 4)
            value = jnp.full((1, points), weight_ref[k], F32)
            total[row, :] = value + total[row, :] if spot else value
    if half:
        total[tops:, :] = before[tops:, :]
    if len(outs) == 2:
        keep, send = outs
        across = points // 2
        keep[...] = total[:, pl.ds(pl.multiple_of(place_ref[1] * across, across), across)]
        send[...] = total[:, pl.ds(pl.multiple_of((1 - place_ref[1]) * across, across), across)]
    else:
        outs[0][...] = total[...]


def pair_sums(half, kpoints, place, weights, freqs, energy_val, energy_cond, orbit_val, orbit_cond, chunks, before, parts):
    _, nval, points = orbit_val.shape
    ncond = orbit_cond.shape[1]
    nfreq = freqs.shape[0]
    height = 3 * nfreq + 4
    depth = ncond // 2
    count = len(kpoints)
    operands = [energy_val, energy_cond, orbit_val, orbit_cond, *chunks, *before]
    return pl.pallas_call(
        functools.partial(pair_kernel, half, kpoints),
        out_shape=[jax.ShapeDtypeStruct((height, points // parts), F32)] * parts,
        in_specs=[SMEM] * 3 + [VMEM] * len(operands),
        out_specs=[VMEM] * parts,
        scratch_shapes=[
            pltpu.VMEM((height, points), F32),
            pltpu.VMEM((count, 3 * nfreq * nval, depth), BF16),
            pltpu.VMEM((count, nval, nval), F32),
            pltpu.VMEM((count, depth, points), BF16),
            pltpu.VMEM((count, nval, points), F32),
        ],
        cost_estimate=pl.CostEstimate(
            flops=count * 2 * 3 * nfreq * nval * depth * points,
            bytes_accessed=count * (12 * nval * depth + 4 * depth * points),
            transcendentals=0,
        ),
        compiler_params=pltpu.CompilerParams(vmem_limit_bytes=20 << 20),
        name="pair_sums",
    )(place, weights, freqs, *operands)


def wing_kernel(place_ref, gathered, zeta, out):
    ways, height, points = gathered.shape
    slab_rows = zeta.shape[0]
    tops = height - 4
    total = jnp.zeros((3 * height, slab_rows), F32)
    last = jnp.zeros((4, points), F32)
    for device in range(ways):
        value = gathered[device]
        last = last + value[tops:]
        pieces = []
        for _ in range(3):
            rounded = value.astype(BF16)
            pieces.append(rounded)
            value = value - rounded.astype(F32)
        start = pl.multiple_of((2 * device + place_ref[1]) * points, points)
        total = total + lax.dot_general(
            jnp.concatenate(pieces, axis=0),
            zeta[:, pl.ds(start, points)],
            (((1,), (1,)), ((), ())),
            preferred_element_type=F32,
        )
    total = total[:height] + total[height : 2 * height] + total[2 * height :]
    out[:tops] = total[:tops]
    lane = lax.broadcasted_iota(jnp.int32, (3, slab_rows), 1)
    across = points // 2
    head = jnp.zeros((3, slab_rows), F32)
    for tile in range(2):
        value = jnp.sum(last[:3, tile * across : (tile + 1) * across], axis=1, keepdims=True)
        head = jnp.where(lane == 2 * place_ref[1] + tile, value, head)
    out[tops : tops + 3] = head
    out[tops + 3 :] = last[3:, :slab_rows]


def wing_sums(place, gathered, zeta):
    ways, height, points = gathered.shape
    slab_rows = zeta.shape[0]
    return pl.pallas_call(
        wing_kernel,
        out_shape=jax.ShapeDtypeStruct((height, slab_rows), F32),
        in_specs=[SMEM, VMEM, VMEM],
        out_specs=VMEM,
        cost_estimate=pl.CostEstimate(
            flops=6 * height * slab_rows * ways * points,
            bytes_accessed=4 * slab_rows * ways * points + 4 * height * ways * points,
            transcendentals=0,
        ),
        compiler_params=pltpu.CompilerParams(vmem_limit_bytes=20 << 20),
        name="wing_sums",
    )(place, gathered, zeta)


def final_kernel(copies, one, two, three, four, wing, head):
    total = (one[...] + two[...]) + (three[...] + four[...])
    tops = total.shape[0] - 4
    nfreq = wing.shape[1]
    scale = copies / total[tops + 3 :]
    for axis in range(3):
        wing[axis] = total[axis * nfreq : (axis + 1) * nfreq] * scale
    head[...] = total[tops : tops + 3, :nfreq] * scale[:, :nfreq]


def local(
    coeff_val,
    coeff_cond,
    miller,
    energy_val,
    energy_cond,
    orbit_val,
    orbit_cond,
    zeta,
    freqs,
    kweight,
):
    kcount, nval, npw_dev = coeff_val.shape
    nfreq = freqs.shape[0]
    slab_rows = zeta.shape[0]
    ways = lax.axis_size("wa")
    pw_factor = float(npw_dev * ways) ** (-0.5)
    weights = kweight.astype(F32)
    place = jnp.stack([lax.axis_index("wa"), lax.axis_index("ka") & 1]).astype(jnp.int32)

    sends = [partial_momentum(k, 1, place, coeff_val, miller, coeff_cond) for k in range(kcount)]
    keeps = [partial_momentum(k, 0, place, coeff_val, miller, coeff_cond) for k in range(kcount)]
    mine = scattered(list(zip(keeps, sends)))
    mine = (mine + swap(mine, "wa", MASKS[0][0][4])[:, ::-1]) * pw_factor

    (own_0, got_0), (own_1, got_1) = gathered_chunks(mine)
    operands = (place, weights, freqs, energy_val, energy_cond, orbit_val, orbit_cond)
    pair = pair_sums(0, (0, 1), *operands, [own_0, own_1], [], 1)
    pair = pair_sums(1, (0,), *operands, [got_0], pair, 1)
    keep, send = pair_sums(1, (1,), *operands, [got_1], pair, 2)
    pair = keep + swap(send, "ka", 1)
    total = wing_sums(place, everyone(pair, "wa"), zeta)
    total = total + swap(total, "ka", 1)
    return pl.pallas_call(
        functools.partial(final_kernel, float(2 * ways)),
        out_shape=[
            jax.ShapeDtypeStruct((3, nfreq, slab_rows), F32),
            jax.ShapeDtypeStruct((3, nfreq), F32),
        ],
        in_specs=[VMEM] * 4,
        out_specs=[VMEM] * 2,
        compiler_params=pltpu.CompilerParams(vmem_limit_bytes=4 << 20),
        name="final",
    )(total, *[swap(total, "ka", mask) for mask in (2, 4, 6)])


def solution(mesh):
    return jax.shard_map(
        local,
        mesh=mesh,
        in_specs=(
            P("ka", None, "wa"),
            P("ka", None, "wa"),
            P(None, "wa"),
            P("ka", None),
            P("ka", None),
            P("ka", None, "wa"),
            P("ka", None, "wa"),
            P("wa", None),
            P(),
            P("ka"),
        ),
        out_specs=(P(None, None, "wa"), P()),
        check_vma=False,
    )
```

time: 129 us -> 141 us (1.093)
  starting transfers between devices: 44.9 us -> 25.7 us
  waiting for transfers between devices: 38.5 us -> 56.8 us
  Pallas kernels: 16.8 us -> 33.1 us
  local copies, waits for them, and re-layouts: 9.4 us -> 0.16 us
  blocking collectives: 17.7 us -> 21.7 us
  other arithmetic: 0.72 us -> 2.5 us
    ppermute x29 -> x18, starting transfers between devices: 44.9 us -> 25.7 us  [the longest x12 15.8 us: cross(): return lax.ppermute(value, ('ka', 'wa'), pairs)]
    ppermute x29 -> x18, waiting for transfers between devices: 38.5 us -> 56.8 us  [the longest x12 44.9 us: cross(): return lax.ppermute(value, ('ka', 'wa'), pairs)]
    pallas_call x4 -> x7, Pallas kernels: 14.2 us -> 31.2 us  [the longest x4 23.4 us: partial_momentum(): pl.pallas_call(functools.partial(momentum_kernel, kpoint, half), out_shap...]
    squeeze x5 -> x1, local copies, waits for them, and re-layouts: 6.36 us -> 0.05 us  [gathered_chunks(): own = jnp.concatenate([held[kpoint], cross(held[kpoint], kpoint, 1)])]
    all_to_all x1, blocking collectives: 17.7 us -> 21.7 us  [everyone(): lax.all_to_all(jnp.broadcast_to(value[None], (parts,) + value.shape), axi...]
    unnamed x26 -> x18, local copies, waits for them, and re-layouts: 2.99 us -> 0.05 us
  transfers between devices with their start and end apart: 29 -> 18, of which waited for: 18 -> 13; matrix products, arithmetic and copies ran while one was open for 0% -> 1% of each run, Pallas kernels for 6% -> 16%
where the time goes in v3:
time: 141 us
  waiting for transfers between devices  56.8 us (40%)
  Pallas kernels  33.1 us (23%)
  starting transfers between devices  25.7 us (18%)
  blocking collectives  21.7 us (15%)
  other arithmetic  2.5 us (2%)
    ppermute x12, waiting for transfers between devices, cross(): return lax.ppermute(value, ('ka', 'wa'), pairs)  44.9 us
    pallas_call x4, Pallas kernels, partial_momentum(): pl.pallas_call(functools.partial(momentum_kernel, kpoint, half), out_shap...  23.4 us
    all_to_all x1, blocking collectives, everyone(): lax.all_to_all(jnp.broadcast_to(value[None], (parts,) + value.shape), axi...  21.7 us
    ppermute x12, starting transfers between devices, cross(): return lax.ppermute(value, ('ka', 'wa'), pairs)  15.8 us
    ppermute x6, waiting for transfers between devices, swap(): lax.ppermute(value, axis, [(i, i ^ mask) for i in range(lax.axis_size(axi...  11.9 us
    ppermute x6, starting transfers between devices, swap(): lax.ppermute(value, axis, [(i, i ^ mask) for i in range(lax.axis_size(axi...  9.87 us
    pallas_call x3, Pallas kernels, pair_sums(): pl.pallas_call(functools.partial(pair_kernel, half, kpoints), out_shape=[...  7.76 us
  transfers between devices with their start and end apart: 18, of which 13 were waited for; matrix products, arithmetic and copies ran while one was open for 1% of the time, Pallas kernels for 16%

profile of v3, /device:TPU:8, one launch (start us, length us, event | category | flops | bytes accessed | tf_op | source)
XLA Modules:
  0.0 140.8 jit_solution(2659266055913820430)
XLA Ops:
  0.6 0.7 pad_add_fusion.place_ref
  1.3 5.8 %momentum_to_send.2 = f32[16,3,16,256]{3,2,1,0:T(8,128)} custom-call(s32[2]{0:T(128)} %pad_add_fusion.place_ref, s32[3,2048]{1,0:T(4,128)} %miller_ref.7, bf16[2,128,2048]{2,1,0:T(8,128)(2,1)} %val_ref.7, bf16[2,1024,2048]{2,1,0:T(8,128)(2,1)} %cond_ref.7), custom_call_target="tpu_custom_call" | custom-call | flops 805306368 | bytes 3407872 | tf_op jit(solution)/shard_map/momentum_to_send/pallas_call | solution.py:124
  7.2 1.6 %collective-permute-start = (f32[16,3,16,256]{3,2,1,0:T(8,128)}, f32[16,3,16,256]{3,2,1,0:T(8,128)S(1)}, u32[]{:S(2)}, u32[]{:S(2)}) collective-permute-start(f32[16,3,16,256]{3,2,1,0:T(8,128)} %momentum_to_send.2), channel_id=1, source_target_pairs={{0,8},{1,9},{2,10},{3,11},{4,12},{5,13},{6,14},{7,15},{8,0},{9,1},... | collective-permute-start | bytes 2359304 | tf_op jit(solution)/shard_map/ppermute | solution.py:38
  8.7 5.8 %momentum_to_send.3 = f32[16,3,16,256]{3,2,1,0:T(8,128)} custom-call(s32[2]{0:T(128)} %pad_add_fusion.place_ref, s32[3,2048]{1,0:T(4,128)} %miller_ref.7, bf16[2,128,2048]{2,1,0:T(8,128)(2,1)} %val_ref.7, bf16[2,1024,2048]{2,1,0:T(8,128)(2,1)} %cond_ref.7), custom_call_target="tpu_custom_call" | custom-call | flops 805306368 | bytes 3407872 | tf_op jit(solution)/shard_map/momentum_to_send/pallas_call | solution.py:124
  14.6 2.2 %collective-permute-start.2 = (f32[16,3,16,256]{3,2,1,0:T(8,128)}, f32[16,3,16,256]{3,2,1,0:T(8,128)S(1)}, u32[]{:S(2)}, u32[]{:S(2)}) collective-permute-start(f32[16,3,16,256]{3,2,1,0:T(8,128)} %momentum_to_send.3), channel_id=1, source_target_pairs={{0,24},{1,25},{2,26},{3,27},{4,28},{5,29},{6,30},{7,31},{8,16},{9,... | collective-permute-start | bytes 2359304 | tf_op jit(solution)/shard_map/ppermute | solution.py:38
  16.7 5.8 %momentum_to_keep.2 = f32[16,3,16,256]{3,2,1,0:T(8,128)} custom-call(s32[2]{0:T(128)} %pad_add_fusion.place_ref, s32[3,2048]{1,0:T(4,128)} %miller_ref.7, bf16[2,128,2048]{2,1,0:T(8,128)(2,1)} %val_ref.7, bf16[2,1024,2048]{2,1,0:T(8,128)(2,1)} %cond_ref.7), custom_call_target="tpu_custom_call" | custom-call | flops 805306368 | bytes 3407872 | tf_op jit(solution)/shard_map/momentum_to_keep/pallas_call | solution.py:124
  22.6 5.9 %momentum_to_keep.3 = f32[16,3,16,256]{3,2,1,0:T(8,128)} custom-call(s32[2]{0:T(128)} %pad_add_fusion.place_ref, s32[3,2048]{1,0:T(4,128)} %miller_ref.7, bf16[2,128,2048]{2,1,0:T(8,128)(2,1)} %val_ref.7, bf16[2,1024,2048]{2,1,0:T(8,128)(2,1)} %cond_ref.7), custom_call_target="tpu_custom_call" | custom-call | flops 805306368 | bytes 3407872 | tf_op jit(solution)/shard_map/momentum_to_keep/pallas_call | solution.py:124
  28.5 0.1 slice_add_fusion.3
  28.7 1.2 collective-permute-start.1
  29.9 1.3 slice_add_fusion.1
  31.2 0.1 collective-permute-start.3
  31.3 6.5 %collective-permute-done.1 = f32[8,3,16,256]{3,2,1,0:T(8,128)S(1)} collective-permute-done((f32[8,3,16,256]{3,2,1,0:T(8,128)S(1)}, f32[8,3,16,256]{3,2,1,0:T(8,128)S(1)}, u32[]{:S(2)}, u32[]{:S(2)}) %collective-permute-start.1) | collective-permute-done | bytes 393248 | tf_op jit(solution)/shard_map/ppermute | solution.py:38
  37.7 0.1 fusion.6
  37.8 1.4 %collective-permute-done.3 = f32[8,3,16,256]{3,2,1,0:T(8,128)S(1)} collective-permute-done((f32[8,3,16,256]{3,2,1,0:T(8,128)S(1)}, f32[8,3,16,256]{3,2,1,0:T(8,128)S(1)}, u32[]{:S(2)}, u32[]{:S(2)}) %collective-permute-start.3) | collective-permute-done | bytes 393248 | tf_op jit(solution)/shard_map/ppermute | solution.py:38
  39.2 0.1 fusion.5
  39.3 0.6 collective-permute-start.4
  39.9 7.3 %collective-permute-done.4 = f32[2,4,3,16,256]{4,3,2,1,0:T(8,128)S(1)} collective-permute-done((f32[2,4,3,16,256]{4,3,2,1,0:T(8,128)S(1)}, f32[2,4,3,16,256]{4,3,2,1,0:T(8,128)S(1)}, u32[]{:S(2)}, u32[]{:S(2)}) %collective-permute-start.4) | collective-permute-done | bytes 393248 | tf_op jit(solution)/shard_map/ppermute | solution.py:38
  47.3 1.7 %collective-permute-start.5 = (f32[2,2,3,16,256]{4,3,2,1,0:T(8,128)S(1)}, f32[2,2,3,16,256]{4,3,2,1,0:T(8,128)S(1)}, u32[]{:S(2)}, u32[]{:S(2)}) collective-permute-start(f32[2,2,3,16,256]{4,3,2,1,0:T(8,128)S(1)} %slice_add_fusion.4), channel_id=1, source_target_pairs={{0,3},{1,2},{2,1},{3,0},{4,7},{5,6},{6,5},{7,4},{8,11},{9,10},{10,... | collective-permute-start | bytes 589832 | tf_op jit(solution)/shard_map/ppermute | solution.py:38
  49.0 4.1 %collective-permute-done.5 = f32[2,2,3,16,256]{4,3,2,1,0:T(8,128)S(1)} collective-permute-done((f32[2,2,3,16,256]{4,3,2,1,0:T(8,128)S(1)}, f32[2,2,3,16,256]{4,3,2,1,0:T(8,128)S(1)}, u32[]{:S(2)}, u32[]{:S(2)}) %collective-permute-start.5) | collective-permute-done | bytes 196640 | tf_op jit(solution)/shard_map/ppermute | solution.py:38
  53.1 2.0 %collective-permute-start.6 = (f32[2,2,3,16,256]{4,3,2,1,0:T(8,128)S(1)}, f32[2,2,3,16,256]{4,3,2,1,0:T(8,128)S(1)}, u32[]{:S(2)}, u32[]{:S(2)}) collective-permute-start(f32[2,2,3,16,256]{4,3,2,1,0:T(8,128)S(1)} %fusion.2), channel_id=1, source_target_pairs={{0,4},{1,5},{2,6},{3,7},{4,0},{5,1},{6,2},{7,3},{8,12},{9,13},{10,... | collective-permute-start | bytes 589832 | tf_op jit(solution)/shard_map/ppermute | solution.py:28
  55.1 3.7 %collective-permute-done.6 = f32[2,2,3,16,256]{4,3,2,1,0:T(8,128)S(1)} collective-permute-done((f32[2,2,3,16,256]{4,3,2,1,0:T(8,128)S(1)}, f32[2,2,3,16,256]{4,3,2,1,0:T(8,128)S(1)}, u32[]{:S(2)}, u32[]{:S(2)}) %collective-permute-start.6) | collective-permute-done | bytes 196640 | tf_op jit(solution)/shard_map/ppermute | solution.py:28
  58.9 1.7 %collective-permute-start.7 = (f32[2,2,3,16,256]{4,3,2,1,0:T(8,128)S(1)}, f32[2,2,3,16,256]{4,3,2,1,0:T(8,128)S(1)}, u32[]{:S(2)}, u32[]{:S(2)}) collective-permute-start(f32[2,2,3,16,256]{4,3,2,1,0:T(8,128)S(1)} %add_multiply_fusion), channel_id=1, source_target_pairs={{0,3},{1,2},{2,1},{3,0},{4,7},{5,6},{6,5},{7,4},{8,11},{9,10},{10,... | collective-permute-start | bytes 589832 | tf_op jit(solution)/shard_map/ppermute | solution.py:38
  60.6 4.1 %collective-permute-done.7 = f32[2,2,3,16,256]{4,3,2,1,0:T(8,128)S(1)} collective-permute-done((f32[2,2,3,16,256]{4,3,2,1,0:T(8,128)S(1)}, f32[2,2,3,16,256]{4,3,2,1,0:T(8,128)S(1)}, u32[]{:S(2)}, u32[]{:S(2)}) %collective-permute-start.7) | collective-permute-done | bytes 196640 | tf_op jit(solution)/shard_map/ppermute | solution.py:38
  64.7 3.0 %collective-permute-start.8 = (f32[2,4,3,16,256]{4,3,2,1,0:T(8,128)S(1)}, f32[2,4,3,16,256]{4,3,2,1,0:T(8,128)S(1)}, u32[]{:S(2)}, u32[]{:S(2)}) collective-permute-start(f32[2,4,3,16,256]{4,3,2,1,0:T(8,128)S(1)} %pad_maximum_fusion.4), channel_id=1, source_target_pairs={{0,1},{1,0},{2,3},{3,2},{4,5},{5,4},{6,7},{7,6},{8,9},{9,8},{10,11... | collective-permute-start | bytes 1179656 | tf_op jit(solution)/shard_map/ppermute | solution.py:38
  67.7 7.7 %collective-permute-done.8 = f32[2,4,3,16,256]{4,3,2,1,0:T(8,128)S(1)} collective-permute-done((f32[2,4,3,16,256]{4,3,2,1,0:T(8,128)S(1)}, f32[2,4,3,16,256]{4,3,2,1,0:T(8,128)S(1)}, u32[]{:S(2)}, u32[]{:S(2)}) %collective-permute-start.8) | collective-permute-done | bytes 393248 | tf_op jit(solution)/shard_map/ppermute | solution.py:38
  75.4 0.1 pad_maximum_fusion
  75.5 0.1 slice_bitcast_fusion
  75.5 1.3 collective-permute-start.11
  76.8 0.5 collective-permute-start.9
  77.3 7.5 %collective-permute-done.11 = f32[8,3,16,256]{3,2,1,0:T(8,128)S(1)} collective-permute-done((f32[8,3,16,256]{3,2,1,0:T(8,128)S(1)}, f32[8,3,16,256]{3,2,1,0:T(8,128)S(1)}, u32[]{:S(2)}, u32[]{:S(2)}) %collective-permute-start.11) | collective-permute-done | bytes 393248 | tf_op jit(solution)/shard_map/ppermute | solution.py:38
  84.8 0.1 pad_maximum_fusion.2.refs_0_
  84.9 0.3 collective-permute-start.12
  85.2 1.8 %collective-permute-start.10 = (f32[16,3,16,256]{3,2,1,0:T(8,128)S(1)}, f32[16,3,16,256]{3,2,1,0:T(8,128)S(1)}, u32[]{:S(2)}, u32[]{:S(2)}) collective-permute-start(f32[16,3,16,256]{3,2,1,0:T(8,128)S(1)} %pad_maximum_fusion.1.refs_1_), channel_id=1, source_target_pairs={{0,24},{1,25},{2,26},{3,27},{4,28},{5,29},{6,30},{7,31},{8,16},{9,... | collective-permute-start | bytes 2359304 | tf_op jit(solution)/shard_map/ppermute | solution.py:38
  87.0 3.6 %pair_sums.3.refs_1_ = f32[16,512]{1,0:T(8,128)S(1)} custom-call(s32[2]{0:T(128)S(1)} %copy-done.4, f32[2]{0:T(128)S(1)} %convert_element_type.3.weight_ref, f32[4]{0:T(128)S(1)} %copy-done.6, f32[2,128]{1,0:T(2,128)S(1)} %copy-done.5, f32[2,1024]{1,0:T(2,128)S(1)} %copy-done.3, bf16[2,128,512]{2,1,0:T(8,128)(2,1)S(1)} %copy-done.2, ...), custom_call_target="tpu_custom_call" | custom-call | flops 1610612736 | bytes 3670016 | tf_op jit(solution)/shard_map/pair_sums/pallas_call | solution.py:239
  90.6 6.3 %collective-permute-done.12.refs_0_ = f32[16,3,16,256]{3,2,1,0:T(8,128)S(1)} collective-permute-done((f32[16,3,16,256]{3,2,1,0:T(8,128)S(1)}, f32[16,3,16,256]{3,2,1,0:T(8,128)S(1)}, u32[]{:S(2)}, u32[]{:S(2)}) %collective-permute-start.12) | collective-permute-done | bytes 786464 | tf_op jit(solution)/shard_map/ppermute | solution.py:38
  96.9 2.1 %pair_sums.4.refs_1_ = f32[16,512]{1,0:T(8,128)S(1)} custom-call(s32[2]{0:T(128)S(1)} %copy-done.4, f32[2]{0:T(128)S(1)} %convert_element_type.3.weight_ref, f32[4]{0:T(128)S(1)} %copy-done.6, f32[2,128]{1,0:T(2,128)S(1)} %copy-done.5, f32[2,1024]{1,0:T(2,128)S(1)} %copy-done.3, bf16[2,128,512]{2,1,0:T(8,128)(2,1)S(1)} %copy-done.2, ...), custom_call_target="tpu_custom_call" | custom-call | flops 805306368 | bytes 1835008 | tf_op jit(solution)/shard_map/pair_sums/pallas_call | solution.py:239
  99.0 2.1 %pair_sums.5 = (f32[16,256]{1,0:T(8,128)S(1)}, f32[16,256]{1,0:T(8,128)S(1)}) custom-call(s32[2]{0:T(128)S(1)} %copy-done.4, f32[2]{0:T(128)S(1)} %convert_element_type.3.weight_ref, f32[4]{0:T(128)S(1)} %copy-done.6, f32[2,128]{1,0:T(2,128)S(1)} %copy-done.5, f32[2,1024]{1,0:T(2,128)S(1)} %copy-done.3, bf16[2,128,512]{2,1,0:T(8,128)(2,1)S(1)} %copy-done.2, ...), custom_call_target="tpu_custom_call" | custom-call | flops 805306368 | bytes 1835008 | tf_op jit(solution)/shard_map/pair_sums/pallas_call | solution.py:239
  101.1 0.1 collective-permute-start.13
  101.2 1.2 collective-permute-done.13
  102.4 0.1 broadcast_in_dim.2
  102.5 21.7 %all_to_all.5.gathered = f32[32,16,256]{2,1,0:T(8,128)S(1)} all-to-all(f32[32,16,256]{2,1,0:T(8,128)S(1)} %broadcast_in_dim.2), channel_id=1, replica_groups=mesh['ka'=8,'wa'=32] {'wa'}, dimensions={0} | all-to-all | bytes 1048576 | tf_op jit(solution)/shard_map/all_to_all | solution.py:43
  124.1 1.3 wing_sums.1
  125.5 1.2 collective-permute-done.14
  126.6 3.3 %collective-permute-start.15 = (f32[16,128]{1,0:T(8,128)S(1)}, f32[16,128]{1,0:T(8,128)S(1)}, u32[]{:S(2)}, u32[]{:S(2)}) collective-permute-start(f32[16,128]{1,0:T(8,128)S(1)} %add.55.one), channel_id=1, source_target_pairs={{0,64},{32,96},{64,0},{96,32},{128,192},{160,224},{192,128},{224,1... | collective-permute-start | bytes 24584 | tf_op jit(solution)/shard_map/ppermute | solution.py:28
  129.9 4.5 %collective-permute-start.16 = (f32[16,128]{1,0:T(8,128)S(1)}, f32[16,128]{1,0:T(8,128)S(1)}, u32[]{:S(2)}, u32[]{:S(2)}) collective-permute-start(f32[16,128]{1,0:T(8,128)S(1)} %add.55.one), channel_id=1, source_target_pairs={{0,128},{32,160},{64,192},{96,224},{128,0},{160,32},{192,64},{224,... | collective-permute-start | bytes 24584 | tf_op jit(solution)/shard_map/ppermute | solution.py:28
  134.4 3.1 %collective-permute-done.16.three = f32[16,128]{1,0:T(8,128)S(1)} collective-permute-done((f32[16,128]{1,0:T(8,128)S(1)}, f32[16,128]{1,0:T(8,128)S(1)}, u32[]{:S(2)}, u32[]{:S(2)}) %collective-permute-start.16) | collective-permute-done | bytes 8224 | tf_op jit(solution)/shard_map/ppermute | solution.py:28
  137.5 2.7 %collective-permute-done.17.four = f32[16,128]{1,0:T(8,128)S(1)} collective-permute-done((f32[16,128]{1,0:T(8,128)S(1)}, f32[16,128]{1,0:T(8,128)S(1)}, u32[]{:S(2)}, u32[]{:S(2)}) %collective-permute-start.17) | collective-permute-done | bytes 8224 | tf_op jit(solution)/shard_map/ppermute | solution.py:28
  140.2 0.6 final.1
  (34 shorter events, 0.3 us)
Async XLA Ops:
  7.2 21.3 %collective-permute-start = (f32[16,3,16,256]{3,2,1,0:T(8,128)}, f32[16,3,16,256]{3,2,1,0:T(8,128)S(1)}, u32[]{:S(2)}, u32[]{:S(2)}) collective-permute-start(f32[16,3,16,256]{3,2,1,0:T(8,128)} %momentum_to_send.2), channel_id=1, source_target_pairs={{0,8},{1,9},{2,10},{3,11},{4,12},{5,13},{6,14},{7,15},{8,0},{9,1},... | collective-permute-start | bytes 2359304 | tf_op jit(solution)/shard_map/ppermute | solution.py:38
  14.6 15.3 %collective-permute-start.2 = (f32[16,3,16,256]{3,2,1,0:T(8,128)}, f32[16,3,16,256]{3,2,1,0:T(8,128)S(1)}, u32[]{:S(2)}, u32[]{:S(2)}) collective-permute-start(f32[16,3,16,256]{3,2,1,0:T(8,128)} %momentum_to_send.3), channel_id=1, source_target_pairs={{0,24},{1,25},{2,26},{3,27},{4,28},{5,29},{6,30},{7,31},{8,16},{9,... | collective-permute-start | bytes 2359304 | tf_op jit(solution)/shard_map/ppermute | solution.py:38
  22.6 6.0 %copy-start.7 = (f32[16,3,16,256]{3,2,1,0:T(8,128)S(1)}, f32[16,3,16,256]{3,2,1,0:T(8,128)}, u32[]{:S(2)}) copy-start(f32[16,3,16,256]{3,2,1,0:T(8,128)} %momentum_to_keep.2) | copy-start | bytes 2359300
  28.7 9.1 %collective-permute-start.1 = (f32[8,3,16,256]{3,2,1,0:T(8,128)S(1)}, f32[8,3,16,256]{3,2,1,0:T(8,128)S(1)}, u32[]{:S(2)}, u32[]{:S(2)}) collective-permute-start(f32[8,3,16,256]{3,2,1,0:T(8,128)S(1)} %get-tuple-element.7), channel_id=1, source_target_pairs={{0,24},{1,25},{2,26},{3,27},{4,28},{5,29},{6,30},{7,31},{8,16},{9,... | collective-permute-start | bytes 1179656 | tf_op jit(solution)/shard_map/ppermute | solution.py:38
  31.2 8.1 %collective-permute-start.3 = (f32[8,3,16,256]{3,2,1,0:T(8,128)S(1)}, f32[8,3,16,256]{3,2,1,0:T(8,128)S(1)}, u32[]{:S(2)}, u32[]{:S(2)}) collective-permute-start(f32[8,3,16,256]{3,2,1,0:T(8,128)S(1)} %get-tuple-element.9), channel_id=1, source_target_pairs={{0,8},{1,9},{2,10},{3,11},{4,12},{5,13},{6,14},{7,15},{8,0},{9,1},... | collective-permute-start | bytes 1179656 | tf_op jit(solution)/shard_map/ppermute | solution.py:38
  39.3 7.9 %collective-permute-start.4 = (f32[2,4,3,16,256]{4,3,2,1,0:T(8,128)S(1)}, f32[2,4,3,16,256]{4,3,2,1,0:T(8,128)S(1)}, u32[]{:S(2)}, u32[]{:S(2)}) collective-permute-start(f32[2,4,3,16,256]{4,3,2,1,0:T(8,128)S(1)} %pad_maximum_fusion.3), channel_id=1, source_target_pairs={{0,1},{1,0},{2,3},{3,2},{4,5},{5,4},{6,7},{7,6},{8,9},{9,8},{10,11... | collective-permute-start | bytes 1179656 | tf_op jit(solution)/shard_map/ppermute | solution.py:38
  47.2 39.7 %copy-start.8 = (s32[2]{0:T(128)S(1)}, s32[2]{0:T(128)}, u32[]{:S(2)}) copy-start(s32[2]{0:T(128)} %param.19) | copy-start | bytes 28
  47.2 39.7 %copy-start = (bf16[2,1024,512]{2,1,0:T(8,128)(2,1)S(1)}, bf16[2,1024,512]{2,1,0:T(8,128)(2,1)}, u32[]{:S(2)}) copy-start(bf16[2,1024,512]{2,1,0:T(8,128)(2,1)} %orbit_cond.5) | copy-start | bytes 6291460
  47.3 39.7 %copy-start.2 = (bf16[2,128,512]{2,1,0:T(8,128)(2,1)S(1)}, bf16[2,128,512]{2,1,0:T(8,128)(2,1)}, u32[]{:S(2)}) copy-start(bf16[2,128,512]{2,1,0:T(8,128)(2,1)} %orbit_val.5) | copy-start | bytes 786436
  47.3 39.7 %copy-start.3 = (f32[2,1024]{1,0:T(2,128)S(1)}, f32[2,1024]{1,0:T(2,128)}, u32[]{:S(2)}) copy-start(f32[2,1024]{1,0:T(2,128)} %energy_cond.5) | copy-start | bytes 24580
  47.3 39.7 %copy-start.4 = (s32[2]{0:T(128)S(1)}, s32[2]{0:T(128)}, u32[]{:S(2)}) copy-start(s32[2]{0:T(128)} %pad_add_fusion.place_ref) | copy-start | bytes 28
  47.3 39.7 %copy-start.5 = (f32[2,128]{1,0:T(2,128)S(1)}, f32[2,128]{1,0:T(2,128)}, u32[]{:S(2)}) copy-start(f32[2,128]{1,0:T(2,128)} %energy_val.5) | copy-start | bytes 3076
  47.3 39.7 %copy-start.6 = (f32[4]{0:T(128)S(1)}, f32[4]{0:T(128)}, u32[]{:S(2)}) copy-start(f32[4]{0:T(128)} %freq_ref.5) | copy-start | bytes 52
  47.3 5.8 %collective-permute-start.5 = (f32[2,2,3,16,256]{4,3,2,1,0:T(8,128)S(1)}, f32[2,2,3,16,256]{4,3,2,1,0:T(8,128)S(1)}, u32[]{:S(2)}, u32[]{:S(2)}) collective-permute-start(f32[2,2,3,16,256]{4,3,2,1,0:T(8,128)S(1)} %slice_add_fusion.4), channel_id=1, source_target_pairs={{0,3},{1,2},{2,1},{3,0},{4,7},{5,6},{6,5},{7,4},{8,11},{9,10},{10,... | collective-permute-start | bytes 589832 | tf_op jit(solution)/shard_map/ppermute | solution.py:38
  53.1 5.8 %collective-permute-start.6 = (f32[2,2,3,16,256]{4,3,2,1,0:T(8,128)S(1)}, f32[2,2,3,16,256]{4,3,2,1,0:T(8,128)S(1)}, u32[]{:S(2)}, u32[]{:S(2)}) collective-permute-start(f32[2,2,3,16,256]{4,3,2,1,0:T(8,128)S(1)} %fusion.2), channel_id=1, source_target_pairs={{0,4},{1,5},{2,6},{3,7},{4,0},{5,1},{6,2},{7,3},{8,12},{9,13},{10,... | collective-permute-start | bytes 589832 | tf_op jit(solution)/shard_map/ppermute | solution.py:28
  58.9 5.8 %collective-permute-start.7 = (f32[2,2,3,16,256]{4,3,2,1,0:T(8,128)S(1)}, f32[2,2,3,16,256]{4,3,2,1,0:T(8,128)S(1)}, u32[]{:S(2)}, u32[]{:S(2)}) collective-permute-start(f32[2,2,3,16,256]{4,3,2,1,0:T(8,128)S(1)} %add_multiply_fusion), channel_id=1, source_target_pairs={{0,3},{1,2},{2,1},{3,0},{4,7},{5,6},{6,5},{7,4},{8,11},{9,10},{10,... | collective-permute-start | bytes 589832 | tf_op jit(solution)/shard_map/ppermute | solution.py:38
  64.7 10.7 %collective-permute-start.8 = (f32[2,4,3,16,256]{4,3,2,1,0:T(8,128)S(1)}, f32[2,4,3,16,256]{4,3,2,1,0:T(8,128)S(1)}, u32[]{:S(2)}, u32[]{:S(2)}) collective-permute-start(f32[2,4,3,16,256]{4,3,2,1,0:T(8,128)S(1)} %pad_maximum_fusion.4), channel_id=1, source_target_pairs={{0,1},{1,0},{2,3},{3,2},{4,5},{5,4},{6,7},{7,6},{8,9},{9,8},{10,11... | collective-permute-start | bytes 1179656 | tf_op jit(solution)/shard_map/ppermute | solution.py:38
  75.5 9.3 %collective-permute-start.11 = (f32[8,3,16,256]{3,2,1,0:T(8,128)S(1)}, f32[8,3,16,256]{3,2,1,0:T(8,128)S(1)}, u32[]{:S(2)}, u32[]{:S(2)}) collective-permute-start(f32[8,3,16,256]{3,2,1,0:T(8,128)S(1)} %get-tuple-element.10), channel_id=1, source_target_pairs={{0,24},{1,25},{2,26},{3,27},{4,28},{5,29},{6,30},{7,31},{8,16},{9,... | collective-permute-start | bytes 1179656 | tf_op jit(solution)/shard_map/ppermute | solution.py:38
  76.8 8.3 %collective-permute-start.9 = (f32[8,3,16,256]{3,2,1,0:T(8,128)S(1)}, f32[8,3,16,256]{3,2,1,0:T(8,128)S(1)}, u32[]{:S(2)}, u32[]{:S(2)}) collective-permute-start(f32[8,3,16,256]{3,2,1,0:T(8,128)S(1)} %get-tuple-element.11), channel_id=1, source_target_pairs={{0,8},{1,9},{2,10},{3,11},{4,12},{5,13},{6,14},{7,15},{8,0},{9,1},... | collective-permute-start | bytes 1179656 | tf_op jit(solution)/shard_map/ppermute | solution.py:38
  84.9 12.1 %collective-permute-start.12 = (f32[16,3,16,256]{3,2,1,0:T(8,128)S(1)}, f32[16,3,16,256]{3,2,1,0:T(8,128)S(1)}, u32[]{:S(2)}, u32[]{:S(2)}) collective-permute-start(f32[16,3,16,256]{3,2,1,0:T(8,128)S(1)} %pad_maximum_fusion.2.refs_0_), channel_id=1, source_target_pairs={{0,8},{1,9},{2,10},{3,11},{4,12},{5,13},{6,14},{7,15},{8,0},{9,1},... | collective-permute-start | bytes 2359304 | tf_op jit(solution)/shard_map/ppermute | solution.py:38
  85.2 13.8 %collective-permute-start.10 = (f32[16,3,16,256]{3,2,1,0:T(8,128)S(1)}, f32[16,3,16,256]{3,2,1,0:T(8,128)S(1)}, u32[]{:S(2)}, u32[]{:S(2)}) collective-permute-start(f32[16,3,16,256]{3,2,1,0:T(8,128)S(1)} %pad_maximum_fusion.1.refs_1_), channel_id=1, source_target_pairs={{0,24},{1,25},{2,26},{3,27},{4,28},{5,29},{6,30},{7,31},{8,16},{9,... | collective-permute-start | bytes 2359304 | tf_op jit(solution)/shard_map/ppermute | solution.py:38
  90.6 33.5 %copy-start.1 = (bf16[128,16384]{1,0:T(8,128)(2,1)S(1)}, bf16[128,16384]{1,0:T(8,128)(2,1)}, u32[]{:S(2)}) copy-start(bf16[128,16384]{1,0:T(8,128)(2,1)} %zeta.1) | copy-start | bytes 12582916
  101.1 1.3 collective-permute-start.13
  125.4 1.2 collective-permute-start.14
  126.6 7.8 %collective-permute-start.15 = (f32[16,128]{1,0:T(8,128)S(1)}, f32[16,128]{1,0:T(8,128)S(1)}, u32[]{:S(2)}, u32[]{:S(2)}) collective-permute-start(f32[16,128]{1,0:T(8,128)S(1)} %add.55.one), channel_id=1, source_target_pairs={{0,64},{32,96},{64,0},{96,32},{128,192},{160,224},{192,128},{224,1... | collective-permute-start | bytes 24584 | tf_op jit(solution)/shard_map/ppermute | solution.py:28
  129.9 7.6 %collective-permute-start.16 = (f32[16,128]{1,0:T(8,128)S(1)}, f32[16,128]{1,0:T(8,128)S(1)}, u32[]{:S(2)}, u32[]{:S(2)}) collective-permute-start(f32[16,128]{1,0:T(8,128)S(1)} %add.55.one), channel_id=1, source_target_pairs={{0,128},{32,160},{64,192},{96,224},{128,0},{160,32},{192,64},{224,... | collective-permute-start | bytes 24584 | tf_op jit(solution)/shard_map/ppermute | solution.py:28
  134.4 5.8 %collective-permute-start.17 = (f32[16,128]{1,0:T(8,128)S(1)}, f32[16,128]{1,0:T(8,128)S(1)}, u32[]{:S(2)}, u32[]{:S(2)}) collective-permute-start(f32[16,128]{1,0:T(8,128)S(1)} %add.55.one), channel_id=1, source_target_pairs={{0,192},{32,224},{64,128},{96,160},{128,64},{160,96},{192,0},{224,... | collective-permute-start | bytes 24584 | tf_op jit(solution)/shard_map/ppermute | solution.py:28

commit v4 on v3

v4 whole, which is shorter than its diff:
```python
import functools

import jax
import jax.numpy as jnp
from jax import lax
from jax.experimental import pallas as pl
from jax.experimental.pallas import tpu as pltpu
from jax.sharding import PartitionSpec as P

MASKS = (((8, 24, 1, 3, 4), (1, 3, 8, 24, 4)), ((24, 8, 1, 3, 4), (3, 1, 8, 24, 4)))
CB, VB = 4, 8
F32, BF16 = jnp.float32, jnp.bfloat16
VMEM, SMEM = pl.BlockSpec(memory_space=pltpu.VMEM), pl.BlockSpec(memory_space=pltpu.SMEM)

def code_of(place, kpoint):
    index, core = place[0], place[1]
    x, z, y = index >> 3, (index >> 2) & 1, index & 3

    first, second = x + (y - x) * core, y + (x - y) * core
    one, two = (first ^ (first >> 1)) & 1, first >> 1
    quarter = one << 1 | two if kpoint == 0 else two << 1 | one
    return quarter, ((second ^ (second >> 1)) & 1) << 2 | (second >> 1) << 1 | z


def swap(value, axis, mask):
    return lax.ppermute(value, axis, [(i, i ^ mask) for i in range(lax.axis_size(axis))])


def cross(value, kpoint, *dims):
    groups, ways = lax.axis_size("ka"), lax.axis_size("wa")
    pairs = []
    for group in range(groups):
        mask = 0
        for dim in dims:
            mask ^= MASKS[kpoint][group & 1][dim]
        pairs += [(group * ways + i, group * ways + (i ^ mask)) for i in range(ways)]
    return lax.ppermute(value, ("ka", "wa"), pairs)


def everyone(value, axis):
    parts = lax.axis_size(axis)
    return lax.all_to_all(jnp.broadcast_to(value[None], (parts,) + value.shape), axis, 0, 0)


def scattered(parts):
    held = []
    for kpoint, (own, second, first, both) in enumerate(parts):
        second = second + cross(both, kpoint, 0)
        held.append((own, cross(first, kpoint, 0), cross(second, kpoint, 1)))

    def summed(place):
        lines = slice(2 * place, 2 * place + 2)
        return jnp.stack([(own[lines] + one[lines]) + two[lines] for own, one, two in held])

    return (summed(0) + cross(summed(2), 0, 2)) + (cross(summed(1), 0, 3) + cross(summed(3), 0, 2, 3))


def gathered_chunks(held):
    others = [cross(held, 0, *dims) for dims in ((3,), (2,), (2, 3))]
    held = jnp.concatenate([held] + others, axis=1)
    quarters = []
    for kpoint in range(held.shape[0]):
        own = held[kpoint]
        first, second = cross(own, kpoint, 0), cross(own, kpoint, 1)
        quarters.append((own, second, first, cross(first, kpoint, 1)))
    return quarters


def momentum_kernel(kpoint, quarters, place_ref, val_ref, miller_ref, cond_ref, *refs):
    outs, weighted = refs[:-1], refs[-1]
    nval = val_ref.shape[1]
    rows, cols = outs[0].shape[2:]
    me_c, me_v = code_of(place_ref, kpoint)
    for place in range(VB):
        source = pl.multiple_of((place ^ me_v) * rows, rows)
        block = val_ref[kpoint, pl.ds(source, rows), :].astype(F32)
        for axis in range(3):
            factor = miller_ref[axis : axis + 1, :].astype(F32)
            weighted[axis * nval + place * rows : axis * nval + (place + 1) * rows, :] = (
                block * factor
            ).astype(BF16)
    for quarter, out in zip(quarters, outs):
        start = pl.multiple_of((quarter ^ me_c) * cols, cols)
        result = lax.dot_general(
            weighted[...],
            cond_ref[kpoint, pl.ds(start, cols), :],
            (((1,), (1,)), ((), ())),
            preferred_element_type=F32,
        )
        for eighth in range(VB):
            for axis in range(3):
                start = axis * nval + eighth * rows
                out[eighth, axis] = result[start : start + rows]


def partial_momentum(kpoint, quarters, place, coeff_val, miller, coeff_cond):
    _, nval, depth = coeff_val.shape
    ncond = coeff_cond.shape[1]
    count = len(quarters)
    return pl.pallas_call(
        functools.partial(momentum_kernel, kpoint, quarters),
        out_shape=[jax.ShapeDtypeStruct((VB, 3, nval // VB, ncond // CB), F32)] * count,
        in_specs=[SMEM, VMEM, VMEM, VMEM],
        out_specs=[VMEM] * count,
        scratch_shapes=[pltpu.VMEM((3 * nval, depth), BF16)],
        cost_estimate=pl.CostEstimate(
            flops=2 * 3 * nval * ncond * depth * count // CB,
            bytes_accessed=(2 * nval + 2 * ncond * count // CB) * depth + 12 * nval * ncond * count // CB,
            transcendentals=0,
        ),
        compiler_params=pltpu.CompilerParams(vmem_limit_bytes=24 << 20),
        name="partial_momentum",
    )(place, coeff_val, miller, coeff_cond)


def pair_kernel(groups, place_ref, weight_ref, freq_ref, energy_val, energy_cond, orbit_val, orbit_cond, *refs):
    _, nval, points = orbit_val.shape
    ncond = orbit_cond.shape[1]
    nfreq = freq_ref.shape[0]
    count = sum(len(quarters) for _, quarters in groups)
    chunks, refs = refs[:count], refs[count:]
    begins = groups[0][1][0] == 0
    before, refs = (None, refs) if begins else (refs[0], refs[1:])
    outs, (total, amplitude, level, orbits, weight) = refs[:-5], refs[-5:]
    rows, cols = chunks[0].shape[2:]
    scale = float(nval * ncond) ** (-0.5)
    tops = 3 * nfreq
    for spot, (k, quarters) in enumerate(groups):
        mine, chunks = chunks[: len(quarters)], chunks[len(quarters) :]
        depth = len(quarters) * cols
        me_c, me_v = code_of(place_ref, k)
        level[spot] = jnp.transpose(jnp.broadcast_to(energy_val[k : k + 1, :], (nval, nval)))
        top = []
        for part, quarter in enumerate(quarters):
            start = pl.multiple_of((quarter ^ me_c) * cols, cols)
            top.append(energy_cond[k : k + 1, pl.ds(start, cols)])
            orbits[spot, part * cols : (part + 1) * cols, :] = orbit_cond[k, pl.ds(start, cols), :]

        def bottom_of(where, spot=spot):
            return jnp.concatenate([level[spot, where, :]] * (cols // nval), axis=1)

        def factors_of(gap):
            square = gap * gap
            return [4.0 / (square + freq_ref[w] * freq_ref[w]) for w in range(nfreq)]

        def eighth(place, carry, k=k, spot=spot, me_v=me_v, top=top, mine=mine, bottom_of=bottom_of):
            here = pl.ds(pl.multiple_of(place * rows, rows), rows)
            there = pl.ds(pl.multiple_of((place ^ me_v) * rows, rows), rows)
            weight[spot, here, :] = orbit_val[k, there, :].astype(F32) * (weight_ref[k] * scale)
            bottom = bottom_of(there)
            for part, chunk in enumerate(mine):
                factors = factors_of(top[part] - bottom)
                for axis in range(3):
                    momentum = chunk[place, axis]
                    for w in range(nfreq):
                        start = pl.multiple_of((axis * nfreq + w) * nval + place * rows, rows)
                        amplitude[spot, pl.ds(start, rows), part * cols : (part + 1) * cols] = (
                            momentum * factors[w]
                        ).astype(BF16)
            return carry

        lax.fori_loop(0, VB, eighth, 0, unroll=2)
        for axis in range(3):
            start = axis * nfreq * nval
            expanded = jnp.dot(
                amplitude[spot, start : start + nfreq * nval, :depth],
                orbits[spot, :depth, :],
                preferred_element_type=F32,
            )
            for w in range(nfreq):
                row = slice(axis * nfreq + w, axis * nfreq + w + 1)
                value = jnp.sum(expanded[w * nval : (w + 1) * nval] * weight[spot], axis=0, keepdims=True)
                if spot > 0:
                    value = value + total[row, :]
                elif not begins:
                    value = value + before[row, :]
                total[row, :] = value

        if begins:
            bottom = bottom_of(pl.ds(pl.multiple_of(me_v * rows, rows), rows))
            gap = top[0] - bottom
            ratios = [factor / gap for factor in factors_of(gap)]
            for axis in range(3):
                square = mine[0][0, axis] * mine[0][0, axis]
                row = slice(tops + axis, tops + axis + 1)
                for w in range(nfreq):
                    value = jnp.sum(square * ratios[w], axis=0, keepdims=True)
                    value = (value[:, :nval] + value[:, nval:]) * (weight_ref[k] / float(nval * ncond))
                    lanes = slice(w * nval, (w + 1) * nval)
                    total[row, lanes] = value + total[row, lanes] if spot else value
            row = slice(tops + 3, tops + 4)
            value = jnp.full((1, points), weight_ref[k], F32)
            total[row, :] = value + total[row, :] if spot else value
    if not begins:
        total[tops:, :] = before[tops:, :]
    if len(outs) == 2:
        keep, send = outs
        across = points // 2
        keep[...] = total[:, pl.ds(pl.multiple_of(place_ref[1] * across, across), across)]
        send[...] = total[:, pl.ds(pl.multiple_of((1 - place_ref[1]) * across, across), across)]
    else:
        outs[0][...] = total[...]


def pair_sums(groups, place, weights, freqs, energy_val, energy_cond, orbit_val, orbit_cond, chunks, before, parts):
    _, nval, points = orbit_val.shape
    ncond = orbit_cond.shape[1]
    nfreq = freqs.shape[0]
    height = 3 * nfreq + 4
    depth = ncond // CB * max(len(quarters) for _, quarters in groups)
    count = len(groups)
    operands = [energy_val, energy_cond, orbit_val, orbit_cond]
    operands += [chunks[k][quarter] for k, quarters in groups for quarter in quarters]
    operands += before
    return list(
        pl.pallas_call(
            functools.partial(pair_kernel, groups),
            out_shape=[jax.ShapeDtypeStruct((height, points // parts), F32)] * parts,
            in_specs=[SMEM] * 3 + [VMEM] * len(operands),
            out_specs=[VMEM] * parts,
            scratch_shapes=[
                pltpu.VMEM((height, points), F32),
                pltpu.VMEM((count, 3 * nfreq * nval, depth), BF16),
                pltpu.VMEM((count, nval, nval), F32),
                pltpu.VMEM((count, depth, points), BF16),
                pltpu.VMEM((count, nval, points), F32),
            ],
            cost_estimate=pl.CostEstimate(
                flops=count * 2 * 3 * nfreq * nval * depth * points,
                bytes_accessed=count * (12 * nval * depth + 4 * depth * points),
                transcendentals=0,
            ),
            compiler_params=pltpu.CompilerParams(vmem_limit_bytes=20 << 20),
            name="pair_sums",
        )(place, weights, freqs, *operands)
    )


def wing_kernel(place_ref, gathered, zeta, out):
    ways, height, points = gathered.shape
    slab_rows = zeta.shape[0]
    tops = height - 4
    total = jnp.zeros((3 * height, slab_rows), F32)
    last = jnp.zeros((4, points), F32)
    for device in range(ways):
        value = gathered[device]
        last = last + value[tops:]
        pieces = []
        for _ in range(3):
            rounded = value.astype(BF16)
            pieces.append(rounded)
            value = value - rounded.astype(F32)
        start = pl.multiple_of((2 * device + place_ref[1]) * points, points)
        total = total + lax.dot_general(
            jnp.concatenate(pieces, axis=0),
            zeta[:, pl.ds(start, points)],
            (((1,), (1,)), ((), ())),
            preferred_element_type=F32,
        )
    total = total[:height] + total[height : 2 * height] + total[2 * height :]
    out[:tops] = total[:tops]
    lane = lax.broadcasted_iota(jnp.int32, (3, slab_rows), 1)
    across = points // 2
    head = jnp.zeros((3, slab_rows), F32)
    for tile in range(2):
        value = jnp.sum(last[:3, tile * across : (tile + 1) * across], axis=1, keepdims=True)
        head = jnp.where(lane == 2 * place_ref[1] + tile, value, head)
    out[tops : tops + 3] = head
    out[tops + 3 :] = last[3:, :slab_rows]


def wing_sums(place, gathered, zeta):
    ways, height, points = gathered.shape
    slab_rows = zeta.shape[0]
    return pl.pallas_call(
        wing_kernel,
        out_shape=jax.ShapeDtypeStruct((height, slab_rows), F32),
        in_specs=[SMEM, VMEM, VMEM],
        out_specs=VMEM,
        cost_estimate=pl.CostEstimate(
            flops=6 * height * slab_rows * ways * points,
            bytes_accessed=4 * slab_rows * ways * points + 4 * height * ways * points,
            transcendentals=0,
        ),
        compiler_params=pltpu.CompilerParams(vmem_limit_bytes=20 << 20),
        name="wing_sums",
    )(place, gathered, zeta)


def final_kernel(copies, one, two, wing, head):
    total = one[...] + two[...]
    tops = total.shape[0] - 4
    nfreq = wing.shape[1]
    scale = copies / total[tops + 3 :]
    for axis in range(3):
        wing[axis] = total[axis * nfreq : (axis + 1) * nfreq] * scale
    head[...] = total[tops : tops + 3, :nfreq] * scale[:, :nfreq]


def local(
    coeff_val,
    coeff_cond,
    miller,
    energy_val,
    energy_cond,
    orbit_val,
    orbit_cond,
    zeta,
    freqs,
    kweight,
):
    kcount, nval, npw_dev = coeff_val.shape
    nfreq = freqs.shape[0]
    slab_rows = zeta.shape[0]
    ways = lax.axis_size("wa")
    pw_factor = float(npw_dev * ways) ** (-0.5)
    weights = kweight.astype(F32)
    place = jnp.stack([lax.axis_index("wa"), lax.axis_index("ka") & 1]).astype(jnp.int32)

    operands = (place, coeff_val, miller, coeff_cond)
    sends = [partial_momentum(k, (3, 2), *operands) for k in range(kcount)]
    keeps = [partial_momentum(k, (1, 0), *operands) for k in range(kcount)]
    parts = [(own, second, first, both) for (both, first), (second, own) in zip(sends, keeps)]
    mine = scattered(parts)
    mine = (mine + swap(mine, "wa", MASKS[0][0][4])[:, ::-1]) * pw_factor

    chunks = gathered_chunks(mine)
    operands = (place, weights, freqs, energy_val, energy_cond, orbit_val, orbit_cond, chunks)
    pair = pair_sums(((0, (0,)), (1, (0,))), *operands, [], 1)
    pair = pair_sums(((0, (1, 2)), (1, (1, 2))), *operands, pair, 1)
    pair = pair_sums(((0, (3,)),), *operands, pair, 1)
    keep, send = pair_sums(((1, (3,)),), *operands, pair, 2)
    pair = keep + swap(send, "ka", 1)
    total = wing_sums(place, everyone(pair, "wa"), zeta)
    total = total + swap(total, "ka", 1)
    total = total + swap(total, "ka", 2)
    return pl.pallas_call(
        functools.partial(final_kernel, float(2 * ways)),
        out_shape=[
            jax.ShapeDtypeStruct((3, nfreq, slab_rows), F32),
            jax.ShapeDtypeStruct((3, nfreq), F32),
        ],
        in_specs=[VMEM] * 2,
        out_specs=[VMEM] * 2,
        compiler_params=pltpu.CompilerParams(vmem_limit_bytes=4 << 20),
        name="final",
    )(total, swap(total, "ka", 6))


def solution(mesh):
    return jax.shard_map(
        local,
        mesh=mesh,
        in_specs=(
            P("ka", None, "wa"),
            P("ka", None, "wa"),
            P(None, "wa"),
            P("ka", None),
            P("ka", None),
            P("ka", None, "wa"),
            P("ka", None, "wa"),
            P("wa", None),
            P(),
            P("ka"),
        ),
        out_specs=(P(None, None, "wa"), P()),
        check_vma=False,
    )
```

time: 141 us -> 114 us (0.81)
  waiting for transfers between devices: 56.8 us -> 34.9 us
  Pallas kernels: 33.1 us -> 17 us
  starting transfers between devices: 25.7 us -> 34.8 us
  local copies, waits for them, and re-layouts: 0.16 us -> 5.5 us
  other arithmetic: 2.5 us -> 0.6 us
  blocking collectives: 21.7 us -> 20 us
    ppermute x12 -> x18, waiting for transfers between devices: 44.9 us -> 25.4 us  [cross(): return lax.ppermute(value, ('ka', 'wa'), pairs)]
    pallas_call x7 -> x8, Pallas kernels: 31.2 us -> 15.1 us  [the longest x4 8.87 us: pair_sums(): pl.pallas_call(functools.partial(pair_kernel, groups), out_shape=[jax.Sha...]
    ppermute x12 -> x18, starting transfers between devices: 15.8 us -> 24.5 us  [cross(): return lax.ppermute(value, ('ka', 'wa'), pairs)]
    unnamed x18 -> x20, local copies, waits for them, and re-layouts: 0.05 us -> 5.4 us
    ppermute x6 -> x5, waiting for transfers between devices: 11.9 us -> 9.45 us  [swap(): lax.ppermute(value, axis, [(i, i ^ mask) for i in range(lax.axis_size(axi...]
    all_to_all x1, blocking collectives: 21.7 us -> 20 us  [everyone(): lax.all_to_all(jnp.broadcast_to(value[None], (parts,) + value.shape), axi...]
    ppermute x6 -> x5, starting transfers between devices: 9.87 us -> 10.3 us  [swap(): lax.ppermute(value, axis, [(i, i ^ mask) for i in range(lax.axis_size(axi...]
  transfers between devices with their start and end apart: 18 -> 23, of which waited for: 13 -> 17; matrix products, arithmetic and copies ran while one was open for 1% -> 0% of each run, Pallas kernels for 16% -> 11%
where the time goes in v4:
time: 114 us
  waiting for transfers between devices  34.9 us (31%)
  starting transfers between devices  34.8 us (31%)
  blocking collectives  20 us (18%)
  Pallas kernels  17 us (15%)
  local copies, waits for them, and re-layouts  5.5 us (5%)
    ppermute x18, waiting for transfers between devices, cross(): return lax.ppermute(value, ('ka', 'wa'), pairs)  25.4 us
    ppermute x18, starting transfers between devices, cross(): return lax.ppermute(value, ('ka', 'wa'), pairs)  24.5 us
    all_to_all x1, blocking collectives, everyone(): lax.all_to_all(jnp.broadcast_to(value[None], (parts,) + value.shape), axi...  20 us
    ppermute x5, starting transfers between devices, swap(): lax.ppermute(value, axis, [(i, i ^ mask) for i in range(lax.axis_size(axi...  10.3 us
    ppermute x5, waiting for transfers between devices, swap(): lax.ppermute(value, axis, [(i, i ^ mask) for i in range(lax.axis_size(axi...  9.45 us
    pallas_call x4, Pallas kernels, pair_sums(): pl.pallas_call(functools.partial(pair_kernel, groups), out_shape=[jax.Sha...  8.87 us
    pallas_call x4, Pallas kernels, partial_momentum(): pl.pallas_call(functools.partial(momentum_kernel, kpoint, quarters), out_...  6.24 us
    unnamed x20, local copies, waits for them, and re-layouts  5.4 us
  transfers between devices with their start and end apart: 23, of which 17 were waited for; matrix products, arithmetic and copies ran while one was open for 0% of the time, Pallas kernels for 11%

profile of v4, /device:TPU:8, one launch (start us, length us, event | category | flops | bytes accessed | tf_op | source)
XLA Modules:
  0.0 113.7 jit_solution(16146547403294091488)
XLA Ops:
  0.7 3.4 %copy-done = bf16[2,1024,2048]{2,1,0:T(8,128)(2,1)S(1)} copy-done((bf16[2,1024,2048]{2,1,0:T(8,128)(2,1)S(1)}, bf16[2,1024,2048]{2,1,0:T(8,128)(2,1)}, u32[]{:S(2)}) %copy-start) | copy-done | bytes 8388632
  4.1 1.2 %copy-done.2 = bf16[2,128,2048]{2,1,0:T(8,128)(2,1)S(1)} copy-done((bf16[2,128,2048]{2,1,0:T(8,128)(2,1)S(1)}, bf16[2,128,2048]{2,1,0:T(8,128)(2,1)}, u32[]{:S(2)}) %copy-start.2) | copy-done | bytes 1048600
  5.3 0.8 copy-done.5
  6.1 1.6 %partial_momentum.5 = (f32[8,3,16,256]{3,2,1,0:T(8,128)S(1)}, f32[8,3,16,256]{3,2,1,0:T(8,128)S(1)}) custom-call(s32[2]{0:T(128)S(1)} %pad_add_fusion.place_ref, bf16[2,128,2048]{2,1,0:T(8,128)(2,1)S(1)} %copy-done.2, s32[3,2048]{1,0:T(4,128)S(1)} %copy-done.5, bf16[2,1024,2048]{2,1,0:T(8,128)(2,1)S(1)} %copy-done), custom_call_target="tpu_custom_call" | custom-call | flops 805306368 | bytes 3407872 | tf_op jit(solution)/shard_map/partial_momentum/pallas_call | solution.py:100
  7.6 1.6 %collective-permute-start.1 = (f32[8,3,16,256]{3,2,1,0:T(8,128)S(1)}, f32[8,3,16,256]{3,2,1,0:T(8,128)S(1)}, u32[]{:S(2)}, u32[]{:S(2)}) collective-permute-start(f32[8,3,16,256]{3,2,1,0:T(8,128)S(1)} %get-tuple-element.15), channel_id=1, source_target_pairs={{0,8},{1,9},{2,10},{3,11},{4,12},{5,13},{6,14},{7,15},{8,0},{9,1},... | collective-permute-start | bytes 1179656 | tf_op jit(solution)/shard_map/ppermute | solution.py:37
  9.2 1.6 %partial_momentum.7 = (f32[8,3,16,256]{3,2,1,0:T(8,128)S(1)}, f32[8,3,16,256]{3,2,1,0:T(8,128)S(1)}) custom-call(s32[2]{0:T(128)S(1)} %pad_add_fusion.place_ref, bf16[2,128,2048]{2,1,0:T(8,128)(2,1)S(1)} %copy-done.2, s32[3,2048]{1,0:T(4,128)S(1)} %copy-done.5, bf16[2,1024,2048]{2,1,0:T(8,128)(2,1)S(1)} %copy-done), custom_call_target="tpu_custom_call" | custom-call | flops 805306368 | bytes 3407872 | tf_op jit(solution)/shard_map/partial_momentum/pallas_call | solution.py:100
  10.8 2.2 %collective-permute-start.4 = (f32[8,3,16,256]{3,2,1,0:T(8,128)S(1)}, f32[8,3,16,256]{3,2,1,0:T(8,128)S(1)}, u32[]{:S(2)}, u32[]{:S(2)}) collective-permute-start(f32[8,3,16,256]{3,2,1,0:T(8,128)S(1)} %get-tuple-element.19), channel_id=1, source_target_pairs={{0,24},{1,25},{2,26},{3,27},{4,28},{5,29},{6,30},{7,31},{8,16},{9,... | collective-permute-start | bytes 1179656 | tf_op jit(solution)/shard_map/ppermute | solution.py:37
  13.0 0.6 collective-permute-start
  13.6 1.6 %partial_momentum.4 = (f32[8,3,16,256]{3,2,1,0:T(8,128)S(1)}, f32[8,3,16,256]{3,2,1,0:T(8,128)S(1)}) custom-call(s32[2]{0:T(128)S(1)} %pad_add_fusion.place_ref, bf16[2,128,2048]{2,1,0:T(8,128)(2,1)S(1)} %copy-done.2, s32[3,2048]{1,0:T(4,128)S(1)} %copy-done.5, bf16[2,1024,2048]{2,1,0:T(8,128)(2,1)S(1)} %copy-done), custom_call_target="tpu_custom_call" | custom-call | flops 805306368 | bytes 3407872 | tf_op jit(solution)/shard_map/partial_momentum/pallas_call | solution.py:100
  15.1 0.4 collective-permute-done.1
  15.6 2.8 %collective-permute-start.2 = (f32[8,3,16,256]{3,2,1,0:T(8,128)S(1)}, f32[8,3,16,256]{3,2,1,0:T(8,128)S(1)}, u32[]{:S(2)}, u32[]{:S(2)}) collective-permute-start(f32[8,3,16,256]{3,2,1,0:T(8,128)S(1)} %add.76), channel_id=1, source_target_pairs={{0,24},{1,25},{2,26},{3,27},{4,28},{5,29},{6,30},{7,31},{8,16},{9,... | collective-permute-start | bytes 1179656 | tf_op jit(solution)/shard_map/ppermute | solution.py:37
  18.4 0.5 collective-permute-start.3
  18.9 1.6 %partial_momentum.6 = (f32[8,3,16,256]{3,2,1,0:T(8,128)S(1)}, f32[8,3,16,256]{3,2,1,0:T(8,128)S(1)}) custom-call(s32[2]{0:T(128)S(1)} %pad_add_fusion.place_ref, bf16[2,128,2048]{2,1,0:T(8,128)(2,1)S(1)} %copy-done.2, s32[3,2048]{1,0:T(4,128)S(1)} %copy-done.5, bf16[2,1024,2048]{2,1,0:T(8,128)(2,1)S(1)} %copy-done), custom_call_target="tpu_custom_call" | custom-call | flops 805306368 | bytes 3407872 | tf_op jit(solution)/shard_map/partial_momentum/pallas_call | solution.py:100
  20.5 0.4 collective-permute-start.5
  20.9 3.7 %collective-permute-done.2 = f32[8,3,16,256]{3,2,1,0:T(8,128)S(1)} collective-permute-done((f32[8,3,16,256]{3,2,1,0:T(8,128)S(1)}, f32[8,3,16,256]{3,2,1,0:T(8,128)S(1)}, u32[]{:S(2)}, u32[]{:S(2)}) %collective-permute-start.2) | collective-permute-done | bytes 393248 | tf_op jit(solution)/shard_map/ppermute | solution.py:37
  24.8 4.1 %collective-permute-done.3 = f32[8,3,16,256]{3,2,1,0:T(8,128)S(1)} collective-permute-done((f32[8,3,16,256]{3,2,1,0:T(8,128)S(1)}, f32[8,3,16,256]{3,2,1,0:T(8,128)S(1)}, u32[]{:S(2)}, u32[]{:S(2)}) %collective-permute-start.3) | collective-permute-done | bytes 393248 | tf_op jit(solution)/shard_map/ppermute | solution.py:37
  29.0 2.4 %collective-permute-start.8 = (f32[2,2,3,16,256]{4,3,2,1,0:T(8,128)S(1)}, f32[2,2,3,16,256]{4,3,2,1,0:T(8,128)S(1)}, u32[]{:S(2)}, u32[]{:S(2)}) collective-permute-start(f32[2,2,3,16,256]{4,3,2,1,0:T(8,128)S(1)} %pad_maximum_fusion.3), channel_id=1, source_target_pairs={{0,2},{1,3},{2,0},{3,1},{4,6},{5,7},{6,4},{7,5},{8,10},{9,11},{10,... | collective-permute-start | bytes 589832 | tf_op jit(solution)/shard_map/ppermute | solution.py:37
  31.4 1.4 %collective-permute-start.7 = (f32[2,2,3,16,256]{4,3,2,1,0:T(8,128)S(1)}, f32[2,2,3,16,256]{4,3,2,1,0:T(8,128)S(1)}, u32[]{:S(2)}, u32[]{:S(2)}) collective-permute-start(f32[2,2,3,16,256]{4,3,2,1,0:T(8,128)S(1)} %pad_maximum_fusion.2), channel_id=1, source_target_pairs={{0,3},{1,2},{2,1},{3,0},{4,7},{5,6},{6,5},{7,4},{8,11},{9,10},{10,... | collective-permute-start | bytes 589832 | tf_op jit(solution)/shard_map/ppermute | solution.py:37
  32.8 1.1 collective-permute-start.6
  34.0 2.4 %collective-permute-done.8 = f32[2,2,3,16,256]{4,3,2,1,0:T(8,128)S(1)} collective-permute-done((f32[2,2,3,16,256]{4,3,2,1,0:T(8,128)S(1)}, f32[2,2,3,16,256]{4,3,2,1,0:T(8,128)S(1)}, u32[]{:S(2)}, u32[]{:S(2)}) %collective-permute-start.8) | collective-permute-done | bytes 196640 | tf_op jit(solution)/shard_map/ppermute | solution.py:37
  36.3 2.0 %collective-permute-done.7 = f32[2,2,3,16,256]{4,3,2,1,0:T(8,128)S(1)} collective-permute-done((f32[2,2,3,16,256]{4,3,2,1,0:T(8,128)S(1)}, f32[2,2,3,16,256]{4,3,2,1,0:T(8,128)S(1)}, u32[]{:S(2)}, u32[]{:S(2)}) %collective-permute-start.7) | collective-permute-done | bytes 196640 | tf_op jit(solution)/shard_map/ppermute | solution.py:37
  38.7 1.9 %collective-permute-start.9 = (f32[2,2,3,16,256]{4,3,2,1,0:T(8,128)S(1)}, f32[2,2,3,16,256]{4,3,2,1,0:T(8,128)S(1)}, u32[]{:S(2)}, u32[]{:S(2)}) collective-permute-start(f32[2,2,3,16,256]{4,3,2,1,0:T(8,128)S(1)} %fusion), channel_id=1, source_target_pairs={{0,4},{1,5},{2,6},{3,7},{4,0},{5,1},{6,2},{7,3},{8,12},{9,13},{10,... | collective-permute-start | bytes 589832 | tf_op jit(solution)/shard_map/ppermute | solution.py:26
  40.6 3.8 %collective-permute-done.9 = f32[2,2,3,16,256]{4,3,2,1,0:T(8,128)S(1)} collective-permute-done((f32[2,2,3,16,256]{4,3,2,1,0:T(8,128)S(1)}, f32[2,2,3,16,256]{4,3,2,1,0:T(8,128)S(1)}, u32[]{:S(2)}, u32[]{:S(2)}) %collective-permute-start.9) | collective-permute-done | bytes 196640 | tf_op jit(solution)/shard_map/ppermute | solution.py:26
  44.5 1.4 %collective-permute-start.10 = (f32[2,2,3,16,256]{4,3,2,1,0:T(8,128)S(1)}, f32[2,2,3,16,256]{4,3,2,1,0:T(8,128)S(1)}, u32[]{:S(2)}, u32[]{:S(2)}) collective-permute-start(f32[2,2,3,16,256]{4,3,2,1,0:T(8,128)S(1)} %add_multiply_fusion), channel_id=1, source_target_pairs={{0,3},{1,2},{2,1},{3,0},{4,7},{5,6},{6,5},{7,4},{8,11},{9,10},{10,... | collective-permute-start | bytes 589832 | tf_op jit(solution)/shard_map/ppermute | solution.py:37
  45.9 1.9 %collective-permute-start.11 = (f32[2,2,3,16,256]{4,3,2,1,0:T(8,128)S(1)}, f32[2,2,3,16,256]{4,3,2,1,0:T(8,128)S(1)}, u32[]{:S(2)}, u32[]{:S(2)}) collective-permute-start(f32[2,2,3,16,256]{4,3,2,1,0:T(8,128)S(1)} %add_multiply_fusion), channel_id=1, source_target_pairs={{0,1},{1,0},{2,3},{3,2},{4,5},{5,4},{6,7},{7,6},{8,9},{9,8},{10,11... | collective-permute-start | bytes 589832 | tf_op jit(solution)/shard_map/ppermute | solution.py:37
  47.8 0.8 collective-permute-start.12
  48.6 1.7 %collective-permute-done.10 = f32[2,2,3,16,256]{4,3,2,1,0:T(8,128)S(1)} collective-permute-done((f32[2,2,3,16,256]{4,3,2,1,0:T(8,128)S(1)}, f32[2,2,3,16,256]{4,3,2,1,0:T(8,128)S(1)}, u32[]{:S(2)}, u32[]{:S(2)}) %collective-permute-start.10) | collective-permute-done | bytes 196640 | tf_op jit(solution)/shard_map/ppermute | solution.py:37
  50.2 1.3 %collective-permute-done.11 = f32[2,2,3,16,256]{4,3,2,1,0:T(8,128)S(1)} collective-permute-done((f32[2,2,3,16,256]{4,3,2,1,0:T(8,128)S(1)}, f32[2,2,3,16,256]{4,3,2,1,0:T(8,128)S(1)}, u32[]{:S(2)}, u32[]{:S(2)}) %collective-permute-start.11) | collective-permute-done | bytes 196640 | tf_op jit(solution)/shard_map/ppermute | solution.py:37
  51.5 5.2 %collective-permute-done.12 = f32[2,2,3,16,256]{4,3,2,1,0:T(8,128)S(1)} collective-permute-done((f32[2,2,3,16,256]{4,3,2,1,0:T(8,128)S(1)}, f32[2,2,3,16,256]{4,3,2,1,0:T(8,128)S(1)}, u32[]{:S(2)}, u32[]{:S(2)}) %collective-permute-start.12) | collective-permute-done | bytes 196640 | tf_op jit(solution)/shard_map/ppermute | solution.py:37
  57.0 3.2 %collective-permute-start.13 = (f32[8,3,16,256]{3,2,1,0:T(8,128)S(1)}, f32[8,3,16,256]{3,2,1,0:T(8,128)S(1)}, u32[]{:S(2)}, u32[]{:S(2)}) collective-permute-start(f32[8,3,16,256]{3,2,1,0:T(8,128)S(1)} %get-tuple-element.31.refs_1_), channel_id=1, source_target_pairs={{0,24},{1,25},{2,26},{3,27},{4,28},{5,29},{6,30},{7,31},{8,16},{9,... | collective-permute-start | bytes 1179656 | tf_op jit(solution)/shard_map/ppermute | solution.py:37
  60.5 0.8 collective-permute-start.18
  61.3 3.4 %collective-permute-done.15.refs_1_ = f32[8,3,16,256]{3,2,1,0:T(8,128)S(1)} collective-permute-done((f32[8,3,16,256]{3,2,1,0:T(8,128)S(1)}, f32[8,3,16,256]{3,2,1,0:T(8,128)S(1)}, u32[]{:S(2)}, u32[]{:S(2)}) %collective-permute-start.15) | collective-permute-done | bytes 393248 | tf_op jit(solution)/shard_map/ppermute | solution.py:37
  64.8 2.9 %collective-permute-start.16 = (f32[8,3,16,256]{3,2,1,0:T(8,128)S(1)}, f32[8,3,16,256]{3,2,1,0:T(8,128)S(1)}, u32[]{:S(2)}, u32[]{:S(2)}) collective-permute-start(f32[8,3,16,256]{3,2,1,0:T(8,128)S(1)} %collective-permute-done.15.refs_1_), channel_id=1, source_target_pairs={{0,24},{1,25},{2,26},{3,27},{4,28},{5,29},{6,30},{7,31},{8,16},{9,... | collective-permute-start | bytes 1179656 | tf_op jit(solution)/shard_map/ppermute | solution.py:37
  67.7 2.4 %pair_sums.4.refs_4_ = f32[16,512]{1,0:T(8,128)S(1)} custom-call(s32[2]{0:T(128)S(1)} %pad_add_fusion.place_ref, f32[2]{0:T(128)S(1)} %convert_element_type.3.weight_ref, f32[4]{0:T(128)S(1)} %copy-done.8, f32[2,128]{1,0:T(2,128)S(1)} %copy-done.7, f32[2,1024]{1,0:T(2,128)S(1)} %copy-done.6, bf16[2,128,512]{2,1,0:T(8,128)(2,1)S(1)} %copy-done.4, ...), custom_call_target="tpu_custom_call" | custom-call | flops 805306368 | bytes 1835008 | tf_op jit(solution)/shard_map/pair_sums/pallas_call | solution.py:216
  70.1 0.4 collective-permute-done.17.refs_0_
  70.5 3.5 %pair_sums.5.refs_1_ = f32[16,512]{1,0:T(8,128)S(1)} custom-call(s32[2]{0:T(128)S(1)} %pad_add_fusion.place_ref, f32[2]{0:T(128)S(1)} %convert_element_type.3.weight_ref, f32[4]{0:T(128)S(1)} %copy-done.8, f32[2,128]{1,0:T(2,128)S(1)} %copy-done.7, f32[2,1024]{1,0:T(2,128)S(1)} %copy-done.6, bf16[2,128,512]{2,1,0:T(8,128)(2,1)S(1)} %copy-done.4, ...), custom_call_target="tpu_custom_call" | custom-call | flops 1610612736 | bytes 3670016 | tf_op jit(solution)/shard_map/pair_sums/pallas_call | solution.py:216
  74.0 0.7 collective-permute-done.16.refs_0_
  74.7 1.5 %pair_sums.6.refs_1_ = f32[16,512]{1,0:T(8,128)S(1)} custom-call(s32[2]{0:T(128)S(1)} %pad_add_fusion.place_ref, f32[2]{0:T(128)S(1)} %convert_element_type.3.weight_ref, f32[4]{0:T(128)S(1)} %copy-done.8, f32[2,128]{1,0:T(2,128)S(1)} %copy-done.7, f32[2,1024]{1,0:T(2,128)S(1)} %copy-done.6, bf16[2,128,512]{2,1,0:T(8,128)(2,1)S(1)} %copy-done.4, ...), custom_call_target="tpu_custom_call" | custom-call | flops 402653184 | bytes 917504 | tf_op jit(solution)/shard_map/pair_sums/pallas_call | solution.py:216
  76.2 1.5 %pair_sums.7 = (f32[16,256]{1,0:T(8,128)S(1)}, f32[16,256]{1,0:T(8,128)S(1)}) custom-call(s32[2]{0:T(128)S(1)} %pad_add_fusion.place_ref, f32[2]{0:T(128)S(1)} %convert_element_type.3.weight_ref, f32[4]{0:T(128)S(1)} %copy-done.8, f32[2,128]{1,0:T(2,128)S(1)} %copy-done.7, f32[2,1024]{1,0:T(2,128)S(1)} %copy-done.6, bf16[2,128,512]{2,1,0:T(8,128)(2,1)S(1)} %copy-done.4, ...), custom_call_target="tpu_custom_call" | custom-call | flops 402653184 | bytes 917504 | tf_op jit(solution)/shard_map/pair_sums/pallas_call | solution.py:216
  77.8 1.2 %collective-permute-done.19 = f32[16,256]{1,0:T(8,128)S(1)} collective-permute-done((f32[16,256]{1,0:T(8,128)S(1)}, f32[16,256]{1,0:T(8,128)S(1)}, u32[]{:S(2)}, u32[]{:S(2)}) %collective-permute-start.19) | collective-permute-done | bytes 16416 | tf_op jit(solution)/shard_map/ppermute | solution.py:26
  79.0 20.0 %all_to_all.5.gathered = f32[32,16,256]{2,1,0:T(8,128)S(1)} all-to-all(f32[32,16,256]{2,1,0:T(8,128)S(1)} %broadcast_in_dim.2), channel_id=1, replica_groups=mesh['ka'=8,'wa'=32] {'wa'}, dimensions={0} | all-to-all | bytes 1048576 | tf_op jit(solution)/shard_map/all_to_all | solution.py:42
  99.0 1.3 %wing_sums.1 = f32[16,128]{1,0:T(8,128)S(1)} custom-call(s32[2]{0:T(128)S(1)} %pad_add_fusion.place_ref, f32[32,16,256]{2,1,0:T(8,128)S(1)} %all_to_all.5.gathered, bf16[128,16384]{1,0:T(8,128)(2,1)S(1)} %copy-done.3), custom_call_target="tpu_custom_call" | custom-call | flops 100663296 | bytes 4718592 | tf_op jit(solution)/shard_map/wing_sums/pallas_call | solution.py:275
  100.3 1.2 %collective-permute-done.20 = f32[16,128]{1,0:T(8,128)S(1)} collective-permute-done((f32[16,128]{1,0:T(8,128)S(1)}, f32[16,128]{1,0:T(8,128)S(1)}, u32[]{:S(2)}, u32[]{:S(2)}) %collective-permute-start.20) | collective-permute-done | bytes 8224 | tf_op jit(solution)/shard_map/ppermute | solution.py:26
  101.5 3.3 %collective-permute-start.21 = (f32[16,128]{1,0:T(8,128)S(1)}, f32[16,128]{1,0:T(8,128)S(1)}, u32[]{:S(2)}, u32[]{:S(2)}) collective-permute-start(f32[16,128]{1,0:T(8,128)S(1)} %add.98), channel_id=1, source_target_pairs={{0,64},{32,96},{64,0},{96,32},{128,192},{160,224},{192,128},{224,1... | collective-permute-start | bytes 24584 | tf_op jit(solution)/shard_map/ppermute | solution.py:26
  104.8 1.6 %collective-permute-done.21 = f32[16,128]{1,0:T(8,128)S(1)} collective-permute-done((f32[16,128]{1,0:T(8,128)S(1)}, f32[16,128]{1,0:T(8,128)S(1)}, u32[]{:S(2)}, u32[]{:S(2)}) %collective-permute-start.21) | collective-permute-done | bytes 8224 | tf_op jit(solution)/shard_map/ppermute | solution.py:26
  106.4 5.1 %collective-permute-start.22 = (f32[16,128]{1,0:T(8,128)S(1)}, f32[16,128]{1,0:T(8,128)S(1)}, u32[]{:S(2)}, u32[]{:S(2)}) collective-permute-start(f32[16,128]{1,0:T(8,128)S(1)} %add.99.one), channel_id=1, source_target_pairs={{0,192},{32,224},{64,128},{96,160},{128,64},{160,96},{192,0},{224,... | collective-permute-start | bytes 24584 | tf_op jit(solution)/shard_map/ppermute | solution.py:26
  111.4 1.6 %collective-permute-done.22.two = f32[16,128]{1,0:T(8,128)S(1)} collective-permute-done((f32[16,128]{1,0:T(8,128)S(1)}, f32[16,128]{1,0:T(8,128)S(1)}, u32[]{:S(2)}, u32[]{:S(2)}) %collective-permute-start.22) | collective-permute-done | bytes 8224 | tf_op jit(solution)/shard_map/ppermute | solution.py:26
  113.1 0.6 final.1
  (46 shorter events, 1.5 us)
Async XLA Ops:
  0.7 3.4 %copy-start = (bf16[2,1024,2048]{2,1,0:T(8,128)(2,1)S(1)}, bf16[2,1024,2048]{2,1,0:T(8,128)(2,1)}, u32[]{:S(2)}) copy-start(bf16[2,1024,2048]{2,1,0:T(8,128)(2,1)} %cond_ref.7) | copy-start | bytes 25165828
  4.1 1.2 %copy-start.2 = (bf16[2,128,2048]{2,1,0:T(8,128)(2,1)S(1)}, bf16[2,128,2048]{2,1,0:T(8,128)(2,1)}, u32[]{:S(2)}) copy-start(bf16[2,128,2048]{2,1,0:T(8,128)(2,1)} %val_ref.7) | copy-start | bytes 3145732
  5.3 0.8 copy-start.5
  7.6 7.9 %collective-permute-start.1 = (f32[8,3,16,256]{3,2,1,0:T(8,128)S(1)}, f32[8,3,16,256]{3,2,1,0:T(8,128)S(1)}, u32[]{:S(2)}, u32[]{:S(2)}) collective-permute-start(f32[8,3,16,256]{3,2,1,0:T(8,128)S(1)} %get-tuple-element.15), channel_id=1, source_target_pairs={{0,8},{1,9},{2,10},{3,11},{4,12},{5,13},{6,14},{7,15},{8,0},{9,1},... | collective-permute-start | bytes 1179656 | tf_op jit(solution)/shard_map/ppermute | solution.py:37
  10.8 9.7 %collective-permute-start.4 = (f32[8,3,16,256]{3,2,1,0:T(8,128)S(1)}, f32[8,3,16,256]{3,2,1,0:T(8,128)S(1)}, u32[]{:S(2)}, u32[]{:S(2)}) collective-permute-start(f32[8,3,16,256]{3,2,1,0:T(8,128)S(1)} %get-tuple-element.19), channel_id=1, source_target_pairs={{0,24},{1,25},{2,26},{3,27},{4,28},{5,29},{6,30},{7,31},{8,16},{9,... | collective-permute-start | bytes 1179656 | tf_op jit(solution)/shard_map/ppermute | solution.py:37
  13.0 7.9 %collective-permute-start = (f32[8,3,16,256]{3,2,1,0:T(8,128)S(1)}, f32[8,3,16,256]{3,2,1,0:T(8,128)S(1)}, u32[]{:S(2)}, u32[]{:S(2)}) collective-permute-start(f32[8,3,16,256]{3,2,1,0:T(8,128)S(1)} %get-tuple-element.13), channel_id=1, source_target_pairs={{0,8},{1,9},{2,10},{3,11},{4,12},{5,13},{6,14},{7,15},{8,0},{9,1},... | collective-permute-start | bytes 1179656 | tf_op jit(solution)/shard_map/ppermute | solution.py:37
  15.6 9.1 %collective-permute-start.2 = (f32[8,3,16,256]{3,2,1,0:T(8,128)S(1)}, f32[8,3,16,256]{3,2,1,0:T(8,128)S(1)}, u32[]{:S(2)}, u32[]{:S(2)}) collective-permute-start(f32[8,3,16,256]{3,2,1,0:T(8,128)S(1)} %add.76), channel_id=1, source_target_pairs={{0,24},{1,25},{2,26},{3,27},{4,28},{5,29},{6,30},{7,31},{8,16},{9,... | collective-permute-start | bytes 1179656 | tf_op jit(solution)/shard_map/ppermute | solution.py:37
  18.4 10.4 %collective-permute-start.3 = (f32[8,3,16,256]{3,2,1,0:T(8,128)S(1)}, f32[8,3,16,256]{3,2,1,0:T(8,128)S(1)}, u32[]{:S(2)}, u32[]{:S(2)}) collective-permute-start(f32[8,3,16,256]{3,2,1,0:T(8,128)S(1)} %get-tuple-element.17), channel_id=1, source_target_pairs={{0,24},{1,25},{2,26},{3,27},{4,28},{5,29},{6,30},{7,31},{8,16},{9,... | collective-permute-start | bytes 1179656 | tf_op jit(solution)/shard_map/ppermute | solution.py:37
  20.5 8.3 %collective-permute-start.5 = (f32[8,3,16,256]{3,2,1,0:T(8,128)S(1)}, f32[8,3,16,256]{3,2,1,0:T(8,128)S(1)}, u32[]{:S(2)}, u32[]{:S(2)}) collective-permute-start(f32[8,3,16,256]{3,2,1,0:T(8,128)S(1)} %add.79), channel_id=1, source_target_pairs={{0,8},{1,9},{2,10},{3,11},{4,12},{5,13},{6,14},{7,15},{8,0},{9,1},... | collective-permute-start | bytes 1179656 | tf_op jit(solution)/shard_map/ppermute | solution.py:37
  24.6 43.0 %copy-start.9 = (s32[2]{0:T(128)S(1)}, s32[2]{0:T(128)}, u32[]{:S(2)}) copy-start(s32[2]{0:T(128)} %param.19) | copy-start | bytes 28
  24.6 43.0 %copy-start.1 = (bf16[2,1024,512]{2,1,0:T(8,128)(2,1)S(1)}, bf16[2,1024,512]{2,1,0:T(8,128)(2,1)}, u32[]{:S(2)}) copy-start(bf16[2,1024,512]{2,1,0:T(8,128)(2,1)} %orbit_cond.7) | copy-start | bytes 6291460
  24.6 43.1 %copy-start.4 = (bf16[2,128,512]{2,1,0:T(8,128)(2,1)S(1)}, bf16[2,128,512]{2,1,0:T(8,128)(2,1)}, u32[]{:S(2)}) copy-start(bf16[2,128,512]{2,1,0:T(8,128)(2,1)} %orbit_val.7) | copy-start | bytes 786436
  24.6 43.1 %copy-start.6 = (f32[2,1024]{1,0:T(2,128)S(1)}, f32[2,1024]{1,0:T(2,128)}, u32[]{:S(2)}) copy-start(f32[2,1024]{1,0:T(2,128)} %energy_cond.7) | copy-start | bytes 24580
  24.7 43.1 %copy-start.7 = (f32[2,128]{1,0:T(2,128)S(1)}, f32[2,128]{1,0:T(2,128)}, u32[]{:S(2)}) copy-start(f32[2,128]{1,0:T(2,128)} %energy_val.7) | copy-start | bytes 3076
  24.7 43.1 %copy-start.8 = (f32[4]{0:T(128)S(1)}, f32[4]{0:T(128)}, u32[]{:S(2)}) copy-start(f32[4]{0:T(128)} %freq_ref.7) | copy-start | bytes 52
  29.0 7.4 %collective-permute-start.8 = (f32[2,2,3,16,256]{4,3,2,1,0:T(8,128)S(1)}, f32[2,2,3,16,256]{4,3,2,1,0:T(8,128)S(1)}, u32[]{:S(2)}, u32[]{:S(2)}) collective-permute-start(f32[2,2,3,16,256]{4,3,2,1,0:T(8,128)S(1)} %pad_maximum_fusion.3), channel_id=1, source_target_pairs={{0,2},{1,3},{2,0},{3,1},{4,6},{5,7},{6,4},{7,5},{8,10},{9,11},{10,... | collective-permute-start | bytes 589832 | tf_op jit(solution)/shard_map/ppermute | solution.py:37
  31.4 7.0 %collective-permute-start.7 = (f32[2,2,3,16,256]{4,3,2,1,0:T(8,128)S(1)}, f32[2,2,3,16,256]{4,3,2,1,0:T(8,128)S(1)}, u32[]{:S(2)}, u32[]{:S(2)}) collective-permute-start(f32[2,2,3,16,256]{4,3,2,1,0:T(8,128)S(1)} %pad_maximum_fusion.2), channel_id=1, source_target_pairs={{0,3},{1,2},{2,1},{3,0},{4,7},{5,6},{6,5},{7,4},{8,11},{9,10},{10,... | collective-permute-start | bytes 589832 | tf_op jit(solution)/shard_map/ppermute | solution.py:37
  32.8 5.8 %collective-permute-start.6 = (f32[2,2,3,16,256]{4,3,2,1,0:T(8,128)S(1)}, f32[2,2,3,16,256]{4,3,2,1,0:T(8,128)S(1)}, u32[]{:S(2)}, u32[]{:S(2)}) collective-permute-start(f32[2,2,3,16,256]{4,3,2,1,0:T(8,128)S(1)} %pad_maximum_fusion.1), channel_id=1, source_target_pairs={{0,1},{1,0},{2,3},{3,2},{4,5},{5,4},{6,7},{7,6},{8,9},{9,8},{10,11... | collective-permute-start | bytes 589832 | tf_op jit(solution)/shard_map/ppermute | solution.py:37
  38.7 5.8 %collective-permute-start.9 = (f32[2,2,3,16,256]{4,3,2,1,0:T(8,128)S(1)}, f32[2,2,3,16,256]{4,3,2,1,0:T(8,128)S(1)}, u32[]{:S(2)}, u32[]{:S(2)}) collective-permute-start(f32[2,2,3,16,256]{4,3,2,1,0:T(8,128)S(1)} %fusion), channel_id=1, source_target_pairs={{0,4},{1,5},{2,6},{3,7},{4,0},{5,1},{6,2},{7,3},{8,12},{9,13},{10,... | collective-permute-start | bytes 589832 | tf_op jit(solution)/shard_map/ppermute | solution.py:26
  44.5 5.8 %collective-permute-start.10 = (f32[2,2,3,16,256]{4,3,2,1,0:T(8,128)S(1)}, f32[2,2,3,16,256]{4,3,2,1,0:T(8,128)S(1)}, u32[]{:S(2)}, u32[]{:S(2)}) collective-permute-start(f32[2,2,3,16,256]{4,3,2,1,0:T(8,128)S(1)} %add_multiply_fusion), channel_id=1, source_target_pairs={{0,3},{1,2},{2,1},{3,0},{4,7},{5,6},{6,5},{7,4},{8,11},{9,10},{10,... | collective-permute-start | bytes 589832 | tf_op jit(solution)/shard_map/ppermute | solution.py:37
  45.9 5.7 %collective-permute-start.11 = (f32[2,2,3,16,256]{4,3,2,1,0:T(8,128)S(1)}, f32[2,2,3,16,256]{4,3,2,1,0:T(8,128)S(1)}, u32[]{:S(2)}, u32[]{:S(2)}) collective-permute-start(f32[2,2,3,16,256]{4,3,2,1,0:T(8,128)S(1)} %add_multiply_fusion), channel_id=1, source_target_pairs={{0,1},{1,0},{2,3},{3,2},{4,5},{5,4},{6,7},{7,6},{8,9},{9,8},{10,11... | collective-permute-start | bytes 589832 | tf_op jit(solution)/shard_map/ppermute | solution.py:37
  47.8 9.0 %collective-permute-start.12 = (f32[2,2,3,16,256]{4,3,2,1,0:T(8,128)S(1)}, f32[2,2,3,16,256]{4,3,2,1,0:T(8,128)S(1)}, u32[]{:S(2)}, u32[]{:S(2)}) collective-permute-start(f32[2,2,3,16,256]{4,3,2,1,0:T(8,128)S(1)} %add_multiply_fusion), channel_id=1, source_target_pairs={{0,2},{1,3},{2,0},{3,1},{4,6},{5,7},{6,4},{7,5},{8,10},{9,11},{10,... | collective-permute-start | bytes 589832 | tf_op jit(solution)/shard_map/ppermute | solution.py:37
  56.9 7.9 %collective-permute-start.15 = (f32[8,3,16,256]{3,2,1,0:T(8,128)S(1)}, f32[8,3,16,256]{3,2,1,0:T(8,128)S(1)}, u32[]{:S(2)}, u32[]{:S(2)}) collective-permute-start(f32[8,3,16,256]{3,2,1,0:T(8,128)S(1)} %get-tuple-element.30.refs_0_), channel_id=1, source_target_pairs={{0,8},{1,9},{2,10},{3,11},{4,12},{5,13},{6,14},{7,15},{8,0},{9,1},... | collective-permute-start | bytes 1179656 | tf_op jit(solution)/shard_map/ppermute | solution.py:37
  57.0 10.7 %collective-permute-start.13 = (f32[8,3,16,256]{3,2,1,0:T(8,128)S(1)}, f32[8,3,16,256]{3,2,1,0:T(8,128)S(1)}, u32[]{:S(2)}, u32[]{:S(2)}) collective-permute-start(f32[8,3,16,256]{3,2,1,0:T(8,128)S(1)} %get-tuple-element.31.refs_1_), channel_id=1, source_target_pairs={{0,24},{1,25},{2,26},{3,27},{4,28},{5,29},{6,30},{7,31},{8,16},{9,... | collective-permute-start | bytes 1179656 | tf_op jit(solution)/shard_map/ppermute | solution.py:37
  60.2 10.3 %collective-permute-start.17 = (f32[8,3,16,256]{3,2,1,0:T(8,128)S(1)}, f32[8,3,16,256]{3,2,1,0:T(8,128)S(1)}, u32[]{:S(2)}, u32[]{:S(2)}) collective-permute-start(f32[8,3,16,256]{3,2,1,0:T(8,128)S(1)} %get-tuple-element.30.refs_0_), channel_id=1, source_target_pairs={{0,24},{1,25},{2,26},{3,27},{4,28},{5,29},{6,30},{7,31},{8,16},{9,... | collective-permute-start | bytes 1179656 | tf_op jit(solution)/shard_map/ppermute | solution.py:37
  60.5 10.0 %collective-permute-start.18 = (f32[8,3,16,256]{3,2,1,0:T(8,128)S(1)}, f32[8,3,16,256]{3,2,1,0:T(8,128)S(1)}, u32[]{:S(2)}, u32[]{:S(2)}) collective-permute-start(f32[8,3,16,256]{3,2,1,0:T(8,128)S(1)} %get-tuple-element.31.refs_1_), channel_id=1, source_target_pairs={{0,8},{1,9},{2,10},{3,11},{4,12},{5,13},{6,14},{7,15},{8,0},{9,1},... | collective-permute-start | bytes 1179656 | tf_op jit(solution)/shard_map/ppermute | solution.py:37
  64.8 9.9 %collective-permute-start.16 = (f32[8,3,16,256]{3,2,1,0:T(8,128)S(1)}, f32[8,3,16,256]{3,2,1,0:T(8,128)S(1)}, u32[]{:S(2)}, u32[]{:S(2)}) collective-permute-start(f32[8,3,16,256]{3,2,1,0:T(8,128)S(1)} %collective-permute-done.15.refs_1_), channel_id=1, source_target_pairs={{0,24},{1,25},{2,26},{3,27},{4,28},{5,29},{6,30},{7,31},{8,16},{9,... | collective-permute-start | bytes 1179656 | tf_op jit(solution)/shard_map/ppermute | solution.py:37
  67.7 8.5 %collective-permute-start.14 = (f32[8,3,16,256]{3,2,1,0:T(8,128)S(1)}, f32[8,3,16,256]{3,2,1,0:T(8,128)S(1)}, u32[]{:S(2)}, u32[]{:S(2)}) collective-permute-start(f32[8,3,16,256]{3,2,1,0:T(8,128)S(1)} %collective-permute-done.13.refs_3_), channel_id=1, source_target_pairs={{0,8},{1,9},{2,10},{3,11},{4,12},{5,13},{6,14},{7,15},{8,0},{9,1},... | collective-permute-start | bytes 1179656 | tf_op jit(solution)/shard_map/ppermute | solution.py:37
  74.0 25.0 %copy-start.3 = (bf16[128,16384]{1,0:T(8,128)(2,1)S(1)}, bf16[128,16384]{1,0:T(8,128)(2,1)}, u32[]{:S(2)}) copy-start(bf16[128,16384]{1,0:T(8,128)(2,1)} %zeta.1) | copy-start | bytes 12582916
  77.7 1.3 %collective-permute-start.19 = (f32[16,256]{1,0:T(8,128)S(1)}, f32[16,256]{1,0:T(8,128)S(1)}, u32[]{:S(2)}, u32[]{:S(2)}) collective-permute-start(f32[16,256]{1,0:T(8,128)S(1)} %get-tuple-element.21), channel_id=1, source_target_pairs={{0,32},{32,0},{64,96},{96,64},{128,160},{160,128},{192,224},{224,1... | collective-permute-start | bytes 49160 | tf_op jit(solution)/shard_map/ppermute | solution.py:26
  100.3 1.2 %collective-permute-start.20 = (f32[16,128]{1,0:T(8,128)S(1)}, f32[16,128]{1,0:T(8,128)S(1)}, u32[]{:S(2)}, u32[]{:S(2)}) collective-permute-start(f32[16,128]{1,0:T(8,128)S(1)} %wing_sums.1), channel_id=1, source_target_pairs={{0,32},{32,0},{64,96},{96,64},{128,160},{160,128},{192,224},{224,1... | collective-permute-start | bytes 24584 | tf_op jit(solution)/shard_map/ppermute | solution.py:26
  101.5 4.9 %collective-permute-start.21 = (f32[16,128]{1,0:T(8,128)S(1)}, f32[16,128]{1,0:T(8,128)S(1)}, u32[]{:S(2)}, u32[]{:S(2)}) collective-permute-start(f32[16,128]{1,0:T(8,128)S(1)} %add.98), channel_id=1, source_target_pairs={{0,64},{32,96},{64,0},{96,32},{128,192},{160,224},{192,128},{224,1... | collective-permute-start | bytes 24584 | tf_op jit(solution)/shard_map/ppermute | solution.py:26
  106.4 6.7 %collective-permute-start.22 = (f32[16,128]{1,0:T(8,128)S(1)}, f32[16,128]{1,0:T(8,128)S(1)}, u32[]{:S(2)}, u32[]{:S(2)}) collective-permute-start(f32[16,128]{1,0:T(8,128)S(1)} %add.99.one), channel_id=1, source_target_pairs={{0,192},{32,224},{64,128},{96,160},{128,64},{160,96},{192,0},{224,... | collective-permute-start | bytes 24584 | tf_op jit(solution)/shard_map/ppermute | solution.py:26

commit v5 on v4

--- a/solution.py
+++ b/solution.py
@@ -42,28 +42,23 @@
     return lax.all_to_all(jnp.broadcast_to(value[None], (parts,) + value.shape), axis, 0, 0)
 
 
-def scattered(parts):
-    held = []
-    for kpoint, (own, second, first, both) in enumerate(parts):
-        second = second + cross(both, kpoint, 0)
-        held.append((own, cross(first, kpoint, 0), cross(second, kpoint, 1)))
+def gathered_chunks(kpoint, partial, factor):
+    own, second, first, both = partial
+    second = second + cross(both, kpoint, 0)
+    one, two = cross(first, kpoint, 0), cross(second, kpoint, 1)
 
     def summed(place):
         lines = slice(2 * place, 2 * place + 2)
-        return jnp.stack([(own[lines] + one[lines]) + two[lines] for own, one, two in held])
-
-    return (summed(0) + cross(summed(2), 0, 2)) + (cross(summed(1), 0, 3) + cross(summed(3), 0, 2, 3))
-
-
-def gathered_chunks(held):
-    others = [cross(held, 0, *dims) for dims in ((3,), (2,), (2, 3))]
-    held = jnp.concatenate([held] + others, axis=1)
-    quarters = []
-    for kpoint in range(held.shape[0]):
-        own = held[kpoint]
-        first, second = cross(own, kpoint, 0), cross(own, kpoint, 1)
-        quarters.append((own, second, first, cross(first, kpoint, 1)))
-    return quarters
+        return (own[lines] + one[lines]) + two[lines]
+
+    held = (summed(0) + cross(summed(2), kpoint, 2)) + (
+        cross(summed(1), kpoint, 3) + cross(summed(3), kpoint, 2, 3)
+    )
+    held = (held + cross(held, kpoint, 4)[::-1]) * factor
+    others = [cross(held, kpoint, *dims) for dims in ((3,), (2,), (2, 3))]
+    held = jnp.concatenate([held] + others)
+    first, second = cross(held, kpoint, 0), cross(held, kpoint, 1)
+    return held, second, first, cross(first, kpoint, 1)
 
 
 def momentum_kernel(kpoint, quarters, place_ref, val_ref, miller_ref, cond_ref, *refs):
@@ -321,10 +316,7 @@
     sends = [partial_momentum(k, (3, 2), *operands) for k in range(kcount)]
     keeps = [partial_momentum(k, (1, 0), *operands) for k in range(kcount)]
     parts = [(own, second, first, both) for (both, first), (second, own) in zip(sends, keeps)]
-    mine = scattered(parts)
-    mine = (mine + swap(mine, "wa", MASKS[0][0][4])[:, ::-1]) * pw_factor
-
-    chunks = gathered_chunks(mine)
+    chunks = [gathered_chunks(k, parts[k], pw_factor) for k in range(kcount)]
     operands = (place, weights, freqs, energy_val, energy_cond, orbit_val, orbit_cond, chunks)
     pair = pair_sums(((0, (0,)), (1, (0,))), *operands, [], 1)
     pair = pair_sums(((0, (1, 2)), (1, (1, 2))), *operands, pair, 1)

time: 114 us -> 114 us (level)
  starting transfers between devices: 34.8 us -> 45.6 us
  waiting for transfers between devices: 34.9 us -> 25.4 us
  blocking collectives: 20 us -> 18.6 us
    ppermute x18 -> x26, starting transfers between devices: 24.5 us -> 36.7 us  [cross(): return lax.ppermute(value, ('ka', 'wa'), pairs)]
    ppermute x18 -> x26, waiting for transfers between devices: 25.4 us -> 19.7 us  [cross(): return lax.ppermute(value, ('ka', 'wa'), pairs)]
    ppermute x5 -> x4, waiting for transfers between devices: 9.45 us -> 5.61 us  [swap(): lax.ppermute(value, axis, [(i, i ^ mask) for i in range(lax.axis_size(axi...]
    ppermute x5 -> x4, starting transfers between devices: 10.3 us -> 8.87 us  [swap(): lax.ppermute(value, axis, [(i, i ^ mask) for i in range(lax.axis_size(axi...]
    all_to_all x1, blocking collectives: 20 us -> 18.6 us  [everyone(): lax.all_to_all(jnp.broadcast_to(value[None], (parts,) + value.shape), axi...]
  transfers between devices with their start and end apart: 23 -> 30, of which waited for: 17 -> 17; matrix products, arithmetic and copies ran while one was open for 0% -> 0% of each run, Pallas kernels for 11% -> 11%
where the time goes in v5:
time: 114 us; the launch traced here: 113 us
  starting transfers between devices  45.6 us (40%)
  waiting for transfers between devices  25.4 us (22%)
  blocking collectives  18.6 us (16%)
  Pallas kernels  17 us (15%)
  local copies, waits for them, and re-layouts  5.46 us (5%)
    ppermute x26, starting transfers between devices, cross(): return lax.ppermute(value, ('ka', 'wa'), pairs)  36.7 us
    ppermute x26, waiting for transfers between devices, cross(): return lax.ppermute(value, ('ka', 'wa'), pairs)  19.7 us
    all_to_all x1, blocking collectives, everyone(): lax.all_to_all(jnp.broadcast_to(value[None], (parts,) + value.shape), axi...  18.6 us
    pallas_call x4, Pallas kernels, pair_sums(): pl.pallas_call(functools.partial(pair_kernel, groups), out_shape=[jax.Sha...  8.87 us
    ppermute x4, starting transfers between devices, swap(): lax.ppermute(value, axis, [(i, i ^ mask) for i in range(lax.axis_size(axi...  8.87 us
    pallas_call x4, Pallas kernels, partial_momentum(): pl.pallas_call(functools.partial(momentum_kernel, kpoint, quarters), out_...  6.24 us
    ppermute x4, waiting for transfers between devices, swap(): lax.ppermute(value, axis, [(i, i ^ mask) for i in range(lax.axis_size(axi...  5.61 us
    unnamed x20, local copies, waits for them, and re-layouts  5.41 us
  transfers between devices with their start and end apart: 30, of which 17 were waited for; matrix products, arithmetic and copies ran while one was open for 0% of the time, Pallas kernels for 11%

profile of v5, /device:TPU:8, one launch (start us, length us, event | category | flops | bytes accessed | tf_op | source)
XLA Modules:
  0.0 113.4 jit_solution(3952271959876467457)
XLA Ops:
  0.7 3.4 %copy-done = bf16[2,1024,2048]{2,1,0:T(8,128)(2,1)S(1)} copy-done((bf16[2,1024,2048]{2,1,0:T(8,128)(2,1)S(1)}, bf16[2,1024,2048]{2,1,0:T(8,128)(2,1)}, u32[]{:S(2)}) %copy-start) | copy-done | bytes 8388632
  4.1 1.2 %copy-done.2 = bf16[2,128,2048]{2,1,0:T(8,128)(2,1)S(1)} copy-done((bf16[2,128,2048]{2,1,0:T(8,128)(2,1)S(1)}, bf16[2,128,2048]{2,1,0:T(8,128)(2,1)}, u32[]{:S(2)}) %copy-start.2) | copy-done | bytes 1048600
  5.3 0.8 copy-done.5
  6.1 1.6 %partial_momentum.7 = (f32[8,3,16,256]{3,2,1,0:T(8,128)S(1)}, f32[8,3,16,256]{3,2,1,0:T(8,128)S(1)}) custom-call(s32[2]{0:T(128)S(1)} %pad_add_fusion.place_ref, bf16[2,128,2048]{2,1,0:T(8,128)(2,1)S(1)} %copy-done.2, s32[3,2048]{1,0:T(4,128)S(1)} %copy-done.5, bf16[2,1024,2048]{2,1,0:T(8,128)(2,1)S(1)} %copy-done), custom_call_target="tpu_custom_call" | custom-call | flops 805306368 | bytes 3407872 | tf_op jit(solution)/shard_map/partial_momentum/pallas_call | solution.py:95
  7.6 1.6 %collective-permute-start.13 = (f32[8,3,16,256]{3,2,1,0:T(8,128)S(1)}, f32[8,3,16,256]{3,2,1,0:T(8,128)S(1)}, u32[]{:S(2)}, u32[]{:S(2)}) collective-permute-start(f32[8,3,16,256]{3,2,1,0:T(8,128)S(1)} %get-tuple-element.19), channel_id=1, source_target_pairs={{0,8},{1,9},{2,10},{3,11},{4,12},{5,13},{6,14},{7,15},{8,0},{9,1},... | collective-permute-start | bytes 1179656 | tf_op jit(solution)/shard_map/ppermute | solution.py:37
  9.2 1.6 %partial_momentum.5 = (f32[8,3,16,256]{3,2,1,0:T(8,128)S(1)}, f32[8,3,16,256]{3,2,1,0:T(8,128)S(1)}) custom-call(s32[2]{0:T(128)S(1)} %pad_add_fusion.place_ref, bf16[2,128,2048]{2,1,0:T(8,128)(2,1)S(1)} %copy-done.2, s32[3,2048]{1,0:T(4,128)S(1)} %copy-done.5, bf16[2,1024,2048]{2,1,0:T(8,128)(2,1)S(1)} %copy-done), custom_call_target="tpu_custom_call" | custom-call | flops 805306368 | bytes 3407872 | tf_op jit(solution)/shard_map/partial_momentum/pallas_call | solution.py:95
  10.8 2.2 %collective-permute-start.1 = (f32[8,3,16,256]{3,2,1,0:T(8,128)S(1)}, f32[8,3,16,256]{3,2,1,0:T(8,128)S(1)}, u32[]{:S(2)}, u32[]{:S(2)}) collective-permute-start(f32[8,3,16,256]{3,2,1,0:T(8,128)S(1)} %get-tuple-element.15), channel_id=1, source_target_pairs={{0,24},{1,25},{2,26},{3,27},{4,28},{5,29},{6,30},{7,31},{8,16},{9,... | collective-permute-start | bytes 1179656 | tf_op jit(solution)/shard_map/ppermute | solution.py:37
  13.6 1.6 %partial_momentum.6 = (f32[8,3,16,256]{3,2,1,0:T(8,128)S(1)}, f32[8,3,16,256]{3,2,1,0:T(8,128)S(1)}) custom-call(s32[2]{0:T(128)S(1)} %pad_add_fusion.place_ref, bf16[2,128,2048]{2,1,0:T(8,128)(2,1)S(1)} %copy-done.2, s32[3,2048]{1,0:T(4,128)S(1)} %copy-done.5, bf16[2,1024,2048]{2,1,0:T(8,128)(2,1)S(1)} %copy-done), custom_call_target="tpu_custom_call" | custom-call | flops 805306368 | bytes 3407872 | tf_op jit(solution)/shard_map/partial_momentum/pallas_call | solution.py:95
  15.6 2.8 %collective-permute-start.14 = (f32[8,3,16,256]{3,2,1,0:T(8,128)S(1)}, f32[8,3,16,256]{3,2,1,0:T(8,128)S(1)}, u32[]{:S(2)}, u32[]{:S(2)}) collective-permute-start(f32[8,3,16,256]{3,2,1,0:T(8,128)S(1)} %add.101), channel_id=1, source_target_pairs={{0,24},{1,25},{2,26},{3,27},{4,28},{5,29},{6,30},{7,31},{8,16},{9,... | collective-permute-start | bytes 1179656 | tf_op jit(solution)/shard_map/ppermute | solution.py:37
  18.9 1.6 %partial_momentum.4 = (f32[8,3,16,256]{3,2,1,0:T(8,128)S(1)}, f32[8,3,16,256]{3,2,1,0:T(8,128)S(1)}) custom-call(s32[2]{0:T(128)S(1)} %pad_add_fusion.place_ref, bf16[2,128,2048]{2,1,0:T(8,128)(2,1)S(1)} %copy-done.2, s32[3,2048]{1,0:T(4,128)S(1)} %copy-done.5, bf16[2,1024,2048]{2,1,0:T(8,128)(2,1)S(1)} %copy-done), custom_call_target="tpu_custom_call" | custom-call | flops 805306368 | bytes 3407872 | tf_op jit(solution)/shard_map/partial_momentum/pallas_call | solution.py:95
  21.0 3.7 %collective-permute-done.14 = f32[8,3,16,256]{3,2,1,0:T(8,128)S(1)} collective-permute-done((f32[8,3,16,256]{3,2,1,0:T(8,128)S(1)}, f32[8,3,16,256]{3,2,1,0:T(8,128)S(1)}, u32[]{:S(2)}, u32[]{:S(2)}) %collective-permute-start.14) | collective-permute-done | bytes 393248 | tf_op jit(solution)/shard_map/ppermute | solution.py:37
  24.7 2.3 %collective-permute-start.15 = (f32[2,3,16,256]{3,2,1,0:T(8,128)S(1)}, f32[2,3,16,256]{3,2,1,0:T(8,128)S(1)}, u32[]{:S(2)}, u32[]{:S(2)}) collective-permute-start(f32[2,3,16,256]{3,2,1,0:T(8,128)S(1)} %get-tuple-element.24), channel_id=1, source_target_pairs={{0,1},{1,0},{2,3},{3,2},{4,5},{5,4},{6,7},{7,6},{8,9},{9,8},{10,11... | collective-permute-start | bytes 294920 | tf_op jit(solution)/shard_map/ppermute | solution.py:37
  27.0 0.7 collective-permute-start.16
  27.7 1.5 %collective-permute-start.17 = (f32[2,3,16,256]{3,2,1,0:T(8,128)S(1)}, f32[2,3,16,256]{3,2,1,0:T(8,128)S(1)}, u32[]{:S(2)}, u32[]{:S(2)}) collective-permute-start(f32[2,3,16,256]{3,2,1,0:T(8,128)S(1)} %get-tuple-element.22), channel_id=1, source_target_pairs={{0,2},{1,3},{2,0},{3,1},{4,6},{5,7},{6,4},{7,5},{8,10},{9,11},{10,... | collective-permute-start | bytes 294920 | tf_op jit(solution)/shard_map/ppermute | solution.py:37
  29.2 1.7 %collective-permute-done = f32[8,3,16,256]{3,2,1,0:T(8,128)S(1)} collective-permute-done((f32[8,3,16,256]{3,2,1,0:T(8,128)S(1)}, f32[8,3,16,256]{3,2,1,0:T(8,128)S(1)}, u32[]{:S(2)}, u32[]{:S(2)}) %collective-permute-start) | collective-permute-done | bytes 393248 | tf_op jit(solution)/shard_map/ppermute | solution.py:37
  30.9 0.8 collective-permute-done.2
  31.7 2.2 %collective-permute-start.3 = (f32[2,3,16,256]{3,2,1,0:T(8,128)S(1)}, f32[2,3,16,256]{3,2,1,0:T(8,128)S(1)}, u32[]{:S(2)}, u32[]{:S(2)}) collective-permute-start(f32[2,3,16,256]{3,2,1,0:T(8,128)S(1)} %get-tuple-element.27), channel_id=1, source_target_pairs={{0,1},{1,0},{2,3},{3,2},{4,5},{5,4},{6,7},{7,6},{8,9},{9,8},{10,11... | collective-permute-start | bytes 294920 | tf_op jit(solution)/shard_map/ppermute | solution.py:37
  34.0 2.2 %collective-permute-start.5 = (f32[2,3,16,256]{3,2,1,0:T(8,128)S(1)}, f32[2,3,16,256]{3,2,1,0:T(8,128)S(1)}, u32[]{:S(2)}, u32[]{:S(2)}) collective-permute-start(f32[2,3,16,256]{3,2,1,0:T(8,128)S(1)} %get-tuple-element.25), channel_id=1, source_target_pairs={{0,2},{1,3},{2,0},{3,1},{4,6},{5,7},{6,4},{7,5},{8,10},{9,11},{10,... | collective-permute-start | bytes 294920 | tf_op jit(solution)/shard_map/ppermute | solution.py:37
  36.2 1.8 %collective-permute-start.18 = (f32[2,3,16,256]{3,2,1,0:T(8,128)S(1)}, f32[2,3,16,256]{3,2,1,0:T(8,128)S(1)}, u32[]{:S(2)}, u32[]{:S(2)}) collective-permute-start(f32[2,3,16,256]{3,2,1,0:T(8,128)S(1)} %fusion.1), channel_id=1, source_target_pairs={{0,4},{1,5},{2,6},{3,7},{4,0},{5,1},{6,2},{7,3},{8,12},{9,13},{10,... | collective-permute-start | bytes 294920 | tf_op jit(solution)/shard_map/ppermute | solution.py:37
  38.0 0.6 collective-permute-done.4
  38.6 1.5 %collective-permute-done.5 = f32[2,3,16,256]{3,2,1,0:T(8,128)S(1)} collective-permute-done((f32[2,3,16,256]{3,2,1,0:T(8,128)S(1)}, f32[2,3,16,256]{3,2,1,0:T(8,128)S(1)}, u32[]{:S(2)}, u32[]{:S(2)}) %collective-permute-start.5) | collective-permute-done | bytes 98336 | tf_op jit(solution)/shard_map/ppermute | solution.py:37
  40.2 1.8 %collective-permute-start.6 = (f32[2,3,16,256]{3,2,1,0:T(8,128)S(1)}, f32[2,3,16,256]{3,2,1,0:T(8,128)S(1)}, u32[]{:S(2)}, u32[]{:S(2)}) collective-permute-start(f32[2,3,16,256]{3,2,1,0:T(8,128)S(1)} %fusion.3), channel_id=1, source_target_pairs={{0,4},{1,5},{2,6},{3,7},{4,0},{5,1},{6,2},{7,3},{8,12},{9,13},{10,... | collective-permute-start | bytes 294920 | tf_op jit(solution)/shard_map/ppermute | solution.py:37
  42.0 0.6 collective-permute-start.19
  42.6 3.0 %collective-permute-start.20 = (f32[2,3,16,256]{3,2,1,0:T(8,128)S(1)}, f32[2,3,16,256]{3,2,1,0:T(8,128)S(1)}, u32[]{:S(2)}, u32[]{:S(2)}) collective-permute-start(f32[2,3,16,256]{3,2,1,0:T(8,128)S(1)} %add_multiply_fusion), channel_id=1, source_target_pairs={{0,1},{1,0},{2,3},{3,2},{4,5},{5,4},{6,7},{7,6},{8,9},{9,8},{10,11... | collective-permute-start | bytes 294920 | tf_op jit(solution)/shard_map/ppermute | solution.py:37
  45.6 1.0 collective-permute-start.21
  46.6 0.7 collective-permute-start.7
  47.3 3.1 %collective-permute-start.8 = (f32[2,3,16,256]{3,2,1,0:T(8,128)S(1)}, f32[2,3,16,256]{3,2,1,0:T(8,128)S(1)}, u32[]{:S(2)}, u32[]{:S(2)}) collective-permute-start(f32[2,3,16,256]{3,2,1,0:T(8,128)S(1)} %add_multiply_fusion.1), channel_id=1, source_target_pairs={{0,1},{1,0},{2,3},{3,2},{4,5},{5,4},{6,7},{7,6},{8,9},{9,8},{10,11... | collective-permute-start | bytes 294920 | tf_op jit(solution)/shard_map/ppermute | solution.py:37
  50.4 1.0 collective-permute-start.9
  51.4 1.4 %collective-permute-done.21 = f32[2,3,16,256]{3,2,1,0:T(8,128)S(1)} collective-permute-done((f32[2,3,16,256]{3,2,1,0:T(8,128)S(1)}, f32[2,3,16,256]{3,2,1,0:T(8,128)S(1)}, u32[]{:S(2)}, u32[]{:S(2)}) %collective-permute-start.21) | collective-permute-done | bytes 98336 | tf_op jit(solution)/shard_map/ppermute | solution.py:37
  53.3 1.7 %collective-permute-done.8 = f32[2,3,16,256]{3,2,1,0:T(8,128)S(1)} collective-permute-done((f32[2,3,16,256]{3,2,1,0:T(8,128)S(1)}, f32[2,3,16,256]{3,2,1,0:T(8,128)S(1)}, u32[]{:S(2)}, u32[]{:S(2)}) %collective-permute-start.8) | collective-permute-done | bytes 98336 | tf_op jit(solution)/shard_map/ppermute | solution.py:37
  55.0 2.6 %collective-permute-done.9 = f32[2,3,16,256]{3,2,1,0:T(8,128)S(1)} collective-permute-done((f32[2,3,16,256]{3,2,1,0:T(8,128)S(1)}, f32[2,3,16,256]{3,2,1,0:T(8,128)S(1)}, u32[]{:S(2)}, u32[]{:S(2)}) %collective-permute-start.9) | collective-permute-done | bytes 98336 | tf_op jit(solution)/shard_map/ppermute | solution.py:37
  57.6 3.5 %collective-permute-start.10 = (f32[8,3,16,256]{3,2,1,0:T(8,128)S(1)}, f32[8,3,16,256]{3,2,1,0:T(8,128)S(1)}, u32[]{:S(2)}, u32[]{:S(2)}) collective-permute-start(f32[8,3,16,256]{3,2,1,0:T(8,128)S(1)} %pad_maximum_fusion.refs_1_), channel_id=1, source_target_pairs={{0,24},{1,25},{2,26},{3,27},{4,28},{5,29},{6,30},{7,31},{8,16},{9,... | collective-permute-start | bytes 1179656 | tf_op jit(solution)/shard_map/ppermute | solution.py:37
  61.3 3.1 %collective-permute-start.23 = (f32[8,3,16,256]{3,2,1,0:T(8,128)S(1)}, f32[8,3,16,256]{3,2,1,0:T(8,128)S(1)}, u32[]{:S(2)}, u32[]{:S(2)}) collective-permute-start(f32[8,3,16,256]{3,2,1,0:T(8,128)S(1)} %collective-permute-done.22.refs_1_), channel_id=1, source_target_pairs={{0,24},{1,25},{2,26},{3,27},{4,28},{5,29},{6,30},{7,31},{8,16},{9,... | collective-permute-start | bytes 1179656 | tf_op jit(solution)/shard_map/ppermute | solution.py:37
  64.4 2.5 %collective-permute-done.10.refs_3_ = f32[8,3,16,256]{3,2,1,0:T(8,128)S(1)} collective-permute-done((f32[8,3,16,256]{3,2,1,0:T(8,128)S(1)}, f32[8,3,16,256]{3,2,1,0:T(8,128)S(1)}, u32[]{:S(2)}, u32[]{:S(2)}) %collective-permute-start.10) | collective-permute-done | bytes 393248 | tf_op jit(solution)/shard_map/ppermute | solution.py:37
  67.0 2.4 %pair_sums.4.refs_4_ = f32[16,512]{1,0:T(8,128)S(1)} custom-call(s32[2]{0:T(128)S(1)} %pad_add_fusion.place_ref, f32[2]{0:T(128)S(1)} %convert_element_type.3.weight_ref, f32[4]{0:T(128)S(1)} %copy-done.8, f32[2,128]{1,0:T(2,128)S(1)} %copy-done.7, f32[2,1024]{1,0:T(2,128)S(1)} %copy-done.6, bf16[2,128,512]{2,1,0:T(8,128)(2,1)S(1)} %copy-done.4, ...), custom_call_target="tpu_custom_call" | custom-call | flops 805306368 | bytes 1835008 | tf_op jit(solution)/shard_map/pair_sums/pallas_call | solution.py:211
  69.3 1.8 %collective-permute-done.24.refs_0_ = f32[8,3,16,256]{3,2,1,0:T(8,128)S(1)} collective-permute-done((f32[8,3,16,256]{3,2,1,0:T(8,128)S(1)}, f32[8,3,16,256]{3,2,1,0:T(8,128)S(1)}, u32[]{:S(2)}, u32[]{:S(2)}) %collective-permute-start.24) | collective-permute-done | bytes 393248 | tf_op jit(solution)/shard_map/ppermute | solution.py:37
  71.1 3.5 %pair_sums.5.refs_1_ = f32[16,512]{1,0:T(8,128)S(1)} custom-call(s32[2]{0:T(128)S(1)} %pad_add_fusion.place_ref, f32[2]{0:T(128)S(1)} %convert_element_type.3.weight_ref, f32[4]{0:T(128)S(1)} %copy-done.8, f32[2,128]{1,0:T(2,128)S(1)} %copy-done.7, f32[2,1024]{1,0:T(2,128)S(1)} %copy-done.6, bf16[2,128,512]{2,1,0:T(8,128)(2,1)S(1)} %copy-done.4, ...), custom_call_target="tpu_custom_call" | custom-call | flops 1610612736 | bytes 3670016 | tf_op jit(solution)/shard_map/pair_sums/pallas_call | solution.py:211
  74.7 0.7 collective-permute-done.23.refs_0_
  75.3 1.5 %pair_sums.6.refs_1_ = f32[16,512]{1,0:T(8,128)S(1)} custom-call(s32[2]{0:T(128)S(1)} %pad_add_fusion.place_ref, f32[2]{0:T(128)S(1)} %convert_element_type.3.weight_ref, f32[4]{0:T(128)S(1)} %copy-done.8, f32[2,128]{1,0:T(2,128)S(1)} %copy-done.7, f32[2,1024]{1,0:T(2,128)S(1)} %copy-done.6, bf16[2,128,512]{2,1,0:T(8,128)(2,1)S(1)} %copy-done.4, ...), custom_call_target="tpu_custom_call" | custom-call | flops 402653184 | bytes 917504 | tf_op jit(solution)/shard_map/pair_sums/pallas_call | solution.py:211
  76.8 1.5 %pair_sums.7 = (f32[16,256]{1,0:T(8,128)S(1)}, f32[16,256]{1,0:T(8,128)S(1)}) custom-call(s32[2]{0:T(128)S(1)} %pad_add_fusion.place_ref, f32[2]{0:T(128)S(1)} %convert_element_type.3.weight_ref, f32[4]{0:T(128)S(1)} %copy-done.8, f32[2,128]{1,0:T(2,128)S(1)} %copy-done.7, f32[2,1024]{1,0:T(2,128)S(1)} %copy-done.6, bf16[2,128,512]{2,1,0:T(8,128)(2,1)S(1)} %copy-done.4, ...), custom_call_target="tpu_custom_call" | custom-call | flops 402653184 | bytes 917504 | tf_op jit(solution)/shard_map/pair_sums/pallas_call | solution.py:211
  78.4 1.2 %collective-permute-done.26 = f32[16,256]{1,0:T(8,128)S(1)} collective-permute-done((f32[16,256]{1,0:T(8,128)S(1)}, f32[16,256]{1,0:T(8,128)S(1)}, u32[]{:S(2)}, u32[]{:S(2)}) %collective-permute-start.26) | collective-permute-done | bytes 16416 | tf_op jit(solution)/shard_map/ppermute | solution.py:26
  79.7 18.6 %all_to_all.5.gathered = f32[32,16,256]{2,1,0:T(8,128)S(1)} all-to-all(f32[32,16,256]{2,1,0:T(8,128)S(1)} %broadcast_in_dim.2), channel_id=1, replica_groups=mesh['ka'=8,'wa'=32] {'wa'}, dimensions={0} | all-to-all | bytes 1048576 | tf_op jit(solution)/shard_map/all_to_all | solution.py:42
  98.3 1.3 %wing_sums.1 = f32[16,128]{1,0:T(8,128)S(1)} custom-call(s32[2]{0:T(128)S(1)} %pad_add_fusion.place_ref, f32[32,16,256]{2,1,0:T(8,128)S(1)} %all_to_all.5.gathered, bf16[128,16384]{1,0:T(8,128)(2,1)S(1)} %copy-done.3), custom_call_target="tpu_custom_call" | custom-call | flops 100663296 | bytes 4718592 | tf_op jit(solution)/shard_map/wing_sums/pallas_call | solution.py:270
  99.6 1.2 %collective-permute-done.27 = f32[16,128]{1,0:T(8,128)S(1)} collective-permute-done((f32[16,128]{1,0:T(8,128)S(1)}, f32[16,128]{1,0:T(8,128)S(1)}, u32[]{:S(2)}, u32[]{:S(2)}) %collective-permute-start.27) | collective-permute-done | bytes 8224 | tf_op jit(solution)/shard_map/ppermute | solution.py:26
  100.8 3.3 %collective-permute-start.28 = (f32[16,128]{1,0:T(8,128)S(1)}, f32[16,128]{1,0:T(8,128)S(1)}, u32[]{:S(2)}, u32[]{:S(2)}) collective-permute-start(f32[16,128]{1,0:T(8,128)S(1)} %add.114), channel_id=1, source_target_pairs={{0,64},{32,96},{64,0},{96,32},{128,192},{160,224},{192,128},{224,1... | collective-permute-start | bytes 24584 | tf_op jit(solution)/shard_map/ppermute | solution.py:26
  104.0 1.6 %collective-permute-done.28 = f32[16,128]{1,0:T(8,128)S(1)} collective-permute-done((f32[16,128]{1,0:T(8,128)S(1)}, f32[16,128]{1,0:T(8,128)S(1)}, u32[]{:S(2)}, u32[]{:S(2)}) %collective-permute-start.28) | collective-permute-done | bytes 8224 | tf_op jit(solution)/shard_map/ppermute | solution.py:26
  105.7 5.5 %collective-permute-start.29 = (f32[16,128]{1,0:T(8,128)S(1)}, f32[16,128]{1,0:T(8,128)S(1)}, u32[]{:S(2)}, u32[]{:S(2)}) collective-permute-start(f32[16,128]{1,0:T(8,128)S(1)} %add.115.one), channel_id=1, source_target_pairs={{0,192},{32,224},{64,128},{96,160},{128,64},{160,96},{192,0},{224,... | collective-permute-start | bytes 24584 | tf_op jit(solution)/shard_map/ppermute | solution.py:26
  111.2 1.6 %collective-permute-done.29.two = f32[16,128]{1,0:T(8,128)S(1)} collective-permute-done((f32[16,128]{1,0:T(8,128)S(1)}, f32[16,128]{1,0:T(8,128)S(1)}, u32[]{:S(2)}, u32[]{:S(2)}) %collective-permute-start.29) | collective-permute-done | bytes 8224 | tf_op jit(solution)/shard_map/ppermute | solution.py:26
  (59 shorter events, 3.8 us)
Async XLA Ops:
  0.7 3.4 %copy-start = (bf16[2,1024,2048]{2,1,0:T(8,128)(2,1)S(1)}, bf16[2,1024,2048]{2,1,0:T(8,128)(2,1)}, u32[]{:S(2)}) copy-start(bf16[2,1024,2048]{2,1,0:T(8,128)(2,1)} %cond_ref.7) | copy-start | bytes 25165828
  4.1 1.2 %copy-start.2 = (bf16[2,128,2048]{2,1,0:T(8,128)(2,1)S(1)}, bf16[2,128,2048]{2,1,0:T(8,128)(2,1)}, u32[]{:S(2)}) copy-start(bf16[2,128,2048]{2,1,0:T(8,128)(2,1)} %val_ref.7) | copy-start | bytes 3145732
  5.3 0.8 copy-start.5
  7.6 7.9 %collective-permute-start.13 = (f32[8,3,16,256]{3,2,1,0:T(8,128)S(1)}, f32[8,3,16,256]{3,2,1,0:T(8,128)S(1)}, u32[]{:S(2)}, u32[]{:S(2)}) collective-permute-start(f32[8,3,16,256]{3,2,1,0:T(8,128)S(1)} %get-tuple-element.19), channel_id=1, source_target_pairs={{0,8},{1,9},{2,10},{3,11},{4,12},{5,13},{6,14},{7,15},{8,0},{9,1},... | collective-permute-start | bytes 1179656 | tf_op jit(solution)/shard_map/ppermute | solution.py:37
  10.8 9.7 %collective-permute-start.1 = (f32[8,3,16,256]{3,2,1,0:T(8,128)S(1)}, f32[8,3,16,256]{3,2,1,0:T(8,128)S(1)}, u32[]{:S(2)}, u32[]{:S(2)}) collective-permute-start(f32[8,3,16,256]{3,2,1,0:T(8,128)S(1)} %get-tuple-element.15), channel_id=1, source_target_pairs={{0,24},{1,25},{2,26},{3,27},{4,28},{5,29},{6,30},{7,31},{8,16},{9,... | collective-permute-start | bytes 1179656 | tf_op jit(solution)/shard_map/ppermute | solution.py:37
  13.0 8.0 %collective-permute-start.12 = (f32[8,3,16,256]{3,2,1,0:T(8,128)S(1)}, f32[8,3,16,256]{3,2,1,0:T(8,128)S(1)}, u32[]{:S(2)}, u32[]{:S(2)}) collective-permute-start(f32[8,3,16,256]{3,2,1,0:T(8,128)S(1)} %get-tuple-element.17), channel_id=1, source_target_pairs={{0,8},{1,9},{2,10},{3,11},{4,12},{5,13},{6,14},{7,15},{8,0},{9,1},... | collective-permute-start | bytes 1179656 | tf_op jit(solution)/shard_map/ppermute | solution.py:37
  15.6 9.1 %collective-permute-start.14 = (f32[8,3,16,256]{3,2,1,0:T(8,128)S(1)}, f32[8,3,16,256]{3,2,1,0:T(8,128)S(1)}, u32[]{:S(2)}, u32[]{:S(2)}) collective-permute-start(f32[8,3,16,256]{3,2,1,0:T(8,128)S(1)} %add.101), channel_id=1, source_target_pairs={{0,24},{1,25},{2,26},{3,27},{4,28},{5,29},{6,30},{7,31},{8,16},{9,... | collective-permute-start | bytes 1179656 | tf_op jit(solution)/shard_map/ppermute | solution.py:37
  18.4 12.5 %collective-permute-start = (f32[8,3,16,256]{3,2,1,0:T(8,128)S(1)}, f32[8,3,16,256]{3,2,1,0:T(8,128)S(1)}, u32[]{:S(2)}, u32[]{:S(2)}) collective-permute-start(f32[8,3,16,256]{3,2,1,0:T(8,128)S(1)} %get-tuple-element.13), channel_id=1, source_target_pairs={{0,24},{1,25},{2,26},{3,27},{4,28},{5,29},{6,30},{7,31},{8,16},{9,... | collective-permute-start | bytes 1179656 | tf_op jit(solution)/shard_map/ppermute | solution.py:37
  20.5 46.5 %copy-start.9 = (s32[2]{0:T(128)S(1)}, s32[2]{0:T(128)}, u32[]{:S(2)}) copy-start(s32[2]{0:T(128)} %param.19) | copy-start | bytes 28
  20.5 46.5 %copy-start.1 = (bf16[2,1024,512]{2,1,0:T(8,128)(2,1)S(1)}, bf16[2,1024,512]{2,1,0:T(8,128)(2,1)}, u32[]{:S(2)}) copy-start(bf16[2,1024,512]{2,1,0:T(8,128)(2,1)} %orbit_cond.7) | copy-start | bytes 6291460
  20.5 46.4 %copy-start.4 = (bf16[2,128,512]{2,1,0:T(8,128)(2,1)S(1)}, bf16[2,128,512]{2,1,0:T(8,128)(2,1)}, u32[]{:S(2)}) copy-start(bf16[2,128,512]{2,1,0:T(8,128)(2,1)} %orbit_val.7) | copy-start | bytes 786436
  20.5 46.4 %copy-start.6 = (f32[2,1024]{1,0:T(2,128)S(1)}, f32[2,1024]{1,0:T(2,128)}, u32[]{:S(2)}) copy-start(f32[2,1024]{1,0:T(2,128)} %energy_cond.7) | copy-start | bytes 24580
  20.5 46.4 %copy-start.7 = (f32[2,128]{1,0:T(2,128)S(1)}, f32[2,128]{1,0:T(2,128)}, u32[]{:S(2)}) copy-start(f32[2,128]{1,0:T(2,128)} %energy_val.7) | copy-start | bytes 3076
  20.5 46.4 %copy-start.8 = (f32[4]{0:T(128)S(1)}, f32[4]{0:T(128)}, u32[]{:S(2)}) copy-start(f32[4]{0:T(128)} %freq_ref.7) | copy-start | bytes 52
  20.6 11.1 %collective-permute-start.2 = (f32[8,3,16,256]{3,2,1,0:T(8,128)S(1)}, f32[8,3,16,256]{3,2,1,0:T(8,128)S(1)}, u32[]{:S(2)}, u32[]{:S(2)}) collective-permute-start(f32[8,3,16,256]{3,2,1,0:T(8,128)S(1)} %add.88), channel_id=1, source_target_pairs={{0,8},{1,9},{2,10},{3,11},{4,12},{5,13},{6,14},{7,15},{8,0},{9,1},... | collective-permute-start | bytes 1179656 | tf_op jit(solution)/shard_map/ppermute | solution.py:37
  24.7 9.3 %collective-permute-start.15 = (f32[2,3,16,256]{3,2,1,0:T(8,128)S(1)}, f32[2,3,16,256]{3,2,1,0:T(8,128)S(1)}, u32[]{:S(2)}, u32[]{:S(2)}) collective-permute-start(f32[2,3,16,256]{3,2,1,0:T(8,128)S(1)} %get-tuple-element.24), channel_id=1, source_target_pairs={{0,1},{1,0},{2,3},{3,2},{4,5},{5,4},{6,7},{7,6},{8,9},{9,8},{10,11... | collective-permute-start | bytes 294920 | tf_op jit(solution)/shard_map/ppermute | solution.py:37
  27.0 9.2 %collective-permute-start.16 = (f32[2,3,16,256]{3,2,1,0:T(8,128)S(1)}, f32[2,3,16,256]{3,2,1,0:T(8,128)S(1)}, u32[]{:S(2)}, u32[]{:S(2)}) collective-permute-start(f32[2,3,16,256]{3,2,1,0:T(8,128)S(1)} %get-tuple-element.23), channel_id=1, source_target_pairs={{0,3},{1,2},{2,1},{3,0},{4,7},{5,6},{6,5},{7,4},{8,11},{9,10},{10,... | collective-permute-start | bytes 294920 | tf_op jit(solution)/shard_map/ppermute | solution.py:37
  27.7 8.5 %collective-permute-start.17 = (f32[2,3,16,256]{3,2,1,0:T(8,128)S(1)}, f32[2,3,16,256]{3,2,1,0:T(8,128)S(1)}, u32[]{:S(2)}, u32[]{:S(2)}) collective-permute-start(f32[2,3,16,256]{3,2,1,0:T(8,128)S(1)} %get-tuple-element.22), channel_id=1, source_target_pairs={{0,2},{1,3},{2,0},{3,1},{4,6},{5,7},{6,4},{7,5},{8,10},{9,11},{10,... | collective-permute-start | bytes 294920 | tf_op jit(solution)/shard_map/ppermute | solution.py:37
  31.7 6.2 %collective-permute-start.3 = (f32[2,3,16,256]{3,2,1,0:T(8,128)S(1)}, f32[2,3,16,256]{3,2,1,0:T(8,128)S(1)}, u32[]{:S(2)}, u32[]{:S(2)}) collective-permute-start(f32[2,3,16,256]{3,2,1,0:T(8,128)S(1)} %get-tuple-element.27), channel_id=1, source_target_pairs={{0,1},{1,0},{2,3},{3,2},{4,5},{5,4},{6,7},{7,6},{8,9},{9,8},{10,11... | collective-permute-start | bytes 294920 | tf_op jit(solution)/shard_map/ppermute | solution.py:37
  34.0 4.6 %collective-permute-start.4 = (f32[2,3,16,256]{3,2,1,0:T(8,128)S(1)}, f32[2,3,16,256]{3,2,1,0:T(8,128)S(1)}, u32[]{:S(2)}, u32[]{:S(2)}) collective-permute-start(f32[2,3,16,256]{3,2,1,0:T(8,128)S(1)} %get-tuple-element.26), channel_id=1, source_target_pairs={{0,3},{1,2},{2,1},{3,0},{4,7},{5,6},{6,5},{7,4},{8,11},{9,10},{10,... | collective-permute-start | bytes 294920 | tf_op jit(solution)/shard_map/ppermute | solution.py:37
  34.0 6.1 %collective-permute-start.5 = (f32[2,3,16,256]{3,2,1,0:T(8,128)S(1)}, f32[2,3,16,256]{3,2,1,0:T(8,128)S(1)}, u32[]{:S(2)}, u32[]{:S(2)}) collective-permute-start(f32[2,3,16,256]{3,2,1,0:T(8,128)S(1)} %get-tuple-element.25), channel_id=1, source_target_pairs={{0,2},{1,3},{2,0},{3,1},{4,6},{5,7},{6,4},{7,5},{8,10},{9,11},{10,... | collective-permute-start | bytes 294920 | tf_op jit(solution)/shard_map/ppermute | solution.py:37
  36.2 5.7 %collective-permute-start.18 = (f32[2,3,16,256]{3,2,1,0:T(8,128)S(1)}, f32[2,3,16,256]{3,2,1,0:T(8,128)S(1)}, u32[]{:S(2)}, u32[]{:S(2)}) collective-permute-start(f32[2,3,16,256]{3,2,1,0:T(8,128)S(1)} %fusion.1), channel_id=1, source_target_pairs={{0,4},{1,5},{2,6},{3,7},{4,0},{5,1},{6,2},{7,3},{8,12},{9,13},{10,... | collective-permute-start | bytes 294920 | tf_op jit(solution)/shard_map/ppermute | solution.py:37
  40.2 6.4 %collective-permute-start.6 = (f32[2,3,16,256]{3,2,1,0:T(8,128)S(1)}, f32[2,3,16,256]{3,2,1,0:T(8,128)S(1)}, u32[]{:S(2)}, u32[]{:S(2)}) collective-permute-start(f32[2,3,16,256]{3,2,1,0:T(8,128)S(1)} %fusion.3), channel_id=1, source_target_pairs={{0,4},{1,5},{2,6},{3,7},{4,0},{5,1},{6,2},{7,3},{8,12},{9,13},{10,... | collective-permute-start | bytes 294920 | tf_op jit(solution)/shard_map/ppermute | solution.py:37
  42.0 8.4 %collective-permute-start.19 = (f32[2,3,16,256]{3,2,1,0:T(8,128)S(1)}, f32[2,3,16,256]{3,2,1,0:T(8,128)S(1)}, u32[]{:S(2)}, u32[]{:S(2)}) collective-permute-start(f32[2,3,16,256]{3,2,1,0:T(8,128)S(1)} %add_multiply_fusion), channel_id=1, source_target_pairs={{0,3},{1,2},{2,1},{3,0},{4,7},{5,6},{6,5},{7,4},{8,11},{9,10},{10,... | collective-permute-start | bytes 294920 | tf_op jit(solution)/shard_map/ppermute | solution.py:37
  42.6 8.8 %collective-permute-start.20 = (f32[2,3,16,256]{3,2,1,0:T(8,128)S(1)}, f32[2,3,16,256]{3,2,1,0:T(8,128)S(1)}, u32[]{:S(2)}, u32[]{:S(2)}) collective-permute-start(f32[2,3,16,256]{3,2,1,0:T(8,128)S(1)} %add_multiply_fusion), channel_id=1, source_target_pairs={{0,1},{1,0},{2,3},{3,2},{4,5},{5,4},{6,7},{7,6},{8,9},{9,8},{10,11... | collective-permute-start | bytes 294920 | tf_op jit(solution)/shard_map/ppermute | solution.py:37
  45.6 7.2 %collective-permute-start.21 = (f32[2,3,16,256]{3,2,1,0:T(8,128)S(1)}, f32[2,3,16,256]{3,2,1,0:T(8,128)S(1)}, u32[]{:S(2)}, u32[]{:S(2)}) collective-permute-start(f32[2,3,16,256]{3,2,1,0:T(8,128)S(1)} %add_multiply_fusion), channel_id=1, source_target_pairs={{0,2},{1,3},{2,0},{3,1},{4,6},{5,7},{6,4},{7,5},{8,10},{9,11},{10,... | collective-permute-start | bytes 294920 | tf_op jit(solution)/shard_map/ppermute | solution.py:37
  46.6 6.7 %collective-permute-start.7 = (f32[2,3,16,256]{3,2,1,0:T(8,128)S(1)}, f32[2,3,16,256]{3,2,1,0:T(8,128)S(1)}, u32[]{:S(2)}, u32[]{:S(2)}) collective-permute-start(f32[2,3,16,256]{3,2,1,0:T(8,128)S(1)} %add_multiply_fusion.1), channel_id=1, source_target_pairs={{0,3},{1,2},{2,1},{3,0},{4,7},{5,6},{6,5},{7,4},{8,11},{9,10},{10,... | collective-permute-start | bytes 294920 | tf_op jit(solution)/shard_map/ppermute | solution.py:37
  47.3 7.8 %collective-permute-start.8 = (f32[2,3,16,256]{3,2,1,0:T(8,128)S(1)}, f32[2,3,16,256]{3,2,1,0:T(8,128)S(1)}, u32[]{:S(2)}, u32[]{:S(2)}) collective-permute-start(f32[2,3,16,256]{3,2,1,0:T(8,128)S(1)} %add_multiply_fusion.1), channel_id=1, source_target_pairs={{0,1},{1,0},{2,3},{3,2},{4,5},{5,4},{6,7},{7,6},{8,9},{9,8},{10,11... | collective-permute-start | bytes 294920 | tf_op jit(solution)/shard_map/ppermute | solution.py:37
  50.4 7.2 %collective-permute-start.9 = (f32[2,3,16,256]{3,2,1,0:T(8,128)S(1)}, f32[2,3,16,256]{3,2,1,0:T(8,128)S(1)}, u32[]{:S(2)}, u32[]{:S(2)}) collective-permute-start(f32[2,3,16,256]{3,2,1,0:T(8,128)S(1)} %add_multiply_fusion.1), channel_id=1, source_target_pairs={{0,2},{1,3},{2,0},{3,1},{4,6},{5,7},{6,4},{7,5},{8,10},{9,11},{10,... | collective-permute-start | bytes 294920 | tf_op jit(solution)/shard_map/ppermute | solution.py:37
  52.8 8.4 %collective-permute-start.22 = (f32[8,3,16,256]{3,2,1,0:T(8,128)S(1)}, f32[8,3,16,256]{3,2,1,0:T(8,128)S(1)}, u32[]{:S(2)}, u32[]{:S(2)}) collective-permute-start(f32[8,3,16,256]{3,2,1,0:T(8,128)S(1)} %pad_maximum_fusion.1.refs_0_), channel_id=1, source_target_pairs={{0,8},{1,9},{2,10},{3,11},{4,12},{5,13},{6,14},{7,15},{8,0},{9,1},... | collective-permute-start | bytes 1179656 | tf_op jit(solution)/shard_map/ppermute | solution.py:37
  57.6 9.3 %collective-permute-start.10 = (f32[8,3,16,256]{3,2,1,0:T(8,128)S(1)}, f32[8,3,16,256]{3,2,1,0:T(8,128)S(1)}, u32[]{:S(2)}, u32[]{:S(2)}) collective-permute-start(f32[8,3,16,256]{3,2,1,0:T(8,128)S(1)} %pad_maximum_fusion.refs_1_), channel_id=1, source_target_pairs={{0,24},{1,25},{2,26},{3,27},{4,28},{5,29},{6,30},{7,31},{8,16},{9,... | collective-permute-start | bytes 1179656 | tf_op jit(solution)/shard_map/ppermute | solution.py:37
  61.2 10.0 %collective-permute-start.24 = (f32[8,3,16,256]{3,2,1,0:T(8,128)S(1)}, f32[8,3,16,256]{3,2,1,0:T(8,128)S(1)}, u32[]{:S(2)}, u32[]{:S(2)}) collective-permute-start(f32[8,3,16,256]{3,2,1,0:T(8,128)S(1)} %pad_maximum_fusion.1.refs_0_), channel_id=1, source_target_pairs={{0,24},{1,25},{2,26},{3,27},{4,28},{5,29},{6,30},{7,31},{8,16},{9,... | collective-permute-start | bytes 1179656 | tf_op jit(solution)/shard_map/ppermute | solution.py:37
  61.3 9.9 %collective-permute-start.25 = (f32[8,3,16,256]{3,2,1,0:T(8,128)S(1)}, f32[8,3,16,256]{3,2,1,0:T(8,128)S(1)}, u32[]{:S(2)}, u32[]{:S(2)}) collective-permute-start(f32[8,3,16,256]{3,2,1,0:T(8,128)S(1)} %pad_maximum_fusion.refs_1_), channel_id=1, source_target_pairs={{0,8},{1,9},{2,10},{3,11},{4,12},{5,13},{6,14},{7,15},{8,0},{9,1},... | collective-permute-start | bytes 1179656 | tf_op jit(solution)/shard_map/ppermute | solution.py:37
  61.3 14.1 %collective-permute-start.23 = (f32[8,3,16,256]{3,2,1,0:T(8,128)S(1)}, f32[8,3,16,256]{3,2,1,0:T(8,128)S(1)}, u32[]{:S(2)}, u32[]{:S(2)}) collective-permute-start(f32[8,3,16,256]{3,2,1,0:T(8,128)S(1)} %collective-permute-done.22.refs_1_), channel_id=1, source_target_pairs={{0,24},{1,25},{2,26},{3,27},{4,28},{5,29},{6,30},{7,31},{8,16},{9,... | collective-permute-start | bytes 1179656 | tf_op jit(solution)/shard_map/ppermute | solution.py:37
  66.9 9.9 %collective-permute-start.11 = (f32[8,3,16,256]{3,2,1,0:T(8,128)S(1)}, f32[8,3,16,256]{3,2,1,0:T(8,128)S(1)}, u32[]{:S(2)}, u32[]{:S(2)}) collective-permute-start(f32[8,3,16,256]{3,2,1,0:T(8,128)S(1)} %collective-permute-done.10.refs_3_), channel_id=1, source_target_pairs={{0,8},{1,9},{2,10},{3,11},{4,12},{5,13},{6,14},{7,15},{8,0},{9,1},... | collective-permute-start | bytes 1179656 | tf_op jit(solution)/shard_map/ppermute | solution.py:37
  74.7 23.6 %copy-start.3 = (bf16[128,16384]{1,0:T(8,128)(2,1)S(1)}, bf16[128,16384]{1,0:T(8,128)(2,1)}, u32[]{:S(2)}) copy-start(bf16[128,16384]{1,0:T(8,128)(2,1)} %zeta.1) | copy-start | bytes 12582916
  78.3 1.3 %collective-permute-start.26 = (f32[16,256]{1,0:T(8,128)S(1)}, f32[16,256]{1,0:T(8,128)S(1)}, u32[]{:S(2)}, u32[]{:S(2)}) collective-permute-start(f32[16,256]{1,0:T(8,128)S(1)} %get-tuple-element.21), channel_id=1, source_target_pairs={{0,32},{32,0},{64,96},{96,64},{128,160},{160,128},{192,224},{224,1... | collective-permute-start | bytes 49160 | tf_op jit(solution)/shard_map/ppermute | solution.py:26
  99.6 1.2 %collective-permute-start.27 = (f32[16,128]{1,0:T(8,128)S(1)}, f32[16,128]{1,0:T(8,128)S(1)}, u32[]{:S(2)}, u32[]{:S(2)}) collective-permute-start(f32[16,128]{1,0:T(8,128)S(1)} %wing_sums.1), channel_id=1, source_target_pairs={{0,32},{32,0},{64,96},{96,64},{128,160},{160,128},{192,224},{224,1... | collective-permute-start | bytes 24584 | tf_op jit(solution)/shard_map/ppermute | solution.py:26
  100.8 4.9 %collective-permute-start.28 = (f32[16,128]{1,0:T(8,128)S(1)}, f32[16,128]{1,0:T(8,128)S(1)}, u32[]{:S(2)}, u32[]{:S(2)}) collective-permute-start(f32[16,128]{1,0:T(8,128)S(1)} %add.114), channel_id=1, source_target_pairs={{0,64},{32,96},{64,0},{96,32},{128,192},{160,224},{192,128},{224,1... | collective-permute-start | bytes 24584 | tf_op jit(solution)/shard_map/ppermute | solution.py:26
  105.7 7.1 %collective-permute-start.29 = (f32[16,128]{1,0:T(8,128)S(1)}, f32[16,128]{1,0:T(8,128)S(1)}, u32[]{:S(2)}, u32[]{:S(2)}) collective-permute-start(f32[16,128]{1,0:T(8,128)S(1)} %add.115.one), channel_id=1, source_target_pairs={{0,192},{32,224},{64,128},{96,160},{128,64},{160,96},{192,0},{224,... | collective-permute-start | bytes 24584 | tf_op jit(solution)/shard_map/ppermute | solution.py:26

commit v6 on v5

--- a/solution.py
+++ b/solution.py
@@ -7,7 +7,7 @@
 from jax.experimental.pallas import tpu as pltpu
 from jax.sharding import PartitionSpec as P
 
-MASKS = (((8, 24, 1, 3, 4), (1, 3, 8, 24, 4)), ((24, 8, 1, 3, 4), (3, 1, 8, 24, 4)))
+MASKS = (((8, 24, 1, 3, 4), (24, 8, 1, 3, 4)), ((1, 3, 8, 24, 4), (3, 1, 8, 24, 4)))
 CB, VB = 4, 8
 F32, BF16 = jnp.float32, jnp.bfloat16
 VMEM, SMEM = pl.BlockSpec(memory_space=pltpu.VMEM), pl.BlockSpec(memory_space=pltpu.SMEM)
@@ -16,9 +16,9 @@
     index, core = place[0], place[1]
     x, z, y = index >> 3, (index >> 2) & 1, index & 3
 
-    first, second = x + (y - x) * core, y + (x - y) * core
+    first, second = (x, y) if kpoint == 0 else (y, x)
     one, two = (first ^ (first >> 1)) & 1, first >> 1
-    quarter = one << 1 | two if kpoint == 0 else two << 1 | one
+    quarter = (one << 1 | two) + ((two << 1 | one) - (one << 1 | two)) * core
     return quarter, ((second ^ (second >> 1)) & 1) << 2 | (second >> 1) << 1 | z
 
 
@@ -58,7 +58,7 @@
     others = [cross(held, kpoint, *dims) for dims in ((3,), (2,), (2, 3))]
     held = jnp.concatenate([held] + others)
     first, second = cross(held, kpoint, 0), cross(held, kpoint, 1)
-    return held, second, first, cross(first, kpoint, 1)
+    return held, second, first
 
 
 def momentum_kernel(kpoint, quarters, place_ref, val_ref, miller_ref, cond_ref, *refs):
@@ -114,7 +114,7 @@
     nfreq = freq_ref.shape[0]
     count = sum(len(quarters) for _, quarters in groups)
     chunks, refs = refs[:count], refs[count:]
-    begins = groups[0][1][0] == 0
+    begins = groups[0] == (0, (0,))
     before, refs = (None, refs) if begins else (refs[0], refs[1:])
     outs, (total, amplitude, level, orbits, weight) = refs[:-5], refs[-5:]
     rows, cols = chunks[0].shape[2:]
@@ -171,7 +171,7 @@
                     value = value + before[row, :]
                 total[row, :] = value
 
-        if begins:
+        if quarters[0] == 0:
             bottom = bottom_of(pl.ds(pl.multiple_of(me_v * rows, rows), rows))
             gap = top[0] - bottom
             ratios = [factor / gap for factor in factors_of(gap)]
@@ -182,11 +182,11 @@
                     value = jnp.sum(square * ratios[w], axis=0, keepdims=True)
                     value = (value[:, :nval] + value[:, nval:]) * (weight_ref[k] / float(nval * ncond))
                     lanes = slice(w * nval, (w + 1) * nval)
-                    total[row, lanes] = value + total[row, lanes] if spot else value
+                    total[row, lanes] = value if begins else value + before[row, lanes]
             row = slice(tops + 3, tops + 4)
             value = jnp.full((1, points), weight_ref[k], F32)
-            total[row, :] = value + total[row, :] if spot else value
-    if not begins:
+            total[row, :] = value if begins else value + before[row, :]
+    if groups[0][1][0] != 0:
         total[tops:, :] = before[tops:, :]
     if len(outs) == 2:
         keep, send = outs
@@ -317,11 +317,16 @@
     keeps = [partial_momentum(k, (1, 0), *operands) for k in range(kcount)]
     parts = [(own, second, first, both) for (both, first), (second, own) in zip(sends, keeps)]
     chunks = [gathered_chunks(k, parts[k], pw_factor) for k in range(kcount)]
-    operands = (place, weights, freqs, energy_val, energy_cond, orbit_val, orbit_cond, chunks)
-    pair = pair_sums(((0, (0,)), (1, (0,))), *operands, [], 1)
-    pair = pair_sums(((0, (1, 2)), (1, (1, 2))), *operands, pair, 1)
-    pair = pair_sums(((0, (3,)),), *operands, pair, 1)
-    keep, send = pair_sums(((1, (3,)),), *operands, pair, 2)
+    operands = (place, weights, freqs, energy_val, energy_cond, orbit_val, orbit_cond)
+    pair = []
+    for k in range(kcount):
+        own, second, first = chunks[k]
+        pair = pair_sums(((k, (0,)),), *operands, {k: (own,)}, pair, 1)
+        first, pair = lax.optimization_barrier((first, pair))
+        chunks[k] = (own, second, first, cross(first, k, 1))
+    pair = pair_sums(((0, (1, 2)), (1, (1, 2))), *operands, chunks, pair, 1)
+    pair = pair_sums(((0, (3,)),), *operands, chunks, pair, 1)
+    keep, send = pair_sums(((1, (3,)),), *operands, chunks, pair, 2)
     pair = keep + swap(send, "ka", 1)
     total = wing_sums(place, everyone(pair, "wa"), zeta)
     total = total + swap(total, "ka", 1)

time: 114 us -> 112 us (0.982)
  waiting for transfers between devices: 25.4 us -> 19.4 us
  starting transfers between devices: 45.6 us -> 48 us
    ppermute x26, waiting for transfers between devices: 19.7 us -> 13.8 us  [cross(): return lax.ppermute(value, ('ka', 'wa'), pairs)]
    ppermute x26, starting transfers between devices: 36.7 us -> 39.2 us  [cross(): return lax.ppermute(value, ('ka', 'wa'), pairs)]
    pallas_call x4 -> x5, Pallas kernels: 8.87 us -> 9.51 us  [pair_sums(): pl.pallas_call(functools.partial(pair_kernel, groups), out_shape=[jax.Sha...]
  transfers between devices with their start and end apart: 30 -> 30, of which waited for: 17 -> 16; matrix products, arithmetic and copies ran while one was open for 0% -> 0% of each run, Pallas kernels for 11% -> 11%
where the time goes in v6:
time: 112 us
  starting transfers between devices  48 us (43%)
  blocking collectives  19.7 us (18%)
  waiting for transfers between devices  19.4 us (17%)
  Pallas kernels  17.7 us (16%)
  local copies, waits for them, and re-layouts  5.46 us (5%)
    ppermute x26, starting transfers between devices, cross(): return lax.ppermute(value, ('ka', 'wa'), pairs)  39.2 us
    all_to_all x1, blocking collectives, everyone(): lax.all_to_all(jnp.broadcast_to(value[None], (parts,) + value.shape), axi...  19.7 us
    ppermute x26, waiting for transfers between devices, cross(): return lax.ppermute(value, ('ka', 'wa'), pairs)  13.8 us
    pallas_call x5, Pallas kernels, pair_sums(): pl.pallas_call(functools.partial(pair_kernel, groups), out_shape=[jax.Sha...  9.51 us
    ppermute x4, starting transfers between devices, swap(): lax.ppermute(value, axis, [(i, i ^ mask) for i in range(lax.axis_size(axi...  8.74 us
    pallas_call x4, Pallas kernels, partial_momentum(): pl.pallas_call(functools.partial(momentum_kernel, kpoint, quarters), out_...  6.24 us
    ppermute x4, waiting for transfers between devices, swap(): lax.ppermute(value, axis, [(i, i ^ mask) for i in range(lax.axis_size(axi...  5.62 us
    unnamed x20, local copies, waits for them, and re-layouts  5.41 us
  transfers between devices with their start and end apart: 30, of which 16 were waited for; matrix products, arithmetic and copies ran while one was open for 0% of the time, Pallas kernels for 11%

profile of v6, /device:TPU:8, one launch (start us, length us, event | category | flops | bytes accessed | tf_op | source)
XLA Modules:
  0.0 111.6 jit_solution(3636193518094747816)
XLA Ops:
  0.7 3.4 %copy-done = bf16[2,1024,2048]{2,1,0:T(8,128)(2,1)S(1)} copy-done((bf16[2,1024,2048]{2,1,0:T(8,128)(2,1)S(1)}, bf16[2,1024,2048]{2,1,0:T(8,128)(2,1)}, u32[]{:S(2)}) %copy-start) | copy-done | bytes 8388632
  4.1 1.2 %copy-done.2 = bf16[2,128,2048]{2,1,0:T(8,128)(2,1)S(1)} copy-done((bf16[2,128,2048]{2,1,0:T(8,128)(2,1)S(1)}, bf16[2,128,2048]{2,1,0:T(8,128)(2,1)}, u32[]{:S(2)}) %copy-start.2) | copy-done | bytes 1048600
  6.1 1.6 %partial_momentum.7 = (f32[8,3,16,256]{3,2,1,0:T(8,128)S(1)}, f32[8,3,16,256]{3,2,1,0:T(8,128)S(1)}) custom-call(s32[2]{0:T(128)S(1)} %pad_add_fusion.place_ref, bf16[2,128,2048]{2,1,0:T(8,128)(2,1)S(1)} %copy-done.2, s32[3,2048]{1,0:T(4,128)S(1)} %copy-done.5, bf16[2,1024,2048]{2,1,0:T(8,128)(2,1)S(1)} %copy-done), custom_call_target="tpu_custom_call" | custom-call | flops 805306368 | bytes 3407872 | tf_op jit(solution)/shard_map/partial_momentum/pallas_call | solution.py:95
  7.6 1.6 %collective-permute-start.12 = (f32[8,3,16,256]{3,2,1,0:T(8,128)S(1)}, f32[8,3,16,256]{3,2,1,0:T(8,128)S(1)}, u32[]{:S(2)}, u32[]{:S(2)}) collective-permute-start(f32[8,3,16,256]{3,2,1,0:T(8,128)S(1)} %get-tuple-element.23), channel_id=1, source_target_pairs={{0,8},{1,9},{2,10},{3,11},{4,12},{5,13},{6,14},{7,15},{8,0},{9,1},... | collective-permute-start | bytes 1179656 | tf_op jit(solution)/shard_map/ppermute | solution.py:37
  9.2 1.6 %partial_momentum.5 = (f32[8,3,16,256]{3,2,1,0:T(8,128)S(1)}, f32[8,3,16,256]{3,2,1,0:T(8,128)S(1)}) custom-call(s32[2]{0:T(128)S(1)} %pad_add_fusion.place_ref, bf16[2,128,2048]{2,1,0:T(8,128)(2,1)S(1)} %copy-done.2, s32[3,2048]{1,0:T(4,128)S(1)} %copy-done.5, bf16[2,1024,2048]{2,1,0:T(8,128)(2,1)S(1)} %copy-done), custom_call_target="tpu_custom_call" | custom-call | flops 805306368 | bytes 3407872 | tf_op jit(solution)/shard_map/partial_momentum/pallas_call | solution.py:95
  10.8 0.8 collective-permute-start.1
  11.6 2.0 %collective-permute-start.11 = (f32[8,3,16,256]{3,2,1,0:T(8,128)S(1)}, f32[8,3,16,256]{3,2,1,0:T(8,128)S(1)}, u32[]{:S(2)}, u32[]{:S(2)}) collective-permute-start(f32[8,3,16,256]{3,2,1,0:T(8,128)S(1)} %get-tuple-element.21), channel_id=1, source_target_pairs={{0,8},{1,9},{2,10},{3,11},{4,12},{5,13},{6,14},{7,15},{8,0},{9,1},... | collective-permute-start | bytes 1179656 | tf_op jit(solution)/shard_map/ppermute | solution.py:37
  13.6 1.6 %partial_momentum.6 = (f32[8,3,16,256]{3,2,1,0:T(8,128)S(1)}, f32[8,3,16,256]{3,2,1,0:T(8,128)S(1)}) custom-call(s32[2]{0:T(128)S(1)} %pad_add_fusion.place_ref, bf16[2,128,2048]{2,1,0:T(8,128)(2,1)S(1)} %copy-done.2, s32[3,2048]{1,0:T(4,128)S(1)} %copy-done.5, bf16[2,1024,2048]{2,1,0:T(8,128)(2,1)S(1)} %copy-done), custom_call_target="tpu_custom_call" | custom-call | flops 805306368 | bytes 3407872 | tf_op jit(solution)/shard_map/partial_momentum/pallas_call | solution.py:95
  15.6 2.8 %collective-permute-start.13 = (f32[8,3,16,256]{3,2,1,0:T(8,128)S(1)}, f32[8,3,16,256]{3,2,1,0:T(8,128)S(1)}, u32[]{:S(2)}, u32[]{:S(2)}) collective-permute-start(f32[8,3,16,256]{3,2,1,0:T(8,128)S(1)} %add.101), channel_id=1, source_target_pairs={{0,24},{1,25},{2,26},{3,27},{4,28},{5,29},{6,30},{7,31},{8,16},{9,... | collective-permute-start | bytes 1179656 | tf_op jit(solution)/shard_map/ppermute | solution.py:37
  18.9 1.6 %partial_momentum.4 = (f32[8,3,16,256]{3,2,1,0:T(8,128)S(1)}, f32[8,3,16,256]{3,2,1,0:T(8,128)S(1)}) custom-call(s32[2]{0:T(128)S(1)} %pad_add_fusion.place_ref, bf16[2,128,2048]{2,1,0:T(8,128)(2,1)S(1)} %copy-done.2, s32[3,2048]{1,0:T(4,128)S(1)} %copy-done.5, bf16[2,1024,2048]{2,1,0:T(8,128)(2,1)S(1)} %copy-done), custom_call_target="tpu_custom_call" | custom-call | flops 805306368 | bytes 3407872 | tf_op jit(solution)/shard_map/partial_momentum/pallas_call | solution.py:95
  20.6 2.5 %collective-permute-start.2 = (f32[8,3,16,256]{3,2,1,0:T(8,128)S(1)}, f32[8,3,16,256]{3,2,1,0:T(8,128)S(1)}, u32[]{:S(2)}, u32[]{:S(2)}) collective-permute-start(f32[8,3,16,256]{3,2,1,0:T(8,128)S(1)} %add.88), channel_id=1, source_target_pairs={{0,3},{1,2},{2,1},{3,0},{4,7},{5,6},{6,5},{7,4},{8,11},{9,10},{10,... | collective-permute-start | bytes 1179656 | tf_op jit(solution)/shard_map/ppermute | solution.py:37
  23.1 2.1 %collective-permute-done.13 = f32[8,3,16,256]{3,2,1,0:T(8,128)S(1)} collective-permute-done((f32[8,3,16,256]{3,2,1,0:T(8,128)S(1)}, f32[8,3,16,256]{3,2,1,0:T(8,128)S(1)}, u32[]{:S(2)}, u32[]{:S(2)}) %collective-permute-start.13) | collective-permute-done | bytes 393248 | tf_op jit(solution)/shard_map/ppermute | solution.py:37
  25.3 2.0 %collective-permute-start.14 = (f32[2,3,16,256]{3,2,1,0:T(8,128)S(1)}, f32[2,3,16,256]{3,2,1,0:T(8,128)S(1)}, u32[]{:S(2)}, u32[]{:S(2)}) collective-permute-start(f32[2,3,16,256]{3,2,1,0:T(8,128)S(1)} %get-tuple-element.32), channel_id=1, source_target_pairs={{0,1},{1,0},{2,3},{3,2},{4,5},{5,4},{6,7},{7,6},{8,9},{9,8},{10,11... | collective-permute-start | bytes 294920 | tf_op jit(solution)/shard_map/ppermute | solution.py:37
  27.7 1.8 %collective-permute-start.16 = (f32[2,3,16,256]{3,2,1,0:T(8,128)S(1)}, f32[2,3,16,256]{3,2,1,0:T(8,128)S(1)}, u32[]{:S(2)}, u32[]{:S(2)}) collective-permute-start(f32[2,3,16,256]{3,2,1,0:T(8,128)S(1)} %get-tuple-element.30), channel_id=1, source_target_pairs={{0,2},{1,3},{2,0},{3,1},{4,6},{5,7},{6,4},{7,5},{8,10},{9,11},{10,... | collective-permute-start | bytes 294920 | tf_op jit(solution)/shard_map/ppermute | solution.py:37
  29.5 0.9 collective-permute-done
  30.6 1.3 %collective-permute-start.4 = (f32[2,3,16,256]{3,2,1,0:T(8,128)S(1)}, f32[2,3,16,256]{3,2,1,0:T(8,128)S(1)}, u32[]{:S(2)}, u32[]{:S(2)}) collective-permute-start(f32[2,3,16,256]{3,2,1,0:T(8,128)S(1)} %get-tuple-element.34), channel_id=1, source_target_pairs={{0,24},{1,25},{2,26},{3,27},{4,28},{5,29},{6,30},{7,31},{8,16},{9,... | collective-permute-start | bytes 294920 | tf_op jit(solution)/shard_map/ppermute | solution.py:37
  32.5 2.2 %collective-permute-start.5 = (f32[2,3,16,256]{3,2,1,0:T(8,128)S(1)}, f32[2,3,16,256]{3,2,1,0:T(8,128)S(1)}, u32[]{:S(2)}, u32[]{:S(2)}) collective-permute-start(f32[2,3,16,256]{3,2,1,0:T(8,128)S(1)} %get-tuple-element.33), channel_id=1, source_target_pairs={{0,16},{1,17},{2,18},{3,19},{4,20},{5,21},{6,22},{7,23},{8,24},{9,... | collective-permute-start | bytes 294920 | tf_op jit(solution)/shard_map/ppermute | solution.py:37
  34.7 0.8 collective-permute-done.16
  35.5 2.0 %collective-permute-start.17 = (f32[2,3,16,256]{3,2,1,0:T(8,128)S(1)}, f32[2,3,16,256]{3,2,1,0:T(8,128)S(1)}, u32[]{:S(2)}, u32[]{:S(2)}) collective-permute-start(f32[2,3,16,256]{3,2,1,0:T(8,128)S(1)} %fusion.1), channel_id=1, source_target_pairs={{0,4},{1,5},{2,6},{3,7},{4,0},{5,1},{6,2},{7,3},{8,12},{9,13},{10,... | collective-permute-start | bytes 294920 | tf_op jit(solution)/shard_map/ppermute | solution.py:37
  37.5 2.0 %collective-permute-done.4 = f32[2,3,16,256]{3,2,1,0:T(8,128)S(1)} collective-permute-done((f32[2,3,16,256]{3,2,1,0:T(8,128)S(1)}, f32[2,3,16,256]{3,2,1,0:T(8,128)S(1)}, u32[]{:S(2)}, u32[]{:S(2)}) %collective-permute-start.4) | collective-permute-done | bytes 98336 | tf_op jit(solution)/shard_map/ppermute | solution.py:37
  39.6 2.0 %collective-permute-start.6 = (f32[2,3,16,256]{3,2,1,0:T(8,128)S(1)}, f32[2,3,16,256]{3,2,1,0:T(8,128)S(1)}, u32[]{:S(2)}, u32[]{:S(2)}) collective-permute-start(f32[2,3,16,256]{3,2,1,0:T(8,128)S(1)} %fusion.3), channel_id=1, source_target_pairs={{0,4},{1,5},{2,6},{3,7},{4,0},{5,1},{6,2},{7,3},{8,12},{9,13},{10,... | collective-permute-start | bytes 294920 | tf_op jit(solution)/shard_map/ppermute | solution.py:37
  41.6 1.0 collective-permute-start.18
  42.6 2.4 %collective-permute-start.19 = (f32[2,3,16,256]{3,2,1,0:T(8,128)S(1)}, f32[2,3,16,256]{3,2,1,0:T(8,128)S(1)}, u32[]{:S(2)}, u32[]{:S(2)}) collective-permute-start(f32[2,3,16,256]{3,2,1,0:T(8,128)S(1)} %add_multiply_fusion), channel_id=1, source_target_pairs={{0,1},{1,0},{2,3},{3,2},{4,5},{5,4},{6,7},{7,6},{8,9},{9,8},{10,11... | collective-permute-start | bytes 294920 | tf_op jit(solution)/shard_map/ppermute | solution.py:37
  45.4 1.3 %collective-permute-start.7 = (f32[2,3,16,256]{3,2,1,0:T(8,128)S(1)}, f32[2,3,16,256]{3,2,1,0:T(8,128)S(1)}, u32[]{:S(2)}, u32[]{:S(2)}) collective-permute-start(f32[2,3,16,256]{3,2,1,0:T(8,128)S(1)} %add_multiply_fusion.1), channel_id=1, source_target_pairs={{0,24},{1,25},{2,26},{3,27},{4,28},{5,29},{6,30},{7,31},{8,16},{9,... | collective-permute-start | bytes 294920 | tf_op jit(solution)/shard_map/ppermute | solution.py:37
  47.3 2.9 %collective-permute-start.9 = (f32[2,3,16,256]{3,2,1,0:T(8,128)S(1)}, f32[2,3,16,256]{3,2,1,0:T(8,128)S(1)}, u32[]{:S(2)}, u32[]{:S(2)}) collective-permute-start(f32[2,3,16,256]{3,2,1,0:T(8,128)S(1)} %add_multiply_fusion.1), channel_id=1, source_target_pairs={{0,16},{1,17},{2,18},{3,19},{4,20},{5,21},{6,22},{7,23},{8,24},{9,... | collective-permute-start | bytes 294920 | tf_op jit(solution)/shard_map/ppermute | solution.py:37
  50.2 0.9 collective-permute-done.20
  51.2 0.8 collective-permute-start.21
  52.4 1.6 %collective-permute-done.9 = f32[2,3,16,256]{3,2,1,0:T(8,128)S(1)} collective-permute-done((f32[2,3,16,256]{3,2,1,0:T(8,128)S(1)}, f32[2,3,16,256]{3,2,1,0:T(8,128)S(1)}, u32[]{:S(2)}, u32[]{:S(2)}) %collective-permute-start.9) | collective-permute-done | bytes 98336 | tf_op jit(solution)/shard_map/ppermute | solution.py:37
  54.0 2.2 %collective-permute-start.10 = (f32[8,3,16,256]{3,2,1,0:T(8,128)S(1)}, f32[8,3,16,256]{3,2,1,0:T(8,128)S(1)}, u32[]{:S(2)}, u32[]{:S(2)}) collective-permute-start(f32[8,3,16,256]{3,2,1,0:T(8,128)S(1)} %pad_maximum_fusion.refs_0_), channel_id=1, source_target_pairs={{0,1},{1,0},{2,3},{3,2},{4,5},{5,4},{6,7},{7,6},{8,9},{9,8},{10,11... | collective-permute-start | bytes 1179656 | tf_op jit(solution)/shard_map/ppermute | solution.py:37
  56.2 1.4 %collective-permute-start.24 = (f32[8,3,16,256]{3,2,1,0:T(8,128)S(1)}, f32[8,3,16,256]{3,2,1,0:T(8,128)S(1)}, u32[]{:S(2)}, u32[]{:S(2)}) collective-permute-start(f32[8,3,16,256]{3,2,1,0:T(8,128)S(1)} %pad_maximum_fusion.1.refs_0_), channel_id=1, source_target_pairs={{0,24},{1,25},{2,26},{3,27},{4,28},{5,29},{6,30},{7,31},{8,16},{9,... | collective-permute-start | bytes 1179656 | tf_op jit(solution)/shard_map/ppermute | solution.py:37
  57.6 1.7 %collective-permute-start.25 = (f32[8,3,16,256]{3,2,1,0:T(8,128)S(1)}, f32[8,3,16,256]{3,2,1,0:T(8,128)S(1)}, u32[]{:S(2)}, u32[]{:S(2)}) collective-permute-start(f32[8,3,16,256]{3,2,1,0:T(8,128)S(1)} %pad_maximum_fusion.refs_0_), channel_id=1, source_target_pairs={{0,3},{1,2},{2,1},{3,0},{4,7},{5,6},{6,5},{7,4},{8,11},{9,10},{10,... | collective-permute-start | bytes 1179656 | tf_op jit(solution)/shard_map/ppermute | solution.py:37
  59.4 1.5 %pair_sums.5.refs_1_ = f32[16,512]{1,0:T(8,128)S(1)} custom-call(s32[2]{0:T(128)S(1)} %pad_add_fusion.place_ref, f32[2]{0:T(128)S(1)} %convert_element_type.3.weight_ref, f32[4]{0:T(128)S(1)} %copy-done.8, f32[2,128]{1,0:T(2,128)S(1)} %copy-done.7, f32[2,1024]{1,0:T(2,128)S(1)} %copy-done.6, bf16[2,128,512]{2,1,0:T(8,128)(2,1)S(1)} %copy-done.4, ...), custom_call_target="tpu_custom_call" | custom-call | flops 402653184 | bytes 917504 | tf_op jit(solution)/shard_map/pair_sums/pallas_call | solution.py:211
  60.9 2.1 %collective-permute-done.21.refs_1_ = f32[8,3,16,256]{3,2,1,0:T(8,128)S(1)} collective-permute-done((f32[8,3,16,256]{3,2,1,0:T(8,128)S(1)}, f32[8,3,16,256]{3,2,1,0:T(8,128)S(1)}, u32[]{:S(2)}, u32[]{:S(2)}) %collective-permute-start.21) | collective-permute-done | bytes 393248 | tf_op jit(solution)/shard_map/ppermute | solution.py:37
  63.0 1.7 %collective-permute-start.23 = (f32[8,3,16,256]{3,2,1,0:T(8,128)S(1)}, f32[8,3,16,256]{3,2,1,0:T(8,128)S(1)}, u32[]{:S(2)}, u32[]{:S(2)}) collective-permute-start(f32[8,3,16,256]{3,2,1,0:T(8,128)S(1)} %collective-permute-done.21.refs_1_), channel_id=1, source_target_pairs={{0,24},{1,25},{2,26},{3,27},{4,28},{5,29},{6,30},{7,31},{8,16},{9,... | collective-permute-start | bytes 1179656 | tf_op jit(solution)/shard_map/ppermute | solution.py:37
  64.7 1.5 %pair_sums.6.refs_4_ = f32[16,512]{1,0:T(8,128)S(1)} custom-call(s32[2]{0:T(128)S(1)} %pad_add_fusion.place_ref, f32[2]{0:T(128)S(1)} %convert_element_type.3.weight_ref, f32[4]{0:T(128)S(1)} %copy-done.8, f32[2,128]{1,0:T(2,128)S(1)} %copy-done.7, f32[2,1024]{1,0:T(2,128)S(1)} %copy-done.6, bf16[2,128,512]{2,1,0:T(8,128)(2,1)S(1)} %copy-done.4, ...), custom_call_target="tpu_custom_call" | custom-call | flops 402653184 | bytes 917504 | tf_op jit(solution)/shard_map/pair_sums/pallas_call | solution.py:211
  66.2 0.9 collective-permute-start.22
  67.1 3.5 %pair_sums.7.refs_1_ = f32[16,512]{1,0:T(8,128)S(1)} custom-call(s32[2]{0:T(128)S(1)} %pad_add_fusion.place_ref, f32[2]{0:T(128)S(1)} %convert_element_type.3.weight_ref, f32[4]{0:T(128)S(1)} %copy-done.8, f32[2,128]{1,0:T(2,128)S(1)} %copy-done.7, f32[2,1024]{1,0:T(2,128)S(1)} %copy-done.6, bf16[2,128,512]{2,1,0:T(8,128)(2,1)S(1)} %copy-done.4, ...), custom_call_target="tpu_custom_call" | custom-call | flops 1610612736 | bytes 3670016 | tf_op jit(solution)/shard_map/pair_sums/pallas_call | solution.py:211
  70.6 1.3 %collective-permute-done.23.refs_0_ = f32[8,3,16,256]{3,2,1,0:T(8,128)S(1)} collective-permute-done((f32[8,3,16,256]{3,2,1,0:T(8,128)S(1)}, f32[8,3,16,256]{3,2,1,0:T(8,128)S(1)}, u32[]{:S(2)}, u32[]{:S(2)}) %collective-permute-start.23) | collective-permute-done | bytes 393248 | tf_op jit(solution)/shard_map/ppermute | solution.py:37
  72.0 1.5 %pair_sums.8.refs_1_ = f32[16,512]{1,0:T(8,128)S(1)} custom-call(s32[2]{0:T(128)S(1)} %pad_add_fusion.place_ref, f32[2]{0:T(128)S(1)} %convert_element_type.3.weight_ref, f32[4]{0:T(128)S(1)} %copy-done.8, f32[2,128]{1,0:T(2,128)S(1)} %copy-done.7, f32[2,1024]{1,0:T(2,128)S(1)} %copy-done.6, bf16[2,128,512]{2,1,0:T(8,128)(2,1)S(1)} %copy-done.4, ...), custom_call_target="tpu_custom_call" | custom-call | flops 402653184 | bytes 917504 | tf_op jit(solution)/shard_map/pair_sums/pallas_call | solution.py:211
  74.0 1.5 %pair_sums.9 = (f32[16,256]{1,0:T(8,128)S(1)}, f32[16,256]{1,0:T(8,128)S(1)}) custom-call(s32[2]{0:T(128)S(1)} %pad_add_fusion.place_ref, f32[2]{0:T(128)S(1)} %convert_element_type.3.weight_ref, f32[4]{0:T(128)S(1)} %copy-done.8, f32[2,128]{1,0:T(2,128)S(1)} %copy-done.7, f32[2,1024]{1,0:T(2,128)S(1)} %copy-done.6, bf16[2,128,512]{2,1,0:T(8,128)(2,1)S(1)} %copy-done.4, ...), custom_call_target="tpu_custom_call" | custom-call | flops 402653184 | bytes 917504 | tf_op jit(solution)/shard_map/pair_sums/pallas_call | solution.py:211
  75.6 1.2 %collective-permute-done.26 = f32[16,256]{1,0:T(8,128)S(1)} collective-permute-done((f32[16,256]{1,0:T(8,128)S(1)}, f32[16,256]{1,0:T(8,128)S(1)}, u32[]{:S(2)}, u32[]{:S(2)}) %collective-permute-start.26) | collective-permute-done | bytes 16416 | tf_op jit(solution)/shard_map/ppermute | solution.py:26
  76.9 19.7 %all_to_all.5.gathered = f32[32,16,256]{2,1,0:T(8,128)S(1)} all-to-all(f32[32,16,256]{2,1,0:T(8,128)S(1)} %broadcast_in_dim.2), channel_id=1, replica_groups=mesh['ka'=8,'wa'=32] {'wa'}, dimensions={0} | all-to-all | bytes 1048576 | tf_op jit(solution)/shard_map/all_to_all | solution.py:42
  96.6 1.3 %wing_sums.1 = f32[16,128]{1,0:T(8,128)S(1)} custom-call(s32[2]{0:T(128)S(1)} %pad_add_fusion.place_ref, f32[32,16,256]{2,1,0:T(8,128)S(1)} %all_to_all.5.gathered, bf16[128,16384]{1,0:T(8,128)(2,1)S(1)} %copy-done.3), custom_call_target="tpu_custom_call" | custom-call | flops 100663296 | bytes 4718592 | tf_op jit(solution)/shard_map/wing_sums/pallas_call | solution.py:270
  97.9 1.2 %collective-permute-done.27 = f32[16,128]{1,0:T(8,128)S(1)} collective-permute-done((f32[16,128]{1,0:T(8,128)S(1)}, f32[16,128]{1,0:T(8,128)S(1)}, u32[]{:S(2)}, u32[]{:S(2)}) %collective-permute-start.27) | collective-permute-done | bytes 8224 | tf_op jit(solution)/shard_map/ppermute | solution.py:26
  99.1 3.3 %collective-permute-start.28 = (f32[16,128]{1,0:T(8,128)S(1)}, f32[16,128]{1,0:T(8,128)S(1)}, u32[]{:S(2)}, u32[]{:S(2)}) collective-permute-start(f32[16,128]{1,0:T(8,128)S(1)} %add.114), channel_id=1, source_target_pairs={{0,64},{32,96},{64,0},{96,32},{128,192},{160,224},{192,128},{224,1... | collective-permute-start | bytes 24584 | tf_op jit(solution)/shard_map/ppermute | solution.py:26
  102.3 1.6 %collective-permute-done.28 = f32[16,128]{1,0:T(8,128)S(1)} collective-permute-done((f32[16,128]{1,0:T(8,128)S(1)}, f32[16,128]{1,0:T(8,128)S(1)}, u32[]{:S(2)}, u32[]{:S(2)}) %collective-permute-start.28) | collective-permute-done | bytes 8224 | tf_op jit(solution)/shard_map/ppermute | solution.py:26
  104.0 5.4 %collective-permute-start.29 = (f32[16,128]{1,0:T(8,128)S(1)}, f32[16,128]{1,0:T(8,128)S(1)}, u32[]{:S(2)}, u32[]{:S(2)}) collective-permute-start(f32[16,128]{1,0:T(8,128)S(1)} %add.115.one), channel_id=1, source_target_pairs={{0,192},{32,224},{64,128},{96,160},{128,64},{160,96},{192,0},{224,... | collective-permute-start | bytes 24584 | tf_op jit(solution)/shard_map/ppermute | solution.py:26
  109.3 1.6 %collective-permute-done.29.two = f32[16,128]{1,0:T(8,128)S(1)} collective-permute-done((f32[16,128]{1,0:T(8,128)S(1)}, f32[16,128]{1,0:T(8,128)S(1)}, u32[]{:S(2)}, u32[]{:S(2)}) %collective-permute-start.29) | collective-permute-done | bytes 8224 | tf_op jit(solution)/shard_map/ppermute | solution.py:26
  (60 shorter events, 6.0 us)
Async XLA Ops:
  0.7 3.4 %copy-start = (bf16[2,1024,2048]{2,1,0:T(8,128)(2,1)S(1)}, bf16[2,1024,2048]{2,1,0:T(8,128)(2,1)}, u32[]{:S(2)}) copy-start(bf16[2,1024,2048]{2,1,0:T(8,128)(2,1)} %cond_ref.7) | copy-start | bytes 25165828
  4.1 1.2 %copy-start.2 = (bf16[2,128,2048]{2,1,0:T(8,128)(2,1)S(1)}, bf16[2,128,2048]{2,1,0:T(8,128)(2,1)}, u32[]{:S(2)}) copy-start(bf16[2,128,2048]{2,1,0:T(8,128)(2,1)} %val_ref.7) | copy-start | bytes 3145732
  5.3 0.8 copy-start.5
  7.6 7.9 %collective-permute-start.12 = (f32[8,3,16,256]{3,2,1,0:T(8,128)S(1)}, f32[8,3,16,256]{3,2,1,0:T(8,128)S(1)}, u32[]{:S(2)}, u32[]{:S(2)}) collective-permute-start(f32[8,3,16,256]{3,2,1,0:T(8,128)S(1)} %get-tuple-element.23), channel_id=1, source_target_pairs={{0,8},{1,9},{2,10},{3,11},{4,12},{5,13},{6,14},{7,15},{8,0},{9,1},... | collective-permute-start | bytes 1179656 | tf_op jit(solution)/shard_map/ppermute | solution.py:37
  10.8 9.7 %collective-permute-start.1 = (f32[8,3,16,256]{3,2,1,0:T(8,128)S(1)}, f32[8,3,16,256]{3,2,1,0:T(8,128)S(1)}, u32[]{:S(2)}, u32[]{:S(2)}) collective-permute-start(f32[8,3,16,256]{3,2,1,0:T(8,128)S(1)} %get-tuple-element.19), channel_id=1, source_target_pairs={{0,1},{1,0},{2,3},{3,2},{4,5},{5,4},{6,7},{7,6},{8,9},{9,8},{10,11... | collective-permute-start | bytes 1179656 | tf_op jit(solution)/shard_map/ppermute | solution.py:37
  11.6 11.5 %collective-permute-start.11 = (f32[8,3,16,256]{3,2,1,0:T(8,128)S(1)}, f32[8,3,16,256]{3,2,1,0:T(8,128)S(1)}, u32[]{:S(2)}, u32[]{:S(2)}) collective-permute-start(f32[8,3,16,256]{3,2,1,0:T(8,128)S(1)} %get-tuple-element.21), channel_id=1, source_target_pairs={{0,8},{1,9},{2,10},{3,11},{4,12},{5,13},{6,14},{7,15},{8,0},{9,1},... | collective-permute-start | bytes 1179656 | tf_op jit(solution)/shard_map/ppermute | solution.py:37
  15.6 9.7 %collective-permute-start.13 = (f32[8,3,16,256]{3,2,1,0:T(8,128)S(1)}, f32[8,3,16,256]{3,2,1,0:T(8,128)S(1)}, u32[]{:S(2)}, u32[]{:S(2)}) collective-permute-start(f32[8,3,16,256]{3,2,1,0:T(8,128)S(1)} %add.101), channel_id=1, source_target_pairs={{0,24},{1,25},{2,26},{3,27},{4,28},{5,29},{6,30},{7,31},{8,16},{9,... | collective-permute-start | bytes 1179656 | tf_op jit(solution)/shard_map/ppermute | solution.py:37
  18.4 12.0 %collective-permute-start = (f32[8,3,16,256]{3,2,1,0:T(8,128)S(1)}, f32[8,3,16,256]{3,2,1,0:T(8,128)S(1)}, u32[]{:S(2)}, u32[]{:S(2)}) collective-permute-start(f32[8,3,16,256]{3,2,1,0:T(8,128)S(1)} %get-tuple-element.17), channel_id=1, source_target_pairs={{0,1},{1,0},{2,3},{3,2},{4,5},{5,4},{6,7},{7,6},{8,9},{9,8},{10,11... | collective-permute-start | bytes 1179656 | tf_op jit(solution)/shard_map/ppermute | solution.py:37
  20.4 38.9 %copy-start.9 = (s32[2]{0:T(128)S(1)}, s32[2]{0:T(128)}, u32[]{:S(2)}) copy-start(s32[2]{0:T(128)} %param.19) | copy-start | bytes 28
  20.4 38.9 %copy-start.1 = (bf16[2,1024,512]{2,1,0:T(8,128)(2,1)S(1)}, bf16[2,1024,512]{2,1,0:T(8,128)(2,1)}, u32[]{:S(2)}) copy-start(bf16[2,1024,512]{2,1,0:T(8,128)(2,1)} %orbit_cond.9) | copy-start | bytes 6291460
  20.5 38.9 %copy-start.4 = (bf16[2,128,512]{2,1,0:T(8,128)(2,1)S(1)}, bf16[2,128,512]{2,1,0:T(8,128)(2,1)}, u32[]{:S(2)}) copy-start(bf16[2,128,512]{2,1,0:T(8,128)(2,1)} %orbit_val.9) | copy-start | bytes 786436
  20.5 38.9 %copy-start.6 = (f32[2,1024]{1,0:T(2,128)S(1)}, f32[2,1024]{1,0:T(2,128)}, u32[]{:S(2)}) copy-start(f32[2,1024]{1,0:T(2,128)} %energy_cond.9) | copy-start | bytes 24580
  20.5 38.9 %copy-start.7 = (f32[2,128]{1,0:T(2,128)S(1)}, f32[2,128]{1,0:T(2,128)}, u32[]{:S(2)}) copy-start(f32[2,128]{1,0:T(2,128)} %energy_val.9) | copy-start | bytes 3076
  20.5 38.9 %copy-start.8 = (f32[4]{0:T(128)S(1)}, f32[4]{0:T(128)}, u32[]{:S(2)}) copy-start(f32[4]{0:T(128)} %freq_ref.9) | copy-start | bytes 52
  20.6 9.8 %collective-permute-start.2 = (f32[8,3,16,256]{3,2,1,0:T(8,128)S(1)}, f32[8,3,16,256]{3,2,1,0:T(8,128)S(1)}, u32[]{:S(2)}, u32[]{:S(2)}) collective-permute-start(f32[8,3,16,256]{3,2,1,0:T(8,128)S(1)} %add.88), channel_id=1, source_target_pairs={{0,3},{1,2},{2,1},{3,0},{4,7},{5,6},{6,5},{7,4},{8,11},{9,10},{10,... | collective-permute-start | bytes 1179656 | tf_op jit(solution)/shard_map/ppermute | solution.py:37
  25.3 7.2 %collective-permute-start.14 = (f32[2,3,16,256]{3,2,1,0:T(8,128)S(1)}, f32[2,3,16,256]{3,2,1,0:T(8,128)S(1)}, u32[]{:S(2)}, u32[]{:S(2)}) collective-permute-start(f32[2,3,16,256]{3,2,1,0:T(8,128)S(1)} %get-tuple-element.32), channel_id=1, source_target_pairs={{0,1},{1,0},{2,3},{3,2},{4,5},{5,4},{6,7},{7,6},{8,9},{9,8},{10,11... | collective-permute-start | bytes 294920 | tf_op jit(solution)/shard_map/ppermute | solution.py:37
  27.3 7.4 %collective-permute-start.15 = (f32[2,3,16,256]{3,2,1,0:T(8,128)S(1)}, f32[2,3,16,256]{3,2,1,0:T(8,128)S(1)}, u32[]{:S(2)}, u32[]{:S(2)}) collective-permute-start(f32[2,3,16,256]{3,2,1,0:T(8,128)S(1)} %get-tuple-element.31), channel_id=1, source_target_pairs={{0,3},{1,2},{2,1},{3,0},{4,7},{5,6},{6,5},{7,4},{8,11},{9,10},{10,... | collective-permute-start | bytes 294920 | tf_op jit(solution)/shard_map/ppermute | solution.py:37
  27.7 7.8 %collective-permute-start.16 = (f32[2,3,16,256]{3,2,1,0:T(8,128)S(1)}, f32[2,3,16,256]{3,2,1,0:T(8,128)S(1)}, u32[]{:S(2)}, u32[]{:S(2)}) collective-permute-start(f32[2,3,16,256]{3,2,1,0:T(8,128)S(1)} %get-tuple-element.30), channel_id=1, source_target_pairs={{0,2},{1,3},{2,0},{3,1},{4,6},{5,7},{6,4},{7,5},{8,10},{9,11},{10,... | collective-permute-start | bytes 294920 | tf_op jit(solution)/shard_map/ppermute | solution.py:37
  30.5 7.0 %collective-permute-start.3 = (f32[2,3,16,256]{3,2,1,0:T(8,128)S(1)}, f32[2,3,16,256]{3,2,1,0:T(8,128)S(1)}, u32[]{:S(2)}, u32[]{:S(2)}) collective-permute-start(f32[2,3,16,256]{3,2,1,0:T(8,128)S(1)} %get-tuple-element.35), channel_id=1, source_target_pairs={{0,8},{1,9},{2,10},{3,11},{4,12},{5,13},{6,14},{7,15},{8,0},{9,1},... | collective-permute-start | bytes 294920 | tf_op jit(solution)/shard_map/ppermute | solution.py:37
  30.6 9.0 %collective-permute-start.4 = (f32[2,3,16,256]{3,2,1,0:T(8,128)S(1)}, f32[2,3,16,256]{3,2,1,0:T(8,128)S(1)}, u32[]{:S(2)}, u32[]{:S(2)}) collective-permute-start(f32[2,3,16,256]{3,2,1,0:T(8,128)S(1)} %get-tuple-element.34), channel_id=1, source_target_pairs={{0,24},{1,25},{2,26},{3,27},{4,28},{5,29},{6,30},{7,31},{8,16},{9,... | collective-permute-start | bytes 294920 | tf_op jit(solution)/shard_map/ppermute | solution.py:37
  32.5 7.1 %collective-permute-start.5 = (f32[2,3,16,256]{3,2,1,0:T(8,128)S(1)}, f32[2,3,16,256]{3,2,1,0:T(8,128)S(1)}, u32[]{:S(2)}, u32[]{:S(2)}) collective-permute-start(f32[2,3,16,256]{3,2,1,0:T(8,128)S(1)} %get-tuple-element.33), channel_id=1, source_target_pairs={{0,16},{1,17},{2,18},{3,19},{4,20},{5,21},{6,22},{7,23},{8,24},{9,... | collective-permute-start | bytes 294920 | tf_op jit(solution)/shard_map/ppermute | solution.py:37
  35.5 6.1 %collective-permute-start.17 = (f32[2,3,16,256]{3,2,1,0:T(8,128)S(1)}, f32[2,3,16,256]{3,2,1,0:T(8,128)S(1)}, u32[]{:S(2)}, u32[]{:S(2)}) collective-permute-start(f32[2,3,16,256]{3,2,1,0:T(8,128)S(1)} %fusion.1), channel_id=1, source_target_pairs={{0,4},{1,5},{2,6},{3,7},{4,0},{5,1},{6,2},{7,3},{8,12},{9,13},{10,... | collective-permute-start | bytes 294920 | tf_op jit(solution)/shard_map/ppermute | solution.py:37
  39.6 5.8 %collective-permute-start.6 = (f32[2,3,16,256]{3,2,1,0:T(8,128)S(1)}, f32[2,3,16,256]{3,2,1,0:T(8,128)S(1)}, u32[]{:S(2)}, u32[]{:S(2)}) collective-permute-start(f32[2,3,16,256]{3,2,1,0:T(8,128)S(1)} %fusion.3), channel_id=1, source_target_pairs={{0,4},{1,5},{2,6},{3,7},{4,0},{5,1},{6,2},{7,3},{8,12},{9,13},{10,... | collective-permute-start | bytes 294920 | tf_op jit(solution)/shard_map/ppermute | solution.py:37
  41.6 5.6 %collective-permute-start.18 = (f32[2,3,16,256]{3,2,1,0:T(8,128)S(1)}, f32[2,3,16,256]{3,2,1,0:T(8,128)S(1)}, u32[]{:S(2)}, u32[]{:S(2)}) collective-permute-start(f32[2,3,16,256]{3,2,1,0:T(8,128)S(1)} %add_multiply_fusion), channel_id=1, source_target_pairs={{0,3},{1,2},{2,1},{3,0},{4,7},{5,6},{6,5},{7,4},{8,11},{9,10},{10,... | collective-permute-start | bytes 294920 | tf_op jit(solution)/shard_map/ppermute | solution.py:37
  42.6 7.6 %collective-permute-start.19 = (f32[2,3,16,256]{3,2,1,0:T(8,128)S(1)}, f32[2,3,16,256]{3,2,1,0:T(8,128)S(1)}, u32[]{:S(2)}, u32[]{:S(2)}) collective-permute-start(f32[2,3,16,256]{3,2,1,0:T(8,128)S(1)} %add_multiply_fusion), channel_id=1, source_target_pairs={{0,1},{1,0},{2,3},{3,2},{4,5},{5,4},{6,7},{7,6},{8,9},{9,8},{10,11... | collective-permute-start | bytes 294920 | tf_op jit(solution)/shard_map/ppermute | solution.py:37
  45.0 6.1 %collective-permute-start.20 = (f32[2,3,16,256]{3,2,1,0:T(8,128)S(1)}, f32[2,3,16,256]{3,2,1,0:T(8,128)S(1)}, u32[]{:S(2)}, u32[]{:S(2)}) collective-permute-start(f32[2,3,16,256]{3,2,1,0:T(8,128)S(1)} %add_multiply_fusion), channel_id=1, source_target_pairs={{0,2},{1,3},{2,0},{3,1},{4,6},{5,7},{6,4},{7,5},{8,10},{9,11},{10,... | collective-permute-start | bytes 294920 | tf_op jit(solution)/shard_map/ppermute | solution.py:37
  45.4 7.0 %collective-permute-start.7 = (f32[2,3,16,256]{3,2,1,0:T(8,128)S(1)}, f32[2,3,16,256]{3,2,1,0:T(8,128)S(1)}, u32[]{:S(2)}, u32[]{:S(2)}) collective-permute-start(f32[2,3,16,256]{3,2,1,0:T(8,128)S(1)} %add_multiply_fusion.1), channel_id=1, source_target_pairs={{0,24},{1,25},{2,26},{3,27},{4,28},{5,29},{6,30},{7,31},{8,16},{9,... | collective-permute-start | bytes 294920 | tf_op jit(solution)/shard_map/ppermute | solution.py:37
  46.7 5.7 %collective-permute-start.8 = (f32[2,3,16,256]{3,2,1,0:T(8,128)S(1)}, f32[2,3,16,256]{3,2,1,0:T(8,128)S(1)}, u32[]{:S(2)}, u32[]{:S(2)}) collective-permute-start(f32[2,3,16,256]{3,2,1,0:T(8,128)S(1)} %add_multiply_fusion.1), channel_id=1, source_target_pairs={{0,8},{1,9},{2,10},{3,11},{4,12},{5,13},{6,14},{7,15},{8,0},{9,1},... | collective-permute-start | bytes 294920 | tf_op jit(solution)/shard_map/ppermute | solution.py:37
  47.3 6.7 %collective-permute-start.9 = (f32[2,3,16,256]{3,2,1,0:T(8,128)S(1)}, f32[2,3,16,256]{3,2,1,0:T(8,128)S(1)}, u32[]{:S(2)}, u32[]{:S(2)}) collective-permute-start(f32[2,3,16,256]{3,2,1,0:T(8,128)S(1)} %add_multiply_fusion.1), channel_id=1, source_target_pairs={{0,16},{1,17},{2,18},{3,19},{4,20},{5,21},{6,22},{7,23},{8,24},{9,... | collective-permute-start | bytes 294920 | tf_op jit(solution)/shard_map/ppermute | solution.py:37
  51.2 11.8 %collective-permute-start.21 = (f32[8,3,16,256]{3,2,1,0:T(8,128)S(1)}, f32[8,3,16,256]{3,2,1,0:T(8,128)S(1)}, u32[]{:S(2)}, u32[]{:S(2)}) collective-permute-start(f32[8,3,16,256]{3,2,1,0:T(8,128)S(1)} %pad_maximum_fusion.1.refs_0_), channel_id=1, source_target_pairs={{0,8},{1,9},{2,10},{3,11},{4,12},{5,13},{6,14},{7,15},{8,0},{9,1},... | collective-permute-start | bytes 1179656 | tf_op jit(solution)/shard_map/ppermute | solution.py:37
  54.0 12.2 %collective-permute-start.10 = (f32[8,3,16,256]{3,2,1,0:T(8,128)S(1)}, f32[8,3,16,256]{3,2,1,0:T(8,128)S(1)}, u32[]{:S(2)}, u32[]{:S(2)}) collective-permute-start(f32[8,3,16,256]{3,2,1,0:T(8,128)S(1)} %pad_maximum_fusion.refs_0_), channel_id=1, source_target_pairs={{0,1},{1,0},{2,3},{3,2},{4,5},{5,4},{6,7},{7,6},{8,9},{9,8},{10,11... | collective-permute-start | bytes 1179656 | tf_op jit(solution)/shard_map/ppermute | solution.py:37
  56.2 10.9 %collective-permute-start.24 = (f32[8,3,16,256]{3,2,1,0:T(8,128)S(1)}, f32[8,3,16,256]{3,2,1,0:T(8,128)S(1)}, u32[]{:S(2)}, u32[]{:S(2)}) collective-permute-start(f32[8,3,16,256]{3,2,1,0:T(8,128)S(1)} %pad_maximum_fusion.1.refs_0_), channel_id=1, source_target_pairs={{0,24},{1,25},{2,26},{3,27},{4,28},{5,29},{6,30},{7,31},{8,16},{9,... | collective-permute-start | bytes 1179656 | tf_op jit(solution)/shard_map/ppermute | solution.py:37
  57.6 9.5 %collective-permute-start.25 = (f32[8,3,16,256]{3,2,1,0:T(8,128)S(1)}, f32[8,3,16,256]{3,2,1,0:T(8,128)S(1)}, u32[]{:S(2)}, u32[]{:S(2)}) collective-permute-start(f32[8,3,16,256]{3,2,1,0:T(8,128)S(1)} %pad_maximum_fusion.refs_0_), channel_id=1, source_target_pairs={{0,3},{1,2},{2,1},{3,0},{4,7},{5,6},{6,5},{7,4},{8,11},{9,10},{10,... | collective-permute-start | bytes 1179656 | tf_op jit(solution)/shard_map/ppermute | solution.py:37
  63.0 9.0 %collective-permute-start.23 = (f32[8,3,16,256]{3,2,1,0:T(8,128)S(1)}, f32[8,3,16,256]{3,2,1,0:T(8,128)S(1)}, u32[]{:S(2)}, u32[]{:S(2)}) collective-permute-start(f32[8,3,16,256]{3,2,1,0:T(8,128)S(1)} %collective-permute-done.21.refs_1_), channel_id=1, source_target_pairs={{0,24},{1,25},{2,26},{3,27},{4,28},{5,29},{6,30},{7,31},{8,16},{9,... | collective-permute-start | bytes 1179656 | tf_op jit(solution)/shard_map/ppermute | solution.py:37
  66.2 7.8 %collective-permute-start.22 = (f32[8,3,16,256]{3,2,1,0:T(8,128)S(1)}, f32[8,3,16,256]{3,2,1,0:T(8,128)S(1)}, u32[]{:S(2)}, u32[]{:S(2)}) collective-permute-start(f32[8,3,16,256]{3,2,1,0:T(8,128)S(1)} %collective-permute-done.10.refs_3_), channel_id=1, source_target_pairs={{0,3},{1,2},{2,1},{3,0},{4,7},{5,6},{6,5},{7,4},{8,11},{9,10},{10,... | collective-permute-start | bytes 1179656 | tf_op jit(solution)/shard_map/ppermute | solution.py:37
  70.6 25.9 %copy-start.3 = (bf16[128,16384]{1,0:T(8,128)(2,1)S(1)}, bf16[128,16384]{1,0:T(8,128)(2,1)}, u32[]{:S(2)}) copy-start(bf16[128,16384]{1,0:T(8,128)(2,1)} %zeta.1) | copy-start | bytes 12582916
  75.5 1.3 %collective-permute-start.26 = (f32[16,256]{1,0:T(8,128)S(1)}, f32[16,256]{1,0:T(8,128)S(1)}, u32[]{:S(2)}, u32[]{:S(2)}) collective-permute-start(f32[16,256]{1,0:T(8,128)S(1)} %get-tuple-element.29), channel_id=1, source_target_pairs={{0,32},{32,0},{64,96},{96,64},{128,160},{160,128},{192,224},{224,1... | collective-permute-start | bytes 49160 | tf_op jit(solution)/shard_map/ppermute | solution.py:26
  97.9 1.2 %collective-permute-start.27 = (f32[16,128]{1,0:T(8,128)S(1)}, f32[16,128]{1,0:T(8,128)S(1)}, u32[]{:S(2)}, u32[]{:S(2)}) collective-permute-start(f32[16,128]{1,0:T(8,128)S(1)} %wing_sums.1), channel_id=1, source_target_pairs={{0,32},{32,0},{64,96},{96,64},{128,160},{160,128},{192,224},{224,1... | collective-permute-start | bytes 24584 | tf_op jit(solution)/shard_map/ppermute | solution.py:26
  99.1 4.9 %collective-permute-start.28 = (f32[16,128]{1,0:T(8,128)S(1)}, f32[16,128]{1,0:T(8,128)S(1)}, u32[]{:S(2)}, u32[]{:S(2)}) collective-permute-start(f32[16,128]{1,0:T(8,128)S(1)} %add.114), channel_id=1, source_target_pairs={{0,64},{32,96},{64,0},{96,32},{128,192},{160,224},{192,128},{224,1... | collective-permute-start | bytes 24584 | tf_op jit(solution)/shard_map/ppermute | solution.py:26
  104.0 7.0 %collective-permute-start.29 = (f32[16,128]{1,0:T(8,128)S(1)}, f32[16,128]{1,0:T(8,128)S(1)}, u32[]{:S(2)}, u32[]{:S(2)}) collective-permute-start(f32[16,128]{1,0:T(8,128)S(1)} %add.115.one), channel_id=1, source_target_pairs={{0,192},{32,224},{64,128},{96,160},{128,64},{160,96},{192,0},{224,... | collective-permute-start | bytes 24584 | tf_op jit(solution)/shard_map/ppermute | solution.py:26

commit v7 on v6

--- a/solution.py
+++ b/solution.py
@@ -61,23 +61,43 @@
     return held, second, first
 
 
-def momentum_kernel(kpoint, quarters, place_ref, val_ref, miller_ref, cond_ref, *refs):
-    outs, weighted = refs[:-1], refs[-1]
-    nval = val_ref.shape[1]
+def weight_kernel(place_ref, val_ref, miller_ref, out):
+    kcount, nval, _ = val_ref.shape
+    rows = nval // VB
+    factors = [miller_ref[axis : axis + 1, :].astype(F32) for axis in range(3)]
+    for k in range(kcount):
+        _, me_v = code_of(place_ref, k)
+        for place in range(VB):
+            source = pl.multiple_of((place ^ me_v) * rows, rows)
+            block = val_ref[k, pl.ds(source, rows), :].astype(F32)
+            for axis in range(3):
+                start = axis * nval + place * rows
+                out[k, start : start + rows, :] = (block * factors[axis]).astype(BF16)
+
+
+def weighted_values(place, coeff_val, miller):
+    kcount, nval, depth = coeff_val.shape
+    return pl.pallas_call(
+        weight_kernel,
+        out_shape=jax.ShapeDtypeStruct((kcount, 3 * nval, depth), BF16),
+        in_specs=[SMEM, VMEM, VMEM],
+        out_specs=VMEM,
+        cost_estimate=pl.CostEstimate(
+            flops=3 * kcount * nval * depth, bytes_accessed=8 * kcount * nval * depth, transcendentals=0
+        ),
+        compiler_params=pltpu.CompilerParams(vmem_limit_bytes=16 << 20),
+        name="weighted_values",
+    )(place, coeff_val, miller)
+
+
+def momentum_kernel(kpoint, quarters, place_ref, weighted, cond_ref, *outs):
+    nval = weighted.shape[1] // 3
     rows, cols = outs[0].shape[2:]
-    me_c, me_v = code_of(place_ref, kpoint)
-    for place in range(VB):
-        source = pl.multiple_of((place ^ me_v) * rows, rows)
-        block = val_ref[kpoint, pl.ds(source, rows), :].astype(F32)
-        for axis in range(3):
-            factor = miller_ref[axis : axis + 1, :].astype(F32)
-            weighted[axis * nval + place * rows : axis * nval + (place + 1) * rows, :] = (
-                block * factor
-            ).astype(BF16)
+    me_c, _ = code_of(place_ref, kpoint)
     for quarter, out in zip(quarters, outs):
         start = pl.multiple_of((quarter ^ me_c) * cols, cols)
         result = lax.dot_general(
-            weighted[...],
+            weighted[kpoint],
             cond_ref[kpoint, pl.ds(start, cols), :],
             (((1,), (1,)), ((), ())),
             preferred_element_type=F32,
@@ -88,24 +108,23 @@
                 out[eighth, axis] = result[start : start + rows]
 
 
-def partial_momentum(kpoint, quarters, place, coeff_val, miller, coeff_cond):
-    _, nval, depth = coeff_val.shape
+def partial_momentum(kpoint, quarters, place, weighted, coeff_cond):
+    _, height, depth = weighted.shape
     ncond = coeff_cond.shape[1]
     count = len(quarters)
     return pl.pallas_call(
         functools.partial(momentum_kernel, kpoint, quarters),
-        out_shape=[jax.ShapeDtypeStruct((VB, 3, nval // VB, ncond // CB), F32)] * count,
-        in_specs=[SMEM, VMEM, VMEM, VMEM],
+        out_shape=[jax.ShapeDtypeStruct((VB, 3, height // 3 // VB, ncond // CB), F32)] * count,
+        in_specs=[SMEM, VMEM, VMEM],
         out_specs=[VMEM] * count,
-        scratch_shapes=[pltpu.VMEM((3 * nval, depth), BF16)],
         cost_estimate=pl.CostEstimate(
-            flops=2 * 3 * nval * ncond * depth * count // CB,
-            bytes_accessed=(2 * nval + 2 * ncond * count // CB) * depth + 12 * nval * ncond * count // CB,
+            flops=2 * height * ncond * depth * count // CB,
+            bytes_accessed=2 * (height + ncond * count // CB) * depth + 4 * height * ncond * count // CB,
             transcendentals=0,
         ),
         compiler_params=pltpu.CompilerParams(vmem_limit_bytes=24 << 20),
         name="partial_momentum",
-    )(place, coeff_val, miller, coeff_cond)
+    )(place, weighted, coeff_cond)
 
 
 def pair_kernel(groups, place_ref, weight_ref, freq_ref, energy_val, energy_cond, orbit_val, orbit_cond, *refs):
@@ -312,10 +331,11 @@
     weights = kweight.astype(F32)
     place = jnp.stack([lax.axis_index("wa"), lax.axis_index("ka") & 1]).astype(jnp.int32)
 
-    operands = (place, coeff_val, miller, coeff_cond)
-    sends = [partial_momentum(k, (3, 2), *operands) for k in range(kcount)]
-    keeps = [partial_momentum(k, (1, 0), *operands) for k in range(kcount)]
-    parts = [(own, second, first, both) for (both, first), (second, own) in zip(sends, keeps)]
+    operands = (place, weighted_values(place, coeff_val, miller), coeff_cond)
+    opposite = [partial_momentum(k, (3,), *operands) for k in range(kcount)]
+    neighbour = [partial_momentum(k, (2,), *operands) for k in range(kcount)]
+    others = [partial_momentum(k, (1, 0), *operands) for k in range(kcount)]
+    parts = [(own, second, first, both) for (both,), (first,), (second, own) in zip(opposite, neighbour, others)]
     chunks = [gathered_chunks(k, parts[k], pw_factor) for k in range(kcount)]
     operands = (place, weights, freqs, energy_val, energy_cond, orbit_val, orbit_cond)
     pair = []
@@ -323,7 +343,9 @@
         own, second, first = chunks[k]
         pair = pair_sums(((k, (0,)),), *operands, {k: (own,)}, pair, 1)
         first, pair = lax.optimization_barrier((first, pair))
-        chunks[k] = (own, second, first, cross(first, k, 1))
+        half = first.shape[0] // 2
+        passed = jnp.concatenate([cross(first[:half], k, 1), cross(second[half:], k, 0)])
+        chunks[k] = (own, second, first, passed)
     pair = pair_sums(((0, (1, 2)), (1, (1, 2))), *operands, chunks, pair, 1)
     pair = pair_sums(((0, (3,)),), *operands, chunks, pair, 1)
     keep, send = pair_sums(((1, (3,)),), *operands, chunks, pair, 2)

time: 112 us -> 114 us (1.018)
  starting transfers between devices: 48 us -> 53 us
  waiting for transfers between devices: 19.4 us -> 15 us
  Pallas kernels: 17.7 us -> 20.1 us
  blocking collectives: 19.7 us -> 18.3 us
    ppermute x26 -> x28, starting transfers between devices: 39.2 us -> 44.5 us  [cross(): return lax.ppermute(value, ('ka', 'wa'), pairs)]
    ppermute x26 -> x28, waiting for transfers between devices: 13.8 us -> 9.35 us  [cross(): return lax.ppermute(value, ('ka', 'wa'), pairs)]
    pallas_call x4 -> x6, Pallas kernels: 6.24 us -> 7.72 us  [partial_momentum(): pl.pallas_call(functools.partial(momentum_kernel, kpoint, quarters), out_...]
    all_to_all x1, blocking collectives: 19.7 us -> 18.3 us  [everyone(): lax.all_to_all(jnp.broadcast_to(value[None], (parts,) + value.shape), axi...]
  transfers between devices with their start and end apart: 30 -> 32, of which waited for: 16 -> 13; matrix products, arithmetic and copies ran while one was open for 0% -> 0% of each run, Pallas kernels for 11% -> 13%
where the time goes in v7:
time: 114 us; the launch traced here: 113 us
  starting transfers between devices  53 us (46%)
  Pallas kernels  20.1 us (18%)
  blocking collectives  18.3 us (16%)
  waiting for transfers between devices  15 us (13%)
  local copies, waits for them, and re-layouts  5.51 us (5%)
    ppermute x28, starting transfers between devices, cross(): return lax.ppermute(value, ('ka', 'wa'), pairs)  44.5 us
    all_to_all x1, blocking collectives, everyone(): lax.all_to_all(jnp.broadcast_to(value[None], (parts,) + value.shape), axi...  18.3 us
    pallas_call x5, Pallas kernels, pair_sums(): pl.pallas_call(functools.partial(pair_kernel, groups), out_shape=[jax.Sha...  9.52 us
    ppermute x28, waiting for transfers between devices, cross(): return lax.ppermute(value, ('ka', 'wa'), pairs)  9.35 us
    ppermute x4, starting transfers between devices, swap(): lax.ppermute(value, axis, [(i, i ^ mask) for i in range(lax.axis_size(axi...  8.5 us
    pallas_call x6, Pallas kernels, partial_momentum(): pl.pallas_call(functools.partial(momentum_kernel, kpoint, quarters), out_...  7.72 us
    ppermute x4, waiting for transfers between devices, swap(): lax.ppermute(value, axis, [(i, i ^ mask) for i in range(lax.axis_size(axi...  5.61 us
    unnamed x20, local copies, waits for them, and re-layouts  5.4 us
  transfers between devices with their start and end apart: 32, of which 13 were waited for; matrix products, arithmetic and copies ran while one was open for 0% of the time, Pallas kernels for 13%

profile of v7, /device:TPU:8, one launch (start us, length us, event | category | flops | bytes accessed | tf_op | source)
XLA Modules:
  0.0 113.5 jit_solution(9359615699265606945)
XLA Ops:
  0.7 1.2 %copy-done.4 = bf16[2,128,2048]{2,1,0:T(8,128)(2,1)S(1)} copy-done((bf16[2,128,2048]{2,1,0:T(8,128)(2,1)S(1)}, bf16[2,128,2048]{2,1,0:T(8,128)(2,1)}, u32[]{:S(2)}) %copy-start.4) | copy-done | bytes 1048600
  1.9 0.8 copy-done.6
  2.7 1.0 weighted_values.1.weighted
  3.7 3.4 %copy-done = bf16[2,1024,2048]{2,1,0:T(8,128)(2,1)S(1)} copy-done((bf16[2,1024,2048]{2,1,0:T(8,128)(2,1)S(1)}, bf16[2,1024,2048]{2,1,0:T(8,128)(2,1)}, u32[]{:S(2)}) %copy-start) | copy-done | bytes 8388632
  7.1 1.2 %partial_momentum.11 = f32[8,3,16,256]{3,2,1,0:T(8,128)S(1)} custom-call(s32[2]{0:T(128)S(1)} %pad_add_fusion.place_ref, bf16[2,384,2048]{2,1,0:T(8,128)(2,1)S(1)} %weighted_values.1.weighted, bf16[2,1024,2048]{2,1,0:T(8,128)(2,1)S(1)} %copy-done), custom_call_target="tpu_custom_call" | custom-call | flops 402653184 | bytes 3014656 | tf_op jit(solution)/shard_map/partial_momentum/pallas_call | solution.py:115
  8.2 1.6 %collective-permute-start.12 = (f32[8,3,16,256]{3,2,1,0:T(8,128)S(1)}, f32[8,3,16,256]{3,2,1,0:T(8,128)S(1)}, u32[]{:S(2)}, u32[]{:S(2)}) collective-permute-start(f32[8,3,16,256]{3,2,1,0:T(8,128)S(1)} %partial_momentum.11), channel_id=1, source_target_pairs={{0,8},{1,9},{2,10},{3,11},{4,12},{5,13},{6,14},{7,15},{8,0},{9,1},... | collective-permute-start | bytes 1179656 | tf_op jit(solution)/shard_map/ppermute | solution.py:37
  9.8 1.2 %partial_momentum.8 = f32[8,3,16,256]{3,2,1,0:T(8,128)S(1)} custom-call(s32[2]{0:T(128)S(1)} %pad_add_fusion.place_ref, bf16[2,384,2048]{2,1,0:T(8,128)(2,1)S(1)} %weighted_values.1.weighted, bf16[2,1024,2048]{2,1,0:T(8,128)(2,1)S(1)} %copy-done), custom_call_target="tpu_custom_call" | custom-call | flops 402653184 | bytes 3014656 | tf_op jit(solution)/shard_map/partial_momentum/pallas_call | solution.py:115
  10.9 0.8 collective-permute-start.1
  11.7 1.1 %partial_momentum.10 = f32[8,3,16,256]{3,2,1,0:T(8,128)S(1)} custom-call(s32[2]{0:T(128)S(1)} %pad_add_fusion.place_ref, bf16[2,384,2048]{2,1,0:T(8,128)(2,1)S(1)} %weighted_values.1.weighted, bf16[2,1024,2048]{2,1,0:T(8,128)(2,1)S(1)} %copy-done), custom_call_target="tpu_custom_call" | custom-call | flops 402653184 | bytes 3014656 | tf_op jit(solution)/shard_map/partial_momentum/pallas_call | solution.py:115
  12.9 2.1 %collective-permute-start.11 = (f32[8,3,16,256]{3,2,1,0:T(8,128)S(1)}, f32[8,3,16,256]{3,2,1,0:T(8,128)S(1)}, u32[]{:S(2)}, u32[]{:S(2)}) collective-permute-start(f32[8,3,16,256]{3,2,1,0:T(8,128)S(1)} %partial_momentum.10), channel_id=1, source_target_pairs={{0,8},{1,9},{2,10},{3,11},{4,12},{5,13},{6,14},{7,15},{8,0},{9,1},... | collective-permute-start | bytes 1179656 | tf_op jit(solution)/shard_map/ppermute | solution.py:37
  15.0 1.6 %partial_momentum.9 = (f32[8,3,16,256]{3,2,1,0:T(8,128)S(1)}, f32[8,3,16,256]{3,2,1,0:T(8,128)S(1)}) custom-call(s32[2]{0:T(128)S(1)} %pad_add_fusion.place_ref, bf16[2,384,2048]{2,1,0:T(8,128)(2,1)S(1)} %weighted_values.1.weighted, bf16[2,1024,2048]{2,1,0:T(8,128)(2,1)S(1)} %copy-done), custom_call_target="tpu_custom_call" | custom-call | flops 805306368 | bytes 4456448 | tf_op jit(solution)/shard_map/partial_momentum/pallas_call | solution.py:115
  16.6 2.3 %collective-permute-start.13 = (f32[8,3,16,256]{3,2,1,0:T(8,128)S(1)}, f32[8,3,16,256]{3,2,1,0:T(8,128)S(1)}, u32[]{:S(2)}, u32[]{:S(2)}) collective-permute-start(f32[8,3,16,256]{3,2,1,0:T(8,128)S(1)} %add.101), channel_id=1, source_target_pairs={{0,24},{1,25},{2,26},{3,27},{4,28},{5,29},{6,30},{7,31},{8,16},{9,... | collective-permute-start | bytes 1179656 | tf_op jit(solution)/shard_map/ppermute | solution.py:37
  19.0 1.2 %partial_momentum.7 = f32[8,3,16,256]{3,2,1,0:T(8,128)S(1)} custom-call(s32[2]{0:T(128)S(1)} %pad_add_fusion.place_ref, bf16[2,384,2048]{2,1,0:T(8,128)(2,1)S(1)} %weighted_values.1.weighted, bf16[2,1024,2048]{2,1,0:T(8,128)(2,1)S(1)} %copy-done), custom_call_target="tpu_custom_call" | custom-call | flops 402653184 | bytes 3014656 | tf_op jit(solution)/shard_map/partial_momentum/pallas_call | solution.py:115
  20.7 1.6 %partial_momentum.6 = (f32[8,3,16,256]{3,2,1,0:T(8,128)S(1)}, f32[8,3,16,256]{3,2,1,0:T(8,128)S(1)}) custom-call(s32[2]{0:T(128)S(1)} %pad_add_fusion.place_ref, bf16[2,384,2048]{2,1,0:T(8,128)(2,1)S(1)} %weighted_values.1.weighted, bf16[2,1024,2048]{2,1,0:T(8,128)(2,1)S(1)} %copy-done), custom_call_target="tpu_custom_call" | custom-call | flops 805306368 | bytes 4456448 | tf_op jit(solution)/shard_map/partial_momentum/pallas_call | solution.py:115
  22.4 2.5 %collective-permute-start.2 = (f32[8,3,16,256]{3,2,1,0:T(8,128)S(1)}, f32[8,3,16,256]{3,2,1,0:T(8,128)S(1)}, u32[]{:S(2)}, u32[]{:S(2)}) collective-permute-start(f32[8,3,16,256]{3,2,1,0:T(8,128)S(1)} %add.88), channel_id=1, source_target_pairs={{0,3},{1,2},{2,1},{3,0},{4,7},{5,6},{6,5},{7,4},{8,11},{9,10},{10,... | collective-permute-start | bytes 1179656 | tf_op jit(solution)/shard_map/ppermute | solution.py:37
  24.9 1.7 %collective-permute-done.13 = f32[8,3,16,256]{3,2,1,0:T(8,128)S(1)} collective-permute-done((f32[8,3,16,256]{3,2,1,0:T(8,128)S(1)}, f32[8,3,16,256]{3,2,1,0:T(8,128)S(1)}, u32[]{:S(2)}, u32[]{:S(2)}) %collective-permute-start.13) | collective-permute-done | bytes 393248 | tf_op jit(solution)/shard_map/ppermute | solution.py:37
  26.7 2.0 %collective-permute-start.14 = (f32[2,3,16,256]{3,2,1,0:T(8,128)S(1)}, f32[2,3,16,256]{3,2,1,0:T(8,128)S(1)}, u32[]{:S(2)}, u32[]{:S(2)}) collective-permute-start(f32[2,3,16,256]{3,2,1,0:T(8,128)S(1)} %get-tuple-element.24), channel_id=1, source_target_pairs={{0,1},{1,0},{2,3},{3,2},{4,5},{5,4},{6,7},{7,6},{8,9},{9,8},{10,11... | collective-permute-start | bytes 294920 | tf_op jit(solution)/shard_map/ppermute | solution.py:37
  28.7 2.2 %collective-permute-start.16 = (f32[2,3,16,256]{3,2,1,0:T(8,128)S(1)}, f32[2,3,16,256]{3,2,1,0:T(8,128)S(1)}, u32[]{:S(2)}, u32[]{:S(2)}) collective-permute-start(f32[2,3,16,256]{3,2,1,0:T(8,128)S(1)} %get-tuple-element.22), channel_id=1, source_target_pairs={{0,2},{1,3},{2,0},{3,1},{4,6},{5,7},{6,4},{7,5},{8,10},{9,11},{10,... | collective-permute-start | bytes 294920 | tf_op jit(solution)/shard_map/ppermute | solution.py:37
  30.9 1.3 %collective-permute-done = f32[8,3,16,256]{3,2,1,0:T(8,128)S(1)} collective-permute-done((f32[8,3,16,256]{3,2,1,0:T(8,128)S(1)}, f32[8,3,16,256]{3,2,1,0:T(8,128)S(1)}, u32[]{:S(2)}, u32[]{:S(2)}) %collective-permute-start) | collective-permute-done | bytes 393248 | tf_op jit(solution)/shard_map/ppermute | solution.py:37
  32.4 1.7 %collective-permute-start.4 = (f32[2,3,16,256]{3,2,1,0:T(8,128)S(1)}, f32[2,3,16,256]{3,2,1,0:T(8,128)S(1)}, u32[]{:S(2)}, u32[]{:S(2)}) collective-permute-start(f32[2,3,16,256]{3,2,1,0:T(8,128)S(1)} %get-tuple-element.26), channel_id=1, source_target_pairs={{0,24},{1,25},{2,26},{3,27},{4,28},{5,29},{6,30},{7,31},{8,16},{9,... | collective-permute-start | bytes 294920 | tf_op jit(solution)/shard_map/ppermute | solution.py:37
  34.3 2.2 %collective-permute-start.5 = (f32[2,3,16,256]{3,2,1,0:T(8,128)S(1)}, f32[2,3,16,256]{3,2,1,0:T(8,128)S(1)}, u32[]{:S(2)}, u32[]{:S(2)}) collective-permute-start(f32[2,3,16,256]{3,2,1,0:T(8,128)S(1)} %get-tuple-element.25), channel_id=1, source_target_pairs={{0,16},{1,17},{2,18},{3,19},{4,20},{5,21},{6,22},{7,23},{8,24},{9,... | collective-permute-start | bytes 294920 | tf_op jit(solution)/shard_map/ppermute | solution.py:37
  36.6 2.0 %collective-permute-start.17 = (f32[2,3,16,256]{3,2,1,0:T(8,128)S(1)}, f32[2,3,16,256]{3,2,1,0:T(8,128)S(1)}, u32[]{:S(2)}, u32[]{:S(2)}) collective-permute-start(f32[2,3,16,256]{3,2,1,0:T(8,128)S(1)} %fusion.1), channel_id=1, source_target_pairs={{0,4},{1,5},{2,6},{3,7},{4,0},{5,1},{6,2},{7,3},{8,12},{9,13},{10,... | collective-permute-start | bytes 294920 | tf_op jit(solution)/shard_map/ppermute | solution.py:37
  38.6 2.8 %collective-permute-done.4 = f32[2,3,16,256]{3,2,1,0:T(8,128)S(1)} collective-permute-done((f32[2,3,16,256]{3,2,1,0:T(8,128)S(1)}, f32[2,3,16,256]{3,2,1,0:T(8,128)S(1)}, u32[]{:S(2)}, u32[]{:S(2)}) %collective-permute-start.4) | collective-permute-done | bytes 98336 | tf_op jit(solution)/shard_map/ppermute | solution.py:37
  41.4 2.2 %collective-permute-start.6 = (f32[2,3,16,256]{3,2,1,0:T(8,128)S(1)}, f32[2,3,16,256]{3,2,1,0:T(8,128)S(1)}, u32[]{:S(2)}, u32[]{:S(2)}) collective-permute-start(f32[2,3,16,256]{3,2,1,0:T(8,128)S(1)} %fusion.3), channel_id=1, source_target_pairs={{0,4},{1,5},{2,6},{3,7},{4,0},{5,1},{6,2},{7,3},{8,12},{9,13},{10,... | collective-permute-start | bytes 294920 | tf_op jit(solution)/shard_map/ppermute | solution.py:37
  43.6 1.3 %collective-permute-start.18 = (f32[2,3,16,256]{3,2,1,0:T(8,128)S(1)}, f32[2,3,16,256]{3,2,1,0:T(8,128)S(1)}, u32[]{:S(2)}, u32[]{:S(2)}) collective-permute-start(f32[2,3,16,256]{3,2,1,0:T(8,128)S(1)} %add_multiply_fusion), channel_id=1, source_target_pairs={{0,3},{1,2},{2,1},{3,0},{4,7},{5,6},{6,5},{7,4},{8,11},{9,10},{10,... | collective-permute-start | bytes 294920 | tf_op jit(solution)/shard_map/ppermute | solution.py:37
  45.0 2.4 %collective-permute-start.19 = (f32[2,3,16,256]{3,2,1,0:T(8,128)S(1)}, f32[2,3,16,256]{3,2,1,0:T(8,128)S(1)}, u32[]{:S(2)}, u32[]{:S(2)}) collective-permute-start(f32[2,3,16,256]{3,2,1,0:T(8,128)S(1)} %add_multiply_fusion), channel_id=1, source_target_pairs={{0,1},{1,0},{2,3},{3,2},{4,5},{5,4},{6,7},{7,6},{8,9},{9,8},{10,11... | collective-permute-start | bytes 294920 | tf_op jit(solution)/shard_map/ppermute | solution.py:37
  47.4 0.8 collective-permute-start.20
  48.1 1.1 collective-permute-start.7
  49.2 3.7 %collective-permute-start.9 = (f32[2,3,16,256]{3,2,1,0:T(8,128)S(1)}, f32[2,3,16,256]{3,2,1,0:T(8,128)S(1)}, u32[]{:S(2)}, u32[]{:S(2)}) collective-permute-start(f32[2,3,16,256]{3,2,1,0:T(8,128)S(1)} %add_multiply_fusion.1), channel_id=1, source_target_pairs={{0,16},{1,17},{2,18},{3,19},{4,20},{5,21},{6,22},{7,23},{8,24},{9,... | collective-permute-start | bytes 294920 | tf_op jit(solution)/shard_map/ppermute | solution.py:37
  53.8 2.0 %collective-permute-start.26 = (f32[8,3,16,256]{3,2,1,0:T(8,128)S(1)}, f32[8,3,16,256]{3,2,1,0:T(8,128)S(1)}, u32[]{:S(2)}, u32[]{:S(2)}) collective-permute-start(f32[8,3,16,256]{3,2,1,0:T(8,128)S(1)} %pad_maximum_fusion.1.refs_0_), channel_id=1, source_target_pairs={{0,24},{1,25},{2,26},{3,27},{4,28},{5,29},{6,30},{7,31},{8,16},{9,... | collective-permute-start | bytes 1179656 | tf_op jit(solution)/shard_map/ppermute | solution.py:37
  55.8 2.1 %collective-permute-done.9 = f32[2,3,16,256]{3,2,1,0:T(8,128)S(1)} collective-permute-done((f32[2,3,16,256]{3,2,1,0:T(8,128)S(1)}, f32[2,3,16,256]{3,2,1,0:T(8,128)S(1)}, u32[]{:S(2)}, u32[]{:S(2)}) %collective-permute-start.9) | collective-permute-done | bytes 98336 | tf_op jit(solution)/shard_map/ppermute | solution.py:37
  57.9 3.5 %collective-permute-start.10 = (f32[8,3,16,256]{3,2,1,0:T(8,128)S(1)}, f32[8,3,16,256]{3,2,1,0:T(8,128)S(1)}, u32[]{:S(2)}, u32[]{:S(2)}) collective-permute-start(f32[8,3,16,256]{3,2,1,0:T(8,128)S(1)} %pad_maximum_fusion.refs_0_), channel_id=1, source_target_pairs={{0,1},{1,0},{2,3},{3,2},{4,5},{5,4},{6,7},{7,6},{8,9},{9,8},{10,11... | collective-permute-start | bytes 1179656 | tf_op jit(solution)/shard_map/ppermute | solution.py:37
  62.2 1.5 %pair_sums.5.refs_1_ = f32[16,512]{1,0:T(8,128)S(1)} custom-call(s32[2]{0:T(128)S(1)} %pad_add_fusion.place_ref, f32[2]{0:T(128)S(1)} %convert_element_type.3.weight_ref, f32[4]{0:T(128)S(1)} %copy-done.8, f32[2,128]{1,0:T(2,128)S(1)} %copy-done.7, f32[2,1024]{1,0:T(2,128)S(1)} %copy-done.5, bf16[2,128,512]{2,1,0:T(8,128)(2,1)S(1)} %copy-done.3, ...), custom_call_target="tpu_custom_call" | custom-call | flops 402653184 | bytes 917504 | tf_op jit(solution)/shard_map/pair_sums/pallas_call | solution.py:230
  63.7 2.0 %collective-permute-start.25 = (f32[4,3,16,256]{3,2,1,0:T(8,128)S(1)}, f32[4,3,16,256]{3,2,1,0:T(8,128)S(1)}, u32[]{:S(2)}, u32[]{:S(2)}) collective-permute-start(f32[4,3,16,256]{3,2,1,0:T(8,128)S(1)} %slice.110), channel_id=1, source_target_pairs={{0,24},{1,25},{2,26},{3,27},{4,28},{5,29},{6,30},{7,31},{8,16},{9,... | collective-permute-start | bytes 589832 | tf_op jit(solution)/shard_map/ppermute | solution.py:37
  65.9 1.5 %pair_sums.6.refs_4_ = f32[16,512]{1,0:T(8,128)S(1)} custom-call(s32[2]{0:T(128)S(1)} %pad_add_fusion.place_ref, f32[2]{0:T(128)S(1)} %convert_element_type.3.weight_ref, f32[4]{0:T(128)S(1)} %copy-done.8, f32[2,128]{1,0:T(2,128)S(1)} %copy-done.7, f32[2,1024]{1,0:T(2,128)S(1)} %copy-done.5, bf16[2,128,512]{2,1,0:T(8,128)(2,1)S(1)} %copy-done.3, ...), custom_call_target="tpu_custom_call" | custom-call | flops 402653184 | bytes 917504 | tf_op jit(solution)/shard_map/pair_sums/pallas_call | solution.py:230
  67.5 1.2 %collective-permute-start.22 = (f32[4,3,16,256]{3,2,1,0:T(8,128)S(1)}, f32[4,3,16,256]{3,2,1,0:T(8,128)S(1)}, u32[]{:S(2)}, u32[]{:S(2)}) collective-permute-start(f32[4,3,16,256]{3,2,1,0:T(8,128)S(1)} %slice.108), channel_id=1, source_target_pairs={{0,3},{1,2},{2,1},{3,0},{4,7},{5,6},{6,5},{7,4},{8,11},{9,10},{10,... | collective-permute-start | bytes 589832 | tf_op jit(solution)/shard_map/ppermute | solution.py:37
  69.2 3.2 %collective-permute-start.24 = (f32[4,3,16,256]{3,2,1,0:T(8,128)S(1)}, f32[4,3,16,256]{3,2,1,0:T(8,128)S(1)}, u32[]{:S(2)}, u32[]{:S(2)}) collective-permute-start(f32[4,3,16,256]{3,2,1,0:T(8,128)S(1)} %slice.128), channel_id=1, source_target_pairs={{0,1},{1,0},{2,3},{3,2},{4,5},{5,4},{6,7},{7,6},{8,9},{9,8},{10,11... | collective-permute-start | bytes 589832 | tf_op jit(solution)/shard_map/ppermute | solution.py:37
  72.4 3.5 %pair_sums.7.refs_1_ = f32[16,512]{1,0:T(8,128)S(1)} custom-call(s32[2]{0:T(128)S(1)} %pad_add_fusion.place_ref, f32[2]{0:T(128)S(1)} %convert_element_type.3.weight_ref, f32[4]{0:T(128)S(1)} %copy-done.8, f32[2,128]{1,0:T(2,128)S(1)} %copy-done.7, f32[2,1024]{1,0:T(2,128)S(1)} %copy-done.5, bf16[2,128,512]{2,1,0:T(8,128)(2,1)S(1)} %copy-done.3, ...), custom_call_target="tpu_custom_call" | custom-call | flops 1610612736 | bytes 3670016 | tf_op jit(solution)/shard_map/pair_sums/pallas_call | solution.py:230
  76.0 1.5 %pair_sums.8.refs_1_ = f32[16,512]{1,0:T(8,128)S(1)} custom-call(s32[2]{0:T(128)S(1)} %pad_add_fusion.place_ref, f32[2]{0:T(128)S(1)} %convert_element_type.3.weight_ref, f32[4]{0:T(128)S(1)} %copy-done.8, f32[2,128]{1,0:T(2,128)S(1)} %copy-done.7, f32[2,1024]{1,0:T(2,128)S(1)} %copy-done.5, bf16[2,128,512]{2,1,0:T(8,128)(2,1)S(1)} %copy-done.3, ...), custom_call_target="tpu_custom_call" | custom-call | flops 402653184 | bytes 917504 | tf_op jit(solution)/shard_map/pair_sums/pallas_call | solution.py:230
  77.5 1.5 %pair_sums.9 = (f32[16,256]{1,0:T(8,128)S(1)}, f32[16,256]{1,0:T(8,128)S(1)}) custom-call(s32[2]{0:T(128)S(1)} %pad_add_fusion.place_ref, f32[2]{0:T(128)S(1)} %convert_element_type.3.weight_ref, f32[4]{0:T(128)S(1)} %copy-done.8, f32[2,128]{1,0:T(2,128)S(1)} %copy-done.7, f32[2,1024]{1,0:T(2,128)S(1)} %copy-done.5, bf16[2,128,512]{2,1,0:T(8,128)(2,1)S(1)} %copy-done.3, ...), custom_call_target="tpu_custom_call" | custom-call | flops 402653184 | bytes 917504 | tf_op jit(solution)/shard_map/pair_sums/pallas_call | solution.py:230
  79.1 1.2 %collective-permute-done.28 = f32[16,256]{1,0:T(8,128)S(1)} collective-permute-done((f32[16,256]{1,0:T(8,128)S(1)}, f32[16,256]{1,0:T(8,128)S(1)}, u32[]{:S(2)}, u32[]{:S(2)}) %collective-permute-start.28) | collective-permute-done | bytes 16416 | tf_op jit(solution)/shard_map/ppermute | solution.py:26
  80.4 18.3 %all_to_all.5.gathered = f32[32,16,256]{2,1,0:T(8,128)S(1)} all-to-all(f32[32,16,256]{2,1,0:T(8,128)S(1)} %broadcast_in_dim.2), channel_id=1, replica_groups=mesh['ka'=8,'wa'=32] {'wa'}, dimensions={0} | all-to-all | bytes 1048576 | tf_op jit(solution)/shard_map/all_to_all | solution.py:42
  98.7 1.3 %wing_sums.1 = f32[16,128]{1,0:T(8,128)S(1)} custom-call(s32[2]{0:T(128)S(1)} %pad_add_fusion.place_ref, f32[32,16,256]{2,1,0:T(8,128)S(1)} %all_to_all.5.gathered, bf16[128,16384]{1,0:T(8,128)(2,1)S(1)} %copy-done.2), custom_call_target="tpu_custom_call" | custom-call | flops 100663296 | bytes 4718592 | tf_op jit(solution)/shard_map/wing_sums/pallas_call | solution.py:289
  100.0 1.2 %collective-permute-done.29 = f32[16,128]{1,0:T(8,128)S(1)} collective-permute-done((f32[16,128]{1,0:T(8,128)S(1)}, f32[16,128]{1,0:T(8,128)S(1)}, u32[]{:S(2)}, u32[]{:S(2)}) %collective-permute-start.29) | collective-permute-done | bytes 8224 | tf_op jit(solution)/shard_map/ppermute | solution.py:26
  101.2 3.3 %collective-permute-start.30 = (f32[16,128]{1,0:T(8,128)S(1)}, f32[16,128]{1,0:T(8,128)S(1)}, u32[]{:S(2)}, u32[]{:S(2)}) collective-permute-start(f32[16,128]{1,0:T(8,128)S(1)} %add.114), channel_id=1, source_target_pairs={{0,64},{32,96},{64,0},{96,32},{128,192},{160,224},{192,128},{224,1... | collective-permute-start | bytes 24584 | tf_op jit(solution)/shard_map/ppermute | solution.py:26
  104.5 1.6 %collective-permute-done.30 = f32[16,128]{1,0:T(8,128)S(1)} collective-permute-done((f32[16,128]{1,0:T(8,128)S(1)}, f32[16,128]{1,0:T(8,128)S(1)}, u32[]{:S(2)}, u32[]{:S(2)}) %collective-permute-start.30) | collective-permute-done | bytes 8224 | tf_op jit(solution)/shard_map/ppermute | solution.py:26
  106.1 5.1 %collective-permute-start.31 = (f32[16,128]{1,0:T(8,128)S(1)}, f32[16,128]{1,0:T(8,128)S(1)}, u32[]{:S(2)}, u32[]{:S(2)}) collective-permute-start(f32[16,128]{1,0:T(8,128)S(1)} %add.115.one), channel_id=1, source_target_pairs={{0,192},{32,224},{64,128},{96,160},{128,64},{160,96},{192,0},{224,... | collective-permute-start | bytes 24584 | tf_op jit(solution)/shard_map/ppermute | solution.py:26
  111.2 1.6 %collective-permute-done.31.two = f32[16,128]{1,0:T(8,128)S(1)} collective-permute-done((f32[16,128]{1,0:T(8,128)S(1)}, f32[16,128]{1,0:T(8,128)S(1)}, u32[]{:S(2)}, u32[]{:S(2)}) %collective-permute-start.31) | collective-permute-done | bytes 8224 | tf_op jit(solution)/shard_map/ppermute | solution.py:26
  (73 shorter events, 4.7 us)
Async XLA Ops:
  0.7 1.2 %copy-start.4 = (bf16[2,128,2048]{2,1,0:T(8,128)(2,1)S(1)}, bf16[2,128,2048]{2,1,0:T(8,128)(2,1)}, u32[]{:S(2)}) copy-start(bf16[2,128,2048]{2,1,0:T(8,128)(2,1)} %val_ref.1) | copy-start | bytes 3145732
  1.9 0.8 copy-start.6
  3.7 3.4 %copy-start = (bf16[2,1024,2048]{2,1,0:T(8,128)(2,1)S(1)}, bf16[2,1024,2048]{2,1,0:T(8,128)(2,1)}, u32[]{:S(2)}) copy-start(bf16[2,1024,2048]{2,1,0:T(8,128)(2,1)} %cond_ref.11) | copy-start | bytes 25165828
  8.2 8.4 %collective-permute-start.12 = (f32[8,3,16,256]{3,2,1,0:T(8,128)S(1)}, f32[8,3,16,256]{3,2,1,0:T(8,128)S(1)}, u32[]{:S(2)}, u32[]{:S(2)}) collective-permute-start(f32[8,3,16,256]{3,2,1,0:T(8,128)S(1)} %partial_momentum.11), channel_id=1, source_target_pairs={{0,8},{1,9},{2,10},{3,11},{4,12},{5,13},{6,14},{7,15},{8,0},{9,1},... | collective-permute-start | bytes 1179656 | tf_op jit(solution)/shard_map/ppermute | solution.py:37
  10.9 11.4 %collective-permute-start.1 = (f32[8,3,16,256]{3,2,1,0:T(8,128)S(1)}, f32[8,3,16,256]{3,2,1,0:T(8,128)S(1)}, u32[]{:S(2)}, u32[]{:S(2)}) collective-permute-start(f32[8,3,16,256]{3,2,1,0:T(8,128)S(1)} %partial_momentum.8), channel_id=1, source_target_pairs={{0,1},{1,0},{2,3},{3,2},{4,5},{5,4},{6,7},{7,6},{8,9},{9,8},{10,11... | collective-permute-start | bytes 1179656 | tf_op jit(solution)/shard_map/ppermute | solution.py:37
  12.9 12.0 %collective-permute-start.11 = (f32[8,3,16,256]{3,2,1,0:T(8,128)S(1)}, f32[8,3,16,256]{3,2,1,0:T(8,128)S(1)}, u32[]{:S(2)}, u32[]{:S(2)}) collective-permute-start(f32[8,3,16,256]{3,2,1,0:T(8,128)S(1)} %partial_momentum.10), channel_id=1, source_target_pairs={{0,8},{1,9},{2,10},{3,11},{4,12},{5,13},{6,14},{7,15},{8,0},{9,1},... | collective-permute-start | bytes 1179656 | tf_op jit(solution)/shard_map/ppermute | solution.py:37
  16.6 10.0 %collective-permute-start.13 = (f32[8,3,16,256]{3,2,1,0:T(8,128)S(1)}, f32[8,3,16,256]{3,2,1,0:T(8,128)S(1)}, u32[]{:S(2)}, u32[]{:S(2)}) collective-permute-start(f32[8,3,16,256]{3,2,1,0:T(8,128)S(1)} %add.101), channel_id=1, source_target_pairs={{0,24},{1,25},{2,26},{3,27},{4,28},{5,29},{6,30},{7,31},{8,16},{9,... | collective-permute-start | bytes 1179656 | tf_op jit(solution)/shard_map/ppermute | solution.py:37
  20.1 12.1 %collective-permute-start = (f32[8,3,16,256]{3,2,1,0:T(8,128)S(1)}, f32[8,3,16,256]{3,2,1,0:T(8,128)S(1)}, u32[]{:S(2)}, u32[]{:S(2)}) collective-permute-start(f32[8,3,16,256]{3,2,1,0:T(8,128)S(1)} %partial_momentum.7), channel_id=1, source_target_pairs={{0,1},{1,0},{2,3},{3,2},{4,5},{5,4},{6,7},{7,6},{8,9},{9,8},{10,11... | collective-permute-start | bytes 1179656 | tf_op jit(solution)/shard_map/ppermute | solution.py:37
  22.2 39.9 %copy-start.9 = (s32[2]{0:T(128)S(1)}, s32[2]{0:T(128)}, u32[]{:S(2)}) copy-start(s32[2]{0:T(128)} %param.19) | copy-start | bytes 28
  22.3 39.9 %copy-start.1 = (bf16[2,1024,512]{2,1,0:T(8,128)(2,1)S(1)}, bf16[2,1024,512]{2,1,0:T(8,128)(2,1)}, u32[]{:S(2)}) copy-start(bf16[2,1024,512]{2,1,0:T(8,128)(2,1)} %orbit_cond.9) | copy-start | bytes 6291460
  22.3 39.9 %copy-start.3 = (bf16[2,128,512]{2,1,0:T(8,128)(2,1)S(1)}, bf16[2,128,512]{2,1,0:T(8,128)(2,1)}, u32[]{:S(2)}) copy-start(bf16[2,128,512]{2,1,0:T(8,128)(2,1)} %orbit_val.9) | copy-start | bytes 786436
  22.3 39.9 %copy-start.5 = (f32[2,1024]{1,0:T(2,128)S(1)}, f32[2,1024]{1,0:T(2,128)}, u32[]{:S(2)}) copy-start(f32[2,1024]{1,0:T(2,128)} %energy_cond.9) | copy-start | bytes 24580
  22.3 39.9 %copy-start.7 = (f32[2,128]{1,0:T(2,128)S(1)}, f32[2,128]{1,0:T(2,128)}, u32[]{:S(2)}) copy-start(f32[2,128]{1,0:T(2,128)} %energy_val.9) | copy-start | bytes 3076
  22.3 39.9 %copy-start.8 = (f32[4]{0:T(128)S(1)}, f32[4]{0:T(128)}, u32[]{:S(2)}) copy-start(f32[4]{0:T(128)} %freq_ref.9) | copy-start | bytes 52
  22.4 9.8 %collective-permute-start.2 = (f32[8,3,16,256]{3,2,1,0:T(8,128)S(1)}, f32[8,3,16,256]{3,2,1,0:T(8,128)S(1)}, u32[]{:S(2)}, u32[]{:S(2)}) collective-permute-start(f32[8,3,16,256]{3,2,1,0:T(8,128)S(1)} %add.88), channel_id=1, source_target_pairs={{0,3},{1,2},{2,1},{3,0},{4,7},{5,6},{6,5},{7,4},{8,11},{9,10},{10,... | collective-permute-start | bytes 1179656 | tf_op jit(solution)/shard_map/ppermute | solution.py:37
  26.7 7.6 %collective-permute-start.14 = (f32[2,3,16,256]{3,2,1,0:T(8,128)S(1)}, f32[2,3,16,256]{3,2,1,0:T(8,128)S(1)}, u32[]{:S(2)}, u32[]{:S(2)}) collective-permute-start(f32[2,3,16,256]{3,2,1,0:T(8,128)S(1)} %get-tuple-element.24), channel_id=1, source_target_pairs={{0,1},{1,0},{2,3},{3,2},{4,5},{5,4},{6,7},{7,6},{8,9},{9,8},{10,11... | collective-permute-start | bytes 294920 | tf_op jit(solution)/shard_map/ppermute | solution.py:37
  28.7 7.8 %collective-permute-start.15 = (f32[2,3,16,256]{3,2,1,0:T(8,128)S(1)}, f32[2,3,16,256]{3,2,1,0:T(8,128)S(1)}, u32[]{:S(2)}, u32[]{:S(2)}) collective-permute-start(f32[2,3,16,256]{3,2,1,0:T(8,128)S(1)} %get-tuple-element.23), channel_id=1, source_target_pairs={{0,3},{1,2},{2,1},{3,0},{4,7},{5,6},{6,5},{7,4},{8,11},{9,10},{10,... | collective-permute-start | bytes 294920 | tf_op jit(solution)/shard_map/ppermute | solution.py:37
  28.7 7.9 %collective-permute-start.16 = (f32[2,3,16,256]{3,2,1,0:T(8,128)S(1)}, f32[2,3,16,256]{3,2,1,0:T(8,128)S(1)}, u32[]{:S(2)}, u32[]{:S(2)}) collective-permute-start(f32[2,3,16,256]{3,2,1,0:T(8,128)S(1)} %get-tuple-element.22), channel_id=1, source_target_pairs={{0,2},{1,3},{2,0},{3,1},{4,6},{5,7},{6,4},{7,5},{8,10},{9,11},{10,... | collective-permute-start | bytes 294920 | tf_op jit(solution)/shard_map/ppermute | solution.py:37
  32.3 6.3 %collective-permute-start.3 = (f32[2,3,16,256]{3,2,1,0:T(8,128)S(1)}, f32[2,3,16,256]{3,2,1,0:T(8,128)S(1)}, u32[]{:S(2)}, u32[]{:S(2)}) collective-permute-start(f32[2,3,16,256]{3,2,1,0:T(8,128)S(1)} %get-tuple-element.27), channel_id=1, source_target_pairs={{0,8},{1,9},{2,10},{3,11},{4,12},{5,13},{6,14},{7,15},{8,0},{9,1},... | collective-permute-start | bytes 294920 | tf_op jit(solution)/shard_map/ppermute | solution.py:37
  32.4 9.0 %collective-permute-start.4 = (f32[2,3,16,256]{3,2,1,0:T(8,128)S(1)}, f32[2,3,16,256]{3,2,1,0:T(8,128)S(1)}, u32[]{:S(2)}, u32[]{:S(2)}) collective-permute-start(f32[2,3,16,256]{3,2,1,0:T(8,128)S(1)} %get-tuple-element.26), channel_id=1, source_target_pairs={{0,24},{1,25},{2,26},{3,27},{4,28},{5,29},{6,30},{7,31},{8,16},{9,... | collective-permute-start | bytes 294920 | tf_op jit(solution)/shard_map/ppermute | solution.py:37
  34.3 7.1 %collective-permute-start.5 = (f32[2,3,16,256]{3,2,1,0:T(8,128)S(1)}, f32[2,3,16,256]{3,2,1,0:T(8,128)S(1)}, u32[]{:S(2)}, u32[]{:S(2)}) collective-permute-start(f32[2,3,16,256]{3,2,1,0:T(8,128)S(1)} %get-tuple-element.25), channel_id=1, source_target_pairs={{0,16},{1,17},{2,18},{3,19},{4,20},{5,21},{6,22},{7,23},{8,24},{9,... | collective-permute-start | bytes 294920 | tf_op jit(solution)/shard_map/ppermute | solution.py:37
  36.6 7.0 %collective-permute-start.17 = (f32[2,3,16,256]{3,2,1,0:T(8,128)S(1)}, f32[2,3,16,256]{3,2,1,0:T(8,128)S(1)}, u32[]{:S(2)}, u32[]{:S(2)}) collective-permute-start(f32[2,3,16,256]{3,2,1,0:T(8,128)S(1)} %fusion.1), channel_id=1, source_target_pairs={{0,4},{1,5},{2,6},{3,7},{4,0},{5,1},{6,2},{7,3},{8,12},{9,13},{10,... | collective-permute-start | bytes 294920 | tf_op jit(solution)/shard_map/ppermute | solution.py:37
  41.4 6.7 %collective-permute-start.6 = (f32[2,3,16,256]{3,2,1,0:T(8,128)S(1)}, f32[2,3,16,256]{3,2,1,0:T(8,128)S(1)}, u32[]{:S(2)}, u32[]{:S(2)}) collective-permute-start(f32[2,3,16,256]{3,2,1,0:T(8,128)S(1)} %fusion.3), channel_id=1, source_target_pairs={{0,4},{1,5},{2,6},{3,7},{4,0},{5,1},{6,2},{7,3},{8,12},{9,13},{10,... | collective-permute-start | bytes 294920 | tf_op jit(solution)/shard_map/ppermute | solution.py:37
  43.6 5.6 %collective-permute-start.18 = (f32[2,3,16,256]{3,2,1,0:T(8,128)S(1)}, f32[2,3,16,256]{3,2,1,0:T(8,128)S(1)}, u32[]{:S(2)}, u32[]{:S(2)}) collective-permute-start(f32[2,3,16,256]{3,2,1,0:T(8,128)S(1)} %add_multiply_fusion), channel_id=1, source_target_pairs={{0,3},{1,2},{2,1},{3,0},{4,7},{5,6},{6,5},{7,4},{8,11},{9,10},{10,... | collective-permute-start | bytes 294920 | tf_op jit(solution)/shard_map/ppermute | solution.py:37
  45.0 8.0 %collective-permute-start.19 = (f32[2,3,16,256]{3,2,1,0:T(8,128)S(1)}, f32[2,3,16,256]{3,2,1,0:T(8,128)S(1)}, u32[]{:S(2)}, u32[]{:S(2)}) collective-permute-start(f32[2,3,16,256]{3,2,1,0:T(8,128)S(1)} %add_multiply_fusion), channel_id=1, source_target_pairs={{0,1},{1,0},{2,3},{3,2},{4,5},{5,4},{6,7},{7,6},{8,9},{9,8},{10,11... | collective-permute-start | bytes 294920 | tf_op jit(solution)/shard_map/ppermute | solution.py:37
  47.4 6.1 %collective-permute-start.20 = (f32[2,3,16,256]{3,2,1,0:T(8,128)S(1)}, f32[2,3,16,256]{3,2,1,0:T(8,128)S(1)}, u32[]{:S(2)}, u32[]{:S(2)}) collective-permute-start(f32[2,3,16,256]{3,2,1,0:T(8,128)S(1)} %add_multiply_fusion), channel_id=1, source_target_pairs={{0,2},{1,3},{2,0},{3,1},{4,6},{5,7},{6,4},{7,5},{8,10},{9,11},{10,... | collective-permute-start | bytes 294920 | tf_op jit(solution)/shard_map/ppermute | solution.py:37
  48.1 7.7 %collective-permute-start.7 = (f32[2,3,16,256]{3,2,1,0:T(8,128)S(1)}, f32[2,3,16,256]{3,2,1,0:T(8,128)S(1)}, u32[]{:S(2)}, u32[]{:S(2)}) collective-permute-start(f32[2,3,16,256]{3,2,1,0:T(8,128)S(1)} %add_multiply_fusion.1), channel_id=1, source_target_pairs={{0,24},{1,25},{2,26},{3,27},{4,28},{5,29},{6,30},{7,31},{8,16},{9,... | collective-permute-start | bytes 294920 | tf_op jit(solution)/shard_map/ppermute | solution.py:37
  49.2 6.6 %collective-permute-start.8 = (f32[2,3,16,256]{3,2,1,0:T(8,128)S(1)}, f32[2,3,16,256]{3,2,1,0:T(8,128)S(1)}, u32[]{:S(2)}, u32[]{:S(2)}) collective-permute-start(f32[2,3,16,256]{3,2,1,0:T(8,128)S(1)} %add_multiply_fusion.1), channel_id=1, source_target_pairs={{0,8},{1,9},{2,10},{3,11},{4,12},{5,13},{6,14},{7,15},{8,0},{9,1},... | collective-permute-start | bytes 294920 | tf_op jit(solution)/shard_map/ppermute | solution.py:37
  49.2 8.6 %collective-permute-start.9 = (f32[2,3,16,256]{3,2,1,0:T(8,128)S(1)}, f32[2,3,16,256]{3,2,1,0:T(8,128)S(1)}, u32[]{:S(2)}, u32[]{:S(2)}) collective-permute-start(f32[2,3,16,256]{3,2,1,0:T(8,128)S(1)} %add_multiply_fusion.1), channel_id=1, source_target_pairs={{0,16},{1,17},{2,18},{3,19},{4,20},{5,21},{6,22},{7,23},{8,24},{9,... | collective-permute-start | bytes 294920 | tf_op jit(solution)/shard_map/ppermute | solution.py:37
  53.5 10.2 %collective-permute-start.21 = (f32[8,3,16,256]{3,2,1,0:T(8,128)S(1)}, f32[8,3,16,256]{3,2,1,0:T(8,128)S(1)}, u32[]{:S(2)}, u32[]{:S(2)}) collective-permute-start(f32[8,3,16,256]{3,2,1,0:T(8,128)S(1)} %pad_maximum_fusion.1.refs_0_), channel_id=1, source_target_pairs={{0,8},{1,9},{2,10},{3,11},{4,12},{5,13},{6,14},{7,15},{8,0},{9,1},... | collective-permute-start | bytes 1179656 | tf_op jit(solution)/shard_map/ppermute | solution.py:37
  53.8 11.9 %collective-permute-start.26 = (f32[8,3,16,256]{3,2,1,0:T(8,128)S(1)}, f32[8,3,16,256]{3,2,1,0:T(8,128)S(1)}, u32[]{:S(2)}, u32[]{:S(2)}) collective-permute-start(f32[8,3,16,256]{3,2,1,0:T(8,128)S(1)} %pad_maximum_fusion.1.refs_0_), channel_id=1, source_target_pairs={{0,24},{1,25},{2,26},{3,27},{4,28},{5,29},{6,30},{7,31},{8,16},{9,... | collective-permute-start | bytes 1179656 | tf_op jit(solution)/shard_map/ppermute | solution.py:37
  57.9 9.6 %collective-permute-start.10 = (f32[8,3,16,256]{3,2,1,0:T(8,128)S(1)}, f32[8,3,16,256]{3,2,1,0:T(8,128)S(1)}, u32[]{:S(2)}, u32[]{:S(2)}) collective-permute-start(f32[8,3,16,256]{3,2,1,0:T(8,128)S(1)} %pad_maximum_fusion.refs_0_), channel_id=1, source_target_pairs={{0,1},{1,0},{2,3},{3,2},{4,5},{5,4},{6,7},{7,6},{8,9},{9,8},{10,11... | collective-permute-start | bytes 1179656 | tf_op jit(solution)/shard_map/ppermute | solution.py:37
  61.4 7.8 %collective-permute-start.23 = (f32[8,3,16,256]{3,2,1,0:T(8,128)S(1)}, f32[8,3,16,256]{3,2,1,0:T(8,128)S(1)}, u32[]{:S(2)}, u32[]{:S(2)}) collective-permute-start(f32[8,3,16,256]{3,2,1,0:T(8,128)S(1)} %pad_maximum_fusion.refs_0_), channel_id=1, source_target_pairs={{0,3},{1,2},{2,1},{3,0},{4,7},{5,6},{6,5},{7,4},{8,11},{9,10},{10,... | collective-permute-start | bytes 1179656 | tf_op jit(solution)/shard_map/ppermute | solution.py:37
  63.7 12.2 %collective-permute-start.25 = (f32[4,3,16,256]{3,2,1,0:T(8,128)S(1)}, f32[4,3,16,256]{3,2,1,0:T(8,128)S(1)}, u32[]{:S(2)}, u32[]{:S(2)}) collective-permute-start(f32[4,3,16,256]{3,2,1,0:T(8,128)S(1)} %slice.110), channel_id=1, source_target_pairs={{0,24},{1,25},{2,26},{3,27},{4,28},{5,29},{6,30},{7,31},{8,16},{9,... | collective-permute-start | bytes 589832 | tf_op jit(solution)/shard_map/ppermute | solution.py:37
  65.7 10.2 %collective-permute-start.27 = (f32[4,3,16,256]{3,2,1,0:T(8,128)S(1)}, f32[4,3,16,256]{3,2,1,0:T(8,128)S(1)}, u32[]{:S(2)}, u32[]{:S(2)}) collective-permute-start(f32[4,3,16,256]{3,2,1,0:T(8,128)S(1)} %slice.129), channel_id=1, source_target_pairs={{0,8},{1,9},{2,10},{3,11},{4,12},{5,13},{6,14},{7,15},{8,0},{9,1},... | collective-permute-start | bytes 589832 | tf_op jit(solution)/shard_map/ppermute | solution.py:37
  67.5 10.0 %collective-permute-start.22 = (f32[4,3,16,256]{3,2,1,0:T(8,128)S(1)}, f32[4,3,16,256]{3,2,1,0:T(8,128)S(1)}, u32[]{:S(2)}, u32[]{:S(2)}) collective-permute-start(f32[4,3,16,256]{3,2,1,0:T(8,128)S(1)} %slice.108), channel_id=1, source_target_pairs={{0,3},{1,2},{2,1},{3,0},{4,7},{5,6},{6,5},{7,4},{8,11},{9,10},{10,... | collective-permute-start | bytes 589832 | tf_op jit(solution)/shard_map/ppermute | solution.py:37
  69.2 8.3 %collective-permute-start.24 = (f32[4,3,16,256]{3,2,1,0:T(8,128)S(1)}, f32[4,3,16,256]{3,2,1,0:T(8,128)S(1)}, u32[]{:S(2)}, u32[]{:S(2)}) collective-permute-start(f32[4,3,16,256]{3,2,1,0:T(8,128)S(1)} %slice.128), channel_id=1, source_target_pairs={{0,1},{1,0},{2,3},{3,2},{4,5},{5,4},{6,7},{7,6},{8,9},{9,8},{10,11... | collective-permute-start | bytes 589832 | tf_op jit(solution)/shard_map/ppermute | solution.py:37
  76.0 22.7 %copy-start.2 = (bf16[128,16384]{1,0:T(8,128)(2,1)S(1)}, bf16[128,16384]{1,0:T(8,128)(2,1)}, u32[]{:S(2)}) copy-start(bf16[128,16384]{1,0:T(8,128)(2,1)} %zeta.1) | copy-start | bytes 12582916
  79.0 1.3 %collective-permute-start.28 = (f32[16,256]{1,0:T(8,128)S(1)}, f32[16,256]{1,0:T(8,128)S(1)}, u32[]{:S(2)}, u32[]{:S(2)}) collective-permute-start(f32[16,256]{1,0:T(8,128)S(1)} %get-tuple-element.21), channel_id=1, source_target_pairs={{0,32},{32,0},{64,96},{96,64},{128,160},{160,128},{192,224},{224,1... | collective-permute-start | bytes 49160 | tf_op jit(solution)/shard_map/ppermute | solution.py:26
  100.0 1.2 %collective-permute-start.29 = (f32[16,128]{1,0:T(8,128)S(1)}, f32[16,128]{1,0:T(8,128)S(1)}, u32[]{:S(2)}, u32[]{:S(2)}) collective-permute-start(f32[16,128]{1,0:T(8,128)S(1)} %wing_sums.1), channel_id=1, source_target_pairs={{0,32},{32,0},{64,96},{96,64},{128,160},{160,128},{192,224},{224,1... | collective-permute-start | bytes 24584 | tf_op jit(solution)/shard_map/ppermute | solution.py:26
  101.2 4.9 %collective-permute-start.30 = (f32[16,128]{1,0:T(8,128)S(1)}, f32[16,128]{1,0:T(8,128)S(1)}, u32[]{:S(2)}, u32[]{:S(2)}) collective-permute-start(f32[16,128]{1,0:T(8,128)S(1)} %add.114), channel_id=1, source_target_pairs={{0,64},{32,96},{64,0},{96,32},{128,192},{160,224},{192,128},{224,1... | collective-permute-start | bytes 24584 | tf_op jit(solution)/shard_map/ppermute | solution.py:26
  106.1 6.7 %collective-permute-start.31 = (f32[16,128]{1,0:T(8,128)S(1)}, f32[16,128]{1,0:T(8,128)S(1)}, u32[]{:S(2)}, u32[]{:S(2)}) collective-permute-start(f32[16,128]{1,0:T(8,128)S(1)} %add.115.one), channel_id=1, source_target_pairs={{0,192},{32,224},{64,128},{96,160},{128,64},{160,96},{192,0},{224,... | collective-permute-start | bytes 24584 | tf_op jit(solution)/shard_map/ppermute | solution.py:26

commit v8 on v6

--- a/solution.py
+++ b/solution.py
@@ -7,7 +7,7 @@
 from jax.experimental.pallas import tpu as pltpu
 from jax.sharding import PartitionSpec as P
 
-MASKS = (((8, 24, 1, 3, 4), (24, 8, 1, 3, 4)), ((1, 3, 8, 24, 4), (3, 1, 8, 24, 4)))
+MASKS = (((8, 24, 1, 3, 4), (24, 8, 3, 1, 4)), ((1, 3, 8, 24, 4), (3, 1, 24, 8, 4)))
 CB, VB = 4, 8
 F32, BF16 = jnp.float32, jnp.bfloat16
 VMEM, SMEM = pl.BlockSpec(memory_space=pltpu.VMEM), pl.BlockSpec(memory_space=pltpu.SMEM)
@@ -16,10 +16,13 @@
     index, core = place[0], place[1]
     x, z, y = index >> 3, (index >> 2) & 1, index & 3
 
+
+    def pairs(along):
+        one, two = (along ^ (along >> 1)) & 1, along >> 1
+        return (one << 1 | two) + ((two << 1 | one) - (one << 1 | two)) * core
+
     first, second = (x, y) if kpoint == 0 else (y, x)
-    one, two = (first ^ (first >> 1)) & 1, first >> 1
-    quarter = (one << 1 | two) + ((two << 1 | one) - (one << 1 | two)) * core
-    return quarter, ((second ^ (second >> 1)) & 1) << 2 | (second >> 1) << 1 | z
+    return pairs(first), pairs(second) << 1 | z
 
 
 def swap(value, axis, mask):
@@ -47,16 +50,14 @@
     second = second + cross(both, kpoint, 0)
     one, two = cross(first, kpoint, 0), cross(second, kpoint, 1)
 
-    def summed(place):
-        lines = slice(2 * place, 2 * place + 2)
-        return (own[lines] + one[lines]) + two[lines]
-
-    held = (summed(0) + cross(summed(2), kpoint, 2)) + (
-        cross(summed(1), kpoint, 3) + cross(summed(3), kpoint, 2, 3)
-    )
+    half = VB // 2
+    held = (own[:half] + one[:half]) + two[:half]
+    held = held + cross((own[half:] + one[half:]) + two[half:], kpoint, 2)
+    half = half // 2
+    held = held[:half] + cross(held[half:], kpoint, 3)
     held = (held + cross(held, kpoint, 4)[::-1]) * factor
-    others = [cross(held, kpoint, *dims) for dims in ((3,), (2,), (2, 3))]
-    held = jnp.concatenate([held] + others)
+    for dim in (3, 2):
+        held = jnp.concatenate([held, cross(held, kpoint, dim)])
     first, second = cross(held, kpoint, 0), cross(held, kpoint, 1)
     return held, second, first
 

time: 112 us -> 119 us (1.062)
  waiting for transfers between devices: 19.4 us -> 34.8 us
  starting transfers between devices: 48 us -> 39.4 us
    ppermute x26 -> x22, waiting for transfers between devices: 13.8 us -> 29.2 us  [cross(): return lax.ppermute(value, ('ka', 'wa'), pairs)]
    ppermute x26 -> x22, starting transfers between devices: 39.2 us -> 31 us  [cross(): return lax.ppermute(value, ('ka', 'wa'), pairs)]
  transfers between devices with their start and end apart: 30 -> 26, of which waited for: 16 -> 20; matrix products, arithmetic and copies ran while one was open for 0% -> 0% of each run, Pallas kernels for 11% -> 11%
where the time goes in v8:
time: 119 us
  starting transfers between devices  39.4 us (33%)
  waiting for transfers between devices  34.8 us (29%)
  blocking collectives  20.4 us (17%)
  Pallas kernels  17.7 us (15%)
  local copies, waits for them, and re-layouts  5.48 us (5%)
    ppermute x22, starting transfers between devices, cross(): return lax.ppermute(value, ('ka', 'wa'), pairs)  31 us
    ppermute x22, waiting for transfers between devices, cross(): return lax.ppermute(value, ('ka', 'wa'), pairs)  29.2 us
    all_to_all x1, blocking collectives, everyone(): lax.all_to_all(jnp.broadcast_to(value[None], (parts,) + value.shape), axi...  20.4 us
    pallas_call x5, Pallas kernels, pair_sums(): pl.pallas_call(functools.partial(pair_kernel, groups), out_shape=[jax.Sha...  9.51 us
    ppermute x4, starting transfers between devices, swap(): lax.ppermute(value, axis, [(i, i ^ mask) for i in range(lax.axis_size(axi...  8.42 us
    pallas_call x4, Pallas kernels, partial_momentum(): pl.pallas_call(functools.partial(momentum_kernel, kpoint, quarters), out_...  6.24 us
    ppermute x4, waiting for transfers between devices, swap(): lax.ppermute(value, axis, [(i, i ^ mask) for i in range(lax.axis_size(axi...  5.61 us
    unnamed x20, local copies, waits for them, and re-layouts  5.41 us
  transfers between devices with their start and end apart: 26, of which 20 were waited for; matrix products, arithmetic and copies ran while one was open for 0% of the time, Pallas kernels for 11%

profile of v8, /device:TPU:8, one launch (start us, length us, event | category | flops | bytes accessed | tf_op | source)
XLA Modules:
  0.0 119.2 jit_solution(79046892928299989)
XLA Ops:
  0.7 3.4 %copy-done = bf16[2,1024,2048]{2,1,0:T(8,128)(2,1)S(1)} copy-done((bf16[2,1024,2048]{2,1,0:T(8,128)(2,1)S(1)}, bf16[2,1024,2048]{2,1,0:T(8,128)(2,1)}, u32[]{:S(2)}) %copy-start) | copy-done | bytes 8388632
  4.1 1.2 %copy-done.2 = bf16[2,128,2048]{2,1,0:T(8,128)(2,1)S(1)} copy-done((bf16[2,128,2048]{2,1,0:T(8,128)(2,1)S(1)}, bf16[2,128,2048]{2,1,0:T(8,128)(2,1)}, u32[]{:S(2)}) %copy-start.2) | copy-done | bytes 1048600
  5.3 0.8 copy-done.5
  6.1 1.6 %partial_momentum.7 = (f32[8,3,16,256]{3,2,1,0:T(8,128)S(1)}, f32[8,3,16,256]{3,2,1,0:T(8,128)S(1)}) custom-call(s32[2]{0:T(128)S(1)} %pad_add_fusion.place_ref, bf16[2,128,2048]{2,1,0:T(8,128)(2,1)S(1)} %copy-done.2, s32[3,2048]{1,0:T(4,128)S(1)} %copy-done.5, bf16[2,1024,2048]{2,1,0:T(8,128)(2,1)S(1)} %copy-done), custom_call_target="tpu_custom_call" | custom-call | flops 805306368 | bytes 3407872 | tf_op jit(solution)/shard_map/partial_momentum/pallas_call | solution.py:96
  7.6 1.6 %collective-permute-start.10 = (f32[8,3,16,256]{3,2,1,0:T(8,128)S(1)}, f32[8,3,16,256]{3,2,1,0:T(8,128)S(1)}, u32[]{:S(2)}, u32[]{:S(2)}) collective-permute-start(f32[8,3,16,256]{3,2,1,0:T(8,128)S(1)} %get-tuple-element.23), channel_id=1, source_target_pairs={{0,8},{1,9},{2,10},{3,11},{4,12},{5,13},{6,14},{7,15},{8,0},{9,1},... | collective-permute-start | bytes 1179656 | tf_op jit(solution)/shard_map/ppermute | solution.py:40
  9.2 1.6 %partial_momentum.5 = (f32[8,3,16,256]{3,2,1,0:T(8,128)S(1)}, f32[8,3,16,256]{3,2,1,0:T(8,128)S(1)}) custom-call(s32[2]{0:T(128)S(1)} %pad_add_fusion.place_ref, bf16[2,128,2048]{2,1,0:T(8,128)(2,1)S(1)} %copy-done.2, s32[3,2048]{1,0:T(4,128)S(1)} %copy-done.5, bf16[2,1024,2048]{2,1,0:T(8,128)(2,1)S(1)} %copy-done), custom_call_target="tpu_custom_call" | custom-call | flops 805306368 | bytes 3407872 | tf_op jit(solution)/shard_map/partial_momentum/pallas_call | solution.py:96
  10.8 0.8 collective-permute-start.1
  11.6 2.0 %collective-permute-start.9 = (f32[8,3,16,256]{3,2,1,0:T(8,128)S(1)}, f32[8,3,16,256]{3,2,1,0:T(8,128)S(1)}, u32[]{:S(2)}, u32[]{:S(2)}) collective-permute-start(f32[8,3,16,256]{3,2,1,0:T(8,128)S(1)} %get-tuple-element.21), channel_id=1, source_target_pairs={{0,8},{1,9},{2,10},{3,11},{4,12},{5,13},{6,14},{7,15},{8,0},{9,1},... | collective-permute-start | bytes 1179656 | tf_op jit(solution)/shard_map/ppermute | solution.py:40
  13.6 1.6 %partial_momentum.6 = (f32[8,3,16,256]{3,2,1,0:T(8,128)S(1)}, f32[8,3,16,256]{3,2,1,0:T(8,128)S(1)}) custom-call(s32[2]{0:T(128)S(1)} %pad_add_fusion.place_ref, bf16[2,128,2048]{2,1,0:T(8,128)(2,1)S(1)} %copy-done.2, s32[3,2048]{1,0:T(4,128)S(1)} %copy-done.5, bf16[2,1024,2048]{2,1,0:T(8,128)(2,1)S(1)} %copy-done), custom_call_target="tpu_custom_call" | custom-call | flops 805306368 | bytes 3407872 | tf_op jit(solution)/shard_map/partial_momentum/pallas_call | solution.py:96
  15.6 2.8 %collective-permute-start.11 = (f32[8,3,16,256]{3,2,1,0:T(8,128)S(1)}, f32[8,3,16,256]{3,2,1,0:T(8,128)S(1)}, u32[]{:S(2)}, u32[]{:S(2)}) collective-permute-start(f32[8,3,16,256]{3,2,1,0:T(8,128)S(1)} %add.66), channel_id=1, source_target_pairs={{0,24},{1,25},{2,26},{3,27},{4,28},{5,29},{6,30},{7,31},{8,16},{9,... | collective-permute-start | bytes 1179656 | tf_op jit(solution)/shard_map/ppermute | solution.py:40
  18.9 1.6 %partial_momentum.4 = (f32[8,3,16,256]{3,2,1,0:T(8,128)S(1)}, f32[8,3,16,256]{3,2,1,0:T(8,128)S(1)}) custom-call(s32[2]{0:T(128)S(1)} %pad_add_fusion.place_ref, bf16[2,128,2048]{2,1,0:T(8,128)(2,1)S(1)} %copy-done.2, s32[3,2048]{1,0:T(4,128)S(1)} %copy-done.5, bf16[2,1024,2048]{2,1,0:T(8,128)(2,1)S(1)} %copy-done), custom_call_target="tpu_custom_call" | custom-call | flops 805306368 | bytes 3407872 | tf_op jit(solution)/shard_map/partial_momentum/pallas_call | solution.py:96
  20.6 2.5 %collective-permute-start.2 = (f32[8,3,16,256]{3,2,1,0:T(8,128)S(1)}, f32[8,3,16,256]{3,2,1,0:T(8,128)S(1)}, u32[]{:S(2)}, u32[]{:S(2)}) collective-permute-start(f32[8,3,16,256]{3,2,1,0:T(8,128)S(1)} %add.58), channel_id=1, source_target_pairs={{0,3},{1,2},{2,1},{3,0},{4,7},{5,6},{6,5},{7,4},{8,11},{9,10},{10,... | collective-permute-start | bytes 1179656 | tf_op jit(solution)/shard_map/ppermute | solution.py:40
  23.1 2.1 %collective-permute-done.11 = f32[8,3,16,256]{3,2,1,0:T(8,128)S(1)} collective-permute-done((f32[8,3,16,256]{3,2,1,0:T(8,128)S(1)}, f32[8,3,16,256]{3,2,1,0:T(8,128)S(1)}, u32[]{:S(2)}, u32[]{:S(2)}) %collective-permute-start.11) | collective-permute-done | bytes 393248 | tf_op jit(solution)/shard_map/ppermute | solution.py:40
  25.3 2.0 %collective-permute-start.12 = (f32[4,3,16,256]{3,2,1,0:T(8,128)S(1)}, f32[4,3,16,256]{3,2,1,0:T(8,128)S(1)}, u32[]{:S(2)}, u32[]{:S(2)}) collective-permute-start(f32[4,3,16,256]{3,2,1,0:T(8,128)S(1)} %slice_add_fusion), channel_id=1, source_target_pairs={{0,1},{1,0},{2,3},{3,2},{4,5},{5,4},{6,7},{7,6},{8,9},{9,8},{10,11... | collective-permute-start | bytes 589832 | tf_op jit(solution)/shard_map/ppermute | solution.py:40
  27.2 2.9 %collective-permute-done = f32[8,3,16,256]{3,2,1,0:T(8,128)S(1)} collective-permute-done((f32[8,3,16,256]{3,2,1,0:T(8,128)S(1)}, f32[8,3,16,256]{3,2,1,0:T(8,128)S(1)}, u32[]{:S(2)}, u32[]{:S(2)}) %collective-permute-start) | collective-permute-done | bytes 393248 | tf_op jit(solution)/shard_map/ppermute | solution.py:40
  30.1 0.7 collective-permute-done.2
  30.9 1.3 %collective-permute-done.12 = f32[4,3,16,256]{3,2,1,0:T(8,128)S(1)} collective-permute-done((f32[4,3,16,256]{3,2,1,0:T(8,128)S(1)}, f32[4,3,16,256]{3,2,1,0:T(8,128)S(1)}, u32[]{:S(2)}, u32[]{:S(2)}) %collective-permute-start.12) | collective-permute-done | bytes 196640 | tf_op jit(solution)/shard_map/ppermute | solution.py:40
  32.3 1.8 %collective-permute-start.13 = (f32[2,3,16,256]{3,2,1,0:T(8,128)S(1)}, f32[2,3,16,256]{3,2,1,0:T(8,128)S(1)}, u32[]{:S(2)}, u32[]{:S(2)}) collective-permute-start(f32[2,3,16,256]{3,2,1,0:T(8,128)S(1)} %slice.75), channel_id=1, source_target_pairs={{0,3},{1,2},{2,1},{3,0},{4,7},{5,6},{6,5},{7,4},{8,11},{9,10},{10,... | collective-permute-start | bytes 294920 | tf_op jit(solution)/shard_map/ppermute | solution.py:40
  34.1 2.4 %collective-permute-done.3 = f32[4,3,16,256]{3,2,1,0:T(8,128)S(1)} collective-permute-done((f32[4,3,16,256]{3,2,1,0:T(8,128)S(1)}, f32[4,3,16,256]{3,2,1,0:T(8,128)S(1)}, u32[]{:S(2)}, u32[]{:S(2)}) %collective-permute-start.3) | collective-permute-done | bytes 196640 | tf_op jit(solution)/shard_map/ppermute | solution.py:40
  36.7 1.0 collective-permute-start.4
  37.7 1.3 %collective-permute-start.14 = (f32[2,3,16,256]{3,2,1,0:T(8,128)S(1)}, f32[2,3,16,256]{3,2,1,0:T(8,128)S(1)}, u32[]{:S(2)}, u32[]{:S(2)}) collective-permute-start(f32[2,3,16,256]{3,2,1,0:T(8,128)S(1)} %slice_add_fusion.8), channel_id=1, source_target_pairs={{0,4},{1,5},{2,6},{3,7},{4,0},{5,1},{6,2},{7,3},{8,12},{9,13},{10,... | collective-permute-start | bytes 294920 | tf_op jit(solution)/shard_map/ppermute | solution.py:40
  39.0 3.5 %collective-permute-done.4 = f32[2,3,16,256]{3,2,1,0:T(8,128)S(1)} collective-permute-done((f32[2,3,16,256]{3,2,1,0:T(8,128)S(1)}, f32[2,3,16,256]{3,2,1,0:T(8,128)S(1)}, u32[]{:S(2)}, u32[]{:S(2)}) %collective-permute-start.4) | collective-permute-done | bytes 98336 | tf_op jit(solution)/shard_map/ppermute | solution.py:40
  42.6 2.0 %collective-permute-start.5 = (f32[2,3,16,256]{3,2,1,0:T(8,128)S(1)}, f32[2,3,16,256]{3,2,1,0:T(8,128)S(1)}, u32[]{:S(2)}, u32[]{:S(2)}) collective-permute-start(f32[2,3,16,256]{3,2,1,0:T(8,128)S(1)} %slice_add_fusion.9), channel_id=1, source_target_pairs={{0,4},{1,5},{2,6},{3,7},{4,0},{5,1},{6,2},{7,3},{8,12},{9,13},{10,... | collective-permute-start | bytes 294920 | tf_op jit(solution)/shard_map/ppermute | solution.py:40
  44.6 2.3 %collective-permute-start.15 = (f32[2,3,16,256]{3,2,1,0:T(8,128)S(1)}, f32[2,3,16,256]{3,2,1,0:T(8,128)S(1)}, u32[]{:S(2)}, u32[]{:S(2)}) collective-permute-start(f32[2,3,16,256]{3,2,1,0:T(8,128)S(1)} %add_multiply_fusion), channel_id=1, source_target_pairs={{0,3},{1,2},{2,1},{3,0},{4,7},{5,6},{6,5},{7,4},{8,11},{9,10},{10,... | collective-permute-start | bytes 294920 | tf_op jit(solution)/shard_map/ppermute | solution.py:40
  47.3 1.0 collective-permute-start.6
  48.3 2.1 %collective-permute-done.15 = f32[2,3,16,256]{3,2,1,0:T(8,128)S(1)} collective-permute-done((f32[2,3,16,256]{3,2,1,0:T(8,128)S(1)}, f32[2,3,16,256]{3,2,1,0:T(8,128)S(1)}, u32[]{:S(2)}, u32[]{:S(2)}) %collective-permute-start.15) | collective-permute-done | bytes 98336 | tf_op jit(solution)/shard_map/ppermute | solution.py:40
  50.5 3.2 %collective-permute-start.16 = (f32[4,3,16,256]{3,2,1,0:T(8,128)S(1)}, f32[4,3,16,256]{3,2,1,0:T(8,128)S(1)}, u32[]{:S(2)}, u32[]{:S(2)}) collective-permute-start(f32[4,3,16,256]{3,2,1,0:T(8,128)S(1)} %pad_maximum_fusion.3), channel_id=1, source_target_pairs={{0,1},{1,0},{2,3},{3,2},{4,5},{5,4},{6,7},{7,6},{8,9},{9,8},{10,11... | collective-permute-start | bytes 589832 | tf_op jit(solution)/shard_map/ppermute | solution.py:40
  54.3 3.0 %collective-permute-done.16 = f32[4,3,16,256]{3,2,1,0:T(8,128)S(1)} collective-permute-done((f32[4,3,16,256]{3,2,1,0:T(8,128)S(1)}, f32[4,3,16,256]{3,2,1,0:T(8,128)S(1)}, u32[]{:S(2)}, u32[]{:S(2)}) %collective-permute-start.16) | collective-permute-done | bytes 196640 | tf_op jit(solution)/shard_map/ppermute | solution.py:40
  57.5 4.5 %collective-permute-done.7 = f32[4,3,16,256]{3,2,1,0:T(8,128)S(1)} collective-permute-done((f32[4,3,16,256]{3,2,1,0:T(8,128)S(1)}, f32[4,3,16,256]{3,2,1,0:T(8,128)S(1)}, u32[]{:S(2)}, u32[]{:S(2)}) %collective-permute-start.7) | collective-permute-done | bytes 196640 | tf_op jit(solution)/shard_map/ppermute | solution.py:40
  62.0 1.5 %collective-permute-start.8 = (f32[8,3,16,256]{3,2,1,0:T(8,128)S(1)}, f32[8,3,16,256]{3,2,1,0:T(8,128)S(1)}, u32[]{:S(2)}, u32[]{:S(2)}) collective-permute-start(f32[8,3,16,256]{3,2,1,0:T(8,128)S(1)} %pad_maximum_fusion.refs_0_), channel_id=1, source_target_pairs={{0,1},{1,0},{2,3},{3,2},{4,5},{5,4},{6,7},{7,6},{8,9},{9,8},{10,11... | collective-permute-start | bytes 1179656 | tf_op jit(solution)/shard_map/ppermute | solution.py:40
  63.5 2.3 %collective-permute-start.21 = (f32[8,3,16,256]{3,2,1,0:T(8,128)S(1)}, f32[8,3,16,256]{3,2,1,0:T(8,128)S(1)}, u32[]{:S(2)}, u32[]{:S(2)}) collective-permute-start(f32[8,3,16,256]{3,2,1,0:T(8,128)S(1)} %pad_maximum_fusion.refs_0_), channel_id=1, source_target_pairs={{0,3},{1,2},{2,1},{3,0},{4,7},{5,6},{6,5},{7,4},{8,11},{9,10},{10,... | collective-permute-start | bytes 1179656 | tf_op jit(solution)/shard_map/ppermute | solution.py:40
  65.9 1.5 %pair_sums.5.refs_1_ = f32[16,512]{1,0:T(8,128)S(1)} custom-call(s32[2]{0:T(128)S(1)} %pad_add_fusion.place_ref, f32[2]{0:T(128)S(1)} %convert_element_type.3.weight_ref, f32[4]{0:T(128)S(1)} %copy-done.8, f32[2,128]{1,0:T(2,128)S(1)} %copy-done.7, f32[2,1024]{1,0:T(2,128)S(1)} %copy-done.6, bf16[2,128,512]{2,1,0:T(8,128)(2,1)S(1)} %copy-done.4, ...), custom_call_target="tpu_custom_call" | custom-call | flops 402653184 | bytes 917504 | tf_op jit(solution)/shard_map/pair_sums/pallas_call | solution.py:212
  67.4 3.0 %collective-permute-done.17.refs_1_ = f32[8,3,16,256]{3,2,1,0:T(8,128)S(1)} collective-permute-done((f32[8,3,16,256]{3,2,1,0:T(8,128)S(1)}, f32[8,3,16,256]{3,2,1,0:T(8,128)S(1)}, u32[]{:S(2)}, u32[]{:S(2)}) %collective-permute-start.17) | collective-permute-done | bytes 393248 | tf_op jit(solution)/shard_map/ppermute | solution.py:40
  71.0 1.5 %pair_sums.6.refs_4_ = f32[16,512]{1,0:T(8,128)S(1)} custom-call(s32[2]{0:T(128)S(1)} %pad_add_fusion.place_ref, f32[2]{0:T(128)S(1)} %convert_element_type.3.weight_ref, f32[4]{0:T(128)S(1)} %copy-done.8, f32[2,128]{1,0:T(2,128)S(1)} %copy-done.7, f32[2,1024]{1,0:T(2,128)S(1)} %copy-done.6, bf16[2,128,512]{2,1,0:T(8,128)(2,1)S(1)} %copy-done.4, ...), custom_call_target="tpu_custom_call" | custom-call | flops 402653184 | bytes 917504 | tf_op jit(solution)/shard_map/pair_sums/pallas_call | solution.py:212
  72.5 1.0 collective-permute-done.8.refs_3_
  73.5 1.3 %collective-permute-start.18 = (f32[8,3,16,256]{3,2,1,0:T(8,128)S(1)}, f32[8,3,16,256]{3,2,1,0:T(8,128)S(1)}, u32[]{:S(2)}, u32[]{:S(2)}) collective-permute-start(f32[8,3,16,256]{3,2,1,0:T(8,128)S(1)} %collective-permute-done.8.refs_3_), channel_id=1, source_target_pairs={{0,3},{1,2},{2,1},{3,0},{4,7},{5,6},{6,5},{7,4},{8,11},{9,10},{10,... | collective-permute-start | bytes 1179656 | tf_op jit(solution)/shard_map/ppermute | solution.py:40
  74.8 3.5 %pair_sums.7.refs_1_ = f32[16,512]{1,0:T(8,128)S(1)} custom-call(s32[2]{0:T(128)S(1)} %pad_add_fusion.place_ref, f32[2]{0:T(128)S(1)} %convert_element_type.3.weight_ref, f32[4]{0:T(128)S(1)} %copy-done.8, f32[2,128]{1,0:T(2,128)S(1)} %copy-done.7, f32[2,1024]{1,0:T(2,128)S(1)} %copy-done.6, bf16[2,128,512]{2,1,0:T(8,128)(2,1)S(1)} %copy-done.4, ...), custom_call_target="tpu_custom_call" | custom-call | flops 1610612736 | bytes 3670016 | tf_op jit(solution)/shard_map/pair_sums/pallas_call | solution.py:212
  78.4 1.0 collective-permute-done.19.refs_0_
  79.4 1.5 %pair_sums.8.refs_1_ = f32[16,512]{1,0:T(8,128)S(1)} custom-call(s32[2]{0:T(128)S(1)} %pad_add_fusion.place_ref, f32[2]{0:T(128)S(1)} %convert_element_type.3.weight_ref, f32[4]{0:T(128)S(1)} %copy-done.8, f32[2,128]{1,0:T(2,128)S(1)} %copy-done.7, f32[2,1024]{1,0:T(2,128)S(1)} %copy-done.6, bf16[2,128,512]{2,1,0:T(8,128)(2,1)S(1)} %copy-done.4, ...), custom_call_target="tpu_custom_call" | custom-call | flops 402653184 | bytes 917504 | tf_op jit(solution)/shard_map/pair_sums/pallas_call | solution.py:212
  81.3 1.5 %pair_sums.9 = (f32[16,256]{1,0:T(8,128)S(1)}, f32[16,256]{1,0:T(8,128)S(1)}) custom-call(s32[2]{0:T(128)S(1)} %pad_add_fusion.place_ref, f32[2]{0:T(128)S(1)} %convert_element_type.3.weight_ref, f32[4]{0:T(128)S(1)} %copy-done.8, f32[2,128]{1,0:T(2,128)S(1)} %copy-done.7, f32[2,1024]{1,0:T(2,128)S(1)} %copy-done.6, bf16[2,128,512]{2,1,0:T(8,128)(2,1)S(1)} %copy-done.4, ...), custom_call_target="tpu_custom_call" | custom-call | flops 402653184 | bytes 917504 | tf_op jit(solution)/shard_map/pair_sums/pallas_call | solution.py:212
  82.8 1.2 collective-permute-done.22
  84.1 20.4 %all_to_all.5.gathered = f32[32,16,256]{2,1,0:T(8,128)S(1)} all-to-all(f32[32,16,256]{2,1,0:T(8,128)S(1)} %broadcast_in_dim.2), channel_id=1, replica_groups=mesh['ka'=8,'wa'=32] {'wa'}, dimensions={0} | all-to-all | bytes 1048576 | tf_op jit(solution)/shard_map/all_to_all | solution.py:45
  104.5 1.3 %wing_sums.1 = f32[16,128]{1,0:T(8,128)S(1)} custom-call(s32[2]{0:T(128)S(1)} %pad_add_fusion.place_ref, f32[32,16,256]{2,1,0:T(8,128)S(1)} %all_to_all.5.gathered, bf16[128,16384]{1,0:T(8,128)(2,1)S(1)} %copy-done.3), custom_call_target="tpu_custom_call" | custom-call | flops 100663296 | bytes 4718592 | tf_op jit(solution)/shard_map/wing_sums/pallas_call | solution.py:271
  105.8 1.2 collective-permute-done.23
  107.0 3.3 %collective-permute-start.24 = (f32[16,128]{1,0:T(8,128)S(1)}, f32[16,128]{1,0:T(8,128)S(1)}, u32[]{:S(2)}, u32[]{:S(2)}) collective-permute-start(f32[16,128]{1,0:T(8,128)S(1)} %add.74), channel_id=1, source_target_pairs={{0,64},{32,96},{64,0},{96,32},{128,192},{160,224},{192,128},{224,1... | collective-permute-start | bytes 24584 | tf_op jit(solution)/shard_map/ppermute | solution.py:29
  110.3 1.6 %collective-permute-done.24 = f32[16,128]{1,0:T(8,128)S(1)} collective-permute-done((f32[16,128]{1,0:T(8,128)S(1)}, f32[16,128]{1,0:T(8,128)S(1)}, u32[]{:S(2)}, u32[]{:S(2)}) %collective-permute-start.24) | collective-permute-done | bytes 8224 | tf_op jit(solution)/shard_map/ppermute | solution.py:29
  111.9 5.1 %collective-permute-start.25 = (f32[16,128]{1,0:T(8,128)S(1)}, f32[16,128]{1,0:T(8,128)S(1)}, u32[]{:S(2)}, u32[]{:S(2)}) collective-permute-start(f32[16,128]{1,0:T(8,128)S(1)} %add.75.one), channel_id=1, source_target_pairs={{0,192},{32,224},{64,128},{96,160},{128,64},{160,96},{192,0},{224,... | collective-permute-start | bytes 24584 | tf_op jit(solution)/shard_map/ppermute | solution.py:29
  116.9 1.6 %collective-permute-done.25.two = f32[16,128]{1,0:T(8,128)S(1)} collective-permute-done((f32[16,128]{1,0:T(8,128)S(1)}, f32[16,128]{1,0:T(8,128)S(1)}, u32[]{:S(2)}, u32[]{:S(2)}) %collective-permute-start.25) | collective-permute-done | bytes 8224 | tf_op jit(solution)/shard_map/ppermute | solution.py:29
  (58 shorter events, 4.4 us)
Async XLA Ops:
  0.7 3.4 %copy-start = (bf16[2,1024,2048]{2,1,0:T(8,128)(2,1)S(1)}, bf16[2,1024,2048]{2,1,0:T(8,128)(2,1)}, u32[]{:S(2)}) copy-start(bf16[2,1024,2048]{2,1,0:T(8,128)(2,1)} %cond_ref.7) | copy-start | bytes 25165828
  4.1 1.2 %copy-start.2 = (bf16[2,128,2048]{2,1,0:T(8,128)(2,1)S(1)}, bf16[2,128,2048]{2,1,0:T(8,128)(2,1)}, u32[]{:S(2)}) copy-start(bf16[2,128,2048]{2,1,0:T(8,128)(2,1)} %val_ref.7) | copy-start | bytes 3145732
  5.3 0.8 copy-start.5
  7.6 7.9 %collective-permute-start.10 = (f32[8,3,16,256]{3,2,1,0:T(8,128)S(1)}, f32[8,3,16,256]{3,2,1,0:T(8,128)S(1)}, u32[]{:S(2)}, u32[]{:S(2)}) collective-permute-start(f32[8,3,16,256]{3,2,1,0:T(8,128)S(1)} %get-tuple-element.23), channel_id=1, source_target_pairs={{0,8},{1,9},{2,10},{3,11},{4,12},{5,13},{6,14},{7,15},{8,0},{9,1},... | collective-permute-start | bytes 1179656 | tf_op jit(solution)/shard_map/ppermute | solution.py:40
  10.8 9.7 %collective-permute-start.1 = (f32[8,3,16,256]{3,2,1,0:T(8,128)S(1)}, f32[8,3,16,256]{3,2,1,0:T(8,128)S(1)}, u32[]{:S(2)}, u32[]{:S(2)}) collective-permute-start(f32[8,3,16,256]{3,2,1,0:T(8,128)S(1)} %get-tuple-element.19), channel_id=1, source_target_pairs={{0,1},{1,0},{2,3},{3,2},{4,5},{5,4},{6,7},{7,6},{8,9},{9,8},{10,11... | collective-permute-start | bytes 1179656 | tf_op jit(solution)/shard_map/ppermute | solution.py:40
  11.6 11.5 %collective-permute-start.9 = (f32[8,3,16,256]{3,2,1,0:T(8,128)S(1)}, f32[8,3,16,256]{3,2,1,0:T(8,128)S(1)}, u32[]{:S(2)}, u32[]{:S(2)}) collective-permute-start(f32[8,3,16,256]{3,2,1,0:T(8,128)S(1)} %get-tuple-element.21), channel_id=1, source_target_pairs={{0,8},{1,9},{2,10},{3,11},{4,12},{5,13},{6,14},{7,15},{8,0},{9,1},... | collective-permute-start | bytes 1179656 | tf_op jit(solution)/shard_map/ppermute | solution.py:40
  15.6 9.7 %collective-permute-start.11 = (f32[8,3,16,256]{3,2,1,0:T(8,128)S(1)}, f32[8,3,16,256]{3,2,1,0:T(8,128)S(1)}, u32[]{:S(2)}, u32[]{:S(2)}) collective-permute-start(f32[8,3,16,256]{3,2,1,0:T(8,128)S(1)} %add.66), channel_id=1, source_target_pairs={{0,24},{1,25},{2,26},{3,27},{4,28},{5,29},{6,30},{7,31},{8,16},{9,... | collective-permute-start | bytes 1179656 | tf_op jit(solution)/shard_map/ppermute | solution.py:40
  18.4 11.7 %collective-permute-start = (f32[8,3,16,256]{3,2,1,0:T(8,128)S(1)}, f32[8,3,16,256]{3,2,1,0:T(8,128)S(1)}, u32[]{:S(2)}, u32[]{:S(2)}) collective-permute-start(f32[8,3,16,256]{3,2,1,0:T(8,128)S(1)} %get-tuple-element.17), channel_id=1, source_target_pairs={{0,1},{1,0},{2,3},{3,2},{4,5},{5,4},{6,7},{7,6},{8,9},{9,8},{10,11... | collective-permute-start | bytes 1179656 | tf_op jit(solution)/shard_map/ppermute | solution.py:40
  20.4 45.4 %copy-start.9 = (s32[2]{0:T(128)S(1)}, s32[2]{0:T(128)}, u32[]{:S(2)}) copy-start(s32[2]{0:T(128)} %param.19) | copy-start | bytes 28
  20.5 45.4 %copy-start.1 = (bf16[2,1024,512]{2,1,0:T(8,128)(2,1)S(1)}, bf16[2,1024,512]{2,1,0:T(8,128)(2,1)}, u32[]{:S(2)}) copy-start(bf16[2,1024,512]{2,1,0:T(8,128)(2,1)} %orbit_cond.9) | copy-start | bytes 6291460
  20.5 45.4 %copy-start.4 = (bf16[2,128,512]{2,1,0:T(8,128)(2,1)S(1)}, bf16[2,128,512]{2,1,0:T(8,128)(2,1)}, u32[]{:S(2)}) copy-start(bf16[2,128,512]{2,1,0:T(8,128)(2,1)} %orbit_val.9) | copy-start | bytes 786436
  20.5 45.4 %copy-start.6 = (f32[2,1024]{1,0:T(2,128)S(1)}, f32[2,1024]{1,0:T(2,128)}, u32[]{:S(2)}) copy-start(f32[2,1024]{1,0:T(2,128)} %energy_cond.9) | copy-start | bytes 24580
  20.5 45.4 %copy-start.7 = (f32[2,128]{1,0:T(2,128)S(1)}, f32[2,128]{1,0:T(2,128)}, u32[]{:S(2)}) copy-start(f32[2,128]{1,0:T(2,128)} %energy_val.9) | copy-start | bytes 3076
  20.5 45.4 %copy-start.8 = (f32[4]{0:T(128)S(1)}, f32[4]{0:T(128)}, u32[]{:S(2)}) copy-start(f32[4]{0:T(128)} %freq_ref.9) | copy-start | bytes 52
  20.6 10.2 %collective-permute-start.2 = (f32[8,3,16,256]{3,2,1,0:T(8,128)S(1)}, f32[8,3,16,256]{3,2,1,0:T(8,128)S(1)}, u32[]{:S(2)}, u32[]{:S(2)}) collective-permute-start(f32[8,3,16,256]{3,2,1,0:T(8,128)S(1)} %add.58), channel_id=1, source_target_pairs={{0,3},{1,2},{2,1},{3,0},{4,7},{5,6},{6,5},{7,4},{8,11},{9,10},{10,... | collective-permute-start | bytes 1179656 | tf_op jit(solution)/shard_map/ppermute | solution.py:40
  25.3 6.9 %collective-permute-start.12 = (f32[4,3,16,256]{3,2,1,0:T(8,128)S(1)}, f32[4,3,16,256]{3,2,1,0:T(8,128)S(1)}, u32[]{:S(2)}, u32[]{:S(2)}) collective-permute-start(f32[4,3,16,256]{3,2,1,0:T(8,128)S(1)} %slice_add_fusion), channel_id=1, source_target_pairs={{0,1},{1,0},{2,3},{3,2},{4,5},{5,4},{6,7},{7,6},{8,9},{9,8},{10,11... | collective-permute-start | bytes 589832 | tf_op jit(solution)/shard_map/ppermute | solution.py:40
  30.8 5.8 %collective-permute-start.3 = (f32[4,3,16,256]{3,2,1,0:T(8,128)S(1)}, f32[4,3,16,256]{3,2,1,0:T(8,128)S(1)}, u32[]{:S(2)}, u32[]{:S(2)}) collective-permute-start(f32[4,3,16,256]{3,2,1,0:T(8,128)S(1)} %slice_add_fusion.4), channel_id=1, source_target_pairs={{0,8},{1,9},{2,10},{3,11},{4,12},{5,13},{6,14},{7,15},{8,0},{9,1},... | collective-permute-start | bytes 589832 | tf_op jit(solution)/shard_map/ppermute | solution.py:40
  32.3 5.4 %collective-permute-start.13 = (f32[2,3,16,256]{3,2,1,0:T(8,128)S(1)}, f32[2,3,16,256]{3,2,1,0:T(8,128)S(1)}, u32[]{:S(2)}, u32[]{:S(2)}) collective-permute-start(f32[2,3,16,256]{3,2,1,0:T(8,128)S(1)} %slice.75), channel_id=1, source_target_pairs={{0,3},{1,2},{2,1},{3,0},{4,7},{5,6},{6,5},{7,4},{8,11},{9,10},{10,... | collective-permute-start | bytes 294920 | tf_op jit(solution)/shard_map/ppermute | solution.py:40
  36.7 5.9 %collective-permute-start.4 = (f32[2,3,16,256]{3,2,1,0:T(8,128)S(1)}, f32[2,3,16,256]{3,2,1,0:T(8,128)S(1)}, u32[]{:S(2)}, u32[]{:S(2)}) collective-permute-start(f32[2,3,16,256]{3,2,1,0:T(8,128)S(1)} %slice.69), channel_id=1, source_target_pairs={{0,24},{1,25},{2,26},{3,27},{4,28},{5,29},{6,30},{7,31},{8,16},{9,... | collective-permute-start | bytes 294920 | tf_op jit(solution)/shard_map/ppermute | solution.py:40
  37.7 6.9 %collective-permute-start.14 = (f32[2,3,16,256]{3,2,1,0:T(8,128)S(1)}, f32[2,3,16,256]{3,2,1,0:T(8,128)S(1)}, u32[]{:S(2)}, u32[]{:S(2)}) collective-permute-start(f32[2,3,16,256]{3,2,1,0:T(8,128)S(1)} %slice_add_fusion.8), channel_id=1, source_target_pairs={{0,4},{1,5},{2,6},{3,7},{4,0},{5,1},{6,2},{7,3},{8,12},{9,13},{10,... | collective-permute-start | bytes 294920 | tf_op jit(solution)/shard_map/ppermute | solution.py:40
  42.6 4.7 %collective-permute-start.5 = (f32[2,3,16,256]{3,2,1,0:T(8,128)S(1)}, f32[2,3,16,256]{3,2,1,0:T(8,128)S(1)}, u32[]{:S(2)}, u32[]{:S(2)}) collective-permute-start(f32[2,3,16,256]{3,2,1,0:T(8,128)S(1)} %slice_add_fusion.9), channel_id=1, source_target_pairs={{0,4},{1,5},{2,6},{3,7},{4,0},{5,1},{6,2},{7,3},{8,12},{9,13},{10,... | collective-permute-start | bytes 294920 | tf_op jit(solution)/shard_map/ppermute | solution.py:40
  44.6 5.9 %collective-permute-start.15 = (f32[2,3,16,256]{3,2,1,0:T(8,128)S(1)}, f32[2,3,16,256]{3,2,1,0:T(8,128)S(1)}, u32[]{:S(2)}, u32[]{:S(2)}) collective-permute-start(f32[2,3,16,256]{3,2,1,0:T(8,128)S(1)} %add_multiply_fusion), channel_id=1, source_target_pairs={{0,3},{1,2},{2,1},{3,0},{4,7},{5,6},{6,5},{7,4},{8,11},{9,10},{10,... | collective-permute-start | bytes 294920 | tf_op jit(solution)/shard_map/ppermute | solution.py:40
  47.3 6.9 %collective-permute-start.6 = (f32[2,3,16,256]{3,2,1,0:T(8,128)S(1)}, f32[2,3,16,256]{3,2,1,0:T(8,128)S(1)}, u32[]{:S(2)}, u32[]{:S(2)}) collective-permute-start(f32[2,3,16,256]{3,2,1,0:T(8,128)S(1)} %add_multiply_fusion.1), channel_id=1, source_target_pairs={{0,24},{1,25},{2,26},{3,27},{4,28},{5,29},{6,30},{7,31},{8,16},{9,... | collective-permute-start | bytes 294920 | tf_op jit(solution)/shard_map/ppermute | solution.py:40
  50.5 6.9 %collective-permute-start.16 = (f32[4,3,16,256]{3,2,1,0:T(8,128)S(1)}, f32[4,3,16,256]{3,2,1,0:T(8,128)S(1)}, u32[]{:S(2)}, u32[]{:S(2)}) collective-permute-start(f32[4,3,16,256]{3,2,1,0:T(8,128)S(1)} %pad_maximum_fusion.3), channel_id=1, source_target_pairs={{0,1},{1,0},{2,3},{3,2},{4,5},{5,4},{6,7},{7,6},{8,9},{9,8},{10,11... | collective-permute-start | bytes 589832 | tf_op jit(solution)/shard_map/ppermute | solution.py:40
  54.2 7.7 %collective-permute-start.7 = (f32[4,3,16,256]{3,2,1,0:T(8,128)S(1)}, f32[4,3,16,256]{3,2,1,0:T(8,128)S(1)}, u32[]{:S(2)}, u32[]{:S(2)}) collective-permute-start(f32[4,3,16,256]{3,2,1,0:T(8,128)S(1)} %pad_maximum_fusion.2), channel_id=1, source_target_pairs={{0,8},{1,9},{2,10},{3,11},{4,12},{5,13},{6,14},{7,15},{8,0},{9,1},... | collective-permute-start | bytes 589832 | tf_op jit(solution)/shard_map/ppermute | solution.py:40
  57.4 13.0 %collective-permute-start.17 = (f32[8,3,16,256]{3,2,1,0:T(8,128)S(1)}, f32[8,3,16,256]{3,2,1,0:T(8,128)S(1)}, u32[]{:S(2)}, u32[]{:S(2)}) collective-permute-start(f32[8,3,16,256]{3,2,1,0:T(8,128)S(1)} %pad_maximum_fusion.1.refs_0_), channel_id=1, source_target_pairs={{0,8},{1,9},{2,10},{3,11},{4,12},{5,13},{6,14},{7,15},{8,0},{9,1},... | collective-permute-start | bytes 1179656 | tf_op jit(solution)/shard_map/ppermute | solution.py:40
  62.0 11.5 %collective-permute-start.8 = (f32[8,3,16,256]{3,2,1,0:T(8,128)S(1)}, f32[8,3,16,256]{3,2,1,0:T(8,128)S(1)}, u32[]{:S(2)}, u32[]{:S(2)}) collective-permute-start(f32[8,3,16,256]{3,2,1,0:T(8,128)S(1)} %pad_maximum_fusion.refs_0_), channel_id=1, source_target_pairs={{0,1},{1,0},{2,3},{3,2},{4,5},{5,4},{6,7},{7,6},{8,9},{9,8},{10,11... | collective-permute-start | bytes 1179656 | tf_op jit(solution)/shard_map/ppermute | solution.py:40
  63.5 11.3 %collective-permute-start.20 = (f32[8,3,16,256]{3,2,1,0:T(8,128)S(1)}, f32[8,3,16,256]{3,2,1,0:T(8,128)S(1)}, u32[]{:S(2)}, u32[]{:S(2)}) collective-permute-start(f32[8,3,16,256]{3,2,1,0:T(8,128)S(1)} %pad_maximum_fusion.1.refs_0_), channel_id=1, source_target_pairs={{0,24},{1,25},{2,26},{3,27},{4,28},{5,29},{6,30},{7,31},{8,16},{9,... | collective-permute-start | bytes 1179656 | tf_op jit(solution)/shard_map/ppermute | solution.py:40
  63.5 11.3 %collective-permute-start.21 = (f32[8,3,16,256]{3,2,1,0:T(8,128)S(1)}, f32[8,3,16,256]{3,2,1,0:T(8,128)S(1)}, u32[]{:S(2)}, u32[]{:S(2)}) collective-permute-start(f32[8,3,16,256]{3,2,1,0:T(8,128)S(1)} %pad_maximum_fusion.refs_0_), channel_id=1, source_target_pairs={{0,3},{1,2},{2,1},{3,0},{4,7},{5,6},{6,5},{7,4},{8,11},{9,10},{10,... | collective-permute-start | bytes 1179656 | tf_op jit(solution)/shard_map/ppermute | solution.py:40
  70.4 9.0 %collective-permute-start.19 = (f32[8,3,16,256]{3,2,1,0:T(8,128)S(1)}, f32[8,3,16,256]{3,2,1,0:T(8,128)S(1)}, u32[]{:S(2)}, u32[]{:S(2)}) collective-permute-start(f32[8,3,16,256]{3,2,1,0:T(8,128)S(1)} %collective-permute-done.17.refs_1_), channel_id=1, source_target_pairs={{0,24},{1,25},{2,26},{3,27},{4,28},{5,29},{6,30},{7,31},{8,16},{9,... | collective-permute-start | bytes 1179656 | tf_op jit(solution)/shard_map/ppermute | solution.py:40
  73.5 7.8 %collective-permute-start.18 = (f32[8,3,16,256]{3,2,1,0:T(8,128)S(1)}, f32[8,3,16,256]{3,2,1,0:T(8,128)S(1)}, u32[]{:S(2)}, u32[]{:S(2)}) collective-permute-start(f32[8,3,16,256]{3,2,1,0:T(8,128)S(1)} %collective-permute-done.8.refs_3_), channel_id=1, source_target_pairs={{0,3},{1,2},{2,1},{3,0},{4,7},{5,6},{6,5},{7,4},{8,11},{9,10},{10,... | collective-permute-start | bytes 1179656 | tf_op jit(solution)/shard_map/ppermute | solution.py:40
  78.4 26.1 %copy-start.3 = (bf16[128,16384]{1,0:T(8,128)(2,1)S(1)}, bf16[128,16384]{1,0:T(8,128)(2,1)}, u32[]{:S(2)}) copy-start(bf16[128,16384]{1,0:T(8,128)(2,1)} %zeta.1) | copy-start | bytes 12582916
  82.7 1.3 %collective-permute-start.22 = (f32[16,256]{1,0:T(8,128)S(1)}, f32[16,256]{1,0:T(8,128)S(1)}, u32[]{:S(2)}, u32[]{:S(2)}) collective-permute-start(f32[16,256]{1,0:T(8,128)S(1)} %get-tuple-element.29), channel_id=1, source_target_pairs={{0,32},{32,0},{64,96},{96,64},{128,160},{160,128},{192,224},{224,1... | collective-permute-start | bytes 49160 | tf_op jit(solution)/shard_map/ppermute | solution.py:29
  105.8 1.2 %collective-permute-start.23 = (f32[16,128]{1,0:T(8,128)S(1)}, f32[16,128]{1,0:T(8,128)S(1)}, u32[]{:S(2)}, u32[]{:S(2)}) collective-permute-start(f32[16,128]{1,0:T(8,128)S(1)} %wing_sums.1), channel_id=1, source_target_pairs={{0,32},{32,0},{64,96},{96,64},{128,160},{160,128},{192,224},{224,1... | collective-permute-start | bytes 24584 | tf_op jit(solution)/shard_map/ppermute | solution.py:29
  107.0 4.9 %collective-permute-start.24 = (f32[16,128]{1,0:T(8,128)S(1)}, f32[16,128]{1,0:T(8,128)S(1)}, u32[]{:S(2)}, u32[]{:S(2)}) collective-permute-start(f32[16,128]{1,0:T(8,128)S(1)} %add.74), channel_id=1, source_target_pairs={{0,64},{32,96},{64,0},{96,32},{128,192},{160,224},{192,128},{224,1... | collective-permute-start | bytes 24584 | tf_op jit(solution)/shard_map/ppermute | solution.py:29
  111.9 6.7 %collective-permute-start.25 = (f32[16,128]{1,0:T(8,128)S(1)}, f32[16,128]{1,0:T(8,128)S(1)}, u32[]{:S(2)}, u32[]{:S(2)}) collective-permute-start(f32[16,128]{1,0:T(8,128)S(1)} %add.75.one), channel_id=1, source_target_pairs={{0,192},{32,224},{64,128},{96,160},{128,64},{160,96},{192,0},{224,... | collective-permute-start | bytes 24584 | tf_op jit(solution)/shard_map/ppermute | solution.py:29

commit v9 on v5

--- a/solution.py
+++ b/solution.py
@@ -7,7 +7,7 @@
 from jax.experimental.pallas import tpu as pltpu
 from jax.sharding import PartitionSpec as P
 
-MASKS = (((8, 24, 1, 3, 4), (1, 3, 8, 24, 4)), ((24, 8, 1, 3, 4), (3, 1, 8, 24, 4)))
+MASKS = (((8, 24, 1, 3, 4), (24, 8, 1, 3, 4)), ((1, 3, 8, 24, 4), (3, 1, 8, 24, 4)))
 CB, VB = 4, 8
 F32, BF16 = jnp.float32, jnp.bfloat16
 VMEM, SMEM = pl.BlockSpec(memory_space=pltpu.VMEM), pl.BlockSpec(memory_space=pltpu.SMEM)
@@ -16,9 +16,9 @@
     index, core = place[0], place[1]
     x, z, y = index >> 3, (index >> 2) & 1, index & 3
 
-    first, second = x + (y - x) * core, y + (x - y) * core
+    first, second = (x, y) if kpoint == 0 else (y, x)
     one, two = (first ^ (first >> 1)) & 1, first >> 1
-    quarter = one << 1 | two if kpoint == 0 else two << 1 | one
+    quarter = (one << 1 | two) + ((two << 1 | one) - (one << 1 | two)) * core
     return quarter, ((second ^ (second >> 1)) & 1) << 2 | (second >> 1) << 1 | z
 
 
@@ -37,6 +37,10 @@
     return lax.ppermute(value, ("ka", "wa"), pairs)
 
 
+def around(value, kpoint, dim):
+    return swap(value, "wa", MASKS[kpoint][0][dim])
+
+
 def everyone(value, axis):
     parts = lax.axis_size(axis)
     return lax.all_to_all(jnp.broadcast_to(value[None], (parts,) + value.shape), axis, 0, 0)
@@ -57,8 +61,7 @@
     held = (held + cross(held, kpoint, 4)[::-1]) * factor
     others = [cross(held, kpoint, *dims) for dims in ((3,), (2,), (2, 3))]
     held = jnp.concatenate([held] + others)
-    first, second = cross(held, kpoint, 0), cross(held, kpoint, 1)
-    return held, second, first, cross(first, kpoint, 1)
+    return held, around(held, kpoint, 1), around(held, kpoint, 0)
 
 
 def momentum_kernel(kpoint, quarters, place_ref, val_ref, miller_ref, cond_ref, *refs):
@@ -127,6 +130,8 @@
         level[spot] = jnp.transpose(jnp.broadcast_to(energy_val[k : k + 1, :], (nval, nval)))
         top = []
         for part, quarter in enumerate(quarters):
+            if quarter in (1, 2):
+                quarter = quarter + (3 - 2 * quarter) * place_ref[1]
             start = pl.multiple_of((quarter ^ me_c) * cols, cols)
             top.append(energy_cond[k : k + 1, pl.ds(start, cols)])
             orbits[spot, part * cols : (part + 1) * cols, :] = orbit_cond[k, pl.ds(start, cols), :]
@@ -317,11 +322,17 @@
     keeps = [partial_momentum(k, (1, 0), *operands) for k in range(kcount)]
     parts = [(own, second, first, both) for (both, first), (second, own) in zip(sends, keeps)]
     chunks = [gathered_chunks(k, parts[k], pw_factor) for k in range(kcount)]
-    operands = (place, weights, freqs, energy_val, energy_cond, orbit_val, orbit_cond, chunks)
-    pair = pair_sums(((0, (0,)), (1, (0,))), *operands, [], 1)
-    pair = pair_sums(((0, (1, 2)), (1, (1, 2))), *operands, pair, 1)
-    pair = pair_sums(((0, (3,)),), *operands, pair, 1)
-    keep, send = pair_sums(((1, (3,)),), *operands, pair, 2)
+    operands = (place, weights, freqs, energy_val, energy_cond, orbit_val, orbit_cond)
+    own, second, first = chunks[0]
+    chunks[0] = (own, second, first, around(first, 0, 1))
+    own, second, first = chunks[1]
+    pair = pair_sums(((0, (0,)), (1, (0,))), *operands, chunks, [], 1)
+    first, pair = lax.optimization_barrier((first, pair))
+    chunks[1] = (own, second, first, around(first, 1, 1))
+    for k in range(kcount):
+        pair = pair_sums(((k, (1, 2)),), *operands, chunks, pair, 1)
+    pair = pair_sums(((0, (3,)),), *operands, chunks, pair, 1)
+    keep, send = pair_sums(((1, (3,)),), *operands, chunks, pair, 2)
     pair = keep + swap(send, "ka", 1)
     total = wing_sums(place, everyone(pair, "wa"), zeta)
     total = total + swap(total, "ka", 1)

time: 114 us -> 110 us (0.965)
  waiting for transfers between devices: 25.4 us -> 22.8 us
  starting transfers between devices: 45.6 us -> 44.4 us
    ppermute x26 -> x20, waiting for transfers between devices: 19.7 us -> 12 us  [cross(): return lax.ppermute(value, ('ka', 'wa'), pairs)]
    ppermute x26 -> x20, starting transfers between devices: 36.7 us -> 29.7 us  [cross(): return lax.ppermute(value, ('ka', 'wa'), pairs)]
    ppermute x4 -> x10, starting transfers between devices: 8.87 us -> 14.7 us  [swap(): lax.ppermute(value, axis, [(i, i ^ mask) for i in range(lax.axis_size(axi...]
    ppermute x4 -> x10, waiting for transfers between devices: 5.61 us -> 10.8 us  [swap(): lax.ppermute(value, axis, [(i, i ^ mask) for i in range(lax.axis_size(axi...]
    pallas_call x4 -> x5, Pallas kernels: 8.87 us -> 9.5 us  [pair_sums(): pl.pallas_call(functools.partial(pair_kernel, groups), out_shape=[jax.Sha...]
  transfers between devices with their start and end apart: 30 -> 30, of which waited for: 17 -> 16; matrix products, arithmetic and copies ran while one was open for 0% -> 0% of each run, Pallas kernels for 11% -> 12%
where the time goes in v9:
time: 110 us
  starting transfers between devices  44.4 us (40%)
  waiting for transfers between devices  22.8 us (21%)
  blocking collectives  17.8 us (16%)
  Pallas kernels  17.6 us (16%)
  local copies, waits for them, and re-layouts  5.46 us (5%)
    ppermute x20, starting transfers between devices, cross(): return lax.ppermute(value, ('ka', 'wa'), pairs)  29.7 us
    all_to_all x1, blocking collectives, everyone(): lax.all_to_all(jnp.broadcast_to(value[None], (parts,) + value.shape), axi...  17.8 us
    ppermute x10, starting transfers between devices, swap(): lax.ppermute(value, axis, [(i, i ^ mask) for i in range(lax.axis_size(axi...  14.7 us
    ppermute x20, waiting for transfers between devices, cross(): return lax.ppermute(value, ('ka', 'wa'), pairs)  12 us
    ppermute x10, waiting for transfers between devices, swap(): lax.ppermute(value, axis, [(i, i ^ mask) for i in range(lax.axis_size(axi...  10.8 us
    pallas_call x5, Pallas kernels, pair_sums(): pl.pallas_call(functools.partial(pair_kernel, groups), out_shape=[jax.Sha...  9.5 us
    pallas_call x4, Pallas kernels, partial_momentum(): pl.pallas_call(functools.partial(momentum_kernel, kpoint, quarters), out_...  6.24 us
    unnamed x20, local copies, waits for them, and re-layouts  5.41 us
  transfers between devices with their start and end apart: 30, of which 16 were waited for; matrix products, arithmetic and copies ran while one was open for 0% of the time, Pallas kernels for 12%

profile of v9, /device:TPU:8, one launch (start us, length us, event | category | flops | bytes accessed | tf_op | source)
XLA Modules:
  0.0 109.6 jit_solution(8395518510303151524)
XLA Ops:
  0.7 3.4 %copy-done = bf16[2,1024,2048]{2,1,0:T(8,128)(2,1)S(1)} copy-done((bf16[2,1024,2048]{2,1,0:T(8,128)(2,1)S(1)}, bf16[2,1024,2048]{2,1,0:T(8,128)(2,1)}, u32[]{:S(2)}) %copy-start) | copy-done | bytes 8388632
  4.1 1.2 %copy-done.2 = bf16[2,128,2048]{2,1,0:T(8,128)(2,1)S(1)} copy-done((bf16[2,128,2048]{2,1,0:T(8,128)(2,1)S(1)}, bf16[2,128,2048]{2,1,0:T(8,128)(2,1)}, u32[]{:S(2)}) %copy-start.2) | copy-done | bytes 1048600
  6.1 1.6 %partial_momentum.7 = (f32[8,3,16,256]{3,2,1,0:T(8,128)S(1)}, f32[8,3,16,256]{3,2,1,0:T(8,128)S(1)}) custom-call(s32[2]{0:T(128)S(1)} %pad_add_fusion.place_ref, bf16[2,128,2048]{2,1,0:T(8,128)(2,1)S(1)} %copy-done.2, s32[3,2048]{1,0:T(4,128)S(1)} %copy-done.5, bf16[2,1024,2048]{2,1,0:T(8,128)(2,1)S(1)} %copy-done), custom_call_target="tpu_custom_call" | custom-call | flops 805306368 | bytes 3407872 | tf_op jit(solution)/shard_map/partial_momentum/pallas_call | solution.py:98
  7.6 1.6 %collective-permute-start.12 = (f32[8,3,16,256]{3,2,1,0:T(8,128)S(1)}, f32[8,3,16,256]{3,2,1,0:T(8,128)S(1)}, u32[]{:S(2)}, u32[]{:S(2)}) collective-permute-start(f32[8,3,16,256]{3,2,1,0:T(8,128)S(1)} %get-tuple-element.21), channel_id=1, source_target_pairs={{0,8},{1,9},{2,10},{3,11},{4,12},{5,13},{6,14},{7,15},{8,0},{9,1},... | collective-permute-start | bytes 1179656 | tf_op jit(solution)/shard_map/ppermute | solution.py:37
  9.2 1.6 %partial_momentum.5 = (f32[8,3,16,256]{3,2,1,0:T(8,128)S(1)}, f32[8,3,16,256]{3,2,1,0:T(8,128)S(1)}) custom-call(s32[2]{0:T(128)S(1)} %pad_add_fusion.place_ref, bf16[2,128,2048]{2,1,0:T(8,128)(2,1)S(1)} %copy-done.2, s32[3,2048]{1,0:T(4,128)S(1)} %copy-done.5, bf16[2,1024,2048]{2,1,0:T(8,128)(2,1)S(1)} %copy-done), custom_call_target="tpu_custom_call" | custom-call | flops 805306368 | bytes 3407872 | tf_op jit(solution)/shard_map/partial_momentum/pallas_call | solution.py:98
  11.6 2.0 %collective-permute-start.11 = (f32[8,3,16,256]{3,2,1,0:T(8,128)S(1)}, f32[8,3,16,256]{3,2,1,0:T(8,128)S(1)}, u32[]{:S(2)}, u32[]{:S(2)}) collective-permute-start(f32[8,3,16,256]{3,2,1,0:T(8,128)S(1)} %get-tuple-element.19), channel_id=1, source_target_pairs={{0,8},{1,9},{2,10},{3,11},{4,12},{5,13},{6,14},{7,15},{8,0},{9,1},... | collective-permute-start | bytes 1179656 | tf_op jit(solution)/shard_map/ppermute | solution.py:37
  13.6 1.6 %partial_momentum.6 = (f32[8,3,16,256]{3,2,1,0:T(8,128)S(1)}, f32[8,3,16,256]{3,2,1,0:T(8,128)S(1)}) custom-call(s32[2]{0:T(128)S(1)} %pad_add_fusion.place_ref, bf16[2,128,2048]{2,1,0:T(8,128)(2,1)S(1)} %copy-done.2, s32[3,2048]{1,0:T(4,128)S(1)} %copy-done.5, bf16[2,1024,2048]{2,1,0:T(8,128)(2,1)S(1)} %copy-done), custom_call_target="tpu_custom_call" | custom-call | flops 805306368 | bytes 3407872 | tf_op jit(solution)/shard_map/partial_momentum/pallas_call | solution.py:98
  15.6 2.8 %collective-permute-start.13 = (f32[8,3,16,256]{3,2,1,0:T(8,128)S(1)}, f32[8,3,16,256]{3,2,1,0:T(8,128)S(1)}, u32[]{:S(2)}, u32[]{:S(2)}) collective-permute-start(f32[8,3,16,256]{3,2,1,0:T(8,128)S(1)} %add.101), channel_id=1, source_target_pairs={{0,24},{1,25},{2,26},{3,27},{4,28},{5,29},{6,30},{7,31},{8,16},{9,... | collective-permute-start | bytes 1179656 | tf_op jit(solution)/shard_map/ppermute | solution.py:37
  18.9 1.6 %partial_momentum.4 = (f32[8,3,16,256]{3,2,1,0:T(8,128)S(1)}, f32[8,3,16,256]{3,2,1,0:T(8,128)S(1)}) custom-call(s32[2]{0:T(128)S(1)} %pad_add_fusion.place_ref, bf16[2,128,2048]{2,1,0:T(8,128)(2,1)S(1)} %copy-done.2, s32[3,2048]{1,0:T(4,128)S(1)} %copy-done.5, bf16[2,1024,2048]{2,1,0:T(8,128)(2,1)S(1)} %copy-done), custom_call_target="tpu_custom_call" | custom-call | flops 805306368 | bytes 3407872 | tf_op jit(solution)/shard_map/partial_momentum/pallas_call | solution.py:98
  20.6 2.5 %collective-permute-start.2 = (f32[8,3,16,256]{3,2,1,0:T(8,128)S(1)}, f32[8,3,16,256]{3,2,1,0:T(8,128)S(1)}, u32[]{:S(2)}, u32[]{:S(2)}) collective-permute-start(f32[8,3,16,256]{3,2,1,0:T(8,128)S(1)} %add.88), channel_id=1, source_target_pairs={{0,3},{1,2},{2,1},{3,0},{4,7},{5,6},{6,5},{7,4},{8,11},{9,10},{10,... | collective-permute-start | bytes 1179656 | tf_op jit(solution)/shard_map/ppermute | solution.py:37
  23.1 2.1 %collective-permute-done.13 = f32[8,3,16,256]{3,2,1,0:T(8,128)S(1)} collective-permute-done((f32[8,3,16,256]{3,2,1,0:T(8,128)S(1)}, f32[8,3,16,256]{3,2,1,0:T(8,128)S(1)}, u32[]{:S(2)}, u32[]{:S(2)}) %collective-permute-start.13) | collective-permute-done | bytes 393248 | tf_op jit(solution)/shard_map/ppermute | solution.py:37
  25.3 2.0 %collective-permute-start.14 = (f32[2,3,16,256]{3,2,1,0:T(8,128)S(1)}, f32[2,3,16,256]{3,2,1,0:T(8,128)S(1)}, u32[]{:S(2)}, u32[]{:S(2)}) collective-permute-start(f32[2,3,16,256]{3,2,1,0:T(8,128)S(1)} %get-tuple-element.28), channel_id=1, source_target_pairs={{0,1},{1,0},{2,3},{3,2},{4,5},{5,4},{6,7},{7,6},{8,9},{9,8},{10,11... | collective-permute-start | bytes 294920 | tf_op jit(solution)/shard_map/ppermute | solution.py:37
  27.7 1.8 %collective-permute-start.16 = (f32[2,3,16,256]{3,2,1,0:T(8,128)S(1)}, f32[2,3,16,256]{3,2,1,0:T(8,128)S(1)}, u32[]{:S(2)}, u32[]{:S(2)}) collective-permute-start(f32[2,3,16,256]{3,2,1,0:T(8,128)S(1)} %get-tuple-element.26), channel_id=1, source_target_pairs={{0,2},{1,3},{2,0},{3,1},{4,6},{5,7},{6,4},{7,5},{8,10},{9,11},{10,... | collective-permute-start | bytes 294920 | tf_op jit(solution)/shard_map/ppermute | solution.py:37
  29.5 0.9 collective-permute-done
  30.6 1.3 %collective-permute-start.4 = (f32[2,3,16,256]{3,2,1,0:T(8,128)S(1)}, f32[2,3,16,256]{3,2,1,0:T(8,128)S(1)}, u32[]{:S(2)}, u32[]{:S(2)}) collective-permute-start(f32[2,3,16,256]{3,2,1,0:T(8,128)S(1)} %get-tuple-element.30), channel_id=1, source_target_pairs={{0,24},{1,25},{2,26},{3,27},{4,28},{5,29},{6,30},{7,31},{8,16},{9,... | collective-permute-start | bytes 294920 | tf_op jit(solution)/shard_map/ppermute | solution.py:37
  32.5 2.2 %collective-permute-start.5 = (f32[2,3,16,256]{3,2,1,0:T(8,128)S(1)}, f32[2,3,16,256]{3,2,1,0:T(8,128)S(1)}, u32[]{:S(2)}, u32[]{:S(2)}) collective-permute-start(f32[2,3,16,256]{3,2,1,0:T(8,128)S(1)} %get-tuple-element.29), channel_id=1, source_target_pairs={{0,16},{1,17},{2,18},{3,19},{4,20},{5,21},{6,22},{7,23},{8,24},{9,... | collective-permute-start | bytes 294920 | tf_op jit(solution)/shard_map/ppermute | solution.py:37
  34.7 0.8 collective-permute-done.16
  35.5 2.0 %collective-permute-start.17 = (f32[2,3,16,256]{3,2,1,0:T(8,128)S(1)}, f32[2,3,16,256]{3,2,1,0:T(8,128)S(1)}, u32[]{:S(2)}, u32[]{:S(2)}) collective-permute-start(f32[2,3,16,256]{3,2,1,0:T(8,128)S(1)} %fusion.1), channel_id=1, source_target_pairs={{0,4},{1,5},{2,6},{3,7},{4,0},{5,1},{6,2},{7,3},{8,12},{9,13},{10,... | collective-permute-start | bytes 294920 | tf_op jit(solution)/shard_map/ppermute | solution.py:37
  37.5 2.0 %collective-permute-done.4 = f32[2,3,16,256]{3,2,1,0:T(8,128)S(1)} collective-permute-done((f32[2,3,16,256]{3,2,1,0:T(8,128)S(1)}, f32[2,3,16,256]{3,2,1,0:T(8,128)S(1)}, u32[]{:S(2)}, u32[]{:S(2)}) %collective-permute-start.4) | collective-permute-done | bytes 98336 | tf_op jit(solution)/shard_map/ppermute | solution.py:37
  39.6 2.0 %collective-permute-start.6 = (f32[2,3,16,256]{3,2,1,0:T(8,128)S(1)}, f32[2,3,16,256]{3,2,1,0:T(8,128)S(1)}, u32[]{:S(2)}, u32[]{:S(2)}) collective-permute-start(f32[2,3,16,256]{3,2,1,0:T(8,128)S(1)} %fusion.3), channel_id=1, source_target_pairs={{0,4},{1,5},{2,6},{3,7},{4,0},{5,1},{6,2},{7,3},{8,12},{9,13},{10,... | collective-permute-start | bytes 294920 | tf_op jit(solution)/shard_map/ppermute | solution.py:37
  41.6 2.2 %collective-permute-start.20 = (f32[2,3,16,256]{3,2,1,0:T(8,128)S(1)}, f32[2,3,16,256]{3,2,1,0:T(8,128)S(1)}, u32[]{:S(2)}, u32[]{:S(2)}) collective-permute-start(f32[2,3,16,256]{3,2,1,0:T(8,128)S(1)} %add_multiply_fusion), channel_id=1, source_target_pairs={{0,2},{1,3},{2,0},{3,1},{4,6},{5,7},{6,4},{7,5},{8,10},{9,11},{10,... | collective-permute-start | bytes 294920 | tf_op jit(solution)/shard_map/ppermute | solution.py:37
  43.8 0.9 collective-permute-start.19
  44.7 1.3 %collective-permute-start.18 = (f32[2,3,16,256]{3,2,1,0:T(8,128)S(1)}, f32[2,3,16,256]{3,2,1,0:T(8,128)S(1)}, u32[]{:S(2)}, u32[]{:S(2)}) collective-permute-start(f32[2,3,16,256]{3,2,1,0:T(8,128)S(1)} %add_multiply_fusion), channel_id=1, source_target_pairs={{0,3},{1,2},{2,1},{3,0},{4,7},{5,6},{6,5},{7,4},{8,11},{9,10},{10,... | collective-permute-start | bytes 294920 | tf_op jit(solution)/shard_map/ppermute | solution.py:37
  46.0 1.3 %collective-permute-start.9 = (f32[2,3,16,256]{3,2,1,0:T(8,128)S(1)}, f32[2,3,16,256]{3,2,1,0:T(8,128)S(1)}, u32[]{:S(2)}, u32[]{:S(2)}) collective-permute-start(f32[2,3,16,256]{3,2,1,0:T(8,128)S(1)} %add_multiply_fusion.1), channel_id=1, source_target_pairs={{0,16},{1,17},{2,18},{3,19},{4,20},{5,21},{6,22},{7,23},{8,24},{9,... | collective-permute-start | bytes 294920 | tf_op jit(solution)/shard_map/ppermute | solution.py:37
  48.9 1.3 %collective-permute-start.7 = (f32[2,3,16,256]{3,2,1,0:T(8,128)S(1)}, f32[2,3,16,256]{3,2,1,0:T(8,128)S(1)}, u32[]{:S(2)}, u32[]{:S(2)}) collective-permute-start(f32[2,3,16,256]{3,2,1,0:T(8,128)S(1)} %add_multiply_fusion.1), channel_id=1, source_target_pairs={{0,24},{1,25},{2,26},{3,27},{4,28},{5,29},{6,30},{7,31},{8,16},{9,... | collective-permute-start | bytes 294920 | tf_op jit(solution)/shard_map/ppermute | solution.py:37
  50.3 2.0 %collective-permute-done.9 = f32[2,3,16,256]{3,2,1,0:T(8,128)S(1)} collective-permute-done((f32[2,3,16,256]{3,2,1,0:T(8,128)S(1)}, f32[2,3,16,256]{3,2,1,0:T(8,128)S(1)}, u32[]{:S(2)}, u32[]{:S(2)}) %collective-permute-start.9) | collective-permute-done | bytes 98336 | tf_op jit(solution)/shard_map/ppermute | solution.py:37
  52.4 2.4 %collective-permute-done.7 = f32[2,3,16,256]{3,2,1,0:T(8,128)S(1)} collective-permute-done((f32[2,3,16,256]{3,2,1,0:T(8,128)S(1)}, f32[2,3,16,256]{3,2,1,0:T(8,128)S(1)}, u32[]{:S(2)}, u32[]{:S(2)}) %collective-permute-start.7) | collective-permute-done | bytes 98336 | tf_op jit(solution)/shard_map/ppermute | solution.py:37
  54.8 1.0 collective-permute-start.10
  55.7 1.5 %collective-permute-start.25 = (f32[8,3,16,256]{3,2,1,0:T(8,128)S(1)}, f32[8,3,16,256]{3,2,1,0:T(8,128)S(1)}, u32[]{:S(2)}, u32[]{:S(2)}) collective-permute-start(f32[8,3,16,256]{3,2,1,0:T(8,128)S(1)} %pad_maximum_fusion.1.refs_0_), channel_id=1, source_target_pairs={{0,24},{1,25},{2,26},{3,27},{4,28},{5,29},{6,30},{7,31},{8,16},{9,... | collective-permute-start | bytes 1179656 | tf_op jit(solution)/shard_map/ppermute | solution.py:26
  57.2 1.7 %collective-permute-start.24 = (f32[8,3,16,256]{3,2,1,0:T(8,128)S(1)}, f32[8,3,16,256]{3,2,1,0:T(8,128)S(1)}, u32[]{:S(2)}, u32[]{:S(2)}) collective-permute-start(f32[8,3,16,256]{3,2,1,0:T(8,128)S(1)} %pad_maximum_fusion.refs_1_), channel_id=1, source_target_pairs={{0,3},{1,2},{2,1},{3,0},{4,7},{5,6},{6,5},{7,4},{8,11},{9,10},{10,... | collective-permute-start | bytes 1179656 | tf_op jit(solution)/shard_map/ppermute | solution.py:26
  58.9 1.4 %collective-permute-done.22.refs_1_ = f32[8,3,16,256]{3,2,1,0:T(8,128)S(1)} collective-permute-done((f32[8,3,16,256]{3,2,1,0:T(8,128)S(1)}, f32[8,3,16,256]{3,2,1,0:T(8,128)S(1)}, u32[]{:S(2)}, u32[]{:S(2)}) %collective-permute-start.22) | collective-permute-done | bytes 393248 | tf_op jit(solution)/shard_map/ppermute | solution.py:26
  60.4 2.0 %collective-permute-start.23 = (f32[8,3,16,256]{3,2,1,0:T(8,128)S(1)}, f32[8,3,16,256]{3,2,1,0:T(8,128)S(1)}, u32[]{:S(2)}, u32[]{:S(2)}) collective-permute-start(f32[8,3,16,256]{3,2,1,0:T(8,128)S(1)} %collective-permute-done.22.refs_1_), channel_id=1, source_target_pairs={{0,24},{1,25},{2,26},{3,27},{4,28},{5,29},{6,30},{7,31},{8,16},{9,... | collective-permute-start | bytes 1179656 | tf_op jit(solution)/shard_map/ppermute | solution.py:26
  62.4 2.4 %pair_sums.5.refs_2_ = f32[16,512]{1,0:T(8,128)S(1)} custom-call(s32[2]{0:T(128)S(1)} %pad_add_fusion.place_ref, f32[2]{0:T(128)S(1)} %convert_element_type.3.weight_ref, f32[4]{0:T(128)S(1)} %copy-done.8, f32[2,128]{1,0:T(2,128)S(1)} %copy-done.7, f32[2,1024]{1,0:T(2,128)S(1)} %copy-done.6, bf16[2,128,512]{2,1,0:T(8,128)(2,1)S(1)} %copy-done.3, ...), custom_call_target="tpu_custom_call" | custom-call | flops 805306368 | bytes 1835008 | tf_op jit(solution)/shard_map/pair_sums/pallas_call | solution.py:216
  64.7 0.9 collective-permute-start.21
  65.7 1.7 %collective-permute-done.25.refs_0_ = f32[8,3,16,256]{3,2,1,0:T(8,128)S(1)} collective-permute-done((f32[8,3,16,256]{3,2,1,0:T(8,128)S(1)}, f32[8,3,16,256]{3,2,1,0:T(8,128)S(1)}, u32[]{:S(2)}, u32[]{:S(2)}) %collective-permute-start.25) | collective-permute-done | bytes 393248 | tf_op jit(solution)/shard_map/ppermute | solution.py:26
  67.4 2.1 %pair_sums.6.refs_2_ = f32[16,512]{1,0:T(8,128)S(1)} custom-call(s32[2]{0:T(128)S(1)} %pad_add_fusion.place_ref, f32[2]{0:T(128)S(1)} %convert_element_type.3.weight_ref, f32[4]{0:T(128)S(1)} %copy-done.8, f32[2,128]{1,0:T(2,128)S(1)} %copy-done.7, f32[2,1024]{1,0:T(2,128)S(1)} %copy-done.6, bf16[2,128,512]{2,1,0:T(8,128)(2,1)S(1)} %copy-done.3, ...), custom_call_target="tpu_custom_call" | custom-call | flops 805306368 | bytes 1835008 | tf_op jit(solution)/shard_map/pair_sums/pallas_call | solution.py:216
  69.5 2.1 %pair_sums.7.refs_1_ = f32[16,512]{1,0:T(8,128)S(1)} custom-call(s32[2]{0:T(128)S(1)} %pad_add_fusion.place_ref, f32[2]{0:T(128)S(1)} %convert_element_type.3.weight_ref, f32[4]{0:T(128)S(1)} %copy-done.8, f32[2,128]{1,0:T(2,128)S(1)} %copy-done.7, f32[2,1024]{1,0:T(2,128)S(1)} %copy-done.6, bf16[2,128,512]{2,1,0:T(8,128)(2,1)S(1)} %copy-done.3, ...), custom_call_target="tpu_custom_call" | custom-call | flops 805306368 | bytes 1835008 | tf_op jit(solution)/shard_map/pair_sums/pallas_call | solution.py:216
  71.6 1.7 %collective-permute-done.23.refs_0_ = f32[8,3,16,256]{3,2,1,0:T(8,128)S(1)} collective-permute-done((f32[8,3,16,256]{3,2,1,0:T(8,128)S(1)}, f32[8,3,16,256]{3,2,1,0:T(8,128)S(1)}, u32[]{:S(2)}, u32[]{:S(2)}) %collective-permute-start.23) | collective-permute-done | bytes 393248 | tf_op jit(solution)/shard_map/ppermute | solution.py:26
  73.3 1.5 %pair_sums.8.refs_1_ = f32[16,512]{1,0:T(8,128)S(1)} custom-call(s32[2]{0:T(128)S(1)} %pad_add_fusion.place_ref, f32[2]{0:T(128)S(1)} %convert_element_type.3.weight_ref, f32[4]{0:T(128)S(1)} %copy-done.8, f32[2,128]{1,0:T(2,128)S(1)} %copy-done.7, f32[2,1024]{1,0:T(2,128)S(1)} %copy-done.6, bf16[2,128,512]{2,1,0:T(8,128)(2,1)S(1)} %copy-done.3, ...), custom_call_target="tpu_custom_call" | custom-call | flops 402653184 | bytes 917504 | tf_op jit(solution)/shard_map/pair_sums/pallas_call | solution.py:216
  74.8 1.5 %pair_sums.9 = (f32[16,256]{1,0:T(8,128)S(1)}, f32[16,256]{1,0:T(8,128)S(1)}) custom-call(s32[2]{0:T(128)S(1)} %pad_add_fusion.place_ref, f32[2]{0:T(128)S(1)} %convert_element_type.3.weight_ref, f32[4]{0:T(128)S(1)} %copy-done.8, f32[2,128]{1,0:T(2,128)S(1)} %copy-done.7, f32[2,1024]{1,0:T(2,128)S(1)} %copy-done.6, bf16[2,128,512]{2,1,0:T(8,128)(2,1)S(1)} %copy-done.3, ...), custom_call_target="tpu_custom_call" | custom-call | flops 402653184 | bytes 917504 | tf_op jit(solution)/shard_map/pair_sums/pallas_call | solution.py:216
  76.4 1.2 %collective-permute-done.26 = f32[16,256]{1,0:T(8,128)S(1)} collective-permute-done((f32[16,256]{1,0:T(8,128)S(1)}, f32[16,256]{1,0:T(8,128)S(1)}, u32[]{:S(2)}, u32[]{:S(2)}) %collective-permute-start.26) | collective-permute-done | bytes 16416 | tf_op jit(solution)/shard_map/ppermute | solution.py:26
  77.6 17.8 %all_to_all.5.gathered = f32[32,16,256]{2,1,0:T(8,128)S(1)} all-to-all(f32[32,16,256]{2,1,0:T(8,128)S(1)} %broadcast_in_dim.2), channel_id=1, replica_groups=mesh['ka'=8,'wa'=32] {'wa'}, dimensions={0} | all-to-all | bytes 1048576 | tf_op jit(solution)/shard_map/all_to_all | solution.py:46
  95.4 1.3 %wing_sums.1 = f32[16,128]{1,0:T(8,128)S(1)} custom-call(s32[2]{0:T(128)S(1)} %pad_add_fusion.place_ref, f32[32,16,256]{2,1,0:T(8,128)S(1)} %all_to_all.5.gathered, bf16[128,16384]{1,0:T(8,128)(2,1)S(1)} %copy-done.4), custom_call_target="tpu_custom_call" | custom-call | flops 100663296 | bytes 4718592 | tf_op jit(solution)/shard_map/wing_sums/pallas_call | solution.py:275
  96.7 1.2 %collective-permute-done.27 = f32[16,128]{1,0:T(8,128)S(1)} collective-permute-done((f32[16,128]{1,0:T(8,128)S(1)}, f32[16,128]{1,0:T(8,128)S(1)}, u32[]{:S(2)}, u32[]{:S(2)}) %collective-permute-start.27) | collective-permute-done | bytes 8224 | tf_op jit(solution)/shard_map/ppermute | solution.py:26
  97.9 2.6 %collective-permute-start.28 = (f32[16,128]{1,0:T(8,128)S(1)}, f32[16,128]{1,0:T(8,128)S(1)}, u32[]{:S(2)}, u32[]{:S(2)}) collective-permute-start(f32[16,128]{1,0:T(8,128)S(1)} %add.114), channel_id=1, source_target_pairs={{0,64},{32,96},{64,0},{96,32},{128,192},{160,224},{192,128},{224,1... | collective-permute-start | bytes 24584 | tf_op jit(solution)/shard_map/ppermute | solution.py:26
  100.5 2.0 %collective-permute-done.28 = f32[16,128]{1,0:T(8,128)S(1)} collective-permute-done((f32[16,128]{1,0:T(8,128)S(1)}, f32[16,128]{1,0:T(8,128)S(1)}, u32[]{:S(2)}, u32[]{:S(2)}) %collective-permute-start.28) | collective-permute-done | bytes 8224 | tf_op jit(solution)/shard_map/ppermute | solution.py:26
  102.5 4.9 %collective-permute-start.29 = (f32[16,128]{1,0:T(8,128)S(1)}, f32[16,128]{1,0:T(8,128)S(1)}, u32[]{:S(2)}, u32[]{:S(2)}) collective-permute-start(f32[16,128]{1,0:T(8,128)S(1)} %add.115.one), channel_id=1, source_target_pairs={{0,192},{32,224},{64,128},{96,160},{128,64},{160,96},{192,0},{224,... | collective-permute-start | bytes 24584 | tf_op jit(solution)/shard_map/ppermute | solution.py:26
  107.4 1.6 %collective-permute-done.29.two = f32[16,128]{1,0:T(8,128)S(1)} collective-permute-done((f32[16,128]{1,0:T(8,128)S(1)}, f32[16,128]{1,0:T(8,128)S(1)}, u32[]{:S(2)}, u32[]{:S(2)}) %collective-permute-start.29) | collective-permute-done | bytes 8224 | tf_op jit(solution)/shard_map/ppermute | solution.py:26
  (60 shorter events, 6.5 us)
Async XLA Ops:
  0.7 3.4 %copy-start = (bf16[2,1024,2048]{2,1,0:T(8,128)(2,1)S(1)}, bf16[2,1024,2048]{2,1,0:T(8,128)(2,1)}, u32[]{:S(2)}) copy-start(bf16[2,1024,2048]{2,1,0:T(8,128)(2,1)} %cond_ref.7) | copy-start | bytes 25165828
  4.1 1.2 %copy-start.2 = (bf16[2,128,2048]{2,1,0:T(8,128)(2,1)S(1)}, bf16[2,128,2048]{2,1,0:T(8,128)(2,1)}, u32[]{:S(2)}) copy-start(bf16[2,128,2048]{2,1,0:T(8,128)(2,1)} %val_ref.7) | copy-start | bytes 3145732
  5.3 0.8 copy-start.5
  7.6 7.9 %collective-permute-start.12 = (f32[8,3,16,256]{3,2,1,0:T(8,128)S(1)}, f32[8,3,16,256]{3,2,1,0:T(8,128)S(1)}, u32[]{:S(2)}, u32[]{:S(2)}) collective-permute-start(f32[8,3,16,256]{3,2,1,0:T(8,128)S(1)} %get-tuple-element.21), channel_id=1, source_target_pairs={{0,8},{1,9},{2,10},{3,11},{4,12},{5,13},{6,14},{7,15},{8,0},{9,1},... | collective-permute-start | bytes 1179656 | tf_op jit(solution)/shard_map/ppermute | solution.py:37
  10.8 9.7 %collective-permute-start.1 = (f32[8,3,16,256]{3,2,1,0:T(8,128)S(1)}, f32[8,3,16,256]{3,2,1,0:T(8,128)S(1)}, u32[]{:S(2)}, u32[]{:S(2)}) collective-permute-start(f32[8,3,16,256]{3,2,1,0:T(8,128)S(1)} %get-tuple-element.17), channel_id=1, source_target_pairs={{0,1},{1,0},{2,3},{3,2},{4,5},{5,4},{6,7},{7,6},{8,9},{9,8},{10,11... | collective-permute-start | bytes 1179656 | tf_op jit(solution)/shard_map/ppermute | solution.py:37
  11.6 11.5 %collective-permute-start.11 = (f32[8,3,16,256]{3,2,1,0:T(8,128)S(1)}, f32[8,3,16,256]{3,2,1,0:T(8,128)S(1)}, u32[]{:S(2)}, u32[]{:S(2)}) collective-permute-start(f32[8,3,16,256]{3,2,1,0:T(8,128)S(1)} %get-tuple-element.19), channel_id=1, source_target_pairs={{0,8},{1,9},{2,10},{3,11},{4,12},{5,13},{6,14},{7,15},{8,0},{9,1},... | collective-permute-start | bytes 1179656 | tf_op jit(solution)/shard_map/ppermute | solution.py:37
  15.6 9.7 %collective-permute-start.13 = (f32[8,3,16,256]{3,2,1,0:T(8,128)S(1)}, f32[8,3,16,256]{3,2,1,0:T(8,128)S(1)}, u32[]{:S(2)}, u32[]{:S(2)}) collective-permute-start(f32[8,3,16,256]{3,2,1,0:T(8,128)S(1)} %add.101), channel_id=1, source_target_pairs={{0,24},{1,25},{2,26},{3,27},{4,28},{5,29},{6,30},{7,31},{8,16},{9,... | collective-permute-start | bytes 1179656 | tf_op jit(solution)/shard_map/ppermute | solution.py:37
  18.4 12.0 %collective-permute-start = (f32[8,3,16,256]{3,2,1,0:T(8,128)S(1)}, f32[8,3,16,256]{3,2,1,0:T(8,128)S(1)}, u32[]{:S(2)}, u32[]{:S(2)}) collective-permute-start(f32[8,3,16,256]{3,2,1,0:T(8,128)S(1)} %get-tuple-element.15), channel_id=1, source_target_pairs={{0,1},{1,0},{2,3},{3,2},{4,5},{5,4},{6,7},{7,6},{8,9},{9,8},{10,11... | collective-permute-start | bytes 1179656 | tf_op jit(solution)/shard_map/ppermute | solution.py:37
  20.4 38.5 %copy-start.9 = (s32[2]{0:T(128)S(1)}, s32[2]{0:T(128)}, u32[]{:S(2)}) copy-start(s32[2]{0:T(128)} %param.19) | copy-start | bytes 28
  20.4 41.9 %copy-start.1 = (bf16[2,1024,512]{2,1,0:T(8,128)(2,1)S(1)}, bf16[2,1024,512]{2,1,0:T(8,128)(2,1)}, u32[]{:S(2)}) copy-start(bf16[2,1024,512]{2,1,0:T(8,128)(2,1)} %orbit_cond.9) | copy-start | bytes 6291460
  20.5 41.9 %copy-start.3 = (bf16[2,128,512]{2,1,0:T(8,128)(2,1)S(1)}, bf16[2,128,512]{2,1,0:T(8,128)(2,1)}, u32[]{:S(2)}) copy-start(bf16[2,128,512]{2,1,0:T(8,128)(2,1)} %orbit_val.9) | copy-start | bytes 786436
  20.5 41.9 %copy-start.6 = (f32[2,1024]{1,0:T(2,128)S(1)}, f32[2,1024]{1,0:T(2,128)}, u32[]{:S(2)}) copy-start(f32[2,1024]{1,0:T(2,128)} %energy_cond.9) | copy-start | bytes 24580
  20.5 41.9 %copy-start.7 = (f32[2,128]{1,0:T(2,128)S(1)}, f32[2,128]{1,0:T(2,128)}, u32[]{:S(2)}) copy-start(f32[2,128]{1,0:T(2,128)} %energy_val.9) | copy-start | bytes 3076
  20.5 41.9 %copy-start.8 = (f32[4]{0:T(128)S(1)}, f32[4]{0:T(128)}, u32[]{:S(2)}) copy-start(f32[4]{0:T(128)} %freq_ref.9) | copy-start | bytes 52
  20.6 9.8 %collective-permute-start.2 = (f32[8,3,16,256]{3,2,1,0:T(8,128)S(1)}, f32[8,3,16,256]{3,2,1,0:T(8,128)S(1)}, u32[]{:S(2)}, u32[]{:S(2)}) collective-permute-start(f32[8,3,16,256]{3,2,1,0:T(8,128)S(1)} %add.88), channel_id=1, source_target_pairs={{0,3},{1,2},{2,1},{3,0},{4,7},{5,6},{6,5},{7,4},{8,11},{9,10},{10,... | collective-permute-start | bytes 1179656 | tf_op jit(solution)/shard_map/ppermute | solution.py:37
  25.3 7.2 %collective-permute-start.14 = (f32[2,3,16,256]{3,2,1,0:T(8,128)S(1)}, f32[2,3,16,256]{3,2,1,0:T(8,128)S(1)}, u32[]{:S(2)}, u32[]{:S(2)}) collective-permute-start(f32[2,3,16,256]{3,2,1,0:T(8,128)S(1)} %get-tuple-element.28), channel_id=1, source_target_pairs={{0,1},{1,0},{2,3},{3,2},{4,5},{5,4},{6,7},{7,6},{8,9},{9,8},{10,11... | collective-permute-start | bytes 294920 | tf_op jit(solution)/shard_map/ppermute | solution.py:37
  27.3 7.4 %collective-permute-start.15 = (f32[2,3,16,256]{3,2,1,0:T(8,128)S(1)}, f32[2,3,16,256]{3,2,1,0:T(8,128)S(1)}, u32[]{:S(2)}, u32[]{:S(2)}) collective-permute-start(f32[2,3,16,256]{3,2,1,0:T(8,128)S(1)} %get-tuple-element.27), channel_id=1, source_target_pairs={{0,3},{1,2},{2,1},{3,0},{4,7},{5,6},{6,5},{7,4},{8,11},{9,10},{10,... | collective-permute-start | bytes 294920 | tf_op jit(solution)/shard_map/ppermute | solution.py:37
  27.7 7.8 %collective-permute-start.16 = (f32[2,3,16,256]{3,2,1,0:T(8,128)S(1)}, f32[2,3,16,256]{3,2,1,0:T(8,128)S(1)}, u32[]{:S(2)}, u32[]{:S(2)}) collective-permute-start(f32[2,3,16,256]{3,2,1,0:T(8,128)S(1)} %get-tuple-element.26), channel_id=1, source_target_pairs={{0,2},{1,3},{2,0},{3,1},{4,6},{5,7},{6,4},{7,5},{8,10},{9,11},{10,... | collective-permute-start | bytes 294920 | tf_op jit(solution)/shard_map/ppermute | solution.py:37
  30.5 7.0 %collective-permute-start.3 = (f32[2,3,16,256]{3,2,1,0:T(8,128)S(1)}, f32[2,3,16,256]{3,2,1,0:T(8,128)S(1)}, u32[]{:S(2)}, u32[]{:S(2)}) collective-permute-start(f32[2,3,16,256]{3,2,1,0:T(8,128)S(1)} %get-tuple-element.31), channel_id=1, source_target_pairs={{0,8},{1,9},{2,10},{3,11},{4,12},{5,13},{6,14},{7,15},{8,0},{9,1},... | collective-permute-start | bytes 294920 | tf_op jit(solution)/shard_map/ppermute | solution.py:37
  30.6 9.0 %collective-permute-start.4 = (f32[2,3,16,256]{3,2,1,0:T(8,128)S(1)}, f32[2,3,16,256]{3,2,1,0:T(8,128)S(1)}, u32[]{:S(2)}, u32[]{:S(2)}) collective-permute-start(f32[2,3,16,256]{3,2,1,0:T(8,128)S(1)} %get-tuple-element.30), channel_id=1, source_target_pairs={{0,24},{1,25},{2,26},{3,27},{4,28},{5,29},{6,30},{7,31},{8,16},{9,... | collective-permute-start | bytes 294920 | tf_op jit(solution)/shard_map/ppermute | solution.py:37
  32.5 7.1 %collective-permute-start.5 = (f32[2,3,16,256]{3,2,1,0:T(8,128)S(1)}, f32[2,3,16,256]{3,2,1,0:T(8,128)S(1)}, u32[]{:S(2)}, u32[]{:S(2)}) collective-permute-start(f32[2,3,16,256]{3,2,1,0:T(8,128)S(1)} %get-tuple-element.29), channel_id=1, source_target_pairs={{0,16},{1,17},{2,18},{3,19},{4,20},{5,21},{6,22},{7,23},{8,24},{9,... | collective-permute-start | bytes 294920 | tf_op jit(solution)/shard_map/ppermute | solution.py:37
  35.5 6.1 %collective-permute-start.17 = (f32[2,3,16,256]{3,2,1,0:T(8,128)S(1)}, f32[2,3,16,256]{3,2,1,0:T(8,128)S(1)}, u32[]{:S(2)}, u32[]{:S(2)}) collective-permute-start(f32[2,3,16,256]{3,2,1,0:T(8,128)S(1)} %fusion.1), channel_id=1, source_target_pairs={{0,4},{1,5},{2,6},{3,7},{4,0},{5,1},{6,2},{7,3},{8,12},{9,13},{10,... | collective-permute-start | bytes 294920 | tf_op jit(solution)/shard_map/ppermute | solution.py:37
  39.6 6.4 %collective-permute-start.6 = (f32[2,3,16,256]{3,2,1,0:T(8,128)S(1)}, f32[2,3,16,256]{3,2,1,0:T(8,128)S(1)}, u32[]{:S(2)}, u32[]{:S(2)}) collective-permute-start(f32[2,3,16,256]{3,2,1,0:T(8,128)S(1)} %fusion.3), channel_id=1, source_target_pairs={{0,4},{1,5},{2,6},{3,7},{4,0},{5,1},{6,2},{7,3},{8,12},{9,13},{10,... | collective-permute-start | bytes 294920 | tf_op jit(solution)/shard_map/ppermute | solution.py:37
  41.6 7.3 %collective-permute-start.20 = (f32[2,3,16,256]{3,2,1,0:T(8,128)S(1)}, f32[2,3,16,256]{3,2,1,0:T(8,128)S(1)}, u32[]{:S(2)}, u32[]{:S(2)}) collective-permute-start(f32[2,3,16,256]{3,2,1,0:T(8,128)S(1)} %add_multiply_fusion), channel_id=1, source_target_pairs={{0,2},{1,3},{2,0},{3,1},{4,6},{5,7},{6,4},{7,5},{8,10},{9,11},{10,... | collective-permute-start | bytes 294920 | tf_op jit(solution)/shard_map/ppermute | solution.py:37
  43.8 6.4 %collective-permute-start.19 = (f32[2,3,16,256]{3,2,1,0:T(8,128)S(1)}, f32[2,3,16,256]{3,2,1,0:T(8,128)S(1)}, u32[]{:S(2)}, u32[]{:S(2)}) collective-permute-start(f32[2,3,16,256]{3,2,1,0:T(8,128)S(1)} %add_multiply_fusion), channel_id=1, source_target_pairs={{0,1},{1,0},{2,3},{3,2},{4,5},{5,4},{6,7},{7,6},{8,9},{9,8},{10,11... | collective-permute-start | bytes 294920 | tf_op jit(solution)/shard_map/ppermute | solution.py:37
  44.7 5.5 %collective-permute-start.18 = (f32[2,3,16,256]{3,2,1,0:T(8,128)S(1)}, f32[2,3,16,256]{3,2,1,0:T(8,128)S(1)}, u32[]{:S(2)}, u32[]{:S(2)}) collective-permute-start(f32[2,3,16,256]{3,2,1,0:T(8,128)S(1)} %add_multiply_fusion), channel_id=1, source_target_pairs={{0,3},{1,2},{2,1},{3,0},{4,7},{5,6},{6,5},{7,4},{8,11},{9,10},{10,... | collective-permute-start | bytes 294920 | tf_op jit(solution)/shard_map/ppermute | solution.py:37
  46.0 6.3 %collective-permute-start.9 = (f32[2,3,16,256]{3,2,1,0:T(8,128)S(1)}, f32[2,3,16,256]{3,2,1,0:T(8,128)S(1)}, u32[]{:S(2)}, u32[]{:S(2)}) collective-permute-start(f32[2,3,16,256]{3,2,1,0:T(8,128)S(1)} %add_multiply_fusion.1), channel_id=1, source_target_pairs={{0,16},{1,17},{2,18},{3,19},{4,20},{5,21},{6,22},{7,23},{8,24},{9,... | collective-permute-start | bytes 294920 | tf_op jit(solution)/shard_map/ppermute | solution.py:37
  47.3 5.0 %collective-permute-start.8 = (f32[2,3,16,256]{3,2,1,0:T(8,128)S(1)}, f32[2,3,16,256]{3,2,1,0:T(8,128)S(1)}, u32[]{:S(2)}, u32[]{:S(2)}) collective-permute-start(f32[2,3,16,256]{3,2,1,0:T(8,128)S(1)} %add_multiply_fusion.1), channel_id=1, source_target_pairs={{0,8},{1,9},{2,10},{3,11},{4,12},{5,13},{6,14},{7,15},{8,0},{9,1},... | collective-permute-start | bytes 294920 | tf_op jit(solution)/shard_map/ppermute | solution.py:37
  48.9 5.8 %collective-permute-start.7 = (f32[2,3,16,256]{3,2,1,0:T(8,128)S(1)}, f32[2,3,16,256]{3,2,1,0:T(8,128)S(1)}, u32[]{:S(2)}, u32[]{:S(2)}) collective-permute-start(f32[2,3,16,256]{3,2,1,0:T(8,128)S(1)} %add_multiply_fusion.1), channel_id=1, source_target_pairs={{0,24},{1,25},{2,26},{3,27},{4,28},{5,29},{6,30},{7,31},{8,16},{9,... | collective-permute-start | bytes 294920 | tf_op jit(solution)/shard_map/ppermute | solution.py:37
  50.2 10.1 %collective-permute-start.22 = (f32[8,3,16,256]{3,2,1,0:T(8,128)S(1)}, f32[8,3,16,256]{3,2,1,0:T(8,128)S(1)}, u32[]{:S(2)}, u32[]{:S(2)}) collective-permute-start(f32[8,3,16,256]{3,2,1,0:T(8,128)S(1)} %pad_maximum_fusion.1.refs_0_), channel_id=1, source_target_pairs={{0,8},{1,9},{2,10},{3,11},{4,12},{5,13},{6,14},{7,15},{8,0},{9,1},... | collective-permute-start | bytes 1179656 | tf_op jit(solution)/shard_map/ppermute | solution.py:26
  54.8 10.0 %collective-permute-start.10 = (f32[8,3,16,256]{3,2,1,0:T(8,128)S(1)}, f32[8,3,16,256]{3,2,1,0:T(8,128)S(1)}, u32[]{:S(2)}, u32[]{:S(2)}) collective-permute-start(f32[8,3,16,256]{3,2,1,0:T(8,128)S(1)} %pad_maximum_fusion.refs_1_), channel_id=1, source_target_pairs={{0,1},{1,0},{2,3},{3,2},{4,5},{5,4},{6,7},{7,6},{8,9},{9,8},{10,11... | collective-permute-start | bytes 1179656 | tf_op jit(solution)/shard_map/ppermute | solution.py:26
  55.7 11.6 %collective-permute-start.25 = (f32[8,3,16,256]{3,2,1,0:T(8,128)S(1)}, f32[8,3,16,256]{3,2,1,0:T(8,128)S(1)}, u32[]{:S(2)}, u32[]{:S(2)}) collective-permute-start(f32[8,3,16,256]{3,2,1,0:T(8,128)S(1)} %pad_maximum_fusion.1.refs_0_), channel_id=1, source_target_pairs={{0,24},{1,25},{2,26},{3,27},{4,28},{5,29},{6,30},{7,31},{8,16},{9,... | collective-permute-start | bytes 1179656 | tf_op jit(solution)/shard_map/ppermute | solution.py:26
  57.2 12.3 %collective-permute-start.24 = (f32[8,3,16,256]{3,2,1,0:T(8,128)S(1)}, f32[8,3,16,256]{3,2,1,0:T(8,128)S(1)}, u32[]{:S(2)}, u32[]{:S(2)}) collective-permute-start(f32[8,3,16,256]{3,2,1,0:T(8,128)S(1)} %pad_maximum_fusion.refs_1_), channel_id=1, source_target_pairs={{0,3},{1,2},{2,1},{3,0},{4,7},{5,6},{6,5},{7,4},{8,11},{9,10},{10,... | collective-permute-start | bytes 1179656 | tf_op jit(solution)/shard_map/ppermute | solution.py:26
  60.4 12.9 %collective-permute-start.23 = (f32[8,3,16,256]{3,2,1,0:T(8,128)S(1)}, f32[8,3,16,256]{3,2,1,0:T(8,128)S(1)}, u32[]{:S(2)}, u32[]{:S(2)}) collective-permute-start(f32[8,3,16,256]{3,2,1,0:T(8,128)S(1)} %collective-permute-done.22.refs_1_), channel_id=1, source_target_pairs={{0,24},{1,25},{2,26},{3,27},{4,28},{5,29},{6,30},{7,31},{8,16},{9,... | collective-permute-start | bytes 1179656 | tf_op jit(solution)/shard_map/ppermute | solution.py:26
  64.7 10.0 %collective-permute-start.21 = (f32[8,3,16,256]{3,2,1,0:T(8,128)S(1)}, f32[8,3,16,256]{3,2,1,0:T(8,128)S(1)}, u32[]{:S(2)}, u32[]{:S(2)}) collective-permute-start(f32[8,3,16,256]{3,2,1,0:T(8,128)S(1)} %collective-permute-done.10.refs_1_), channel_id=1, source_target_pairs={{0,3},{1,2},{2,1},{3,0},{4,7},{5,6},{6,5},{7,4},{8,11},{9,10},{10,... | collective-permute-start | bytes 1179656 | tf_op jit(solution)/shard_map/ppermute | solution.py:26
  71.6 23.8 %copy-start.4 = (bf16[128,16384]{1,0:T(8,128)(2,1)S(1)}, bf16[128,16384]{1,0:T(8,128)(2,1)}, u32[]{:S(2)}) copy-start(bf16[128,16384]{1,0:T(8,128)(2,1)} %zeta.1) | copy-start | bytes 12582916
  76.3 1.3 %collective-permute-start.26 = (f32[16,256]{1,0:T(8,128)S(1)}, f32[16,256]{1,0:T(8,128)S(1)}, u32[]{:S(2)}, u32[]{:S(2)}) collective-permute-start(f32[16,256]{1,0:T(8,128)S(1)} %get-tuple-element.25), channel_id=1, source_target_pairs={{0,32},{32,0},{64,96},{96,64},{128,160},{160,128},{192,224},{224,1... | collective-permute-start | bytes 49160 | tf_op jit(solution)/shard_map/ppermute | solution.py:26
  96.7 1.2 %collective-permute-start.27 = (f32[16,128]{1,0:T(8,128)S(1)}, f32[16,128]{1,0:T(8,128)S(1)}, u32[]{:S(2)}, u32[]{:S(2)}) collective-permute-start(f32[16,128]{1,0:T(8,128)S(1)} %wing_sums.1), channel_id=1, source_target_pairs={{0,32},{32,0},{64,96},{96,64},{128,160},{160,128},{192,224},{224,1... | collective-permute-start | bytes 24584 | tf_op jit(solution)/shard_map/ppermute | solution.py:26
  97.9 4.5 %collective-permute-start.28 = (f32[16,128]{1,0:T(8,128)S(1)}, f32[16,128]{1,0:T(8,128)S(1)}, u32[]{:S(2)}, u32[]{:S(2)}) collective-permute-start(f32[16,128]{1,0:T(8,128)S(1)} %add.114), channel_id=1, source_target_pairs={{0,64},{32,96},{64,0},{96,32},{128,192},{160,224},{192,128},{224,1... | collective-permute-start | bytes 24584 | tf_op jit(solution)/shard_map/ppermute | solution.py:26
  102.5 6.5 %collective-permute-start.29 = (f32[16,128]{1,0:T(8,128)S(1)}, f32[16,128]{1,0:T(8,128)S(1)}, u32[]{:S(2)}, u32[]{:S(2)}) collective-permute-start(f32[16,128]{1,0:T(8,128)S(1)} %add.115.one), channel_id=1, source_target_pairs={{0,192},{32,224},{64,128},{96,160},{128,64},{160,96},{192,0},{224,... | collective-permute-start | bytes 24584 | tf_op jit(solution)/shard_map/ppermute | solution.py:26

commit v10 on v9

--- a/solution.py
+++ b/solution.py
@@ -323,12 +323,14 @@
     parts = [(own, second, first, both) for (both, first), (second, own) in zip(sends, keeps)]
     chunks = [gathered_chunks(k, parts[k], pw_factor) for k in range(kcount)]
     operands = (place, weights, freqs, energy_val, energy_cond, orbit_val, orbit_cond)
-    own, second, first = chunks[0]
-    chunks[0] = (own, second, first, around(first, 0, 1))
-    own, second, first = chunks[1]
     pair = pair_sums(((0, (0,)), (1, (0,))), *operands, chunks, [], 1)
-    first, pair = lax.optimization_barrier((first, pair))
-    chunks[1] = (own, second, first, around(first, 1, 1))
+    for k in range(kcount):
+        own, second, first = chunks[k]
+        if k == 0:
+            first, pair = lax.optimization_barrier((first, pair))
+        half = first.shape[0] // 2
+        passed = jnp.concatenate([around(first[:half], k, 1), around(second[half:], k, 0)])
+        chunks[k] = (own, second, first, passed)
     for k in range(kcount):
         pair = pair_sums(((k, (1, 2)),), *operands, chunks, pair, 1)
     pair = pair_sums(((0, (3,)),), *operands, chunks, pair, 1)

time: 110 us -> 110 us (level)
  waiting for transfers between devices: 22.8 us -> 17.3 us
  starting transfers between devices: 44.4 us -> 49.5 us
    ppermute x10 -> x12, starting transfers between devices: 14.7 us -> 19 us  [swap(): lax.ppermute(value, axis, [(i, i ^ mask) for i in range(lax.axis_size(axi...]
    ppermute x10 -> x12, waiting for transfers between devices: 10.8 us -> 7.93 us  [swap(): lax.ppermute(value, axis, [(i, i ^ mask) for i in range(lax.axis_size(axi...]
    ppermute x20, waiting for transfers between devices: 12 us -> 9.37 us  [cross(): return lax.ppermute(value, ('ka', 'wa'), pairs)]
  transfers between devices with their start and end apart: 30 -> 32, of which waited for: 16 -> 13; matrix products, arithmetic and copies ran while one was open for 0% -> 0% of each run, Pallas kernels for 12% -> 12%
where the time goes in v10:
time: 110 us
  starting transfers between devices  49.5 us (45%)
  blocking collectives  18.2 us (17%)
  Pallas kernels  17.7 us (16%)
  waiting for transfers between devices  17.3 us (16%)
  local copies, waits for them, and re-layouts  5.52 us (5%)
    ppermute x20, starting transfers between devices, cross(): return lax.ppermute(value, ('ka', 'wa'), pairs)  30.5 us
    ppermute x12, starting transfers between devices, swap(): lax.ppermute(value, axis, [(i, i ^ mask) for i in range(lax.axis_size(axi...  19 us
    all_to_all x1, blocking collectives, everyone(): lax.all_to_all(jnp.broadcast_to(value[None], (parts,) + value.shape), axi...  18.2 us
    pallas_call x5, Pallas kernels, pair_sums(): pl.pallas_call(functools.partial(pair_kernel, groups), out_shape=[jax.Sha...  9.5 us
    ppermute x20, waiting for transfers between devices, cross(): return lax.ppermute(value, ('ka', 'wa'), pairs)  9.37 us
    ppermute x12, waiting for transfers between devices, swap(): lax.ppermute(value, axis, [(i, i ^ mask) for i in range(lax.axis_size(axi...  7.93 us
    pallas_call x4, Pallas kernels, partial_momentum(): pl.pallas_call(functools.partial(momentum_kernel, kpoint, quarters), out_...  6.24 us
    unnamed x20, local copies, waits for them, and re-layouts  5.41 us
  transfers between devices with their start and end apart: 32, of which 13 were waited for; matrix products, arithmetic and copies ran while one was open for 0% of the time, Pallas kernels for 12%

profile of v10, /device:TPU:8, one launch (start us, length us, event | category | flops | bytes accessed | tf_op | source)
XLA Modules:
  0.0 109.7 jit_solution(12070087934424616112)
XLA Ops:
  0.7 3.4 %copy-done = bf16[2,1024,2048]{2,1,0:T(8,128)(2,1)S(1)} copy-done((bf16[2,1024,2048]{2,1,0:T(8,128)(2,1)S(1)}, bf16[2,1024,2048]{2,1,0:T(8,128)(2,1)}, u32[]{:S(2)}) %copy-start) | copy-done | bytes 8388632
  4.1 1.2 %copy-done.2 = bf16[2,128,2048]{2,1,0:T(8,128)(2,1)S(1)} copy-done((bf16[2,128,2048]{2,1,0:T(8,128)(2,1)S(1)}, bf16[2,128,2048]{2,1,0:T(8,128)(2,1)}, u32[]{:S(2)}) %copy-start.2) | copy-done | bytes 1048600
  5.3 0.8 copy-done.5
  6.1 1.6 %partial_momentum.7 = (f32[8,3,16,256]{3,2,1,0:T(8,128)S(1)}, f32[8,3,16,256]{3,2,1,0:T(8,128)S(1)}) custom-call(s32[2]{0:T(128)S(1)} %pad_add_fusion.place_ref, bf16[2,128,2048]{2,1,0:T(8,128)(2,1)S(1)} %copy-done.2, s32[3,2048]{1,0:T(4,128)S(1)} %copy-done.5, bf16[2,1024,2048]{2,1,0:T(8,128)(2,1)S(1)} %copy-done), custom_call_target="tpu_custom_call" | custom-call | flops 805306368 | bytes 3407872 | tf_op jit(solution)/shard_map/partial_momentum/pallas_call | solution.py:98
  7.6 1.6 %collective-permute-start.15 = (f32[8,3,16,256]{3,2,1,0:T(8,128)S(1)}, f32[8,3,16,256]{3,2,1,0:T(8,128)S(1)}, u32[]{:S(2)}, u32[]{:S(2)}) collective-permute-start(f32[8,3,16,256]{3,2,1,0:T(8,128)S(1)} %get-tuple-element.21), channel_id=1, source_target_pairs={{0,8},{1,9},{2,10},{3,11},{4,12},{5,13},{6,14},{7,15},{8,0},{9,1},... | collective-permute-start | bytes 1179656 | tf_op jit(solution)/shard_map/ppermute | solution.py:37
  9.2 1.6 %partial_momentum.5 = (f32[8,3,16,256]{3,2,1,0:T(8,128)S(1)}, f32[8,3,16,256]{3,2,1,0:T(8,128)S(1)}) custom-call(s32[2]{0:T(128)S(1)} %pad_add_fusion.place_ref, bf16[2,128,2048]{2,1,0:T(8,128)(2,1)S(1)} %copy-done.2, s32[3,2048]{1,0:T(4,128)S(1)} %copy-done.5, bf16[2,1024,2048]{2,1,0:T(8,128)(2,1)S(1)} %copy-done), custom_call_target="tpu_custom_call" | custom-call | flops 805306368 | bytes 3407872 | tf_op jit(solution)/shard_map/partial_momentum/pallas_call | solution.py:98
  10.8 0.8 collective-permute-start.1
  11.6 2.0 %collective-permute-start.14 = (f32[8,3,16,256]{3,2,1,0:T(8,128)S(1)}, f32[8,3,16,256]{3,2,1,0:T(8,128)S(1)}, u32[]{:S(2)}, u32[]{:S(2)}) collective-permute-start(f32[8,3,16,256]{3,2,1,0:T(8,128)S(1)} %get-tuple-element.19), channel_id=1, source_target_pairs={{0,8},{1,9},{2,10},{3,11},{4,12},{5,13},{6,14},{7,15},{8,0},{9,1},... | collective-permute-start | bytes 1179656 | tf_op jit(solution)/shard_map/ppermute | solution.py:37
  13.6 1.6 %partial_momentum.6 = (f32[8,3,16,256]{3,2,1,0:T(8,128)S(1)}, f32[8,3,16,256]{3,2,1,0:T(8,128)S(1)}) custom-call(s32[2]{0:T(128)S(1)} %pad_add_fusion.place_ref, bf16[2,128,2048]{2,1,0:T(8,128)(2,1)S(1)} %copy-done.2, s32[3,2048]{1,0:T(4,128)S(1)} %copy-done.5, bf16[2,1024,2048]{2,1,0:T(8,128)(2,1)S(1)} %copy-done), custom_call_target="tpu_custom_call" | custom-call | flops 805306368 | bytes 3407872 | tf_op jit(solution)/shard_map/partial_momentum/pallas_call | solution.py:98
  15.6 2.8 %collective-permute-start.16 = (f32[8,3,16,256]{3,2,1,0:T(8,128)S(1)}, f32[8,3,16,256]{3,2,1,0:T(8,128)S(1)}, u32[]{:S(2)}, u32[]{:S(2)}) collective-permute-start(f32[8,3,16,256]{3,2,1,0:T(8,128)S(1)} %add.101), channel_id=1, source_target_pairs={{0,24},{1,25},{2,26},{3,27},{4,28},{5,29},{6,30},{7,31},{8,16},{9,... | collective-permute-start | bytes 1179656 | tf_op jit(solution)/shard_map/ppermute | solution.py:37
  18.9 1.6 %partial_momentum.4 = (f32[8,3,16,256]{3,2,1,0:T(8,128)S(1)}, f32[8,3,16,256]{3,2,1,0:T(8,128)S(1)}) custom-call(s32[2]{0:T(128)S(1)} %pad_add_fusion.place_ref, bf16[2,128,2048]{2,1,0:T(8,128)(2,1)S(1)} %copy-done.2, s32[3,2048]{1,0:T(4,128)S(1)} %copy-done.5, bf16[2,1024,2048]{2,1,0:T(8,128)(2,1)S(1)} %copy-done), custom_call_target="tpu_custom_call" | custom-call | flops 805306368 | bytes 3407872 | tf_op jit(solution)/shard_map/partial_momentum/pallas_call | solution.py:98
  20.6 2.5 %collective-permute-start.2 = (f32[8,3,16,256]{3,2,1,0:T(8,128)S(1)}, f32[8,3,16,256]{3,2,1,0:T(8,128)S(1)}, u32[]{:S(2)}, u32[]{:S(2)}) collective-permute-start(f32[8,3,16,256]{3,2,1,0:T(8,128)S(1)} %add.88), channel_id=1, source_target_pairs={{0,3},{1,2},{2,1},{3,0},{4,7},{5,6},{6,5},{7,4},{8,11},{9,10},{10,... | collective-permute-start | bytes 1179656 | tf_op jit(solution)/shard_map/ppermute | solution.py:37
  23.1 2.1 %collective-permute-done.16 = f32[8,3,16,256]{3,2,1,0:T(8,128)S(1)} collective-permute-done((f32[8,3,16,256]{3,2,1,0:T(8,128)S(1)}, f32[8,3,16,256]{3,2,1,0:T(8,128)S(1)}, u32[]{:S(2)}, u32[]{:S(2)}) %collective-permute-start.16) | collective-permute-done | bytes 393248 | tf_op jit(solution)/shard_map/ppermute | solution.py:37
  25.3 2.0 %collective-permute-start.17 = (f32[2,3,16,256]{3,2,1,0:T(8,128)S(1)}, f32[2,3,16,256]{3,2,1,0:T(8,128)S(1)}, u32[]{:S(2)}, u32[]{:S(2)}) collective-permute-start(f32[2,3,16,256]{3,2,1,0:T(8,128)S(1)} %get-tuple-element.28), channel_id=1, source_target_pairs={{0,1},{1,0},{2,3},{3,2},{4,5},{5,4},{6,7},{7,6},{8,9},{9,8},{10,11... | collective-permute-start | bytes 294920 | tf_op jit(solution)/shard_map/ppermute | solution.py:37
  27.7 1.8 %collective-permute-start.19 = (f32[2,3,16,256]{3,2,1,0:T(8,128)S(1)}, f32[2,3,16,256]{3,2,1,0:T(8,128)S(1)}, u32[]{:S(2)}, u32[]{:S(2)}) collective-permute-start(f32[2,3,16,256]{3,2,1,0:T(8,128)S(1)} %get-tuple-element.26), channel_id=1, source_target_pairs={{0,2},{1,3},{2,0},{3,1},{4,6},{5,7},{6,4},{7,5},{8,10},{9,11},{10,... | collective-permute-start | bytes 294920 | tf_op jit(solution)/shard_map/ppermute | solution.py:37
  29.5 0.9 collective-permute-done
  30.6 1.3 %collective-permute-start.4 = (f32[2,3,16,256]{3,2,1,0:T(8,128)S(1)}, f32[2,3,16,256]{3,2,1,0:T(8,128)S(1)}, u32[]{:S(2)}, u32[]{:S(2)}) collective-permute-start(f32[2,3,16,256]{3,2,1,0:T(8,128)S(1)} %get-tuple-element.30), channel_id=1, source_target_pairs={{0,24},{1,25},{2,26},{3,27},{4,28},{5,29},{6,30},{7,31},{8,16},{9,... | collective-permute-start | bytes 294920 | tf_op jit(solution)/shard_map/ppermute | solution.py:37
  32.5 2.2 %collective-permute-start.5 = (f32[2,3,16,256]{3,2,1,0:T(8,128)S(1)}, f32[2,3,16,256]{3,2,1,0:T(8,128)S(1)}, u32[]{:S(2)}, u32[]{:S(2)}) collective-permute-start(f32[2,3,16,256]{3,2,1,0:T(8,128)S(1)} %get-tuple-element.29), channel_id=1, source_target_pairs={{0,16},{1,17},{2,18},{3,19},{4,20},{5,21},{6,22},{7,23},{8,24},{9,... | collective-permute-start | bytes 294920 | tf_op jit(solution)/shard_map/ppermute | solution.py:37
  34.7 0.8 collective-permute-done.19
  35.5 2.0 %collective-permute-start.20 = (f32[2,3,16,256]{3,2,1,0:T(8,128)S(1)}, f32[2,3,16,256]{3,2,1,0:T(8,128)S(1)}, u32[]{:S(2)}, u32[]{:S(2)}) collective-permute-start(f32[2,3,16,256]{3,2,1,0:T(8,128)S(1)} %fusion.1), channel_id=1, source_target_pairs={{0,4},{1,5},{2,6},{3,7},{4,0},{5,1},{6,2},{7,3},{8,12},{9,13},{10,... | collective-permute-start | bytes 294920 | tf_op jit(solution)/shard_map/ppermute | solution.py:37
  37.5 2.0 %collective-permute-done.4 = f32[2,3,16,256]{3,2,1,0:T(8,128)S(1)} collective-permute-done((f32[2,3,16,256]{3,2,1,0:T(8,128)S(1)}, f32[2,3,16,256]{3,2,1,0:T(8,128)S(1)}, u32[]{:S(2)}, u32[]{:S(2)}) %collective-permute-start.4) | collective-permute-done | bytes 98336 | tf_op jit(solution)/shard_map/ppermute | solution.py:37
  39.6 2.0 %collective-permute-start.6 = (f32[2,3,16,256]{3,2,1,0:T(8,128)S(1)}, f32[2,3,16,256]{3,2,1,0:T(8,128)S(1)}, u32[]{:S(2)}, u32[]{:S(2)}) collective-permute-start(f32[2,3,16,256]{3,2,1,0:T(8,128)S(1)} %fusion.3), channel_id=1, source_target_pairs={{0,4},{1,5},{2,6},{3,7},{4,0},{5,1},{6,2},{7,3},{8,12},{9,13},{10,... | collective-permute-start | bytes 294920 | tf_op jit(solution)/shard_map/ppermute | solution.py:37
  41.6 1.0 collective-permute-start.21
  42.6 2.4 %collective-permute-start.22 = (f32[2,3,16,256]{3,2,1,0:T(8,128)S(1)}, f32[2,3,16,256]{3,2,1,0:T(8,128)S(1)}, u32[]{:S(2)}, u32[]{:S(2)}) collective-permute-start(f32[2,3,16,256]{3,2,1,0:T(8,128)S(1)} %add_multiply_fusion), channel_id=1, source_target_pairs={{0,1},{1,0},{2,3},{3,2},{4,5},{5,4},{6,7},{7,6},{8,9},{9,8},{10,11... | collective-permute-start | bytes 294920 | tf_op jit(solution)/shard_map/ppermute | solution.py:37
  45.4 1.3 %collective-permute-start.7 = (f32[2,3,16,256]{3,2,1,0:T(8,128)S(1)}, f32[2,3,16,256]{3,2,1,0:T(8,128)S(1)}, u32[]{:S(2)}, u32[]{:S(2)}) collective-permute-start(f32[2,3,16,256]{3,2,1,0:T(8,128)S(1)} %add_multiply_fusion.1), channel_id=1, source_target_pairs={{0,24},{1,25},{2,26},{3,27},{4,28},{5,29},{6,30},{7,31},{8,16},{9,... | collective-permute-start | bytes 294920 | tf_op jit(solution)/shard_map/ppermute | solution.py:37
  47.3 2.9 %collective-permute-start.9 = (f32[2,3,16,256]{3,2,1,0:T(8,128)S(1)}, f32[2,3,16,256]{3,2,1,0:T(8,128)S(1)}, u32[]{:S(2)}, u32[]{:S(2)}) collective-permute-start(f32[2,3,16,256]{3,2,1,0:T(8,128)S(1)} %add_multiply_fusion.1), channel_id=1, source_target_pairs={{0,16},{1,17},{2,18},{3,19},{4,20},{5,21},{6,22},{7,23},{8,24},{9,... | collective-permute-start | bytes 294920 | tf_op jit(solution)/shard_map/ppermute | solution.py:37
  50.2 0.9 collective-permute-done.23
  51.2 0.8 collective-permute-start.24
  52.0 2.0 %collective-permute-start.26 = (f32[8,3,16,256]{3,2,1,0:T(8,128)S(1)}, f32[8,3,16,256]{3,2,1,0:T(8,128)S(1)}, u32[]{:S(2)}, u32[]{:S(2)}) collective-permute-start(f32[8,3,16,256]{3,2,1,0:T(8,128)S(1)} %pad_maximum_fusion.2.refs_0_), channel_id=1, source_target_pairs={{0,24},{1,25},{2,26},{3,27},{4,28},{5,29},{6,30},{7,31},{8,16},{9,... | collective-permute-start | bytes 1179656 | tf_op jit(solution)/shard_map/ppermute | solution.py:26
  54.0 1.6 %collective-permute-done.9 = f32[2,3,16,256]{3,2,1,0:T(8,128)S(1)} collective-permute-done((f32[2,3,16,256]{3,2,1,0:T(8,128)S(1)}, f32[2,3,16,256]{3,2,1,0:T(8,128)S(1)}, u32[]{:S(2)}, u32[]{:S(2)}) %collective-permute-start.9) | collective-permute-done | bytes 98336 | tf_op jit(solution)/shard_map/ppermute | solution.py:37
  55.6 2.5 %collective-permute-start.10 = (f32[8,3,16,256]{3,2,1,0:T(8,128)S(1)}, f32[8,3,16,256]{3,2,1,0:T(8,128)S(1)}, u32[]{:S(2)}, u32[]{:S(2)}) collective-permute-start(f32[8,3,16,256]{3,2,1,0:T(8,128)S(1)} %pad_maximum_fusion.refs_1_), channel_id=1, source_target_pairs={{0,1},{1,0},{2,3},{3,2},{4,5},{5,4},{6,7},{7,6},{8,9},{9,8},{10,11... | collective-permute-start | bytes 1179656 | tf_op jit(solution)/shard_map/ppermute | solution.py:26
  58.1 1.7 %collective-permute-start.12 = (f32[8,3,16,256]{3,2,1,0:T(8,128)S(1)}, f32[8,3,16,256]{3,2,1,0:T(8,128)S(1)}, u32[]{:S(2)}, u32[]{:S(2)}) collective-permute-start(f32[8,3,16,256]{3,2,1,0:T(8,128)S(1)} %pad_maximum_fusion.refs_1_), channel_id=1, source_target_pairs={{0,3},{1,2},{2,1},{3,0},{4,7},{5,6},{6,5},{7,4},{8,11},{9,10},{10,... | collective-permute-start | bytes 1179656 | tf_op jit(solution)/shard_map/ppermute | solution.py:26
  59.9 2.4 %pair_sums.5.refs_2_ = f32[16,512]{1,0:T(8,128)S(1)} custom-call(s32[2]{0:T(128)S(1)} %pad_add_fusion.place_ref, f32[2]{0:T(128)S(1)} %convert_element_type.3.weight_ref, f32[4]{0:T(128)S(1)} %copy-done.8, f32[2,128]{1,0:T(2,128)S(1)} %copy-done.7, f32[2,1024]{1,0:T(2,128)S(1)} %copy-done.6, bf16[2,128,512]{2,1,0:T(8,128)(2,1)S(1)} %copy-done.3, ...), custom_call_target="tpu_custom_call" | custom-call | flops 805306368 | bytes 1835008 | tf_op jit(solution)/shard_map/pair_sums/pallas_call | solution.py:216
  62.3 1.6 %collective-permute-start.25 = (f32[4,3,16,256]{3,2,1,0:T(8,128)S(1)}, f32[4,3,16,256]{3,2,1,0:T(8,128)S(1)}, u32[]{:S(2)}, u32[]{:S(2)}) collective-permute-start(f32[4,3,16,256]{3,2,1,0:T(8,128)S(1)} %slice.110), channel_id=1, source_target_pairs={{0,24},{1,25},{2,26},{3,27},{4,28},{5,29},{6,30},{7,31},{8,16},{9,... | collective-permute-start | bytes 589832 | tf_op jit(solution)/shard_map/ppermute | solution.py:26
  64.0 1.7 %collective-permute-start.11 = (f32[4,3,16,256]{3,2,1,0:T(8,128)S(1)}, f32[4,3,16,256]{3,2,1,0:T(8,128)S(1)}, u32[]{:S(2)}, u32[]{:S(2)}) collective-permute-start(f32[4,3,16,256]{3,2,1,0:T(8,128)S(1)} %slice.120), channel_id=1, source_target_pairs={{0,3},{1,2},{2,1},{3,0},{4,7},{5,6},{6,5},{7,4},{8,11},{9,10},{10,... | collective-permute-start | bytes 589832 | tf_op jit(solution)/shard_map/ppermute | solution.py:26
  65.7 2.3 %collective-permute-done.12.refs_0_ = f32[8,3,16,256]{3,2,1,0:T(8,128)S(1)} collective-permute-done((f32[8,3,16,256]{3,2,1,0:T(8,128)S(1)}, f32[8,3,16,256]{3,2,1,0:T(8,128)S(1)}, u32[]{:S(2)}, u32[]{:S(2)}) %collective-permute-start.12) | collective-permute-done | bytes 393248 | tf_op jit(solution)/shard_map/ppermute | solution.py:26
  68.4 2.1 %pair_sums.6.refs_2_ = f32[16,512]{1,0:T(8,128)S(1)} custom-call(s32[2]{0:T(128)S(1)} %pad_add_fusion.place_ref, f32[2]{0:T(128)S(1)} %convert_element_type.3.weight_ref, f32[4]{0:T(128)S(1)} %copy-done.8, f32[2,128]{1,0:T(2,128)S(1)} %copy-done.7, f32[2,1024]{1,0:T(2,128)S(1)} %copy-done.6, bf16[2,128,512]{2,1,0:T(8,128)(2,1)S(1)} %copy-done.3, ...), custom_call_target="tpu_custom_call" | custom-call | flops 805306368 | bytes 1835008 | tf_op jit(solution)/shard_map/pair_sums/pallas_call | solution.py:216
  70.5 2.1 %pair_sums.7.refs_1_ = f32[16,512]{1,0:T(8,128)S(1)} custom-call(s32[2]{0:T(128)S(1)} %pad_add_fusion.place_ref, f32[2]{0:T(128)S(1)} %convert_element_type.3.weight_ref, f32[4]{0:T(128)S(1)} %copy-done.8, f32[2,128]{1,0:T(2,128)S(1)} %copy-done.7, f32[2,1024]{1,0:T(2,128)S(1)} %copy-done.6, bf16[2,128,512]{2,1,0:T(8,128)(2,1)S(1)} %copy-done.3, ...), custom_call_target="tpu_custom_call" | custom-call | flops 805306368 | bytes 1835008 | tf_op jit(solution)/shard_map/pair_sums/pallas_call | solution.py:216
  72.7 1.5 %pair_sums.8.refs_1_ = f32[16,512]{1,0:T(8,128)S(1)} custom-call(s32[2]{0:T(128)S(1)} %pad_add_fusion.place_ref, f32[2]{0:T(128)S(1)} %convert_element_type.3.weight_ref, f32[4]{0:T(128)S(1)} %copy-done.8, f32[2,128]{1,0:T(2,128)S(1)} %copy-done.7, f32[2,1024]{1,0:T(2,128)S(1)} %copy-done.6, bf16[2,128,512]{2,1,0:T(8,128)(2,1)S(1)} %copy-done.3, ...), custom_call_target="tpu_custom_call" | custom-call | flops 402653184 | bytes 917504 | tf_op jit(solution)/shard_map/pair_sums/pallas_call | solution.py:216
  74.2 1.5 %pair_sums.9 = (f32[16,256]{1,0:T(8,128)S(1)}, f32[16,256]{1,0:T(8,128)S(1)}) custom-call(s32[2]{0:T(128)S(1)} %pad_add_fusion.place_ref, f32[2]{0:T(128)S(1)} %convert_element_type.3.weight_ref, f32[4]{0:T(128)S(1)} %copy-done.8, f32[2,128]{1,0:T(2,128)S(1)} %copy-done.7, f32[2,1024]{1,0:T(2,128)S(1)} %copy-done.6, bf16[2,128,512]{2,1,0:T(8,128)(2,1)S(1)} %copy-done.3, ...), custom_call_target="tpu_custom_call" | custom-call | flops 402653184 | bytes 917504 | tf_op jit(solution)/shard_map/pair_sums/pallas_call | solution.py:216
  76.0 1.2 %collective-permute-done.28 = f32[16,256]{1,0:T(8,128)S(1)} collective-permute-done((f32[16,256]{1,0:T(8,128)S(1)}, f32[16,256]{1,0:T(8,128)S(1)}, u32[]{:S(2)}, u32[]{:S(2)}) %collective-permute-start.28) | collective-permute-done | bytes 16416 | tf_op jit(solution)/shard_map/ppermute | solution.py:26
  77.3 18.2 %all_to_all.5.gathered = f32[32,16,256]{2,1,0:T(8,128)S(1)} all-to-all(f32[32,16,256]{2,1,0:T(8,128)S(1)} %broadcast_in_dim.2), channel_id=1, replica_groups=mesh['ka'=8,'wa'=32] {'wa'}, dimensions={0} | all-to-all | bytes 1048576 | tf_op jit(solution)/shard_map/all_to_all | solution.py:46
  95.5 1.3 %wing_sums.1 = f32[16,128]{1,0:T(8,128)S(1)} custom-call(s32[2]{0:T(128)S(1)} %pad_add_fusion.place_ref, f32[32,16,256]{2,1,0:T(8,128)S(1)} %all_to_all.5.gathered, bf16[128,16384]{1,0:T(8,128)(2,1)S(1)} %copy-done.4), custom_call_target="tpu_custom_call" | custom-call | flops 100663296 | bytes 4718592 | tf_op jit(solution)/shard_map/wing_sums/pallas_call | solution.py:275
  96.8 1.2 %collective-permute-done.29 = f32[16,128]{1,0:T(8,128)S(1)} collective-permute-done((f32[16,128]{1,0:T(8,128)S(1)}, f32[16,128]{1,0:T(8,128)S(1)}, u32[]{:S(2)}, u32[]{:S(2)}) %collective-permute-start.29) | collective-permute-done | bytes 8224 | tf_op jit(solution)/shard_map/ppermute | solution.py:26
  98.0 3.3 %collective-permute-start.30 = (f32[16,128]{1,0:T(8,128)S(1)}, f32[16,128]{1,0:T(8,128)S(1)}, u32[]{:S(2)}, u32[]{:S(2)}) collective-permute-start(f32[16,128]{1,0:T(8,128)S(1)} %add.114), channel_id=1, source_target_pairs={{0,64},{32,96},{64,0},{96,32},{128,192},{160,224},{192,128},{224,1... | collective-permute-start | bytes 24584 | tf_op jit(solution)/shard_map/ppermute | solution.py:26
  101.2 1.6 %collective-permute-done.30 = f32[16,128]{1,0:T(8,128)S(1)} collective-permute-done((f32[16,128]{1,0:T(8,128)S(1)}, f32[16,128]{1,0:T(8,128)S(1)}, u32[]{:S(2)}, u32[]{:S(2)}) %collective-permute-start.30) | collective-permute-done | bytes 8224 | tf_op jit(solution)/shard_map/ppermute | solution.py:26
  102.9 4.5 %collective-permute-start.31 = (f32[16,128]{1,0:T(8,128)S(1)}, f32[16,128]{1,0:T(8,128)S(1)}, u32[]{:S(2)}, u32[]{:S(2)}) collective-permute-start(f32[16,128]{1,0:T(8,128)S(1)} %add.115.one), channel_id=1, source_target_pairs={{0,192},{32,224},{64,128},{96,160},{128,64},{160,96},{192,0},{224,... | collective-permute-start | bytes 24584 | tf_op jit(solution)/shard_map/ppermute | solution.py:26
  107.4 1.6 %collective-permute-done.31.two = f32[16,128]{1,0:T(8,128)S(1)} collective-permute-done((f32[16,128]{1,0:T(8,128)S(1)}, f32[16,128]{1,0:T(8,128)S(1)}, u32[]{:S(2)}, u32[]{:S(2)}) %collective-permute-start.31) | collective-permute-done | bytes 8224 | tf_op jit(solution)/shard_map/ppermute | solution.py:26
  (70 shorter events, 5.0 us)
Async XLA Ops:
  0.7 3.4 %copy-start = (bf16[2,1024,2048]{2,1,0:T(8,128)(2,1)S(1)}, bf16[2,1024,2048]{2,1,0:T(8,128)(2,1)}, u32[]{:S(2)}) copy-start(bf16[2,1024,2048]{2,1,0:T(8,128)(2,1)} %cond_ref.7) | copy-start | bytes 25165828
  4.1 1.2 %copy-start.2 = (bf16[2,128,2048]{2,1,0:T(8,128)(2,1)S(1)}, bf16[2,128,2048]{2,1,0:T(8,128)(2,1)}, u32[]{:S(2)}) copy-start(bf16[2,128,2048]{2,1,0:T(8,128)(2,1)} %val_ref.7) | copy-start | bytes 3145732
  5.3 0.8 copy-start.5
  7.6 7.9 %collective-permute-start.15 = (f32[8,3,16,256]{3,2,1,0:T(8,128)S(1)}, f32[8,3,16,256]{3,2,1,0:T(8,128)S(1)}, u32[]{:S(2)}, u32[]{:S(2)}) collective-permute-start(f32[8,3,16,256]{3,2,1,0:T(8,128)S(1)} %get-tuple-element.21), channel_id=1, source_target_pairs={{0,8},{1,9},{2,10},{3,11},{4,12},{5,13},{6,14},{7,15},{8,0},{9,1},... | collective-permute-start | bytes 1179656 | tf_op jit(solution)/shard_map/ppermute | solution.py:37
  10.8 9.7 %collective-permute-start.1 = (f32[8,3,16,256]{3,2,1,0:T(8,128)S(1)}, f32[8,3,16,256]{3,2,1,0:T(8,128)S(1)}, u32[]{:S(2)}, u32[]{:S(2)}) collective-permute-start(f32[8,3,16,256]{3,2,1,0:T(8,128)S(1)} %get-tuple-element.17), channel_id=1, source_target_pairs={{0,1},{1,0},{2,3},{3,2},{4,5},{5,4},{6,7},{7,6},{8,9},{9,8},{10,11... | collective-permute-start | bytes 1179656 | tf_op jit(solution)/shard_map/ppermute | solution.py:37
  11.6 11.5 %collective-permute-start.14 = (f32[8,3,16,256]{3,2,1,0:T(8,128)S(1)}, f32[8,3,16,256]{3,2,1,0:T(8,128)S(1)}, u32[]{:S(2)}, u32[]{:S(2)}) collective-permute-start(f32[8,3,16,256]{3,2,1,0:T(8,128)S(1)} %get-tuple-element.19), channel_id=1, source_target_pairs={{0,8},{1,9},{2,10},{3,11},{4,12},{5,13},{6,14},{7,15},{8,0},{9,1},... | collective-permute-start | bytes 1179656 | tf_op jit(solution)/shard_map/ppermute | solution.py:37
  15.6 9.7 %collective-permute-start.16 = (f32[8,3,16,256]{3,2,1,0:T(8,128)S(1)}, f32[8,3,16,256]{3,2,1,0:T(8,128)S(1)}, u32[]{:S(2)}, u32[]{:S(2)}) collective-permute-start(f32[8,3,16,256]{3,2,1,0:T(8,128)S(1)} %add.101), channel_id=1, source_target_pairs={{0,24},{1,25},{2,26},{3,27},{4,28},{5,29},{6,30},{7,31},{8,16},{9,... | collective-permute-start | bytes 1179656 | tf_op jit(solution)/shard_map/ppermute | solution.py:37
  18.4 12.0 %collective-permute-start = (f32[8,3,16,256]{3,2,1,0:T(8,128)S(1)}, f32[8,3,16,256]{3,2,1,0:T(8,128)S(1)}, u32[]{:S(2)}, u32[]{:S(2)}) collective-permute-start(f32[8,3,16,256]{3,2,1,0:T(8,128)S(1)} %get-tuple-element.15), channel_id=1, source_target_pairs={{0,1},{1,0},{2,3},{3,2},{4,5},{5,4},{6,7},{7,6},{8,9},{9,8},{10,11... | collective-permute-start | bytes 1179656 | tf_op jit(solution)/shard_map/ppermute | solution.py:37
  20.4 39.4 %copy-start.9 = (s32[2]{0:T(128)S(1)}, s32[2]{0:T(128)}, u32[]{:S(2)}) copy-start(s32[2]{0:T(128)} %param.19) | copy-start | bytes 28
  20.4 39.4 %copy-start.1 = (bf16[2,1024,512]{2,1,0:T(8,128)(2,1)S(1)}, bf16[2,1024,512]{2,1,0:T(8,128)(2,1)}, u32[]{:S(2)}) copy-start(bf16[2,1024,512]{2,1,0:T(8,128)(2,1)} %orbit_cond.9) | copy-start | bytes 6291460
  20.5 39.4 %copy-start.3 = (bf16[2,128,512]{2,1,0:T(8,128)(2,1)S(1)}, bf16[2,128,512]{2,1,0:T(8,128)(2,1)}, u32[]{:S(2)}) copy-start(bf16[2,128,512]{2,1,0:T(8,128)(2,1)} %orbit_val.9) | copy-start | bytes 786436
  20.5 39.4 %copy-start.6 = (f32[2,1024]{1,0:T(2,128)S(1)}, f32[2,1024]{1,0:T(2,128)}, u32[]{:S(2)}) copy-start(f32[2,1024]{1,0:T(2,128)} %energy_cond.9) | copy-start | bytes 24580
  20.5 39.4 %copy-start.7 = (f32[2,128]{1,0:T(2,128)S(1)}, f32[2,128]{1,0:T(2,128)}, u32[]{:S(2)}) copy-start(f32[2,128]{1,0:T(2,128)} %energy_val.9) | copy-start | bytes 3076
  20.5 39.4 %copy-start.8 = (f32[4]{0:T(128)S(1)}, f32[4]{0:T(128)}, u32[]{:S(2)}) copy-start(f32[4]{0:T(128)} %freq_ref.9) | copy-start | bytes 52
  20.6 9.8 %collective-permute-start.2 = (f32[8,3,16,256]{3,2,1,0:T(8,128)S(1)}, f32[8,3,16,256]{3,2,1,0:T(8,128)S(1)}, u32[]{:S(2)}, u32[]{:S(2)}) collective-permute-start(f32[8,3,16,256]{3,2,1,0:T(8,128)S(1)} %add.88), channel_id=1, source_target_pairs={{0,3},{1,2},{2,1},{3,0},{4,7},{5,6},{6,5},{7,4},{8,11},{9,10},{10,... | collective-permute-start | bytes 1179656 | tf_op jit(solution)/shard_map/ppermute | solution.py:37
  25.3 7.2 %collective-permute-start.17 = (f32[2,3,16,256]{3,2,1,0:T(8,128)S(1)}, f32[2,3,16,256]{3,2,1,0:T(8,128)S(1)}, u32[]{:S(2)}, u32[]{:S(2)}) collective-permute-start(f32[2,3,16,256]{3,2,1,0:T(8,128)S(1)} %get-tuple-element.28), channel_id=1, source_target_pairs={{0,1},{1,0},{2,3},{3,2},{4,5},{5,4},{6,7},{7,6},{8,9},{9,8},{10,11... | collective-permute-start | bytes 294920 | tf_op jit(solution)/shard_map/ppermute | solution.py:37
  27.3 7.4 %collective-permute-start.18 = (f32[2,3,16,256]{3,2,1,0:T(8,128)S(1)}, f32[2,3,16,256]{3,2,1,0:T(8,128)S(1)}, u32[]{:S(2)}, u32[]{:S(2)}) collective-permute-start(f32[2,3,16,256]{3,2,1,0:T(8,128)S(1)} %get-tuple-element.27), channel_id=1, source_target_pairs={{0,3},{1,2},{2,1},{3,0},{4,7},{5,6},{6,5},{7,4},{8,11},{9,10},{10,... | collective-permute-start | bytes 294920 | tf_op jit(solution)/shard_map/ppermute | solution.py:37
  27.7 7.8 %collective-permute-start.19 = (f32[2,3,16,256]{3,2,1,0:T(8,128)S(1)}, f32[2,3,16,256]{3,2,1,0:T(8,128)S(1)}, u32[]{:S(2)}, u32[]{:S(2)}) collective-permute-start(f32[2,3,16,256]{3,2,1,0:T(8,128)S(1)} %get-tuple-element.26), channel_id=1, source_target_pairs={{0,2},{1,3},{2,0},{3,1},{4,6},{5,7},{6,4},{7,5},{8,10},{9,11},{10,... | collective-permute-start | bytes 294920 | tf_op jit(solution)/shard_map/ppermute | solution.py:37
  30.5 7.0 %collective-permute-start.3 = (f32[2,3,16,256]{3,2,1,0:T(8,128)S(1)}, f32[2,3,16,256]{3,2,1,0:T(8,128)S(1)}, u32[]{:S(2)}, u32[]{:S(2)}) collective-permute-start(f32[2,3,16,256]{3,2,1,0:T(8,128)S(1)} %get-tuple-element.31), channel_id=1, source_target_pairs={{0,8},{1,9},{2,10},{3,11},{4,12},{5,13},{6,14},{7,15},{8,0},{9,1},... | collective-permute-start | bytes 294920 | tf_op jit(solution)/shard_map/ppermute | solution.py:37
  30.6 9.0 %collective-permute-start.4 = (f32[2,3,16,256]{3,2,1,0:T(8,128)S(1)}, f32[2,3,16,256]{3,2,1,0:T(8,128)S(1)}, u32[]{:S(2)}, u32[]{:S(2)}) collective-permute-start(f32[2,3,16,256]{3,2,1,0:T(8,128)S(1)} %get-tuple-element.30), channel_id=1, source_target_pairs={{0,24},{1,25},{2,26},{3,27},{4,28},{5,29},{6,30},{7,31},{8,16},{9,... | collective-permute-start | bytes 294920 | tf_op jit(solution)/shard_map/ppermute | solution.py:37
  32.5 7.1 %collective-permute-start.5 = (f32[2,3,16,256]{3,2,1,0:T(8,128)S(1)}, f32[2,3,16,256]{3,2,1,0:T(8,128)S(1)}, u32[]{:S(2)}, u32[]{:S(2)}) collective-permute-start(f32[2,3,16,256]{3,2,1,0:T(8,128)S(1)} %get-tuple-element.29), channel_id=1, source_target_pairs={{0,16},{1,17},{2,18},{3,19},{4,20},{5,21},{6,22},{7,23},{8,24},{9,... | collective-permute-start | bytes 294920 | tf_op jit(solution)/shard_map/ppermute | solution.py:37
  35.5 6.1 %collective-permute-start.20 = (f32[2,3,16,256]{3,2,1,0:T(8,128)S(1)}, f32[2,3,16,256]{3,2,1,0:T(8,128)S(1)}, u32[]{:S(2)}, u32[]{:S(2)}) collective-permute-start(f32[2,3,16,256]{3,2,1,0:T(8,128)S(1)} %fusion.1), channel_id=1, source_target_pairs={{0,4},{1,5},{2,6},{3,7},{4,0},{5,1},{6,2},{7,3},{8,12},{9,13},{10,... | collective-permute-start | bytes 294920 | tf_op jit(solution)/shard_map/ppermute | solution.py:37
  39.6 5.8 %collective-permute-start.6 = (f32[2,3,16,256]{3,2,1,0:T(8,128)S(1)}, f32[2,3,16,256]{3,2,1,0:T(8,128)S(1)}, u32[]{:S(2)}, u32[]{:S(2)}) collective-permute-start(f32[2,3,16,256]{3,2,1,0:T(8,128)S(1)} %fusion.3), channel_id=1, source_target_pairs={{0,4},{1,5},{2,6},{3,7},{4,0},{5,1},{6,2},{7,3},{8,12},{9,13},{10,... | collective-permute-start | bytes 294920 | tf_op jit(solution)/shard_map/ppermute | solution.py:37
  41.6 5.6 %collective-permute-start.21 = (f32[2,3,16,256]{3,2,1,0:T(8,128)S(1)}, f32[2,3,16,256]{3,2,1,0:T(8,128)S(1)}, u32[]{:S(2)}, u32[]{:S(2)}) collective-permute-start(f32[2,3,16,256]{3,2,1,0:T(8,128)S(1)} %add_multiply_fusion), channel_id=1, source_target_pairs={{0,3},{1,2},{2,1},{3,0},{4,7},{5,6},{6,5},{7,4},{8,11},{9,10},{10,... | collective-permute-start | bytes 294920 | tf_op jit(solution)/shard_map/ppermute | solution.py:37
  42.6 7.6 %collective-permute-start.22 = (f32[2,3,16,256]{3,2,1,0:T(8,128)S(1)}, f32[2,3,16,256]{3,2,1,0:T(8,128)S(1)}, u32[]{:S(2)}, u32[]{:S(2)}) collective-permute-start(f32[2,3,16,256]{3,2,1,0:T(8,128)S(1)} %add_multiply_fusion), channel_id=1, source_target_pairs={{0,1},{1,0},{2,3},{3,2},{4,5},{5,4},{6,7},{7,6},{8,9},{9,8},{10,11... | collective-permute-start | bytes 294920 | tf_op jit(solution)/shard_map/ppermute | solution.py:37
  45.0 6.1 %collective-permute-start.23 = (f32[2,3,16,256]{3,2,1,0:T(8,128)S(1)}, f32[2,3,16,256]{3,2,1,0:T(8,128)S(1)}, u32[]{:S(2)}, u32[]{:S(2)}) collective-permute-start(f32[2,3,16,256]{3,2,1,0:T(8,128)S(1)} %add_multiply_fusion), channel_id=1, source_target_pairs={{0,2},{1,3},{2,0},{3,1},{4,6},{5,7},{6,4},{7,5},{8,10},{9,11},{10,... | collective-permute-start | bytes 294920 | tf_op jit(solution)/shard_map/ppermute | solution.py:37
  45.4 8.6 %collective-permute-start.7 = (f32[2,3,16,256]{3,2,1,0:T(8,128)S(1)}, f32[2,3,16,256]{3,2,1,0:T(8,128)S(1)}, u32[]{:S(2)}, u32[]{:S(2)}) collective-permute-start(f32[2,3,16,256]{3,2,1,0:T(8,128)S(1)} %add_multiply_fusion.1), channel_id=1, source_target_pairs={{0,24},{1,25},{2,26},{3,27},{4,28},{5,29},{6,30},{7,31},{8,16},{9,... | collective-permute-start | bytes 294920 | tf_op jit(solution)/shard_map/ppermute | solution.py:37
  46.7 7.3 %collective-permute-start.8 = (f32[2,3,16,256]{3,2,1,0:T(8,128)S(1)}, f32[2,3,16,256]{3,2,1,0:T(8,128)S(1)}, u32[]{:S(2)}, u32[]{:S(2)}) collective-permute-start(f32[2,3,16,256]{3,2,1,0:T(8,128)S(1)} %add_multiply_fusion.1), channel_id=1, source_target_pairs={{0,8},{1,9},{2,10},{3,11},{4,12},{5,13},{6,14},{7,15},{8,0},{9,1},... | collective-permute-start | bytes 294920 | tf_op jit(solution)/shard_map/ppermute | solution.py:37
  47.3 8.3 %collective-permute-start.9 = (f32[2,3,16,256]{3,2,1,0:T(8,128)S(1)}, f32[2,3,16,256]{3,2,1,0:T(8,128)S(1)}, u32[]{:S(2)}, u32[]{:S(2)}) collective-permute-start(f32[2,3,16,256]{3,2,1,0:T(8,128)S(1)} %add_multiply_fusion.1), channel_id=1, source_target_pairs={{0,16},{1,17},{2,18},{3,19},{4,20},{5,21},{6,22},{7,23},{8,24},{9,... | collective-permute-start | bytes 294920 | tf_op jit(solution)/shard_map/ppermute | solution.py:37
  51.2 11.1 %collective-permute-start.24 = (f32[8,3,16,256]{3,2,1,0:T(8,128)S(1)}, f32[8,3,16,256]{3,2,1,0:T(8,128)S(1)}, u32[]{:S(2)}, u32[]{:S(2)}) collective-permute-start(f32[8,3,16,256]{3,2,1,0:T(8,128)S(1)} %pad_maximum_fusion.2.refs_0_), channel_id=1, source_target_pairs={{0,8},{1,9},{2,10},{3,11},{4,12},{5,13},{6,14},{7,15},{8,0},{9,1},... | collective-permute-start | bytes 1179656 | tf_op jit(solution)/shard_map/ppermute | solution.py:26
  52.0 11.9 %collective-permute-start.26 = (f32[8,3,16,256]{3,2,1,0:T(8,128)S(1)}, f32[8,3,16,256]{3,2,1,0:T(8,128)S(1)}, u32[]{:S(2)}, u32[]{:S(2)}) collective-permute-start(f32[8,3,16,256]{3,2,1,0:T(8,128)S(1)} %pad_maximum_fusion.2.refs_0_), channel_id=1, source_target_pairs={{0,24},{1,25},{2,26},{3,27},{4,28},{5,29},{6,30},{7,31},{8,16},{9,... | collective-permute-start | bytes 1179656 | tf_op jit(solution)/shard_map/ppermute | solution.py:26
  55.6 8.4 %collective-permute-start.10 = (f32[8,3,16,256]{3,2,1,0:T(8,128)S(1)}, f32[8,3,16,256]{3,2,1,0:T(8,128)S(1)}, u32[]{:S(2)}, u32[]{:S(2)}) collective-permute-start(f32[8,3,16,256]{3,2,1,0:T(8,128)S(1)} %pad_maximum_fusion.refs_1_), channel_id=1, source_target_pairs={{0,1},{1,0},{2,3},{3,2},{4,5},{5,4},{6,7},{7,6},{8,9},{9,8},{10,11... | collective-permute-start | bytes 1179656 | tf_op jit(solution)/shard_map/ppermute | solution.py:26
  58.1 9.9 %collective-permute-start.12 = (f32[8,3,16,256]{3,2,1,0:T(8,128)S(1)}, f32[8,3,16,256]{3,2,1,0:T(8,128)S(1)}, u32[]{:S(2)}, u32[]{:S(2)}) collective-permute-start(f32[8,3,16,256]{3,2,1,0:T(8,128)S(1)} %pad_maximum_fusion.refs_1_), channel_id=1, source_target_pairs={{0,3},{1,2},{2,1},{3,0},{4,7},{5,6},{6,5},{7,4},{8,11},{9,10},{10,... | collective-permute-start | bytes 1179656 | tf_op jit(solution)/shard_map/ppermute | solution.py:26
  62.3 10.3 %collective-permute-start.25 = (f32[4,3,16,256]{3,2,1,0:T(8,128)S(1)}, f32[4,3,16,256]{3,2,1,0:T(8,128)S(1)}, u32[]{:S(2)}, u32[]{:S(2)}) collective-permute-start(f32[4,3,16,256]{3,2,1,0:T(8,128)S(1)} %slice.110), channel_id=1, source_target_pairs={{0,24},{1,25},{2,26},{3,27},{4,28},{5,29},{6,30},{7,31},{8,16},{9,... | collective-permute-start | bytes 589832 | tf_op jit(solution)/shard_map/ppermute | solution.py:26
  63.9 8.7 %collective-permute-start.27 = (f32[4,3,16,256]{3,2,1,0:T(8,128)S(1)}, f32[4,3,16,256]{3,2,1,0:T(8,128)S(1)}, u32[]{:S(2)}, u32[]{:S(2)}) collective-permute-start(f32[4,3,16,256]{3,2,1,0:T(8,128)S(1)} %slice.130), channel_id=1, source_target_pairs={{0,8},{1,9},{2,10},{3,11},{4,12},{5,13},{6,14},{7,15},{8,0},{9,1},... | collective-permute-start | bytes 589832 | tf_op jit(solution)/shard_map/ppermute | solution.py:26
  64.0 10.1 %collective-permute-start.11 = (f32[4,3,16,256]{3,2,1,0:T(8,128)S(1)}, f32[4,3,16,256]{3,2,1,0:T(8,128)S(1)}, u32[]{:S(2)}, u32[]{:S(2)}) collective-permute-start(f32[4,3,16,256]{3,2,1,0:T(8,128)S(1)} %slice.120), channel_id=1, source_target_pairs={{0,3},{1,2},{2,1},{3,0},{4,7},{5,6},{6,5},{7,4},{8,11},{9,10},{10,... | collective-permute-start | bytes 589832 | tf_op jit(solution)/shard_map/ppermute | solution.py:26
  68.0 6.2 %collective-permute-start.13 = (f32[4,3,16,256]{3,2,1,0:T(8,128)S(1)}, f32[4,3,16,256]{3,2,1,0:T(8,128)S(1)}, u32[]{:S(2)}, u32[]{:S(2)}) collective-permute-start(f32[4,3,16,256]{3,2,1,0:T(8,128)S(1)} %slice.121), channel_id=1, source_target_pairs={{0,1},{1,0},{2,3},{3,2},{4,5},{5,4},{6,7},{7,6},{8,9},{9,8},{10,11... | collective-permute-start | bytes 589832 | tf_op jit(solution)/shard_map/ppermute | solution.py:26
  72.7 22.8 %copy-start.4 = (bf16[128,16384]{1,0:T(8,128)(2,1)S(1)}, bf16[128,16384]{1,0:T(8,128)(2,1)}, u32[]{:S(2)}) copy-start(bf16[128,16384]{1,0:T(8,128)(2,1)} %zeta.1) | copy-start | bytes 12582916
  75.7 1.5 %collective-permute-start.28 = (f32[16,256]{1,0:T(8,128)S(1)}, f32[16,256]{1,0:T(8,128)S(1)}, u32[]{:S(2)}, u32[]{:S(2)}) collective-permute-start(f32[16,256]{1,0:T(8,128)S(1)} %get-tuple-element.25), channel_id=1, source_target_pairs={{0,32},{32,0},{64,96},{96,64},{128,160},{160,128},{192,224},{224,1... | collective-permute-start | bytes 49160 | tf_op jit(solution)/shard_map/ppermute | solution.py:26
  96.8 1.2 %collective-permute-start.29 = (f32[16,128]{1,0:T(8,128)S(1)}, f32[16,128]{1,0:T(8,128)S(1)}, u32[]{:S(2)}, u32[]{:S(2)}) collective-permute-start(f32[16,128]{1,0:T(8,128)S(1)} %wing_sums.1), channel_id=1, source_target_pairs={{0,32},{32,0},{64,96},{96,64},{128,160},{160,128},{192,224},{224,1... | collective-permute-start | bytes 24584 | tf_op jit(solution)/shard_map/ppermute | solution.py:26
  98.0 4.9 %collective-permute-start.30 = (f32[16,128]{1,0:T(8,128)S(1)}, f32[16,128]{1,0:T(8,128)S(1)}, u32[]{:S(2)}, u32[]{:S(2)}) collective-permute-start(f32[16,128]{1,0:T(8,128)S(1)} %add.114), channel_id=1, source_target_pairs={{0,64},{32,96},{64,0},{96,32},{128,192},{160,224},{192,128},{224,1... | collective-permute-start | bytes 24584 | tf_op jit(solution)/shard_map/ppermute | solution.py:26
  102.9 6.2 %collective-permute-start.31 = (f32[16,128]{1,0:T(8,128)S(1)}, f32[16,128]{1,0:T(8,128)S(1)}, u32[]{:S(2)}, u32[]{:S(2)}) collective-permute-start(f32[16,128]{1,0:T(8,128)S(1)} %add.115.one), channel_id=1, source_target_pairs={{0,192},{32,224},{64,128},{96,160},{128,64},{160,96},{192,0},{224,... | collective-permute-start | bytes 24584 | tf_op jit(solution)/shard_map/ppermute | solution.py:26

commit v11 on v10

--- a/solution.py
+++ b/solution.py
@@ -333,8 +333,7 @@
         chunks[k] = (own, second, first, passed)
     for k in range(kcount):
         pair = pair_sums(((k, (1, 2)),), *operands, chunks, pair, 1)
-    pair = pair_sums(((0, (3,)),), *operands, chunks, pair, 1)
-    keep, send = pair_sums(((1, (3,)),), *operands, chunks, pair, 2)
+    keep, send = pair_sums(((0, (3,)), (1, (3,))), *operands, chunks, pair, 2)
     pair = keep + swap(send, "ka", 1)
     total = wing_sums(place, everyone(pair, "wa"), zeta)
     total = total + swap(total, "ka", 1)

time: 110 us -> 111 us (level)
  waiting for transfers between devices: 17.3 us -> 20.1 us
  blocking collectives: 18.2 us -> 17 us
    ppermute x12, waiting for transfers between devices: 7.93 us -> 10.6 us  [swap(): lax.ppermute(value, axis, [(i, i ^ mask) for i in range(lax.axis_size(axi...]
    all_to_all x1, blocking collectives: 18.2 us -> 17 us  [everyone(): lax.all_to_all(jnp.broadcast_to(value[None], (parts,) + value.shape), axi...]
    pallas_call x5 -> x4, Pallas kernels: 9.5 us -> 8.87 us  [pair_sums(): pl.pallas_call(functools.partial(pair_kernel, groups), out_shape=[jax.Sha...]
  transfers between devices with their start and end apart: 32 -> 32, of which waited for: 13 -> 14; matrix products, arithmetic and copies ran while one was open for 0% -> 0% of each run, Pallas kernels for 12% -> 10%
where the time goes in v11:
time: 111 us
  starting transfers between devices  49.5 us (45%)
  waiting for transfers between devices  20.1 us (18%)
  Pallas kernels  17 us (15%)
  blocking collectives  17 us (15%)
  local copies, waits for them, and re-layouts  5.52 us (5%)
    ppermute x20, starting transfers between devices, cross(): return lax.ppermute(value, ('ka', 'wa'), pairs)  30.9 us
    ppermute x12, starting transfers between devices, swap(): lax.ppermute(value, axis, [(i, i ^ mask) for i in range(lax.axis_size(axi...  18.7 us
    all_to_all x1, blocking collectives, everyone(): lax.all_to_all(jnp.broadcast_to(value[None], (parts,) + value.shape), axi...  17 us
    ppermute x12, waiting for transfers between devices, swap(): lax.ppermute(value, axis, [(i, i ^ mask) for i in range(lax.axis_size(axi...  10.6 us
    ppermute x20, waiting for transfers between devices, cross(): return lax.ppermute(value, ('ka', 'wa'), pairs)  9.43 us
    pallas_call x4, Pallas kernels, pair_sums(): pl.pallas_call(functools.partial(pair_kernel, groups), out_shape=[jax.Sha...  8.87 us
    pallas_call x4, Pallas kernels, partial_momentum(): pl.pallas_call(functools.partial(momentum_kernel, kpoint, quarters), out_...  6.23 us
    unnamed x20, local copies, waits for them, and re-layouts  5.41 us
  transfers between devices with their start and end apart: 32, of which 14 were waited for; matrix products, arithmetic and copies ran while one was open for 0% of the time, Pallas kernels for 10%

profile of v11, /device:TPU:8, one launch (start us, length us, event | category | flops | bytes accessed | tf_op | source)
XLA Modules:
  0.0 110.6 jit_solution(448829880859067628)
XLA Ops:
  0.7 3.4 %copy-done = bf16[2,1024,2048]{2,1,0:T(8,128)(2,1)S(1)} copy-done((bf16[2,1024,2048]{2,1,0:T(8,128)(2,1)S(1)}, bf16[2,1024,2048]{2,1,0:T(8,128)(2,1)}, u32[]{:S(2)}) %copy-start) | copy-done | bytes 8388632
  4.1 1.2 %copy-done.2 = bf16[2,128,2048]{2,1,0:T(8,128)(2,1)S(1)} copy-done((bf16[2,128,2048]{2,1,0:T(8,128)(2,1)S(1)}, bf16[2,128,2048]{2,1,0:T(8,128)(2,1)}, u32[]{:S(2)}) %copy-start.2) | copy-done | bytes 1048600
  5.3 0.8 copy-done.5
  6.1 1.6 %partial_momentum.7 = (f32[8,3,16,256]{3,2,1,0:T(8,128)S(1)}, f32[8,3,16,256]{3,2,1,0:T(8,128)S(1)}) custom-call(s32[2]{0:T(128)S(1)} %pad_add_fusion.place_ref, bf16[2,128,2048]{2,1,0:T(8,128)(2,1)S(1)} %copy-done.2, s32[3,2048]{1,0:T(4,128)S(1)} %copy-done.5, bf16[2,1024,2048]{2,1,0:T(8,128)(2,1)S(1)} %copy-done), custom_call_target="tpu_custom_call" | custom-call | flops 805306368 | bytes 3407872 | tf_op jit(solution)/shard_map/partial_momentum/pallas_call | solution.py:98
  7.6 2.3 %collective-permute-start.12 = (f32[8,3,16,256]{3,2,1,0:T(8,128)S(1)}, f32[8,3,16,256]{3,2,1,0:T(8,128)S(1)}, u32[]{:S(2)}, u32[]{:S(2)}) collective-permute-start(f32[8,3,16,256]{3,2,1,0:T(8,128)S(1)} %get-tuple-element.21), channel_id=1, source_target_pairs={{0,1},{1,0},{2,3},{3,2},{4,5},{5,4},{6,7},{7,6},{8,9},{9,8},{10,11... | collective-permute-start | bytes 1179656 | tf_op jit(solution)/shard_map/ppermute | solution.py:37
  9.9 1.6 %partial_momentum.5 = (f32[8,3,16,256]{3,2,1,0:T(8,128)S(1)}, f32[8,3,16,256]{3,2,1,0:T(8,128)S(1)}) custom-call(s32[2]{0:T(128)S(1)} %pad_add_fusion.place_ref, bf16[2,128,2048]{2,1,0:T(8,128)(2,1)S(1)} %copy-done.2, s32[3,2048]{1,0:T(4,128)S(1)} %copy-done.5, bf16[2,1024,2048]{2,1,0:T(8,128)(2,1)S(1)} %copy-done), custom_call_target="tpu_custom_call" | custom-call | flops 805306368 | bytes 3407872 | tf_op jit(solution)/shard_map/partial_momentum/pallas_call | solution.py:98
  11.6 1.3 %collective-permute-start.11 = (f32[8,3,16,256]{3,2,1,0:T(8,128)S(1)}, f32[8,3,16,256]{3,2,1,0:T(8,128)S(1)}, u32[]{:S(2)}, u32[]{:S(2)}) collective-permute-start(f32[8,3,16,256]{3,2,1,0:T(8,128)S(1)} %get-tuple-element.19), channel_id=1, source_target_pairs={{0,1},{1,0},{2,3},{3,2},{4,5},{5,4},{6,7},{7,6},{8,9},{9,8},{10,11... | collective-permute-start | bytes 1179656 | tf_op jit(solution)/shard_map/ppermute | solution.py:37
  12.9 1.6 %partial_momentum.6 = (f32[8,3,16,256]{3,2,1,0:T(8,128)S(1)}, f32[8,3,16,256]{3,2,1,0:T(8,128)S(1)}) custom-call(s32[2]{0:T(128)S(1)} %pad_add_fusion.place_ref, bf16[2,128,2048]{2,1,0:T(8,128)(2,1)S(1)} %copy-done.2, s32[3,2048]{1,0:T(4,128)S(1)} %copy-done.5, bf16[2,1024,2048]{2,1,0:T(8,128)(2,1)S(1)} %copy-done), custom_call_target="tpu_custom_call" | custom-call | flops 805306368 | bytes 3407872 | tf_op jit(solution)/shard_map/partial_momentum/pallas_call | solution.py:98
  14.5 1.2 %collective-permute-done.12 = f32[8,3,16,256]{3,2,1,0:T(8,128)S(1)} collective-permute-done((f32[8,3,16,256]{3,2,1,0:T(8,128)S(1)}, f32[8,3,16,256]{3,2,1,0:T(8,128)S(1)}, u32[]{:S(2)}, u32[]{:S(2)}) %collective-permute-start.12) | collective-permute-done | bytes 393248 | tf_op jit(solution)/shard_map/ppermute | solution.py:37
  15.7 1.5 %collective-permute-start.13 = (f32[8,3,16,256]{3,2,1,0:T(8,128)S(1)}, f32[8,3,16,256]{3,2,1,0:T(8,128)S(1)}, u32[]{:S(2)}, u32[]{:S(2)}) collective-permute-start(f32[8,3,16,256]{3,2,1,0:T(8,128)S(1)} %add.101), channel_id=1, source_target_pairs={{0,3},{1,2},{2,1},{3,0},{4,7},{5,6},{6,5},{7,4},{8,11},{9,10},{10,... | collective-permute-start | bytes 1179656 | tf_op jit(solution)/shard_map/ppermute | solution.py:37
  17.2 1.5 %collective-permute-start = (f32[8,3,16,256]{3,2,1,0:T(8,128)S(1)}, f32[8,3,16,256]{3,2,1,0:T(8,128)S(1)}, u32[]{:S(2)}, u32[]{:S(2)}) collective-permute-start(f32[8,3,16,256]{3,2,1,0:T(8,128)S(1)} %get-tuple-element.15), channel_id=1, source_target_pairs={{0,8},{1,9},{2,10},{3,11},{4,12},{5,13},{6,14},{7,15},{8,0},{9,1},... | collective-permute-start | bytes 1179656 | tf_op jit(solution)/shard_map/ppermute | solution.py:37
  18.7 1.6 %partial_momentum.4 = (f32[8,3,16,256]{3,2,1,0:T(8,128)S(1)}, f32[8,3,16,256]{3,2,1,0:T(8,128)S(1)}) custom-call(s32[2]{0:T(128)S(1)} %pad_add_fusion.place_ref, bf16[2,128,2048]{2,1,0:T(8,128)(2,1)S(1)} %copy-done.2, s32[3,2048]{1,0:T(4,128)S(1)} %copy-done.5, bf16[2,1024,2048]{2,1,0:T(8,128)(2,1)S(1)} %copy-done), custom_call_target="tpu_custom_call" | custom-call | flops 805306368 | bytes 3407872 | tf_op jit(solution)/shard_map/partial_momentum/pallas_call | solution.py:98
  20.4 2.2 %collective-permute-start.2 = (f32[8,3,16,256]{3,2,1,0:T(8,128)S(1)}, f32[8,3,16,256]{3,2,1,0:T(8,128)S(1)}, u32[]{:S(2)}, u32[]{:S(2)}) collective-permute-start(f32[8,3,16,256]{3,2,1,0:T(8,128)S(1)} %add.88), channel_id=1, source_target_pairs={{0,24},{1,25},{2,26},{3,27},{4,28},{5,29},{6,30},{7,31},{8,16},{9,... | collective-permute-start | bytes 1179656 | tf_op jit(solution)/shard_map/ppermute | solution.py:37
  22.6 1.4 %collective-permute-done.13 = f32[8,3,16,256]{3,2,1,0:T(8,128)S(1)} collective-permute-done((f32[8,3,16,256]{3,2,1,0:T(8,128)S(1)}, f32[8,3,16,256]{3,2,1,0:T(8,128)S(1)}, u32[]{:S(2)}, u32[]{:S(2)}) %collective-permute-start.13) | collective-permute-done | bytes 393248 | tf_op jit(solution)/shard_map/ppermute | solution.py:37
  24.1 1.0 collective-permute-start.14
  25.1 2.1 %collective-permute-start.15 = (f32[2,3,16,256]{3,2,1,0:T(8,128)S(1)}, f32[2,3,16,256]{3,2,1,0:T(8,128)S(1)}, u32[]{:S(2)}, u32[]{:S(2)}) collective-permute-start(f32[2,3,16,256]{3,2,1,0:T(8,128)S(1)} %get-tuple-element.27), channel_id=1, source_target_pairs={{0,24},{1,25},{2,26},{3,27},{4,28},{5,29},{6,30},{7,31},{8,16},{9,... | collective-permute-start | bytes 294920 | tf_op jit(solution)/shard_map/ppermute | solution.py:37
  27.2 1.1 collective-permute-start.16
  28.3 1.3 %collective-permute-done.2 = f32[8,3,16,256]{3,2,1,0:T(8,128)S(1)} collective-permute-done((f32[8,3,16,256]{3,2,1,0:T(8,128)S(1)}, f32[8,3,16,256]{3,2,1,0:T(8,128)S(1)}, u32[]{:S(2)}, u32[]{:S(2)}) %collective-permute-start.2) | collective-permute-done | bytes 393248 | tf_op jit(solution)/shard_map/ppermute | solution.py:37
  29.6 3.0 %collective-permute-start.3 = (f32[2,3,16,256]{3,2,1,0:T(8,128)S(1)}, f32[2,3,16,256]{3,2,1,0:T(8,128)S(1)}, u32[]{:S(2)}, u32[]{:S(2)}) collective-permute-start(f32[2,3,16,256]{3,2,1,0:T(8,128)S(1)} %get-tuple-element.31), channel_id=1, source_target_pairs={{0,1},{1,0},{2,3},{3,2},{4,5},{5,4},{6,7},{7,6},{8,9},{9,8},{10,11... | collective-permute-start | bytes 294920 | tf_op jit(solution)/shard_map/ppermute | solution.py:37
  32.6 2.2 %collective-permute-start.5 = (f32[2,3,16,256]{3,2,1,0:T(8,128)S(1)}, f32[2,3,16,256]{3,2,1,0:T(8,128)S(1)}, u32[]{:S(2)}, u32[]{:S(2)}) collective-permute-start(f32[2,3,16,256]{3,2,1,0:T(8,128)S(1)} %get-tuple-element.29), channel_id=1, source_target_pairs={{0,2},{1,3},{2,0},{3,1},{4,6},{5,7},{6,4},{7,5},{8,10},{9,11},{10,... | collective-permute-start | bytes 294920 | tf_op jit(solution)/shard_map/ppermute | solution.py:37
  35.4 2.0 %collective-permute-start.17 = (f32[2,3,16,256]{3,2,1,0:T(8,128)S(1)}, f32[2,3,16,256]{3,2,1,0:T(8,128)S(1)}, u32[]{:S(2)}, u32[]{:S(2)}) collective-permute-start(f32[2,3,16,256]{3,2,1,0:T(8,128)S(1)} %fusion.1), channel_id=1, source_target_pairs={{0,4},{1,5},{2,6},{3,7},{4,0},{5,1},{6,2},{7,3},{8,12},{9,13},{10,... | collective-permute-start | bytes 294920 | tf_op jit(solution)/shard_map/ppermute | solution.py:37
  37.4 1.9 %collective-permute-done.5 = f32[2,3,16,256]{3,2,1,0:T(8,128)S(1)} collective-permute-done((f32[2,3,16,256]{3,2,1,0:T(8,128)S(1)}, f32[2,3,16,256]{3,2,1,0:T(8,128)S(1)}, u32[]{:S(2)}, u32[]{:S(2)}) %collective-permute-start.5) | collective-permute-done | bytes 98336 | tf_op jit(solution)/shard_map/ppermute | solution.py:37
  39.4 1.7 %collective-permute-start.6 = (f32[2,3,16,256]{3,2,1,0:T(8,128)S(1)}, f32[2,3,16,256]{3,2,1,0:T(8,128)S(1)}, u32[]{:S(2)}, u32[]{:S(2)}) collective-permute-start(f32[2,3,16,256]{3,2,1,0:T(8,128)S(1)} %fusion.3), channel_id=1, source_target_pairs={{0,4},{1,5},{2,6},{3,7},{4,0},{5,1},{6,2},{7,3},{8,12},{9,13},{10,... | collective-permute-start | bytes 294920 | tf_op jit(solution)/shard_map/ppermute | solution.py:37
  41.1 2.7 %collective-permute-start.18 = (f32[2,3,16,256]{3,2,1,0:T(8,128)S(1)}, f32[2,3,16,256]{3,2,1,0:T(8,128)S(1)}, u32[]{:S(2)}, u32[]{:S(2)}) collective-permute-start(f32[2,3,16,256]{3,2,1,0:T(8,128)S(1)} %add_multiply_fusion), channel_id=1, source_target_pairs={{0,24},{1,25},{2,26},{3,27},{4,28},{5,29},{6,30},{7,31},{8,16},{9,... | collective-permute-start | bytes 294920 | tf_op jit(solution)/shard_map/ppermute | solution.py:37
  43.8 2.3 %collective-permute-start.20 = (f32[2,3,16,256]{3,2,1,0:T(8,128)S(1)}, f32[2,3,16,256]{3,2,1,0:T(8,128)S(1)}, u32[]{:S(2)}, u32[]{:S(2)}) collective-permute-start(f32[2,3,16,256]{3,2,1,0:T(8,128)S(1)} %add_multiply_fusion), channel_id=1, source_target_pairs={{0,16},{1,17},{2,18},{3,19},{4,20},{5,21},{6,22},{7,23},{8,24},{9,... | collective-permute-start | bytes 294920 | tf_op jit(solution)/shard_map/ppermute | solution.py:37
  46.1 1.9 %collective-permute-start.7 = (f32[2,3,16,256]{3,2,1,0:T(8,128)S(1)}, f32[2,3,16,256]{3,2,1,0:T(8,128)S(1)}, u32[]{:S(2)}, u32[]{:S(2)}) collective-permute-start(f32[2,3,16,256]{3,2,1,0:T(8,128)S(1)} %add_multiply_fusion.1), channel_id=1, source_target_pairs={{0,3},{1,2},{2,1},{3,0},{4,7},{5,6},{6,5},{7,4},{8,11},{9,10},{10,... | collective-permute-start | bytes 294920 | tf_op jit(solution)/shard_map/ppermute | solution.py:37
  47.9 1.3 %collective-permute-start.8 = (f32[2,3,16,256]{3,2,1,0:T(8,128)S(1)}, f32[2,3,16,256]{3,2,1,0:T(8,128)S(1)}, u32[]{:S(2)}, u32[]{:S(2)}) collective-permute-start(f32[2,3,16,256]{3,2,1,0:T(8,128)S(1)} %add_multiply_fusion.1), channel_id=1, source_target_pairs={{0,1},{1,0},{2,3},{3,2},{4,5},{5,4},{6,7},{7,6},{8,9},{9,8},{10,11... | collective-permute-start | bytes 294920 | tf_op jit(solution)/shard_map/ppermute | solution.py:37
  49.2 0.9 collective-permute-start.9
  50.2 2.4 %collective-permute-start.24 = (f32[8,3,16,256]{3,2,1,0:T(8,128)S(1)}, f32[8,3,16,256]{3,2,1,0:T(8,128)S(1)}, u32[]{:S(2)}, u32[]{:S(2)}) collective-permute-start(f32[8,3,16,256]{3,2,1,0:T(8,128)S(1)} %pad_maximum_fusion.1.refs_1_), channel_id=1, source_target_pairs={{0,1},{1,0},{2,3},{3,2},{4,5},{5,4},{6,7},{7,6},{8,9},{9,8},{10,11... | collective-permute-start | bytes 1179656 | tf_op jit(solution)/shard_map/ppermute | solution.py:26
  52.6 0.9 collective-permute-start.26
  53.5 2.9 %collective-permute-done.9 = f32[2,3,16,256]{3,2,1,0:T(8,128)S(1)} collective-permute-done((f32[2,3,16,256]{3,2,1,0:T(8,128)S(1)}, f32[2,3,16,256]{3,2,1,0:T(8,128)S(1)}, u32[]{:S(2)}, u32[]{:S(2)}) %collective-permute-start.9) | collective-permute-done | bytes 98336 | tf_op jit(solution)/shard_map/ppermute | solution.py:37
  56.6 2.2 %collective-permute-start.22 = (f32[8,3,16,256]{3,2,1,0:T(8,128)S(1)}, f32[8,3,16,256]{3,2,1,0:T(8,128)S(1)}, u32[]{:S(2)}, u32[]{:S(2)}) collective-permute-start(f32[8,3,16,256]{3,2,1,0:T(8,128)S(1)} %pad_maximum_fusion.refs_0_), channel_id=1, source_target_pairs={{0,24},{1,25},{2,26},{3,27},{4,28},{5,29},{6,30},{7,31},{8,16},{9,... | collective-permute-start | bytes 1179656 | tf_op jit(solution)/shard_map/ppermute | solution.py:26
  58.8 3.6 %collective-permute-done.24.refs_1_ = f32[8,3,16,256]{3,2,1,0:T(8,128)S(1)} collective-permute-done((f32[8,3,16,256]{3,2,1,0:T(8,128)S(1)}, f32[8,3,16,256]{3,2,1,0:T(8,128)S(1)}, u32[]{:S(2)}, u32[]{:S(2)}) %collective-permute-start.24) | collective-permute-done | bytes 393248 | tf_op jit(solution)/shard_map/ppermute | solution.py:26
  62.7 1.8 %collective-permute-start.27 = (f32[4,3,16,256]{3,2,1,0:T(8,128)S(1)}, f32[4,3,16,256]{3,2,1,0:T(8,128)S(1)}, u32[]{:S(2)}, u32[]{:S(2)}) collective-permute-start(f32[4,3,16,256]{3,2,1,0:T(8,128)S(1)} %slice.130), channel_id=1, source_target_pairs={{0,1},{1,0},{2,3},{3,2},{4,5},{5,4},{6,7},{7,6},{8,9},{9,8},{10,11... | collective-permute-start | bytes 589832 | tf_op jit(solution)/shard_map/ppermute | solution.py:26
  64.5 2.4 %pair_sums.4.refs_2_ = f32[16,512]{1,0:T(8,128)S(1)} custom-call(s32[2]{0:T(128)S(1)} %pad_add_fusion.place_ref, f32[2]{0:T(128)S(1)} %convert_element_type.3.weight_ref, f32[4]{0:T(128)S(1)} %copy-done.8, f32[2,128]{1,0:T(2,128)S(1)} %copy-done.7, f32[2,1024]{1,0:T(2,128)S(1)} %copy-done.6, bf16[2,128,512]{2,1,0:T(8,128)(2,1)S(1)} %copy-done.3, ...), custom_call_target="tpu_custom_call" | custom-call | flops 805306368 | bytes 1835008 | tf_op jit(solution)/shard_map/pair_sums/pallas_call | solution.py:216
  66.9 2.2 %collective-permute-start.21 = (f32[4,3,16,256]{3,2,1,0:T(8,128)S(1)}, f32[4,3,16,256]{3,2,1,0:T(8,128)S(1)}, u32[]{:S(2)}, u32[]{:S(2)}) collective-permute-start(f32[4,3,16,256]{3,2,1,0:T(8,128)S(1)} %slice.108), channel_id=1, source_target_pairs={{0,24},{1,25},{2,26},{3,27},{4,28},{5,29},{6,30},{7,31},{8,16},{9,... | collective-permute-start | bytes 589832 | tf_op jit(solution)/shard_map/ppermute | solution.py:26
  69.2 2.1 %pair_sums.5.refs_2_ = f32[16,512]{1,0:T(8,128)S(1)} custom-call(s32[2]{0:T(128)S(1)} %pad_add_fusion.place_ref, f32[2]{0:T(128)S(1)} %convert_element_type.3.weight_ref, f32[4]{0:T(128)S(1)} %copy-done.8, f32[2,128]{1,0:T(2,128)S(1)} %copy-done.7, f32[2,1024]{1,0:T(2,128)S(1)} %copy-done.6, bf16[2,128,512]{2,1,0:T(8,128)(2,1)S(1)} %copy-done.3, ...), custom_call_target="tpu_custom_call" | custom-call | flops 805306368 | bytes 1835008 | tf_op jit(solution)/shard_map/pair_sums/pallas_call | solution.py:216
  71.3 2.1 %pair_sums.6.refs_2_ = f32[16,512]{1,0:T(8,128)S(1)} custom-call(s32[2]{0:T(128)S(1)} %pad_add_fusion.place_ref, f32[2]{0:T(128)S(1)} %convert_element_type.3.weight_ref, f32[4]{0:T(128)S(1)} %copy-done.8, f32[2,128]{1,0:T(2,128)S(1)} %copy-done.7, f32[2,1024]{1,0:T(2,128)S(1)} %copy-done.6, bf16[2,128,512]{2,1,0:T(8,128)(2,1)S(1)} %copy-done.3, ...), custom_call_target="tpu_custom_call" | custom-call | flops 805306368 | bytes 1835008 | tf_op jit(solution)/shard_map/pair_sums/pallas_call | solution.py:216
  73.9 1.0 collective-permute-done.23
  74.9 2.3 %pair_sums.7 = (f32[16,256]{1,0:T(8,128)S(1)}, f32[16,256]{1,0:T(8,128)S(1)}) custom-call(s32[2]{0:T(128)S(1)} %pad_add_fusion.place_ref, f32[2]{0:T(128)S(1)} %convert_element_type.3.weight_ref, f32[4]{0:T(128)S(1)} %copy-done.8, f32[2,128]{1,0:T(2,128)S(1)} %copy-done.7, f32[2,1024]{1,0:T(2,128)S(1)} %copy-done.6, bf16[2,128,512]{2,1,0:T(8,128)(2,1)S(1)} %copy-done.3, ...), custom_call_target="tpu_custom_call" | custom-call | flops 805306368 | bytes 1835008 | tf_op jit(solution)/shard_map/pair_sums/pallas_call | solution.py:216
  77.5 1.2 %collective-permute-done.28 = f32[16,256]{1,0:T(8,128)S(1)} collective-permute-done((f32[16,256]{1,0:T(8,128)S(1)}, f32[16,256]{1,0:T(8,128)S(1)}, u32[]{:S(2)}, u32[]{:S(2)}) %collective-permute-start.28) | collective-permute-done | bytes 16416 | tf_op jit(solution)/shard_map/ppermute | solution.py:26
  78.8 17.0 %all_to_all.5.gathered = f32[32,16,256]{2,1,0:T(8,128)S(1)} all-to-all(f32[32,16,256]{2,1,0:T(8,128)S(1)} %broadcast_in_dim.2), channel_id=1, replica_groups=mesh['ka'=8,'wa'=32] {'wa'}, dimensions={0} | all-to-all | bytes 1048576 | tf_op jit(solution)/shard_map/all_to_all | solution.py:46
  95.8 1.3 %wing_sums.1 = f32[16,128]{1,0:T(8,128)S(1)} custom-call(s32[2]{0:T(128)S(1)} %pad_add_fusion.place_ref, f32[32,16,256]{2,1,0:T(8,128)S(1)} %all_to_all.5.gathered, bf16[128,16384]{1,0:T(8,128)(2,1)S(1)} %copy-done.4), custom_call_target="tpu_custom_call" | custom-call | flops 100663296 | bytes 4718592 | tf_op jit(solution)/shard_map/wing_sums/pallas_call | solution.py:275
  97.1 1.2 %collective-permute-done.29 = f32[16,128]{1,0:T(8,128)S(1)} collective-permute-done((f32[16,128]{1,0:T(8,128)S(1)}, f32[16,128]{1,0:T(8,128)S(1)}, u32[]{:S(2)}, u32[]{:S(2)}) %collective-permute-start.29) | collective-permute-done | bytes 8224 | tf_op jit(solution)/shard_map/ppermute | solution.py:26
  98.3 3.3 %collective-permute-start.30 = (f32[16,128]{1,0:T(8,128)S(1)}, f32[16,128]{1,0:T(8,128)S(1)}, u32[]{:S(2)}, u32[]{:S(2)}) collective-permute-start(f32[16,128]{1,0:T(8,128)S(1)} %add.114), channel_id=1, source_target_pairs={{0,64},{32,96},{64,0},{96,32},{128,192},{160,224},{192,128},{224,1... | collective-permute-start | bytes 24584 | tf_op jit(solution)/shard_map/ppermute | solution.py:26
  101.6 1.6 %collective-permute-done.30 = f32[16,128]{1,0:T(8,128)S(1)} collective-permute-done((f32[16,128]{1,0:T(8,128)S(1)}, f32[16,128]{1,0:T(8,128)S(1)}, u32[]{:S(2)}, u32[]{:S(2)}) %collective-permute-start.30) | collective-permute-done | bytes 8224 | tf_op jit(solution)/shard_map/ppermute | solution.py:26
  103.2 5.2 %collective-permute-start.31 = (f32[16,128]{1,0:T(8,128)S(1)}, f32[16,128]{1,0:T(8,128)S(1)}, u32[]{:S(2)}, u32[]{:S(2)}) collective-permute-start(f32[16,128]{1,0:T(8,128)S(1)} %add.115.one), channel_id=1, source_target_pairs={{0,192},{32,224},{64,128},{96,160},{128,64},{160,96},{192,0},{224,... | collective-permute-start | bytes 24584 | tf_op jit(solution)/shard_map/ppermute | solution.py:26
  108.4 1.6 %collective-permute-done.31.two = f32[16,128]{1,0:T(8,128)S(1)} collective-permute-done((f32[16,128]{1,0:T(8,128)S(1)}, f32[16,128]{1,0:T(8,128)S(1)}, u32[]{:S(2)}, u32[]{:S(2)}) %collective-permute-start.31) | collective-permute-done | bytes 8224 | tf_op jit(solution)/shard_map/ppermute | solution.py:26
  (69 shorter events, 3.3 us)
Async XLA Ops:
  0.7 3.4 %copy-start = (bf16[2,1024,2048]{2,1,0:T(8,128)(2,1)S(1)}, bf16[2,1024,2048]{2,1,0:T(8,128)(2,1)}, u32[]{:S(2)}) copy-start(bf16[2,1024,2048]{2,1,0:T(8,128)(2,1)} %cond_ref.7) | copy-start | bytes 25165828
  4.1 1.2 %copy-start.2 = (bf16[2,128,2048]{2,1,0:T(8,128)(2,1)S(1)}, bf16[2,128,2048]{2,1,0:T(8,128)(2,1)}, u32[]{:S(2)}) copy-start(bf16[2,128,2048]{2,1,0:T(8,128)(2,1)} %val_ref.7) | copy-start | bytes 3145732
  5.3 0.8 copy-start.5
  7.6 8.0 %collective-permute-start.12 = (f32[8,3,16,256]{3,2,1,0:T(8,128)S(1)}, f32[8,3,16,256]{3,2,1,0:T(8,128)S(1)}, u32[]{:S(2)}, u32[]{:S(2)}) collective-permute-start(f32[8,3,16,256]{3,2,1,0:T(8,128)S(1)} %get-tuple-element.21), channel_id=1, source_target_pairs={{0,1},{1,0},{2,3},{3,2},{4,5},{5,4},{6,7},{7,6},{8,9},{9,8},{10,11... | collective-permute-start | bytes 1179656 | tf_op jit(solution)/shard_map/ppermute | solution.py:37
  11.5 8.9 %collective-permute-start.1 = (f32[8,3,16,256]{3,2,1,0:T(8,128)S(1)}, f32[8,3,16,256]{3,2,1,0:T(8,128)S(1)}, u32[]{:S(2)}, u32[]{:S(2)}) collective-permute-start(f32[8,3,16,256]{3,2,1,0:T(8,128)S(1)} %get-tuple-element.17), channel_id=1, source_target_pairs={{0,8},{1,9},{2,10},{3,11},{4,12},{5,13},{6,14},{7,15},{8,0},{9,1},... | collective-permute-start | bytes 1179656 | tf_op jit(solution)/shard_map/ppermute | solution.py:37
  11.6 11.1 %collective-permute-start.11 = (f32[8,3,16,256]{3,2,1,0:T(8,128)S(1)}, f32[8,3,16,256]{3,2,1,0:T(8,128)S(1)}, u32[]{:S(2)}, u32[]{:S(2)}) collective-permute-start(f32[8,3,16,256]{3,2,1,0:T(8,128)S(1)} %get-tuple-element.19), channel_id=1, source_target_pairs={{0,1},{1,0},{2,3},{3,2},{4,5},{5,4},{6,7},{7,6},{8,9},{9,8},{10,11... | collective-permute-start | bytes 1179656 | tf_op jit(solution)/shard_map/ppermute | solution.py:37
  15.7 8.3 %collective-permute-start.13 = (f32[8,3,16,256]{3,2,1,0:T(8,128)S(1)}, f32[8,3,16,256]{3,2,1,0:T(8,128)S(1)}, u32[]{:S(2)}, u32[]{:S(2)}) collective-permute-start(f32[8,3,16,256]{3,2,1,0:T(8,128)S(1)} %add.101), channel_id=1, source_target_pairs={{0,3},{1,2},{2,1},{3,0},{4,7},{5,6},{6,5},{7,4},{8,11},{9,10},{10,... | collective-permute-start | bytes 1179656 | tf_op jit(solution)/shard_map/ppermute | solution.py:37
  17.2 11.0 %collective-permute-start = (f32[8,3,16,256]{3,2,1,0:T(8,128)S(1)}, f32[8,3,16,256]{3,2,1,0:T(8,128)S(1)}, u32[]{:S(2)}, u32[]{:S(2)}) collective-permute-start(f32[8,3,16,256]{3,2,1,0:T(8,128)S(1)} %get-tuple-element.15), channel_id=1, source_target_pairs={{0,8},{1,9},{2,10},{3,11},{4,12},{5,13},{6,14},{7,15},{8,0},{9,1},... | collective-permute-start | bytes 1179656 | tf_op jit(solution)/shard_map/ppermute | solution.py:37
  20.3 38.5 %copy-start.9 = (s32[2]{0:T(128)S(1)}, s32[2]{0:T(128)}, u32[]{:S(2)}) copy-start(s32[2]{0:T(128)} %param.19) | copy-start | bytes 28
  20.3 44.2 %copy-start.1 = (bf16[2,1024,512]{2,1,0:T(8,128)(2,1)S(1)}, bf16[2,1024,512]{2,1,0:T(8,128)(2,1)}, u32[]{:S(2)}) copy-start(bf16[2,1024,512]{2,1,0:T(8,128)(2,1)} %orbit_cond.7) | copy-start | bytes 6291460
  20.3 44.2 %copy-start.3 = (bf16[2,128,512]{2,1,0:T(8,128)(2,1)S(1)}, bf16[2,128,512]{2,1,0:T(8,128)(2,1)}, u32[]{:S(2)}) copy-start(bf16[2,128,512]{2,1,0:T(8,128)(2,1)} %orbit_val.7) | copy-start | bytes 786436
  20.3 44.2 %copy-start.6 = (f32[2,1024]{1,0:T(2,128)S(1)}, f32[2,1024]{1,0:T(2,128)}, u32[]{:S(2)}) copy-start(f32[2,1024]{1,0:T(2,128)} %energy_cond.7) | copy-start | bytes 24580
  20.3 44.2 %copy-start.7 = (f32[2,128]{1,0:T(2,128)S(1)}, f32[2,128]{1,0:T(2,128)}, u32[]{:S(2)}) copy-start(f32[2,128]{1,0:T(2,128)} %energy_val.7) | copy-start | bytes 3076
  20.4 44.2 %copy-start.8 = (f32[4]{0:T(128)S(1)}, f32[4]{0:T(128)}, u32[]{:S(2)}) copy-start(f32[4]{0:T(128)} %freq_ref.7) | copy-start | bytes 52
  20.4 9.1 %collective-permute-start.2 = (f32[8,3,16,256]{3,2,1,0:T(8,128)S(1)}, f32[8,3,16,256]{3,2,1,0:T(8,128)S(1)}, u32[]{:S(2)}, u32[]{:S(2)}) collective-permute-start(f32[8,3,16,256]{3,2,1,0:T(8,128)S(1)} %add.88), channel_id=1, source_target_pairs={{0,24},{1,25},{2,26},{3,27},{4,28},{5,29},{6,30},{7,31},{8,16},{9,... | collective-permute-start | bytes 1179656 | tf_op jit(solution)/shard_map/ppermute | solution.py:37
  24.1 8.5 %collective-permute-start.14 = (f32[2,3,16,256]{3,2,1,0:T(8,128)S(1)}, f32[2,3,16,256]{3,2,1,0:T(8,128)S(1)}, u32[]{:S(2)}, u32[]{:S(2)}) collective-permute-start(f32[2,3,16,256]{3,2,1,0:T(8,128)S(1)} %get-tuple-element.28), channel_id=1, source_target_pairs={{0,8},{1,9},{2,10},{3,11},{4,12},{5,13},{6,14},{7,15},{8,0},{9,1},... | collective-permute-start | bytes 294920 | tf_op jit(solution)/shard_map/ppermute | solution.py:37
  25.1 9.7 %collective-permute-start.15 = (f32[2,3,16,256]{3,2,1,0:T(8,128)S(1)}, f32[2,3,16,256]{3,2,1,0:T(8,128)S(1)}, u32[]{:S(2)}, u32[]{:S(2)}) collective-permute-start(f32[2,3,16,256]{3,2,1,0:T(8,128)S(1)} %get-tuple-element.27), channel_id=1, source_target_pairs={{0,24},{1,25},{2,26},{3,27},{4,28},{5,29},{6,30},{7,31},{8,16},{9,... | collective-permute-start | bytes 294920 | tf_op jit(solution)/shard_map/ppermute | solution.py:37
  27.2 8.1 %collective-permute-start.16 = (f32[2,3,16,256]{3,2,1,0:T(8,128)S(1)}, f32[2,3,16,256]{3,2,1,0:T(8,128)S(1)}, u32[]{:S(2)}, u32[]{:S(2)}) collective-permute-start(f32[2,3,16,256]{3,2,1,0:T(8,128)S(1)} %get-tuple-element.26), channel_id=1, source_target_pairs={{0,16},{1,17},{2,18},{3,19},{4,20},{5,21},{6,22},{7,23},{8,24},{9,... | collective-permute-start | bytes 294920 | tf_op jit(solution)/shard_map/ppermute | solution.py:37
  29.6 7.7 %collective-permute-start.3 = (f32[2,3,16,256]{3,2,1,0:T(8,128)S(1)}, f32[2,3,16,256]{3,2,1,0:T(8,128)S(1)}, u32[]{:S(2)}, u32[]{:S(2)}) collective-permute-start(f32[2,3,16,256]{3,2,1,0:T(8,128)S(1)} %get-tuple-element.31), channel_id=1, source_target_pairs={{0,1},{1,0},{2,3},{3,2},{4,5},{5,4},{6,7},{7,6},{8,9},{9,8},{10,11... | collective-permute-start | bytes 294920 | tf_op jit(solution)/shard_map/ppermute | solution.py:37
  32.6 4.8 %collective-permute-start.4 = (f32[2,3,16,256]{3,2,1,0:T(8,128)S(1)}, f32[2,3,16,256]{3,2,1,0:T(8,128)S(1)}, u32[]{:S(2)}, u32[]{:S(2)}) collective-permute-start(f32[2,3,16,256]{3,2,1,0:T(8,128)S(1)} %get-tuple-element.30), channel_id=1, source_target_pairs={{0,3},{1,2},{2,1},{3,0},{4,7},{5,6},{6,5},{7,4},{8,11},{9,10},{10,... | collective-permute-start | bytes 294920 | tf_op jit(solution)/shard_map/ppermute | solution.py:37
  32.6 6.7 %collective-permute-start.5 = (f32[2,3,16,256]{3,2,1,0:T(8,128)S(1)}, f32[2,3,16,256]{3,2,1,0:T(8,128)S(1)}, u32[]{:S(2)}, u32[]{:S(2)}) collective-permute-start(f32[2,3,16,256]{3,2,1,0:T(8,128)S(1)} %get-tuple-element.29), channel_id=1, source_target_pairs={{0,2},{1,3},{2,0},{3,1},{4,6},{5,7},{6,4},{7,5},{8,10},{9,11},{10,... | collective-permute-start | bytes 294920 | tf_op jit(solution)/shard_map/ppermute | solution.py:37
  35.4 5.7 %collective-permute-start.17 = (f32[2,3,16,256]{3,2,1,0:T(8,128)S(1)}, f32[2,3,16,256]{3,2,1,0:T(8,128)S(1)}, u32[]{:S(2)}, u32[]{:S(2)}) collective-permute-start(f32[2,3,16,256]{3,2,1,0:T(8,128)S(1)} %fusion.1), channel_id=1, source_target_pairs={{0,4},{1,5},{2,6},{3,7},{4,0},{5,1},{6,2},{7,3},{8,12},{9,13},{10,... | collective-permute-start | bytes 294920 | tf_op jit(solution)/shard_map/ppermute | solution.py:37
  39.4 6.7 %collective-permute-start.6 = (f32[2,3,16,256]{3,2,1,0:T(8,128)S(1)}, f32[2,3,16,256]{3,2,1,0:T(8,128)S(1)}, u32[]{:S(2)}, u32[]{:S(2)}) collective-permute-start(f32[2,3,16,256]{3,2,1,0:T(8,128)S(1)} %fusion.3), channel_id=1, source_target_pairs={{0,4},{1,5},{2,6},{3,7},{4,0},{5,1},{6,2},{7,3},{8,12},{9,13},{10,... | collective-permute-start | bytes 294920 | tf_op jit(solution)/shard_map/ppermute | solution.py:37
  41.1 8.2 %collective-permute-start.18 = (f32[2,3,16,256]{3,2,1,0:T(8,128)S(1)}, f32[2,3,16,256]{3,2,1,0:T(8,128)S(1)}, u32[]{:S(2)}, u32[]{:S(2)}) collective-permute-start(f32[2,3,16,256]{3,2,1,0:T(8,128)S(1)} %add_multiply_fusion), channel_id=1, source_target_pairs={{0,24},{1,25},{2,26},{3,27},{4,28},{5,29},{6,30},{7,31},{8,16},{9,... | collective-permute-start | bytes 294920 | tf_op jit(solution)/shard_map/ppermute | solution.py:37
  43.8 6.3 %collective-permute-start.19 = (f32[2,3,16,256]{3,2,1,0:T(8,128)S(1)}, f32[2,3,16,256]{3,2,1,0:T(8,128)S(1)}, u32[]{:S(2)}, u32[]{:S(2)}) collective-permute-start(f32[2,3,16,256]{3,2,1,0:T(8,128)S(1)} %add_multiply_fusion), channel_id=1, source_target_pairs={{0,8},{1,9},{2,10},{3,11},{4,12},{5,13},{6,14},{7,15},{8,0},{9,1},... | collective-permute-start | bytes 294920 | tf_op jit(solution)/shard_map/ppermute | solution.py:37
  43.8 6.3 %collective-permute-start.20 = (f32[2,3,16,256]{3,2,1,0:T(8,128)S(1)}, f32[2,3,16,256]{3,2,1,0:T(8,128)S(1)}, u32[]{:S(2)}, u32[]{:S(2)}) collective-permute-start(f32[2,3,16,256]{3,2,1,0:T(8,128)S(1)} %add_multiply_fusion), channel_id=1, source_target_pairs={{0,16},{1,17},{2,18},{3,19},{4,20},{5,21},{6,22},{7,23},{8,24},{9,... | collective-permute-start | bytes 294920 | tf_op jit(solution)/shard_map/ppermute | solution.py:37
  46.1 7.4 %collective-permute-start.7 = (f32[2,3,16,256]{3,2,1,0:T(8,128)S(1)}, f32[2,3,16,256]{3,2,1,0:T(8,128)S(1)}, u32[]{:S(2)}, u32[]{:S(2)}) collective-permute-start(f32[2,3,16,256]{3,2,1,0:T(8,128)S(1)} %add_multiply_fusion.1), channel_id=1, source_target_pairs={{0,3},{1,2},{2,1},{3,0},{4,7},{5,6},{6,5},{7,4},{8,11},{9,10},{10,... | collective-permute-start | bytes 294920 | tf_op jit(solution)/shard_map/ppermute | solution.py:37
  47.9 5.6 %collective-permute-start.8 = (f32[2,3,16,256]{3,2,1,0:T(8,128)S(1)}, f32[2,3,16,256]{3,2,1,0:T(8,128)S(1)}, u32[]{:S(2)}, u32[]{:S(2)}) collective-permute-start(f32[2,3,16,256]{3,2,1,0:T(8,128)S(1)} %add_multiply_fusion.1), channel_id=1, source_target_pairs={{0,1},{1,0},{2,3},{3,2},{4,5},{5,4},{6,7},{7,6},{8,9},{9,8},{10,11... | collective-permute-start | bytes 294920 | tf_op jit(solution)/shard_map/ppermute | solution.py:37
  49.2 7.2 %collective-permute-start.9 = (f32[2,3,16,256]{3,2,1,0:T(8,128)S(1)}, f32[2,3,16,256]{3,2,1,0:T(8,128)S(1)}, u32[]{:S(2)}, u32[]{:S(2)}) collective-permute-start(f32[2,3,16,256]{3,2,1,0:T(8,128)S(1)} %add_multiply_fusion.1), channel_id=1, source_target_pairs={{0,2},{1,3},{2,0},{3,1},{4,6},{5,7},{6,4},{7,5},{8,10},{9,11},{10,... | collective-permute-start | bytes 294920 | tf_op jit(solution)/shard_map/ppermute | solution.py:37
  50.2 12.2 %collective-permute-start.24 = (f32[8,3,16,256]{3,2,1,0:T(8,128)S(1)}, f32[8,3,16,256]{3,2,1,0:T(8,128)S(1)}, u32[]{:S(2)}, u32[]{:S(2)}) collective-permute-start(f32[8,3,16,256]{3,2,1,0:T(8,128)S(1)} %pad_maximum_fusion.1.refs_1_), channel_id=1, source_target_pairs={{0,1},{1,0},{2,3},{3,2},{4,5},{5,4},{6,7},{7,6},{8,9},{9,8},{10,11... | collective-permute-start | bytes 1179656 | tf_op jit(solution)/shard_map/ppermute | solution.py:26
  52.6 10.1 %collective-permute-start.26 = (f32[8,3,16,256]{3,2,1,0:T(8,128)S(1)}, f32[8,3,16,256]{3,2,1,0:T(8,128)S(1)}, u32[]{:S(2)}, u32[]{:S(2)}) collective-permute-start(f32[8,3,16,256]{3,2,1,0:T(8,128)S(1)} %pad_maximum_fusion.1.refs_1_), channel_id=1, source_target_pairs={{0,3},{1,2},{2,1},{3,0},{4,7},{5,6},{6,5},{7,4},{8,11},{9,10},{10,... | collective-permute-start | bytes 1179656 | tf_op jit(solution)/shard_map/ppermute | solution.py:26
  56.5 10.4 %collective-permute-start.10 = (f32[8,3,16,256]{3,2,1,0:T(8,128)S(1)}, f32[8,3,16,256]{3,2,1,0:T(8,128)S(1)}, u32[]{:S(2)}, u32[]{:S(2)}) collective-permute-start(f32[8,3,16,256]{3,2,1,0:T(8,128)S(1)} %pad_maximum_fusion.refs_0_), channel_id=1, source_target_pairs={{0,8},{1,9},{2,10},{3,11},{4,12},{5,13},{6,14},{7,15},{8,0},{9,1},... | collective-permute-start | bytes 1179656 | tf_op jit(solution)/shard_map/ppermute | solution.py:26
  56.6 12.5 %collective-permute-start.22 = (f32[8,3,16,256]{3,2,1,0:T(8,128)S(1)}, f32[8,3,16,256]{3,2,1,0:T(8,128)S(1)}, u32[]{:S(2)}, u32[]{:S(2)}) collective-permute-start(f32[8,3,16,256]{3,2,1,0:T(8,128)S(1)} %pad_maximum_fusion.refs_0_), channel_id=1, source_target_pairs={{0,24},{1,25},{2,26},{3,27},{4,28},{5,29},{6,30},{7,31},{8,16},{9,... | collective-permute-start | bytes 1179656 | tf_op jit(solution)/shard_map/ppermute | solution.py:26
  62.4 11.0 %collective-permute-start.25 = (f32[4,3,16,256]{3,2,1,0:T(8,128)S(1)}, f32[4,3,16,256]{3,2,1,0:T(8,128)S(1)}, u32[]{:S(2)}, u32[]{:S(2)}) collective-permute-start(f32[4,3,16,256]{3,2,1,0:T(8,128)S(1)} %slice.129), channel_id=1, source_target_pairs={{0,3},{1,2},{2,1},{3,0},{4,7},{5,6},{6,5},{7,4},{8,11},{9,10},{10,... | collective-permute-start | bytes 589832 | tf_op jit(solution)/shard_map/ppermute | solution.py:26
  62.7 10.7 %collective-permute-start.27 = (f32[4,3,16,256]{3,2,1,0:T(8,128)S(1)}, f32[4,3,16,256]{3,2,1,0:T(8,128)S(1)}, u32[]{:S(2)}, u32[]{:S(2)}) collective-permute-start(f32[4,3,16,256]{3,2,1,0:T(8,128)S(1)} %slice.130), channel_id=1, source_target_pairs={{0,1},{1,0},{2,3},{3,2},{4,5},{5,4},{6,7},{7,6},{8,9},{9,8},{10,11... | collective-permute-start | bytes 589832 | tf_op jit(solution)/shard_map/ppermute | solution.py:26
  66.9 7.0 %collective-permute-start.21 = (f32[4,3,16,256]{3,2,1,0:T(8,128)S(1)}, f32[4,3,16,256]{3,2,1,0:T(8,128)S(1)}, u32[]{:S(2)}, u32[]{:S(2)}) collective-permute-start(f32[4,3,16,256]{3,2,1,0:T(8,128)S(1)} %slice.108), channel_id=1, source_target_pairs={{0,24},{1,25},{2,26},{3,27},{4,28},{5,29},{6,30},{7,31},{8,16},{9,... | collective-permute-start | bytes 589832 | tf_op jit(solution)/shard_map/ppermute | solution.py:26
  69.1 5.8 %collective-permute-start.23 = (f32[4,3,16,256]{3,2,1,0:T(8,128)S(1)}, f32[4,3,16,256]{3,2,1,0:T(8,128)S(1)}, u32[]{:S(2)}, u32[]{:S(2)}) collective-permute-start(f32[4,3,16,256]{3,2,1,0:T(8,128)S(1)} %slice.128), channel_id=1, source_target_pairs={{0,8},{1,9},{2,10},{3,11},{4,12},{5,13},{6,14},{7,15},{8,0},{9,1},... | collective-permute-start | bytes 589832 | tf_op jit(solution)/shard_map/ppermute | solution.py:26
  71.3 24.5 %copy-start.4 = (bf16[128,16384]{1,0:T(8,128)(2,1)S(1)}, bf16[128,16384]{1,0:T(8,128)(2,1)}, u32[]{:S(2)}) copy-start(bf16[128,16384]{1,0:T(8,128)(2,1)} %zeta.1) | copy-start | bytes 12582916
  77.2 1.5 %collective-permute-start.28 = (f32[16,256]{1,0:T(8,128)S(1)}, f32[16,256]{1,0:T(8,128)S(1)}, u32[]{:S(2)}, u32[]{:S(2)}) collective-permute-start(f32[16,256]{1,0:T(8,128)S(1)} %get-tuple-element.25), channel_id=1, source_target_pairs={{0,32},{32,0},{64,96},{96,64},{128,160},{160,128},{192,224},{224,1... | collective-permute-start | bytes 49160 | tf_op jit(solution)/shard_map/ppermute | solution.py:26
  97.1 1.2 %collective-permute-start.29 = (f32[16,128]{1,0:T(8,128)S(1)}, f32[16,128]{1,0:T(8,128)S(1)}, u32[]{:S(2)}, u32[]{:S(2)}) collective-permute-start(f32[16,128]{1,0:T(8,128)S(1)} %wing_sums.1), channel_id=1, source_target_pairs={{0,32},{32,0},{64,96},{96,64},{128,160},{160,128},{192,224},{224,1... | collective-permute-start | bytes 24584 | tf_op jit(solution)/shard_map/ppermute | solution.py:26
  98.3 4.9 %collective-permute-start.30 = (f32[16,128]{1,0:T(8,128)S(1)}, f32[16,128]{1,0:T(8,128)S(1)}, u32[]{:S(2)}, u32[]{:S(2)}) collective-permute-start(f32[16,128]{1,0:T(8,128)S(1)} %add.114), channel_id=1, source_target_pairs={{0,64},{32,96},{64,0},{96,32},{128,192},{160,224},{192,128},{224,1... | collective-permute-start | bytes 24584 | tf_op jit(solution)/shard_map/ppermute | solution.py:26
  103.2 6.8 %collective-permute-start.31 = (f32[16,128]{1,0:T(8,128)S(1)}, f32[16,128]{1,0:T(8,128)S(1)}, u32[]{:S(2)}, u32[]{:S(2)}) collective-permute-start(f32[16,128]{1,0:T(8,128)S(1)} %add.115.one), channel_id=1, source_target_pairs={{0,192},{32,224},{64,128},{96,160},{128,64},{160,96},{192,0},{224,... | collective-permute-start | bytes 24584 | tf_op jit(solution)/shard_map/ppermute | solution.py:26
